TPU v7x, 32 devices: a whole 2x2x4 slice. The times are simulated.
32 devices in a mesh: grp: 2 (over x), tile: 16 (over z, y, core).
Axes of the slice: x: 2, y: 2, z: 4, core: 2. Of those that a mesh axis runs over, the one named last changes fastest.
Arguments:
- ct_tracer: float32 [48, 256, 1280], P(None, ('grp', 'tile')), parts along dimension 1, may hold values from -6 to 6
- ct_surface: float32 [256, 1280], P(('grp', 'tile')), parts along dimension 0, may hold values from -6 to 6
- kappa: float32 [48, 128, 1280], P(None, 'tile'), may hold values from 0.02 to 0.2
- kvert: float32 [48, 128, 1280], P(None, 'tile'), may hold values from 0.1 to 10
- land: int32 [48, 128, 1280], P(None, 'tile'), may hold values 0 or 1
- kmt: int32 [128, 1280], P('tile'), may hold values from 24 to 48
- screen: float32 [128, 1280], P('tile'), may hold values from 0.05 to 1
- layer_weight: float32 [48], replicated, may hold values from 0.5 to 2
Outputs:
- adj_tracer: float32 [48, 256, 1280], P(None, ('grp', 'tile')), parts along dimension 1
- adj_surface: float32 [256, 1280], P(('grp', 'tile')), parts along dimension 0
There are 2 independent parts, one for each index of `grp`. A program takes and returns all parts, laid end to end along the dimension named above; an argument that names none is the same for every part. Nothing has to cross between parts.
All inputs are finite; a program needn't handle non-finite values. No bound on the sum of `land` on one device may be relied on, other than what follows from the above.
Results may differ from a plain program's by a relative error of at most 0.0001.
Values sent between devices are 32-bit elements; how exact they have to be, the bound alone decides.
No kernel may reach another device: no remote copies, remote signals or barrier semaphores. Data moves between devices by JAX's collectives and lax.ppermute only.
A program may use at most 64 MiB of HBM per device.

v0:
```python
import jax
import jax.numpy as jnp
from jax import lax
from jax.sharding import PartitionSpec as P

ITERS = 3
SUBSTEPS = 2


def extended(array, sides, width):
    for axis, dim in sides:
        count, length = (lax.axis_size(axis), array.shape[dim])
        up = [(i, (i + 1) % count) for i in range(count - 1)]
        down = [(j, i) for i, j in up]
        last = lax.slice_in_dim(array, length - width, length, axis=dim)
        leading = lax.slice_in_dim(array, 0, width, axis=dim)
        before = lax.ppermute(last, axis, up)
        after = lax.ppermute(leading, axis, down)
        array = jnp.concatenate([before, array, after], axis=dim)
    return array


def wet_cells(land, kmt):
    levels = jnp.arange(land.shape[0], dtype=jnp.int32)[:, None, None]
    return (land * (levels < kmt[None, :, :]).astype(jnp.int32)).astype(jnp.float32)


def solve_columns(source, coupling):
    depth_count = source.shape[0]
    ratios = []
    carried = []
    ratio_prev = jnp.zeros_like(source[0])
    carry_prev = jnp.zeros_like(source[0])
    above_link = jnp.zeros_like(source[0])
    for level_index in range(depth_count):
        divisor = 1.0 + coupling[level_index] + above_link + above_link * ratio_prev
        ratio_prev = -coupling[level_index] / divisor
        carry_prev = (source[level_index] + above_link * carry_prev) / divisor
        ratios.append(ratio_prev)
        carried.append(carry_prev)
        above_link = coupling[level_index]
    result = [carried[-1]]
    for level_index in range(depth_count - 2, -1, -1):
        result.append(carried[level_index] - ratios[level_index] * result[-1])
    return jnp.stack(result[::-1])


def vertical_coupling(kvert, wet):
    return kvert * wet * jnp.concatenate([wet[1:], jnp.zeros_like(wet[:1])], 0)


def diffuse_rows(padded, kap_pad, wet_pad):
    inner = padded[:, 1:-1]
    kap_own = kap_pad[:, 1:-1]
    wet_own = wet_pad[:, 1:-1]
    face_x = 0.5 * (kap_own + jnp.roll(kap_own, -1, 2)) * wet_own * jnp.roll(wet_own, -1, 2)
    flux_x = face_x * (jnp.roll(inner, -1, 2) - inner)
    face_y = 0.5 * (kap_pad[:, 1:] + kap_pad[:, :-1]) * wet_pad[:, 1:] * wet_pad[:, :-1]
    flux_y = face_y * (padded[:, 1:] - padded[:, :-1])
    return inner + flux_x - jnp.roll(flux_x, 1, 2) + flux_y[:, 1:] - flux_y[:, :-1]


def surface_apply(values, height_pad, surface_pad, screen):
    padded = extended(values, (("tile", 0),), 1)
    height_own = height_pad[1:-1]
    surface_own = surface_pad[1:-1]
    face_x = (
        0.5
        * (height_own + jnp.roll(height_own, -1, 1))
        * surface_own
        * jnp.roll(surface_own, -1, 1)
    )
    flux_x = face_x * (jnp.roll(values, -1, 1) - values)
    face_y = 0.5 * (height_pad[1:] + height_pad[:-1]) * surface_pad[1:] * surface_pad[:-1]
    flux_y = face_y * (padded[1:] - padded[:-1])
    return screen * values - (flux_x - jnp.roll(flux_x, 1, 1) + flux_y[1:] - flux_y[:-1])


def squares_total(residual):
    return lax.psum(jnp.sum(residual * residual), "tile")


def body(ct_tracer, ct_surface, kappa, kvert, land, kmt, screen, layer_weight):
    wet = wet_cells(land, kmt)
    share = layer_weight / jnp.sum(layer_weight)
    stacked = extended(jnp.stack([kappa, wet]), (("tile", 2),), 1)
    kap_pad = stacked[0]
    wet_pad = stacked[1]
    height_pad = jnp.sum(share[:, None, None] * wet_pad, axis=0)
    surface_pad = wet_pad[0]
    solution = jnp.zeros_like(ct_surface)
    residual = ct_surface
    direction = residual
    norm_now = squares_total(residual)
    for iteration in range(ITERS):
        image = surface_apply(direction, height_pad, surface_pad, screen)
        alpha = norm_now / lax.psum(jnp.sum(direction * image), "tile")
        solution = solution + alpha * direction
        residual = residual - alpha * image
        if iteration + 1 < ITERS:
            norm_next = squares_total(residual)
            direction = residual + norm_next / norm_now * direction
            norm_now = norm_next
    column = ct_tracer + wet * share[:, None, None] * solution[None]
    values = solve_columns(column, vertical_coupling(kvert, wet))
    remaining = SUBSTEPS
    for sub_index in range(remaining):
        padded = extended(values, (("tile", 1),), 1)
        values = diffuse_rows(padded, kap_pad, wet_pad)
    return (values, solution)


def solution(mesh):
    in_specs = (
        P(None, ("grp", "tile"), None),
        P(("grp", "tile"), None),
        P(None, "tile", None),
        P(None, "tile", None),
        P(None, "tile", None),
        P("tile", None),
        P("tile", None),
        P(),
    )
    out_specs = (P(None, ("grp", "tile"), None), P(("grp", "tile"), None))
    return jax.shard_map(body, mesh=mesh, in_specs=in_specs, out_specs=out_specs, check_vma=False)
```

profile of v0, /device:TPU:1, one launch (start us, length us, event | category | flops | bytes accessed | tf_op | source)
XLA Modules:
  0.0 251.6 jit_solution(17652497359496416036)
XLA Ops:
  0.6 1.9 fusion.248
  2.8 1.4 pad_maximum_fusion.1
  4.2 4.5 %collective-permute-start = (f32[2,48,1,1280]{3,2,1,0:T(1,128)}, f32[2,48,1,1280]{3,2,1,0:T(1,128)S(1)}, u32[]{:S(2)}, u32[]{:S(2)}) collective-permute-start(f32[2,48,1,1280]{3,2,1,0:T(1,128)} %get-tuple-element.136), channel_id=1, source_target_pairs={{0,1},{1,2},{2,3},{3,4},{4,5},{5,6},{6,7},{7,8},{8,9},{9,10},{10,1... | collective-permute-start | bytes 1474568 | tf_op jit(solution)/shard_map/ppermute | solution.py:17
  8.7 1.9 collective-permute-start.1
  10.6 0.6 fusion.247
  11.2 1.9 collective-permute-start.2
  13.2 3.6 %collective-permute-start.3 = (f32[1,1280]{1,0:T(1,128)S(1)}, f32[1,1280]{1,0:T(1,128)S(1)}, u32[]{:S(2)}, u32[]{:S(2)}) collective-permute-start(f32[1,1280]{1,0:T(1,128)S(1)} %get-tuple-element.147), channel_id=1, source_target_pairs={{0,1},{1,2},{2,3},{3,4},{4,5},{5,6},{6,7},{7,8},{8,9},{9,10},{10,1... | collective-permute-start | bytes 15368 | tf_op jit(solution)/shard_map/ppermute | solution.py:17
  17.0 0.7 slice.829
  17.7 0.7 slice.670
  18.4 1.4 slice.854
  21.0 2.8 %pad_maximum_fusion = f32[2,48,10,1280]{3,2,1,0:T(8,128)S(1)} fusion(f32[2,48,1,1280]{3,2,1,0:T(1,128)S(1)} %collective-permute-done.1, f32[1,48,8,1280]{3,2,1,0:T(8,128)S(1)} %fusion.248, f32[1,48,8,1280]{3,2,1,0:T(8,128)} %bitcast.1782, f32[2,48,1,1280]{3,2,1,0:T(1,128)S(1)} %collective-permute-done), kind=kLoop, calls=%fused_computation | loop fusion | flops 3686400 | bytes 9830400 | tf_op jit(solution)/shard_map/concatenate | solution.py:19
  23.8 3.0 %copy-done.3 = f32[2,48,10,1280]{3,2,1,0:T(8,128)} copy-done((f32[2,48,10,1280]{3,2,1,0:T(8,128)}, f32[2,48,10,1280]{3,2,1,0:T(8,128)S(1)}, u32[]{:S(2)}) %copy-start.3) | copy-done | bytes 4915224
  27.9 0.6 copy-done.5
  28.8 0.7 multiply_reduce_fusion.4
  29.5 29.1 %all-reduce.1 = (f32[]{:T(128)}, f32[]{:T(128)}) all-reduce(f32[]{:T(128)} %get-tuple-element.3, f32[]{:T(128)} %get-tuple-element.2), channel_id=1, replica_groups=mesh['grp'=2,'tile'=16] {'tile'}, use_global_device_ids=true, to_apply=%region_2.0 | all-reduce | flops 2 | bytes 16 | tf_op jit(solution)/shard_map/psum | solution.py:80
  59.9 0.6 multiply_reduce_fusion.3
  60.5 33.4 %psum.44 = f32[]{:T(128)} all-reduce(f32[]{:T(128)} %get-tuple-element.126), channel_id=1, replica_groups=mesh['grp'=2,'tile'=16] {'tile'}, use_global_device_ids=true, to_apply=%region_7.8 | all-reduce | flops 1 | bytes 8 | tf_op jit(solution)/shard_map/psum | solution.py:80
  95.3 5.8 %slice_bitcast_fusion = (f32[48,10,1280]{2,1,0:T(8,128)S(1)}, f32[48,10,1280]{2,1,0:T(8,128)}) fusion(f32[2,48,10,1280]{3,2,1,0:T(8,128)} %copy-done.3), kind=kLoop, calls=%fused_computation.5 | loop fusion | bytes 9830400 | tf_op jit(solution)/shard_map/squeeze | solution.py:87
  101.1 2.5 %collective-permute-start.4 = (f32[1,1280]{1,0:T(1,128)S(1)}, f32[1,1280]{1,0:T(1,128)S(1)}, u32[]{:S(2)}, u32[]{:S(2)}) collective-permute-start(f32[1,1280]{1,0:T(1,128)S(1)} %get-tuple-element.146), channel_id=1, source_target_pairs={{1,0},{2,1},{3,2},{4,3},{5,4},{6,5},{7,6},{8,7},{9,8},{10,9},{11,1... | collective-permute-start | bytes 15368 | tf_op jit(solution)/shard_map/ppermute | solution.py:18
  103.6 3.0 %collective-permute-start.5 = (f32[1,1280]{1,0:T(1,128)S(1)}, f32[1,1280]{1,0:T(1,128)S(1)}, u32[]{:S(2)}, u32[]{:S(2)}) collective-permute-start(f32[1,1280]{1,0:T(1,128)S(1)} %get-tuple-element.145), channel_id=1, source_target_pairs={{0,1},{1,2},{2,3},{3,4},{4,5},{5,6},{6,7},{7,8},{8,9},{9,10},{10,1... | collective-permute-start | bytes 15368 | tf_op jit(solution)/shard_map/ppermute | solution.py:17
  106.7 1.9 slice.952
  108.7 0.8 multiply_reduce_fusion.2
  109.5 28.9 %psum.45 = f32[]{:T(128)} all-reduce(f32[]{:T(128)} %get-tuple-element.124), channel_id=1, replica_groups=mesh['grp'=2,'tile'=16] {'tile'}, use_global_device_ids=true, to_apply=%region_9.10 | all-reduce | flops 1 | bytes 8 | tf_op jit(solution)/shard_map/psum | solution.py:97
  139.7 0.6 multiply_reduce_fusion.1
  140.4 4.1 %slice.955 = f32[48,8,1279]{2,1,0:T(8,128)} slice(f32[48,10,1280]{2,1,0:T(8,128)} %get-tuple-element.134), slice={[0:48], [1:9], [1:1280]} | slice | bytes 3929088 | tf_op jit(solution)/shard_map/jit(_roll_static)/slice | solution.py:56
  144.5 31.2 %psum.46 = f32[]{:T(128)} all-reduce(f32[]{:T(128)} %multiply_reduce_fusion.1), channel_id=1, replica_groups=mesh['grp'=2,'tile'=16] {'tile'}, use_global_device_ids=true, to_apply=%region_11.12 | all-reduce | flops 1 | bytes 8 | tf_op jit(solution)/shard_map/psum | solution.py:80
  177.1 2.6 %collective-permute-start.6 = (f32[1,1280]{1,0:T(1,128)S(1)}, f32[1,1280]{1,0:T(1,128)S(1)}, u32[]{:S(2)}, u32[]{:S(2)}) collective-permute-start(f32[1,1280]{1,0:T(1,128)S(1)} %get-tuple-element.144), channel_id=1, source_target_pairs={{1,0},{2,1},{3,2},{4,3},{5,4},{6,5},{7,6},{8,7},{9,8},{10,9},{11,1... | collective-permute-start | bytes 15368 | tf_op jit(solution)/shard_map/ppermute | solution.py:18
  179.7 3.0 %collective-permute-start.7 = (f32[1,1280]{1,0:T(1,128)S(1)}, f32[1,1280]{1,0:T(1,128)S(1)}, u32[]{:S(2)}, u32[]{:S(2)}) collective-permute-start(f32[1,1280]{1,0:T(1,128)S(1)} %get-tuple-element.143), channel_id=1, source_target_pairs={{0,1},{1,2},{2,3},{3,4},{4,5},{5,6},{6,7},{7,8},{8,9},{9,10},{10,1... | collective-permute-start | bytes 15368 | tf_op jit(solution)/shard_map/ppermute | solution.py:17
  183.4 0.7 fusion.17
  184.1 1.0 slice.956
  185.2 29.0 %psum.47 = f32[]{:T(128)} all-reduce(f32[]{:T(128)} %fusion.17), channel_id=1, replica_groups=mesh['grp'=2,'tile'=16] {'tile'}, use_global_device_ids=true, to_apply=%region_13.14 | all-reduce | flops 1 | bytes 8 | tf_op jit(solution)/shard_map/psum | solution.py:97
  215.5 3.3 %multiply_add_fusion = (f32[48,8,1280]{2,1,0:T(8,128)S(1)}, f32[48,8,1280]{2,1,0:T(8,128)S(1)}) fusion(f32[48,8,1280]{2,1,0:T(8,128)} %param.8, f32[8,1280]{1,0:T(8,128)S(1)} %multiply_add_fusion.42, f32[48]{0:T(128)S(1)} %broadcast_divide_fusion, f32[47,8,1280]{2,1,0:T(8,128)} %slice.854, f32[48,8,1280]{2,1,0:T(8,128)} %param.11, ...), kind=kLoop, calls=%fused_computation.27 | loop fusion | flops 3932160 | bytes 11837632 | tf_op jit(solution)/shard_map/add | solution.py:104
  218.9 0.9 fusion.35
  219.8 0.8 add_divide_fusion.1
  222.0 1.8 slice.957
  223.8 0.7 slice.958
  224.5 1.1 fusion.244
  225.6 3.6 %collective-permute-start.8 = (f32[48,1,1280]{2,1,0:T(1,128)}, f32[48,1,1280]{2,1,0:T(1,128)}, u32[]{:S(2)}, u32[]{:S(2)}) collective-permute-start(f32[48,1,1280]{2,1,0:T(1,128)} %get-tuple-element.140), channel_id=1, source_target_pairs={{1,0},{2,1},{3,2},{4,3},{5,4},{6,5},{7,6},{8,7},{9,8},{10,9},{11,1... | collective-permute-start | bytes 737288 | tf_op jit(solution)/shard_map/ppermute | solution.py:18
  229.2 2.2 collective-permute-start.9
  231.4 4.1 %fusion.5 = (f32[48,8,1280]{2,1,0:T(8,128)S(1)}, f32[48,8,1280]{2,1,0:T(8,128)}) fusion(f32[48,8,1280]{2,1,0:T(8,128)S(1)} %constant_dynamic-update-slice_fusion, f32[48,8,1]{2,1,0:T(8,128)} %slice.958, f32[48,8,1279]{2,1,0:T(8,128)} %slice.957, f32[48,8,1]{2,1,0:T(8,128)S(1)} %slice.956, f32[48,8,1279]{2,1,0:T(8,128)S(1)} %copy-done.9, ...), kind=kLoop, calls=%fused_computation.21 | loop fusion | flops 4423680 | bytes 15728640 | tf_op jit(solution)/shard_map/mul | solution.py:57
  235.6 2.9 %fusion.1 = (f32[48,9,1280]{2,1,0:T(8,128)S(1)}, f32[48,9,1280]{2,1,0:T(8,128)S(1)}) fusion(f32[48,1,1280]{2,1,0:T(1,128)} %collective-permute-done.8, f32[48,8,1280]{2,1,0:T(8,128)S(1)} %constant_dynamic-update-slice_fusion, f32[48,1,1280]{2,1,0:T(1,128)} %collective-permute-done.9, f32[48,10,1280]{2,1,0:T(8,128)S(1)} %copy-done.2, ...), kind=kLoop, calls=%fused_computation.8 | loop fusion | flops 4423680 | bytes 15728640 | tf_op jit(solution)/shard_map/mul | solution.py:59
  238.5 0.7 slice_subtract_fusion.1
  240.1 2.8 %collective-permute-start.10 = (f32[48,1,1280]{2,1,0:T(1,128)S(1)}, f32[48,1,1280]{2,1,0:T(1,128)S(1)}, u32[]{:S(2)}, u32[]{:S(2)}) collective-permute-start(f32[48,1,1280]{2,1,0:T(1,128)S(1)} %get-tuple-element.138), channel_id=1, source_target_pairs={{1,0},{2,1},{3,2},{4,3},{5,4},{6,5},{7,6},{8,7},{9,8},{10,9},{11,1... | collective-permute-start | bytes 737288 | tf_op jit(solution)/shard_map/ppermute | solution.py:18
  243.0 2.7 %collective-permute-start.11 = (f32[48,1,1280]{2,1,0:T(1,128)S(1)}, f32[48,1,1280]{2,1,0:T(1,128)S(1)}, u32[]{:S(2)}, u32[]{:S(2)}) collective-permute-start(f32[48,1,1280]{2,1,0:T(1,128)S(1)} %get-tuple-element.137), channel_id=1, source_target_pairs={{0,1},{1,2},{2,3},{3,4},{4,5},{5,6},{6,7},{7,8},{8,9},{9,10},{10,1... | collective-permute-start | bytes 737288 | tf_op jit(solution)/shard_map/ppermute | solution.py:17
  246.2 1.4 collective-permute-done.10
  247.6 1.2 collective-permute-done.11
  248.8 0.9 fusion.2
  249.7 1.9 slice_subtract_fusion
  (133 shorter events, 6.7 us)
Async XLA Ops:
  0.6 2.2 copy-start.4
  2.8 7.8 %copy-start.11 = (f32[8,1280]{1,0:T(8,128)S(1)}, f32[8,1280]{1,0:T(8,128)}, u32[]{:S(2)}) copy-start(f32[8,1280]{1,0:T(8,128)} %param.9) | copy-start | bytes 122884
  2.8 14.0 %copy-start.6 = (s32[48,8,1280]{2,1,0:T(8,128)S(1)}, s32[48,8,1280]{2,1,0:T(8,128)}, u32[]{:S(2)}) copy-start(s32[48,8,1280]{2,1,0:T(8,128)} %param.12) | copy-start | bytes 5898244
  2.8 14.0 %copy-start.14 = (s32[8,1280]{1,0:T(8,128)S(1)}, s32[8,1280]{1,0:T(8,128)}, u32[]{:S(2)}) copy-start(s32[8,1280]{1,0:T(8,128)} %param.13) | copy-start | bytes 122884
  4.2 16.8 %collective-permute-start = (f32[2,48,1,1280]{3,2,1,0:T(1,128)}, f32[2,48,1,1280]{3,2,1,0:T(1,128)S(1)}, u32[]{:S(2)}, u32[]{:S(2)}) collective-permute-start(f32[2,48,1,1280]{3,2,1,0:T(1,128)} %get-tuple-element.136), channel_id=1, source_target_pairs={{0,1},{1,2},{2,3},{3,4},{4,5},{5,6},{6,7},{7,8},{8,9},{9,10},{10,1... | collective-permute-start | bytes 1474568 | tf_op jit(solution)/shard_map/ppermute | solution.py:17
  8.7 12.3 %collective-permute-start.1 = (f32[2,48,1,1280]{3,2,1,0:T(1,128)S(1)}, f32[2,48,1,1280]{3,2,1,0:T(1,128)S(1)}, u32[]{:S(2)}, u32[]{:S(2)}) collective-permute-start(f32[2,48,1,1280]{3,2,1,0:T(1,128)S(1)} %get-tuple-element.135), channel_id=1, source_target_pairs={{1,0},{2,1},{3,2},{4,3},{5,4},{6,5},{7,6},{8,7},{9,8},{10,9},{11,1... | collective-permute-start | bytes 1474568 | tf_op jit(solution)/shard_map/ppermute | solution.py:18
  11.2 16.6 %collective-permute-start.2 = (f32[1,1280]{1,0:T(1,128)}, f32[1,1280]{1,0:T(1,128)S(1)}, u32[]{:S(2)}, u32[]{:S(2)}) collective-permute-start(f32[1,1280]{1,0:T(1,128)} %get-tuple-element.148), channel_id=1, source_target_pairs={{1,0},{2,1},{3,2},{4,3},{5,4},{6,5},{7,6},{8,7},{9,8},{10,9},{11,1... | collective-permute-start | bytes 15368 | tf_op jit(solution)/shard_map/ppermute | solution.py:18
  13.2 14.7 %collective-permute-start.3 = (f32[1,1280]{1,0:T(1,128)S(1)}, f32[1,1280]{1,0:T(1,128)S(1)}, u32[]{:S(2)}, u32[]{:S(2)}) collective-permute-start(f32[1,1280]{1,0:T(1,128)S(1)} %get-tuple-element.147), channel_id=1, source_target_pairs={{0,1},{1,2},{2,3},{3,4},{4,5},{5,6},{6,7},{7,8},{8,9},{9,10},{10,1... | collective-permute-start | bytes 15368 | tf_op jit(solution)/shard_map/ppermute | solution.py:17
  17.0 0.7 copy-start.15
  17.7 2.1 copy-start.19
  23.8 3.0 %copy-start.3 = (f32[2,48,10,1280]{3,2,1,0:T(8,128)}, f32[2,48,10,1280]{3,2,1,0:T(8,128)S(1)}, u32[]{:S(2)}) copy-start(f32[2,48,10,1280]{3,2,1,0:T(8,128)S(1)} %pad_maximum_fusion) | copy-start | bytes 14745604
  26.9 0.8 copy-start.12
  26.9 0.8 slice-start
  26.9 0.8 slice-start.1
  26.9 0.8 copy-start.16
  26.9 0.8 copy-start.17
  26.9 1.6 copy-start.5
  27.9 0.9 copy-start.13
  101.1 7.5 %copy-start = (f32[48,10,1280]{2,1,0:T(8,128)}, f32[48,10,1280]{2,1,0:T(8,128)S(1)}, u32[]{:S(2)}) copy-start(f32[48,10,1280]{2,1,0:T(8,128)S(1)} %get-tuple-element.133) | copy-start | bytes 7372804
  101.1 7.6 %collective-permute-start.4 = (f32[1,1280]{1,0:T(1,128)S(1)}, f32[1,1280]{1,0:T(1,128)S(1)}, u32[]{:S(2)}, u32[]{:S(2)}) collective-permute-start(f32[1,1280]{1,0:T(1,128)S(1)} %get-tuple-element.146), channel_id=1, source_target_pairs={{1,0},{2,1},{3,2},{4,3},{5,4},{6,5},{7,6},{8,7},{9,8},{10,9},{11,1... | collective-permute-start | bytes 15368 | tf_op jit(solution)/shard_map/ppermute | solution.py:18
  103.6 5.1 %collective-permute-start.5 = (f32[1,1280]{1,0:T(1,128)S(1)}, f32[1,1280]{1,0:T(1,128)S(1)}, u32[]{:S(2)}, u32[]{:S(2)}) collective-permute-start(f32[1,1280]{1,0:T(1,128)S(1)} %get-tuple-element.145), channel_id=1, source_target_pairs={{0,1},{1,2},{2,3},{3,4},{4,5},{5,6},{6,7},{7,8},{8,9},{9,10},{10,1... | collective-permute-start | bytes 15368 | tf_op jit(solution)/shard_map/ppermute | solution.py:17
  140.4 75.1 %copy-start.7 = (s32[48,8,1280]{2,1,0:T(8,128)S(1)}, s32[48,8,1280]{2,1,0:T(8,128)}, u32[]{:S(2)}) copy-start(s32[48,8,1280]{2,1,0:T(8,128)} %param.12) | copy-start | bytes 5898244
  177.1 5.7 %collective-permute-start.6 = (f32[1,1280]{1,0:T(1,128)S(1)}, f32[1,1280]{1,0:T(1,128)S(1)}, u32[]{:S(2)}, u32[]{:S(2)}) collective-permute-start(f32[1,1280]{1,0:T(1,128)S(1)} %get-tuple-element.144), channel_id=1, source_target_pairs={{1,0},{2,1},{3,2},{4,3},{5,4},{6,5},{7,6},{8,7},{9,8},{10,9},{11,1... | collective-permute-start | bytes 15368 | tf_op jit(solution)/shard_map/ppermute | solution.py:18
  179.7 3.8 %collective-permute-start.7 = (f32[1,1280]{1,0:T(1,128)S(1)}, f32[1,1280]{1,0:T(1,128)S(1)}, u32[]{:S(2)}, u32[]{:S(2)}) collective-permute-start(f32[1,1280]{1,0:T(1,128)S(1)} %get-tuple-element.143), channel_id=1, source_target_pairs={{0,1},{1,2},{2,3},{3,4},{4,5},{5,6},{6,7},{7,8},{8,9},{9,10},{10,1... | collective-permute-start | bytes 15368 | tf_op jit(solution)/shard_map/ppermute | solution.py:17
  215.5 3.3 %copy-start.18 = (f32[8,1280]{1,0:T(8,128)}, f32[8,1280]{1,0:T(8,128)S(1)}, u32[]{:S(2)}) copy-start(f32[8,1280]{1,0:T(8,128)S(1)} %multiply_add_fusion.42) | copy-start | bytes 122884
  220.6 10.8 %copy-start.9 = (f32[48,8,1279]{2,1,0:T(8,128)S(1)}, f32[48,8,1279]{2,1,0:T(8,128)}, u32[]{:S(2)}) copy-start(f32[48,8,1279]{2,1,0:T(8,128)} %slice.955) | copy-start | bytes 5893636
  221.3 10.0 %copy-start.8 = (f32[48,8,1279]{2,1,0:T(8,128)S(1)}, f32[48,8,1279]{2,1,0:T(8,128)}, u32[]{:S(2)}) copy-start(f32[48,8,1279]{2,1,0:T(8,128)} %slice.952) | copy-start | bytes 5893636
  221.6 9.7 %copy-start.2 = (f32[48,10,1280]{2,1,0:T(8,128)S(1)}, f32[48,10,1280]{2,1,0:T(8,128)}, u32[]{:S(2)}) copy-start(f32[48,10,1280]{2,1,0:T(8,128)} %get-tuple-element.134) | copy-start | bytes 7372804
  222.0 9.4 %copy-start.1 = (f32[48,10,1280]{2,1,0:T(8,128)S(1)}, f32[48,10,1280]{2,1,0:T(8,128)}, u32[]{:S(2)}) copy-start(f32[48,10,1280]{2,1,0:T(8,128)} %copy-done) | copy-start | bytes 7372804
  225.6 10.0 %collective-permute-start.8 = (f32[48,1,1280]{2,1,0:T(1,128)}, f32[48,1,1280]{2,1,0:T(1,128)}, u32[]{:S(2)}, u32[]{:S(2)}) collective-permute-start(f32[48,1,1280]{2,1,0:T(1,128)} %get-tuple-element.140), channel_id=1, source_target_pairs={{1,0},{2,1},{3,2},{4,3},{5,4},{6,5},{7,6},{8,7},{9,8},{10,9},{11,1... | collective-permute-start | bytes 737288 | tf_op jit(solution)/shard_map/ppermute | solution.py:18
  229.2 6.4 %collective-permute-start.9 = (f32[48,1,1280]{2,1,0:T(1,128)}, f32[48,1,1280]{2,1,0:T(1,128)}, u32[]{:S(2)}, u32[]{:S(2)}) collective-permute-start(f32[48,1,1280]{2,1,0:T(1,128)} %get-tuple-element.139), channel_id=1, source_target_pairs={{0,1},{1,2},{2,3},{3,4},{4,5},{5,6},{6,7},{7,8},{8,9},{9,10},{10,1... | collective-permute-start | bytes 737288 | tf_op jit(solution)/shard_map/ppermute | solution.py:17
  239.2 6.5 %copy-start.10 = (f32[48,8,1280]{2,1,0:T(8,128)S(1)}, f32[48,8,1280]{2,1,0:T(8,128)}, u32[]{:S(2)}) copy-start(f32[48,8,1280]{2,1,0:T(8,128)} %get-tuple-element.7) | copy-start | bytes 5898244
  240.1 7.5 %collective-permute-start.10 = (f32[48,1,1280]{2,1,0:T(1,128)S(1)}, f32[48,1,1280]{2,1,0:T(1,128)S(1)}, u32[]{:S(2)}, u32[]{:S(2)}) collective-permute-start(f32[48,1,1280]{2,1,0:T(1,128)S(1)} %get-tuple-element.138), channel_id=1, source_target_pairs={{1,0},{2,1},{3,2},{4,3},{5,4},{6,5},{7,6},{8,7},{9,8},{10,9},{11,1... | collective-permute-start | bytes 737288 | tf_op jit(solution)/shard_map/ppermute | solution.py:18
  243.0 5.8 %collective-permute-start.11 = (f32[48,1,1280]{2,1,0:T(1,128)S(1)}, f32[48,1,1280]{2,1,0:T(1,128)S(1)}, u32[]{:S(2)}, u32[]{:S(2)}) collective-permute-start(f32[48,1,1280]{2,1,0:T(1,128)S(1)} %get-tuple-element.137), channel_id=1, source_target_pairs={{0,1},{1,2},{2,3},{3,4},{4,5},{5,6},{6,7},{7,8},{8,9},{9,10},{10,1... | collective-permute-start | bytes 737288 | tf_op jit(solution)/shard_map/ppermute | solution.py:17
where the time goes:
time: 252 us
  blocking collectives  152 us (60%)
  starting transfers between devices  34.4 us (14%)
  other arithmetic  28.4 us (11%)
  local copies, waits for them, and re-layouts  26.1 us (10%)
  between operations  8.03 us (3%)
  waiting for transfers between devices  3.19 us (1%)
    psum x3, blocking collectives, squares_total(): return lax.psum(jnp.sum(residual * residual), 'tile')  93.7 us
    psum x2, blocking collectives, body(): alpha = norm_now / lax.psum(jnp.sum(direction * image), 'tile')  57.8 us
    ppermute x6, starting transfers between devices, extended(): before = lax.ppermute(last, axis, up)  19.1 us
    ppermute x6, starting transfers between devices, extended(): after = lax.ppermute(leading, axis, down)  15.3 us
    squeeze x1, local copies, waits for them, and re-layouts, body(): kap_pad = stacked[0]  5.79 us
    slice x2, local copies, waits for them, and re-layouts, diffuse_rows(): jnp.roll(wet_own, -1, 2)  5.14 us
  transfers between devices with their start and end apart: 12, of which 3 were waited for; matrix products, arithmetic and copies ran while one was open for 6% of the time, Pallas kernels for 0%

commit v1 on v0

--- a/solution.py
+++ b/solution.py
@@ -60,47 +60,84 @@
     return inner + flux_x - jnp.roll(flux_x, 1, 2) + flux_y[:, 1:] - flux_y[:, :-1]
 
 
-def surface_apply(values, height_pad, surface_pad, screen):
-    padded = extended(values, (("tile", 0),), 1)
-    height_own = height_pad[1:-1]
-    surface_own = surface_pad[1:-1]
-    face_x = (
-        0.5
-        * (height_own + jnp.roll(height_own, -1, 1))
-        * surface_own
-        * jnp.roll(surface_own, -1, 1)
-    )
-    flux_x = face_x * (jnp.roll(values, -1, 1) - values)
-    face_y = 0.5 * (height_pad[1:] + height_pad[:-1]) * surface_pad[1:] * surface_pad[:-1]
-    flux_y = face_y * (padded[1:] - padded[:-1])
-    return screen * values - (flux_x - jnp.roll(flux_x, 1, 1) + flux_y[1:] - flux_y[:-1])
+LOW = 0.05
+HIGH = 9.0
+MID = 0.5 * (HIGH + LOW)
+HALF = 0.5 * (HIGH - LOW)
 
 
-def squares_total(residual):
-    return lax.psum(jnp.sum(residual * residual), "tile")
+def neighbours(array, width):
+    count = lax.axis_size("tile")
+    up = [(i, i + 1) for i in range(count - 1)]
+    down = [(i + 1, i) for i in range(count - 1)]
+    return lax.ppermute(array[-width:], "tile", up), lax.ppermute(array[:width], "tile", down)
+
+
+def surface_image(values, height, surface, screen):
+    face_x = 0.5 * (height + jnp.roll(height, -1, 1)) * surface * jnp.roll(surface, -1, 1)
+    flux_x = face_x * (jnp.roll(values, -1, 1) - values)
+    face_y = 0.5 * (height[1:] + height[:-1]) * surface[1:] * surface[:-1]
+    flux_y = face_y * (values[1:] - values[:-1])
+    across = flux_x - jnp.roll(flux_x, 1, 1)
+    return screen[1:-1] * values[1:-1] - (across[1:-1] + flux_y[1:] - flux_y[:-1])
+
+
+def quadratic(left, form):
+    return sum(left[i] * left[j] * form[i][j] for i in range(3) for j in range(3))
+
+
+def weights(sums):
+    s0, s1, s2, s3, s4, s5 = sums
+    g02 = 2.0 * s2 - s0
+    gram = ((s0, s1, g02), (s1, s2, s3), (g02, s3, s4))
+    shift = ((s1, s2, s3), (s2, 0.5 * (s3 + s1), 0.5 * (s4 + g02)), (s3, 0.5 * (s4 + g02), s5))
+    form = [[MID * gram[i][j] + HALF * shift[i][j] for j in range(3)] for i in range(3)]
+    one, zero = jnp.ones_like(s0), jnp.zeros_like(s0)
+    x, r, d = [zero] * 3, [one, zero, zero], [one, zero, zero]
+    rr = s0
+    for step in range(ITERS):
+        alpha = jnp.clip(rr / quadratic(d, form), 1.0 / HIGH, 1.0 / LOW)
+        x = [x[i] + alpha * d[i] for i in range(3)]
+        if step + 1 < ITERS:
+            image = [
+                MID * d[0] + HALF * 0.5 * d[1],
+                MID * d[1] + HALF * (d[0] + 0.5 * d[2]),
+                MID * d[2] + HALF * 0.5 * d[1],
+            ]
+            r = [r[i] - alpha * image[i] for i in range(3)]
+            new = quadratic(r, gram)
+            beta = jnp.clip(new / rr, 0.0, HIGH / LOW)
+            d = [r[i] + beta * d[i] for i in range(3)]
+            rr = new
+    return x
 
 
 def body(ct_tracer, ct_surface, kappa, kvert, land, kmt, screen, layer_weight):
     wet = wet_cells(land, kmt)
     share = layer_weight / jnp.sum(layer_weight)
+    height = jnp.sum(share[:, None, None] * wet, axis=0)
+    own = jnp.stack([ct_surface, height, wet[0], screen], 1)
+    before, after = neighbours(own, 3)
+    rows = jnp.concatenate([before, own, after], 0)
+    base0, high_ext, surf_ext, screen_ext = (rows[:, i] for i in range(4))
+
+    def shifted(values, cut):
+        cut_rows = slice(cut, rows.shape[0] - cut)
+        image = surface_image(values, high_ext[cut_rows], surf_ext[cut_rows], screen_ext[cut_rows])
+        return (image - MID * values[1:-1]) / HALF
+
+    base1 = shifted(base0, 0)
+    base2 = 2.0 * shifted(base1, 1) - base0[2:-2]
+    next2 = shifted(base2, 2)
+    b0, b1, b2 = base0[3:-3], base1[2:-2], base2[1:-1]
+    partial = jnp.stack([jnp.sum(p * q) for p, q in ((b0, b0), (b0, b1), (b1, b1), (b1, b2), (b2, b2), (b2, next2))])
+    count = lax.axis_size("tile")
+    spread = jnp.broadcast_to(jnp.pad(partial, (0, 122))[None], (count, 128))
+    total = jnp.sum(lax.all_to_all(spread, "tile", 0, 0, tiled=True), 0)
+    mix = weights([total[i] for i in range(6)])
+    solution = mix[0] * b0 + mix[1] * b1 + mix[2] * b2
     stacked = extended(jnp.stack([kappa, wet]), (("tile", 2),), 1)
-    kap_pad = stacked[0]
-    wet_pad = stacked[1]
-    height_pad = jnp.sum(share[:, None, None] * wet_pad, axis=0)
-    surface_pad = wet_pad[0]
-    solution = jnp.zeros_like(ct_surface)
-    residual = ct_surface
-    direction = residual
-    norm_now = squares_total(residual)
-    for iteration in range(ITERS):
-        image = surface_apply(direction, height_pad, surface_pad, screen)
-        alpha = norm_now / lax.psum(jnp.sum(direction * image), "tile")
-        solution = solution + alpha * direction
-        residual = residual - alpha * image
-        if iteration + 1 < ITERS:
-            norm_next = squares_total(residual)
-            direction = residual + norm_next / norm_now * direction
-            norm_now = norm_next
+    kap_pad, wet_pad = stacked[0], stacked[1]
     column = ct_tracer + wet * share[:, None, None] * solution[None]
     values = solve_columns(column, vertical_coupling(kvert, wet))
     remaining = SUBSTEPS

time: 252 us -> 102 us (0.40)
  the two profiles are of different devices: /device:TPU:1 before, /device:TPU:5 now
where the time goes in v1:
time: 102 us; the launch traced here: 101 us
  starting transfers between devices  29.2 us (29%)
  other arithmetic  29.1 us (29%)
  between operations  18 us (18%)
  local copies, waits for them, and re-layouts  14.2 us (14%)
  waiting for transfers between devices  10.7 us (10%)
    ppermute x3, starting transfers between devices, extended(): before = lax.ppermute(last, axis, up)  12.5 us
    ppermute x3, starting transfers between devices, extended(): after = lax.ppermute(leading, axis, down)  5.94 us
    ppermute x3, waiting for transfers between devices, extended(): after = lax.ppermute(leading, axis, down)  5.3 us
    all_to_all x1, starting transfers between devices, body(): total = jnp.sum(lax.all_to_all(spread, 'tile', 0, 0, tiled=True), 0)  5.09 us
    ppermute x1, waiting for transfers between devices, neighbours(): lax.ppermute(array[:width], 'tile', down)  4.72 us
    mul x2, other arithmetic, diffuse_rows(): flux_x = face_x * (jnp.roll(inner, -1, 2) - inner)  4.47 us
    another operation x1, local copies, waits for them, and re-layouts, body(): jnp.stack([jnp.sum(p * q) for p, q in ((b0, b0), (b0, b1), (b1, b1), (b1,...  3.87 us
    mul x2, other arithmetic, diffuse_rows(): flux_y = face_y * (padded[:, 1:] - padded[:, :-1])  3.74 us
  transfers between devices with their start and end apart: 9, of which 3 were waited for; matrix products, arithmetic and copies ran while one was open for 24% of the time, Pallas kernels for 0%

profile of v1, /device:TPU:5, one launch (start us, length us, event | category | flops | bytes accessed | tf_op | source)
XLA Modules:
  0.0 101.2 jit_solution(14854999334417672205)
XLA Ops:
  0.6 1.3 %reduce_sum.81 = f32[]{:T(128)} reduce(f32[48]{0:T(128)} %param.15, f32[]{:T(128)} %constant.15.clone.1), dimensions={0}, to_apply=%region_0.0 | reduce | flops 47 | bytes 200 | tf_op jit(solution)/shard_map/reduce_sum | solution.py:117
  1.9 1.3 %broadcast_divide_fusion = f32[48]{0:T(128)S(1)} fusion(f32[48]{0:T(128)} %param.15, f32[]{:T(128)} %reduce_sum.81), kind=kLoop, calls=%fused_computation.755 | loop fusion | flops 48 | bytes 388 | tf_op jit(solution)/shard_map/div | solution.py:117
  3.2 1.9 %multiply_reduce_fusion = (f32[8,1280]{1,0:T(8,128)S(1)}, f32[48,8,1280]{2,1,0:T(8,128)S(1)}) fusion(f32[48]{0:T(128)S(1)} %broadcast_divide_fusion, s32[48,8,1280]{2,1,0:T(8,128)} %param.12, s32[8,1280]{1,0:T(8,128)} %param.13), kind=kLoop, calls=%fused_computation.29 | loop fusion | flops 2447360 | bytes 4014272 | tf_op jit(solution)/shard_map/reduce_sum | solution.py:118
  5.2 3.7 %collective-permute-start = (f32[3,4,1280]{2,0,1:T(4,128)S(1)}, f32[3,4,1280]{2,0,1:T(4,128)S(1)}, u32[]{:S(2)}, u32[]{:S(2)}) collective-permute-start(f32[3,4,1280]{2,0,1:T(4,128)S(1)} %get-tuple-element.145), channel_id=1, source_target_pairs={{0,1},{1,2},{2,3},{3,4},{4,5},{5,6},{6,7},{7,8},{8,9},{9,10},{10,1... | collective-permute-start | bytes 184328 | tf_op jit(solution)/shard_map/ppermute | solution.py:73
  8.9 1.9 %collective-permute-start.1 = (f32[3,4,1280]{2,0,1:T(4,128)S(1)}, f32[3,4,1280]{2,0,1:T(4,128)S(1)}, u32[]{:S(2)}, u32[]{:S(2)}) collective-permute-start(f32[3,4,1280]{2,0,1:T(4,128)S(1)} %get-tuple-element.146), channel_id=1, source_target_pairs={{1,0},{2,1},{3,2},{4,3},{5,4},{6,5},{7,6},{8,7},{9,8},{10,9},{11,1... | collective-permute-start | bytes 184328 | tf_op jit(solution)/shard_map/ppermute | solution.py:73
  10.8 4.7 %collective-permute-done.1 = f32[3,4,1280]{2,0,1:T(4,128)S(1)} collective-permute-done((f32[3,4,1280]{2,0,1:T(4,128)S(1)}, f32[3,4,1280]{2,0,1:T(4,128)S(1)}, u32[]{:S(2)}, u32[]{:S(2)}) %collective-permute-start.1) | collective-permute-done | bytes 61472 | tf_op jit(solution)/shard_map/ppermute | solution.py:73
  16.4 0.1 fusion.31
  16.6 0.1 fusion.23
  16.8 0.1 fusion.35
  17.0 0.1 fusion.12
  17.2 0.1 fusion.39
  17.4 0.8 fusion.44
  18.2 3.9 %stack.50 = f32[6]{0:T(128)S(1)} concatenate(f32[1]{0:T(128)} %bitcast, f32[1]{0:T(128)} %bitcast.12, f32[1]{0:T(128)} %bitcast.13, f32[1]{0:T(128)} %bitcast.19, f32[1]{0:T(128)} %bitcast.20, f32[1]{0:T(128)} %bitcast.24), dimensions={0} | concatenate | bytes 48 | tf_op jit(solution)/shard_map/stack | solution.py:133
  22.1 0.6 broadcast_in_dim.2
  22.7 5.1 %all-to-all-start = ((f32[16,1,128]{2,1,0:T(1,128)}), f32[16,1,128]{2,1,0:T(1,128)S(1)}, u32[]{:S(2)}, u32[]{:S(2)}) async-start(f32[16,1,128]{2,1,0:T(1,128)} %broadcast_in_dim.2), calls=%async_computation | async-start | bytes 16384 | tf_op jit(solution)/shard_map/all_to_all | solution.py:136
  27.8 3.7 %pad_maximum_fusion.2 = (f32[2,48,1,1280]{3,2,1,0:T(1,128)}, f32[2,48,1,1280]{3,2,1,0:T(1,128)}) fusion(f32[1,48,8,1280]{3,2,1,0:T(8,128)S(1)} %bitcast.1846, f32[1,48,8,1280]{3,2,1,0:T(8,128)} %bitcast.1850), kind=kLoop, calls=%fused_computation.31 | loop fusion | flops 245760 | bytes 4915200 | tf_op jit(solution)/shard_map/slice | solution.py:15
  31.5 3.3 %collective-permute-start.2 = (f32[2,48,1,1280]{3,2,1,0:T(1,128)}, f32[2,48,1,1280]{3,2,1,0:T(1,128)S(1)}, u32[]{:S(2)}, u32[]{:S(2)}) collective-permute-start(f32[2,48,1,1280]{3,2,1,0:T(1,128)} %get-tuple-element.130), channel_id=1, source_target_pairs={{0,1},{1,2},{2,3},{3,4},{4,5},{5,6},{6,7},{7,8},{8,9},{9,10},{10,1... | collective-permute-start | bytes 1474568 | tf_op jit(solution)/shard_map/ppermute | solution.py:17
  34.9 1.9 %collective-permute-start.3 = (f32[2,48,1,1280]{3,2,1,0:T(1,128)}, f32[2,48,1,1280]{3,2,1,0:T(1,128)}, u32[]{:S(2)}, u32[]{:S(2)}) collective-permute-start(f32[2,48,1,1280]{3,2,1,0:T(1,128)} %get-tuple-element.131), channel_id=1, source_target_pairs={{1,0},{2,1},{3,2},{4,3},{5,4},{6,5},{7,6},{8,7},{9,8},{10,9},{11,1... | collective-permute-start | bytes 1474568 | tf_op jit(solution)/shard_map/ppermute | solution.py:18
  36.8 1.4 %slice.1086 = f32[47,8,1280]{2,1,0:T(8,128)} slice(f32[48,8,1280]{2,1,0:T(8,128)S(1)} %get-tuple-element.127), slice={[1:48], [0:8], [0:1280]} | slice | bytes 3850240 | tf_op jit(solution)/shard_map/slice | solution.py:49
  38.2 0.7 fusion.261
  55.4 3.2 %multiply_add_fusion = (f32[48,8,1280]{2,1,0:T(8,128)S(1)}, f32[48,8,1280]{2,1,0:T(8,128)S(1)}) fusion(f32[48,8,1280]{2,1,0:T(8,128)} %param.8, f32[48,8,1280]{2,1,0:T(8,128)S(1)} %get-tuple-element.127, f32[8,1280]{1,0:T(8,128)S(1)} %multiply_add_fusion.42, f32[48]{0:T(128)S(1)} %broadcast_divide_fusion, f32[47,8,1280]{2,1,0:T(8,128)} %slice.1086, ...), kind=kLoop, calls=%fused_computation.26 | loop fusion | flops 2457600 | bytes 11796672 | tf_op jit(solution)/shard_map/add | solution.py:141
  58.7 0.9 fusion.54
  59.6 0.1 add_divide_fusion.36
  59.7 0.8 add_divide_fusion.1
  60.5 0.6 constant_dynamic-update-slice_fusion.47
  61.9 0.6 slice.1190
  62.4 1.1 %fusion.259 = (f32[48,1,1280]{2,1,0:T(1,128)}, f32[48,1,1280]{2,1,0:T(1,128)}) fusion(f32[48,8,1280]{2,1,0:T(8,128)S(1)} %constant_dynamic-update-slice_fusion), kind=kLoop, calls=%fused_computation.757 | loop fusion | bytes 983040 | tf_op jit(solution)/shard_map/slice | solution.py:15
  63.5 4.5 %collective-permute-start.5 = (f32[48,1,1280]{2,1,0:T(1,128)}, f32[48,1,1280]{2,1,0:T(1,128)}, u32[]{:S(2)}, u32[]{:S(2)}) collective-permute-start(f32[48,1,1280]{2,1,0:T(1,128)} %get-tuple-element.134), channel_id=1, source_target_pairs={{0,1},{1,2},{2,3},{3,4},{4,5},{5,6},{6,7},{7,8},{8,9},{9,10},{10,1... | collective-permute-start | bytes 737288 | tf_op jit(solution)/shard_map/ppermute | solution.py:17
  68.1 2.1 %collective-permute-start.4 = (f32[48,1,1280]{2,1,0:T(1,128)}, f32[48,1,1280]{2,1,0:T(1,128)}, u32[]{:S(2)}, u32[]{:S(2)}) collective-permute-start(f32[48,1,1280]{2,1,0:T(1,128)} %get-tuple-element.135), channel_id=1, source_target_pairs={{1,0},{2,1},{3,2},{4,3},{5,4},{6,5},{7,6},{8,7},{9,8},{10,9},{11,1... | collective-permute-start | bytes 737288 | tf_op jit(solution)/shard_map/ppermute | solution.py:18
  70.2 2.6 %pad_maximum_fusion = f32[2,48,10,1280]{3,2,1,0:T(8,128)S(1)} fusion(f32[2,48,1,1280]{3,2,1,0:T(1,128)} %collective-permute-done.3, f32[1,48,8,1280]{3,2,1,0:T(8,128)S(1)} %bitcast.1847, f32[1,48,8,1280]{3,2,1,0:T(8,128)S(1)} %bitcast.1851, f32[2,48,1,1280]{3,2,1,0:T(1,128)S(1)} %collective-permute-done.2), kind=kLoop, calls=%fused_computation | loop fusion | flops 3686400 | bytes 9830400 | tf_op jit(solution)/shard_map/concatenate | solution.py:19
  72.8 0.5 slice_bitcast_fusion.1
  73.4 0.6 slice.1184
  74.0 0.7 slice.1189
  74.7 1.8 %slice.1188 = f32[48,8,1279]{2,1,0:T(8,128)} slice(f32[48,10,1280]{2,1,0:T(8,128)S(1)} %get-tuple-element.129), slice={[0:48], [1:9], [1:1280]} | slice | bytes 3929088 | tf_op jit(solution)/shard_map/jit(_roll_static)/slice | solution.py:56
  76.5 4.1 %fusion.5 = (f32[48,8,1280]{2,1,0:T(8,128)S(1)}, f32[48,8,1280]{2,1,0:T(8,128)}) fusion(f32[48,8,1280]{2,1,0:T(8,128)S(1)} %constant_dynamic-update-slice_fusion, f32[48,8,1]{2,1,0:T(8,128)S(1)} %slice.1191, f32[48,8,1279]{2,1,0:T(8,128)S(1)} %slice.1190, f32[48,8,1]{2,1,0:T(8,128)} %slice.1189, f32[48,8,1279]{2,1,0:T(8,128)} %slice.1188, ...), kind=kLoop, calls=%fused_computation.20 | loop fusion | flops 4423680 | bytes 15728640 | tf_op jit(solution)/shard_map/mul | solution.py:57
  80.6 0.1 slice.1192
  80.8 2.9 %fusion.1 = (f32[48,9,1280]{2,1,0:T(8,128)S(1)}, f32[48,9,1280]{2,1,0:T(8,128)S(1)}) fusion(f32[48,1,1280]{2,1,0:T(1,128)} %collective-permute-done.4, f32[48,8,1280]{2,1,0:T(8,128)S(1)} %constant_dynamic-update-slice_fusion, f32[48,1,1280]{2,1,0:T(1,128)} %collective-permute-done.5, f32[48,10,1280]{2,1,0:T(8,128)S(1)} %get-tuple-element.129, ...), kind=kLoop, calls=%fused_computation.8 | loop fusion | flops 4423680 | bytes 15728640 | tf_op jit(solution)/shard_map/mul | solution.py:59
  83.6 0.7 slice_subtract_fusion.1
  84.4 0.3 fusion.258
  84.7 0.6 slice.1202
  85.3 4.7 %collective-permute-start.7 = (f32[48,1,1280]{2,1,0:T(1,128)S(1)}, f32[48,1,1280]{2,1,0:T(1,128)S(1)}, u32[]{:S(2)}, u32[]{:S(2)}) collective-permute-start(f32[48,1,1280]{2,1,0:T(1,128)S(1)} %get-tuple-element.132), channel_id=1, source_target_pairs={{0,1},{1,2},{2,3},{3,4},{4,5},{5,6},{6,7},{7,8},{8,9},{9,10},{10,1... | collective-permute-start | bytes 737288 | tf_op jit(solution)/shard_map/ppermute | solution.py:17
  90.0 1.9 %collective-permute-start.6 = (f32[48,1,1280]{2,1,0:T(1,128)S(1)}, f32[48,1,1280]{2,1,0:T(1,128)S(1)}, u32[]{:S(2)}, u32[]{:S(2)}) collective-permute-start(f32[48,1,1280]{2,1,0:T(1,128)S(1)} %get-tuple-element.133), channel_id=1, source_target_pairs={{1,0},{2,1},{3,2},{4,3},{5,4},{6,5},{7,6},{8,7},{9,8},{10,9},{11,1... | collective-permute-start | bytes 737288 | tf_op jit(solution)/shard_map/ppermute | solution.py:18
  91.9 0.4 fusion.6
  92.3 0.1 slice.1204
  92.4 0.7 collective-permute-done.7
  93.1 5.3 %collective-permute-done.6 = f32[48,1,1280]{2,1,0:T(1,128)S(1)} collective-permute-done((f32[48,1,1280]{2,1,0:T(1,128)S(1)}, f32[48,1,1280]{2,1,0:T(1,128)S(1)}, u32[]{:S(2)}, u32[]{:S(2)}) %collective-permute-start.6) | collective-permute-done | bytes 245792 | tf_op jit(solution)/shard_map/ppermute | solution.py:18
  98.4 0.9 fusion.2
  99.2 2.0 %slice_subtract_fusion = f32[48,8,1280]{2,1,0:T(8,128)} fusion(f32[48,9,1280]{2,1,0:T(8,128)S(1)} %fusion.2, f32[48,8,1279]{2,1,0:T(8,128)S(1)} %bitcast.1848, f32[48,8,1]{2,1,0:T(8,128)S(1)} %slice.1204, f32[48,8,1280]{2,1,0:T(8,128)S(1)} %slice_subtract_fusion.1, f32[48,8,1280]{2,1,0:T(8,128)S(1)} %fusion.6), kind=kLoop, calls=%fused_computation.11 | loop fusion | flops 2457600 | bytes 11796480 | tf_op jit(solution)/shard_map/sub | solution.py:60
  (100 shorter events, 1.9 us)
Async XLA Ops:
  3.2 1.9 %copy-start.2 = (f32[8,1280]{1,0:T(8,128)S(1)}, f32[8,1280]{1,0:T(8,128)}, u32[]{:S(2)}) copy-start(f32[8,1280]{1,0:T(8,128)} %param.9) | copy-start | bytes 122884
  3.2 1.9 %copy-start.3 = (f32[8,1280]{1,0:T(8,128)S(1)}, f32[8,1280]{1,0:T(8,128)}, u32[]{:S(2)}) copy-start(f32[8,1280]{1,0:T(8,128)} %param.14) | copy-start | bytes 122884
  5.2 5.6 %collective-permute-start = (f32[3,4,1280]{2,0,1:T(4,128)S(1)}, f32[3,4,1280]{2,0,1:T(4,128)S(1)}, u32[]{:S(2)}, u32[]{:S(2)}) collective-permute-start(f32[3,4,1280]{2,0,1:T(4,128)S(1)} %get-tuple-element.145), channel_id=1, source_target_pairs={{0,1},{1,2},{2,3},{3,4},{4,5},{5,6},{6,7},{7,8},{8,9},{9,10},{10,1... | collective-permute-start | bytes 184328 | tf_op jit(solution)/shard_map/ppermute | solution.py:73
  8.9 6.7 %collective-permute-start.1 = (f32[3,4,1280]{2,0,1:T(4,128)S(1)}, f32[3,4,1280]{2,0,1:T(4,128)S(1)}, u32[]{:S(2)}, u32[]{:S(2)}) collective-permute-start(f32[3,4,1280]{2,0,1:T(4,128)S(1)} %get-tuple-element.146), channel_id=1, source_target_pairs={{1,0},{2,1},{3,2},{4,3},{5,4},{6,5},{7,6},{8,7},{9,8},{10,9},{11,1... | collective-permute-start | bytes 184328 | tf_op jit(solution)/shard_map/ppermute | solution.py:73
  22.7 15.5 %all-to-all-start = ((f32[16,1,128]{2,1,0:T(1,128)}), f32[16,1,128]{2,1,0:T(1,128)S(1)}, u32[]{:S(2)}, u32[]{:S(2)}) async-start(f32[16,1,128]{2,1,0:T(1,128)} %broadcast_in_dim.2), calls=%async_computation | async-start | bytes 16384 | tf_op jit(solution)/shard_map/all_to_all | solution.py:136
  31.5 38.7 %collective-permute-start.2 = (f32[2,48,1,1280]{3,2,1,0:T(1,128)}, f32[2,48,1,1280]{3,2,1,0:T(1,128)S(1)}, u32[]{:S(2)}, u32[]{:S(2)}) collective-permute-start(f32[2,48,1,1280]{3,2,1,0:T(1,128)} %get-tuple-element.130), channel_id=1, source_target_pairs={{0,1},{1,2},{2,3},{3,4},{4,5},{5,6},{6,7},{7,8},{8,9},{9,10},{10,1... | collective-permute-start | bytes 1474568 | tf_op jit(solution)/shard_map/ppermute | solution.py:17
  34.9 35.3 %collective-permute-start.3 = (f32[2,48,1,1280]{3,2,1,0:T(1,128)}, f32[2,48,1,1280]{3,2,1,0:T(1,128)}, u32[]{:S(2)}, u32[]{:S(2)}) collective-permute-start(f32[2,48,1,1280]{3,2,1,0:T(1,128)} %get-tuple-element.131), channel_id=1, source_target_pairs={{1,0},{2,1},{3,2},{4,3},{5,4},{6,5},{7,6},{8,7},{9,8},{10,9},{11,1... | collective-permute-start | bytes 1474568 | tf_op jit(solution)/shard_map/ppermute | solution.py:18
  55.4 3.3 %copy-start.4 = (f32[8,1280]{1,0:T(8,128)}, f32[8,1280]{1,0:T(8,128)S(1)}, u32[]{:S(2)}) copy-start(f32[8,1280]{1,0:T(8,128)S(1)} %multiply_add_fusion.42) | copy-start | bytes 122884
  61.9 8.3 %copy-start = (f32[48,8,1280]{2,1,0:T(8,128)S(1)}, f32[48,8,1280]{2,1,0:T(8,128)}, u32[]{:S(2)}) copy-start(f32[48,8,1280]{2,1,0:T(8,128)} %param.10) | copy-start | bytes 5898244
  63.5 17.2 %collective-permute-start.5 = (f32[48,1,1280]{2,1,0:T(1,128)}, f32[48,1,1280]{2,1,0:T(1,128)}, u32[]{:S(2)}, u32[]{:S(2)}) collective-permute-start(f32[48,1,1280]{2,1,0:T(1,128)} %get-tuple-element.134), channel_id=1, source_target_pairs={{0,1},{1,2},{2,3},{3,4},{4,5},{5,6},{6,7},{7,8},{8,9},{9,10},{10,1... | collective-permute-start | bytes 737288 | tf_op jit(solution)/shard_map/ppermute | solution.py:17
  68.1 12.7 %collective-permute-start.4 = (f32[48,1,1280]{2,1,0:T(1,128)}, f32[48,1,1280]{2,1,0:T(1,128)}, u32[]{:S(2)}, u32[]{:S(2)}) collective-permute-start(f32[48,1,1280]{2,1,0:T(1,128)} %get-tuple-element.135), channel_id=1, source_target_pairs={{1,0},{2,1},{3,2},{4,3},{5,4},{6,5},{7,6},{8,7},{9,8},{10,9},{11,1... | collective-permute-start | bytes 737288 | tf_op jit(solution)/shard_map/ppermute | solution.py:18
  84.7 7.2 %copy-start.1 = (f32[48,8,1280]{2,1,0:T(8,128)S(1)}, f32[48,8,1280]{2,1,0:T(8,128)}, u32[]{:S(2)}) copy-start(f32[48,8,1280]{2,1,0:T(8,128)} %get-tuple-element.9) | copy-start | bytes 5898244
  85.3 7.8 %collective-permute-start.7 = (f32[48,1,1280]{2,1,0:T(1,128)S(1)}, f32[48,1,1280]{2,1,0:T(1,128)S(1)}, u32[]{:S(2)}, u32[]{:S(2)}) collective-permute-start(f32[48,1,1280]{2,1,0:T(1,128)S(1)} %get-tuple-element.132), channel_id=1, source_target_pairs={{0,1},{1,2},{2,3},{3,4},{4,5},{5,6},{6,7},{7,8},{8,9},{9,10},{10,1... | collective-permute-start | bytes 737288 | tf_op jit(solution)/shard_map/ppermute | solution.py:17
  90.0 8.4 %collective-permute-start.6 = (f32[48,1,1280]{2,1,0:T(1,128)S(1)}, f32[48,1,1280]{2,1,0:T(1,128)S(1)}, u32[]{:S(2)}, u32[]{:S(2)}) collective-permute-start(f32[48,1,1280]{2,1,0:T(1,128)S(1)} %get-tuple-element.133), channel_id=1, source_target_pairs={{1,0},{2,1},{3,2},{4,3},{5,4},{6,5},{7,6},{8,7},{9,8},{10,9},{11,1... | collective-permute-start | bytes 737288 | tf_op jit(solution)/shard_map/ppermute | solution.py:18

commit v2 on v1

v2 whole, which is shorter than its diff:
```python
import functools

import jax
import jax.numpy as jnp
from jax import lax
from jax.experimental import pallas as pl
from jax.experimental.pallas import tpu as pltpu
from jax.sharding import PartitionSpec as P

ITERS = 3
ROWS = 8
LOW = 0.05
HIGH = 9.0
MID = 0.5 * (HIGH + LOW)
HALF = 0.5 * (HIGH - LOW)
FLOAT = jnp.float32
LIMIT = 12 * 1024 * 1024


def east(values):
    return pltpu.roll(values, values.shape[1] - 1, 1)


def west(values):
    return pltpu.roll(values, 1, 1)


def north(values):
    return pltpu.roll(values, values.shape[0] - 1, 0)


def south(values):
    return pltpu.roll(values, 1, 0)


def stacked(values):
    return jnp.concatenate([values[:, i : i + 128] for i in range(0, values.shape[1], 128)], axis=0)


def unstacked(values):
    return jnp.concatenate([values[i : i + ROWS, :] for i in range(0, values.shape[0], ROWS)], axis=1)


def lane_index(values):
    return lax.broadcasted_iota(jnp.int32, values.shape, 1)


def east_of(values):
    turned = pltpu.roll(values, 127, 1)
    further = jnp.concatenate([turned[ROWS:, :], turned[:ROWS, :]], axis=0)
    return jnp.where(lane_index(values) == 127, further, turned)


def west_of(values):
    turned = pltpu.roll(values, 1, 1)
    further = jnp.concatenate([turned[-ROWS:, :], turned[:-ROWS, :]], axis=0)
    return jnp.where(lane_index(values) == 0, further, turned)


def turned_rows(values, shift):
    return pltpu.roll(values.reshape(-1, ROWS, 128), shift, 1).reshape(values.shape)


def north_of(values):
    return turned_rows(values, ROWS - 1)


def south_of(values):
    return turned_rows(values, 1)


def row_of(ref, block, row, width):
    tall = width // 128 * ROWS
    return jnp.concatenate(
        [ref[pl.ds(block * 8 * tall + j * ROWS + row, 8, stride=tall), :] for j in range(width // 128)], axis=1
    )


def level_at(k, width):
    tall = width // 128 * ROWS
    return pl.ds(pl.multiple_of(k * tall, tall), tall)


def rows_at(k):
    return pl.ds(pl.multiple_of(k * ROWS, ROWS), ROWS)


def row_index(values):
    return lax.broadcasted_iota(jnp.int32, values.shape, 0)


def spread(row, like):
    return jnp.broadcast_to(row, like.shape)


def kernel(body, outs, ins, name, scratch=(), cost=1000000):
    return pl.pallas_call(
        body,
        out_shape=[pltpu.VMEM(shape, FLOAT) for shape in outs],
        in_specs=ins,
        out_specs=[pl.BlockSpec(memory_space=pltpu.VMEM)] * len(outs),
        scratch_shapes=[pltpu.VMEM(shape, FLOAT) for shape in scratch],
        name=name,
        cost_estimate=pl.CostEstimate(flops=cost, bytes_accessed=cost, transcendentals=0),
        compiler_params=pltpu.CompilerParams(vmem_limit_bytes=LIMIT),
    )


def in_vmem(count):
    return [pl.BlockSpec(memory_space=pltpu.VMEM)] * count


def held(array):
    return pltpu.with_memory_space_constraint(array, pltpu.VMEM)


def setup_body(levels, weight, land, kmt, ct, screen, wet_ref, height_ref, surface_ref,
               fx_ref, fn_ref, dg_ref, q1_ref, up_ref, down_ref, buffer, sems):
    chunk = levels // 4
    copies = [
        pltpu.make_async_copy(
            land.at[pl.ds(i * chunk * ROWS, chunk * ROWS)],
            buffer.at[pl.ds(i * chunk * ROWS, chunk * ROWS)],
            sems.at[i],
        )
        for i in range(4)
    ]
    for copy in copies:
        copy.start()
    total = weight[0]
    for k in range(1, levels):
        total = total + weight[k]
    depth = kmt[...]
    height = jnp.zeros(depth.shape, FLOAT)
    for i, copy in enumerate(copies):
        copy.wait()

        def level(k, height):
            wet = jnp.where(k < depth, buffer[rows_at(k), :], 0).astype(FLOAT)
            wet_ref[level_at(k, depth.shape[1]), :] = stacked(wet)
            return height + weight[k] * wet

        height = lax.fori_loop(i * chunk, (i + 1) * chunk, level, height, unroll=4)
    height = height / total
    surface = jnp.where(0 < depth, buffer[0:ROWS, :], 0).astype(FLOAT)
    height_ref[...] = height
    surface_ref[...] = surface
    base = ct[...]
    rows = row_index(base)
    scale = 0.5 / HALF
    fx = scale * (height + east(height)) * surface * east(surface)
    fn = scale * (height + north(height)) * surface * north(surface)
    fn = jnp.where(rows < ROWS - 1, fn, 0.0)
    fs = south(fn)
    fw = west(fx)
    dg = (screen[...] - MID) * (1.0 / HALF) + fx + fw + fn + fs

    def apply(v):
        return dg * v - fx * east(v) - fw * west(v) - fn * north(v) - fs * south(v)

    q1 = apply(base)
    q2 = apply(q1)
    fx_ref[...] = fx
    fn_ref[...] = fn
    dg_ref[...] = dg
    q1_ref[...] = q1
    for ref, row in ((down_ref, 0), (up_ref, ROWS - 1)):
        for place, values in enumerate((base, q1, q2, fx, dg, height, surface)):
            ref[place : place + 1, :] = values[row : row + 1, :]
        ref[7:8, :] = jnp.zeros_like(base[0:1, :])


def basis_body(count, ct, height, surface, fx_ref, fn_ref, dg_ref, q1_ref, before, after, b1_ref, b2_ref, sums_ref):
    b0 = ct[...]
    rows = row_index(b0)
    first, last = rows == 0, rows == ROWS - 1
    fx, fn, dg = fx_ref[...], fn_ref[...], dg_ref[...]
    fw, fs = west(fx), south(fn)

    def halo(ref, row):
        b0_h, q1_h, q2_h, fx_h, dg_h, high_h, wet_h = (ref[i : i + 1, :] for i in range(7))
        face = (0.5 / HALF) * (high_h + height[row : row + 1, :]) * wet_h * surface[row : row + 1, :]
        extra = face * (b0_h - ct[row : row + 1, :])
        return b0_h, q1_h + extra, q2_h, fx_h, dg_h, face, extra

    def lift(row):
        return jnp.broadcast_to(row, b0.shape)

    sides = (halo(before, 0), halo(after, ROWS - 1))
    face_b, face_a = lift(sides[0][5]), lift(sides[1][5])
    b1 = q1_ref[...] - jnp.where(first, lift(sides[0][6]), 0.0) - jnp.where(last, lift(sides[1][6]), 0.0)
    dg = dg + jnp.where(first, face_b, 0.0) + jnp.where(last, face_a, 0.0)
    fn = jnp.where(last, face_a, fn)
    fs = jnp.where(first, face_b, fs)

    def apply(v, v_before, v_after):
        v_n = jnp.where(last, lift(v_after), north(v))
        v_s = jnp.where(first, lift(v_before), south(v))
        return dg * v - fx * east(v) - fw * west(v) - fn * v_n - fs * v_s

    b2 = 2.0 * apply(b1, sides[0][1], sides[1][1]) - b0

    def outer(side, own):
        b0_h, b1_h, q2_h, fx_h, dg_h, face, extra = side
        b0_h, b1_h, q2_h, fx_h, dg_h, face, extra, own = (lift(v) for v in (b0_h, b1_h, q2_h, fx_h, dg_h, face, extra, own))
        turned = dg_h * extra - fx_h * east(extra) - west(fx_h) * west(extra)
        return (2.0 * (q2_h + turned + face * (b1_h - own)) - b0_h)[0:1, :]

    b2_b = outer(sides[0], b1[0:1, :])
    b2_a = outer(sides[1], b1[ROWS - 1 : ROWS, :])
    next2 = apply(b2, b2_b, b2_a)
    b1_ref[...] = b1
    b2_ref[...] = b2
    tile_rows = lax.broadcasted_iota(jnp.int32, (8, 128), 0)
    packed = jnp.zeros((8, 128), FLOAT)
    for place, (p, q) in enumerate(((b0, b0), (b0, b1), (b1, b1), (b1, b2), (b2, b2), (b2, next2))):
        product = p * q
        folded = product[:, 0:128]
        for j in range(1, product.shape[1] // 128):
            folded = folded + product[:, j * 128 : (j + 1) * 128]
        packed = jnp.where(tile_rows == place, jnp.sum(folded, axis=0, keepdims=True), packed)
    for j in range(count):
        sums_ref[j * 8 : (j + 1) * 8, :] = packed


def quadratic(left, form):
    total = None
    for i in range(3):
        for j in range(3):
            if left[i] is not None and left[j] is not None:
                term = left[i] * left[j] * form[i][j]
                total = term if total is None else total + term
    return total


def plus(p, q):
    return q if p is None else p if q is None else p + q


def times(scale, p):
    return None if p is None else scale * p


def weights(sums):
    s0, s1, s2, s3, s4, s5 = sums
    g02 = 2.0 * s2 - s0
    gram = ((s0, s1, g02), (s1, s2, s3), (g02, s3, s4))
    b11, b12 = 0.5 * (s3 + s1), 0.5 * (s4 + g02)
    shift = ((s1, s2, s3), (s2, b11, b12), (s3, b12, s5))
    form = [[MID * gram[i][j] + HALF * shift[i][j] for j in range(3)] for i in range(3)]
    one = jnp.ones_like(s0)
    x, r, d = [None] * 3, [one, None, None], [one, None, None]
    rr = s0
    for step in range(ITERS):
        alpha = jnp.clip(rr / quadratic(d, form), 1.0 / HIGH, 1.0 / LOW)
        x = [plus(x[i], times(alpha, d[i])) for i in range(3)]
        if step + 1 < ITERS:
            image = [
                plus(times(MID, d[0]), times(0.5 * HALF, d[1])),
                plus(plus(times(MID, d[1]), times(HALF, d[0])), times(0.5 * HALF, d[2])),
                plus(times(MID, d[2]), times(0.5 * HALF, d[1])),
            ]
            r = [plus(r[i], times(-1.0, times(alpha, image[i]))) for i in range(3)]
            new = quadratic(r, gram)
            beta = jnp.clip(new / rr, 0.0, HIGH / LOW)
            d = [plus(r[i], times(beta, d[i])) for i in range(3)]
            rr = new
    return x


def edges_body(levels, count, sums, ct, b1, b2, m0, w, fx, fn, s_ref, up_ref, down_ref):
    total = sums[0:8, :]
    for j in range(1, count):
        total = total + sums[j * 8 : (j + 1) * 8, :]
    total = jnp.sum(total, axis=1, keepdims=True)
    mix = weights([total[i : i + 1, :] for i in range(6)])
    s = mix[0] * ct[...] + mix[1] * b1[...] + mix[2] * b2[...]
    s_ref[...] = s
    s_rows = {r: spread(s[r : r + 1, :], s) for r in (0, 1, ROWS - 2, ROWS - 1)}

    def packed(ref, block, r):
        return row_of(ref, block, r, ct.shape[1])

    def across(u, face):
        flux = face * (east(u) - u)
        return flux - west(flux)

    for block in range(levels // 8):
        u = {r: packed(m0, block, r) + s_rows[r] * packed(w, block, r) for r in s_rows}
        at, below = pl.ds(block * 8, 8), pl.ds(levels + block * 8, 8)
        for ref, row, inner, link in ((down_ref, 0, 1, 0), (up_ref, ROWS - 1, ROWS - 2, ROWS - 2)):
            ref[at, :] = u[row]
            ref[below, :] = u[row] + across(u[row], packed(fx, block, row)) + packed(fn, block, link) * (u[inner] - u[row])


def columns_body(levels, weight, source, kvert, wet, m0, w, ratio):
    total = weight[0]
    for k in range(1, levels):
        total = total + weight[k]
    width = source.shape[1]
    shape = (ROWS * width // 128, 128)
    inverse = 1.0 / jnp.full(shape, total, FLOAT)

    def down(k, carry):
        link, m_in, w_in = carry
        at = level_at(k, width)
        here = wet[at, :]
        below = jnp.where(k + 1 < levels, wet[level_at(jnp.minimum(k + 1, levels - 1), width), :], 0.0)
        coupling = stacked(kvert[rows_at(k), :]) * here * below
        over = 1.0 / (1.0 + coupling + link)
        m_here = (stacked(source[rows_at(k), :]) + m_in) * over
        w_here = (here * (weight[k] * inverse) + w_in) * over
        part = coupling * over
        ratio[at, :] = part
        m0[at, :] = m_here
        w[at, :] = w_here
        return coupling - coupling * part, coupling * m_here, coupling * w_here

    zero = jnp.zeros(shape, FLOAT)
    lax.fori_loop(0, levels, down, (zero, zero, zero))

    def up(i, carry):
        at = level_at(levels - 2 - i, width)
        m_below, w_below = carry
        part = ratio[at, :]
        m_here = m0[at, :] + part * m_below
        w_here = w[at, :] + part * w_below
        m0[at, :] = m_here
        w[at, :] = w_here
        return m_here, w_here

    last = level_at(levels - 1, width)
    lax.fori_loop(0, levels - 1, up, (m0[last, :], w[last, :]))


def faces_body(levels, kappa, wet, fx_ref, fn_ref):
    width = kappa.shape[1]
    shape = (ROWS * width // 128, 128)
    inside = lax.rem(lax.broadcasted_iota(jnp.int32, shape, 0), ROWS) < ROWS - 1

    def level(k, carry):
        at = level_at(k, width)
        kap, here = 0.5 * stacked(kappa[rows_at(k), :]), wet[at, :]
        fx_ref[at, :] = (kap + east_of(kap)) * here * east_of(here)
        fn_ref[at, :] = jnp.where(inside, (kap + north_of(kap)) * here * north_of(here), 0.0)
        return carry

    lax.fori_loop(0, levels, level, 0)


def rims_body(levels, kappa, wet, up_ref, down_ref, buffer):
    width = kappa.shape[1]

    def level(k, carry):
        buffer[level_at(k, width), :] = stacked(kappa[rows_at(k), :])
        return carry

    lax.fori_loop(0, levels, level, 0, unroll=4)
    for ref, row in ((down_ref, 0), (up_ref, ROWS - 1)):
        for block in range(levels // 8):
            ref[pl.ds(block * 8, 8), :] = row_of(buffer, block, row, width)
            ref[pl.ds(levels + block * 8, 8), :] = row_of(wet, block, row, width)


def inner_body(levels, m0, w, s_ref, fx_ref, fn_ref, u2_ref):
    width = s_ref.shape[1]
    s = stacked(s_ref[...])

    def level(k, carry):
        at = level_at(k, width)
        fx, fn = fx_ref[at, :], fn_ref[at, :]
        u = m0[at, :] + s * w[at, :]
        for _ in range(2):
            flux_x = fx * (east_of(u) - u)
            flux_y = fn * (north_of(u) - u)
            u = u + (flux_x - west_of(flux_x)) + (flux_y - south_of(flux_y))
        u2_ref[at, :] = u
        return carry

    lax.fori_loop(0, levels, level, 0)


def finish_body(levels, u2, fx, fn, own_up, own_down, rim_up, rim_down, before, after, rim_before, rim_after,
                out, change_ref, buffer, sems):
    width = own_up.shape[1]
    rows = lax.broadcasted_iota(jnp.int32, (ROWS, width), 0)
    sides = (
        (own_down, rim_down, before, rim_before, 0, 1, 0),
        (own_up, rim_up, after, rim_after, ROWS - 1, ROWS - 2, ROWS - 2),
    )
    copies = []
    for block in range(levels // 8):
        at, below = pl.ds(block * 8, 8), pl.ds(levels + block * 8, 8)
        for own, rim, other, rim_other, row, inner, link in sides:
            face = 0.5 * (rim[at, :] + rim_other[at, :]) * rim[below, :] * rim_other[below, :]
            change = face * (other[at, :] - own[at, :])
            flux = row_of(fx, block, row, width) * (east(change) - change)
            passed = row_of(fn, block, link, width) * change
            change_ref[row] = (change + (flux - west(flux)) - passed
                               + face * (other[below, :] - own[below, :] - 2.0 * change))
            change_ref[inner] = passed
        for k in range(8):
            level = block * 8 + k
            values = unstacked(u2[level_at(level, width), :])
            for row in (0, 1, ROWS - 2, ROWS - 1):
                values = values + jnp.where(rows == row, spread(change_ref[row, k : k + 1, :], values), 0.0)
            buffer[rows_at(level), :] = values
        whole = pl.ds(block * 8 * ROWS, 8 * ROWS)
        copy = pltpu.make_async_copy(buffer.at[whole], out.at[whole], sems.at[block])
        copy.start()
        copies.append(copy)
    for copy in copies:
        copy.wait()


def exchange(to_next, to_previous):
    count = lax.axis_size("tile")
    up = [(i, i + 1) for i in range(count - 1)]
    down = [(i + 1, i) for i in range(count - 1)]
    return lax.ppermute(to_next, "tile", up), lax.ppermute(to_previous, "tile", down)


def body(ct_tracer, ct_surface, kappa, kvert, land, kmt, screen, layer_weight):
    levels, rows, width = ct_tracer.shape
    count = lax.axis_size("tile")
    tall = levels * rows
    tile, field, rim = (rows, width), (tall * width // 128, 128), (2 * levels, width)
    flat = lambda array: array.reshape(tall, width)
    scalars = pl.BlockSpec(memory_space=pltpu.SMEM)
    anywhere = pl.BlockSpec(memory_space=pl.ANY)
    ct_tracer, kappa, kvert, land = (flat(a) for a in (ct_tracer, kappa, kvert, land))

    setup = pl.pallas_call(
        functools.partial(setup_body, levels),
        out_shape=[pltpu.VMEM(field, FLOAT)] + [pltpu.VMEM(tile, FLOAT)] * 8,
        in_specs=[scalars, anywhere] + in_vmem(3),
        out_specs=in_vmem(9),
        scratch_shapes=[pltpu.VMEM((tall, width), jnp.int32), pltpu.SemaphoreType.DMA((4,))],
        name="setup",
        compiler_params=pltpu.CompilerParams(vmem_limit_bytes=LIMIT),
    )
    wet, height, surface, s_fx, s_fn, s_dg, q1, to_next, to_previous = setup(layer_weight, land, kmt, ct_surface, screen)
    before, after = exchange(to_next, to_previous)

    kap, kv, source = held(kappa), held(kvert), held(ct_tracer)
    rim_up, rim_down = kernel(functools.partial(rims_body, levels), [rim, rim], in_vmem(2), "rims", [field])(kap, wet)
    rim_before, rim_after = exchange(rim_up, rim_down)

    b1, b2, sums = kernel(
        functools.partial(basis_body, count), [tile, tile, (8 * count, 128)], in_vmem(9), "basis"
    )(ct_surface, height, surface, s_fx, s_fn, s_dg, q1, before, after)
    sums = lax.all_to_all(sums.reshape(count, 8, 128), "tile", 0, 0, tiled=True).reshape(8 * count, 128)

    fx, fn = kernel(functools.partial(faces_body, levels), [field, field], in_vmem(2), "faces")(kap, wet)
    m0, w = kernel(
        functools.partial(columns_body, levels), [field, field], [scalars] + in_vmem(3), "columns", [field]
    )(layer_weight, source, kv, wet)

    solution, up, down = kernel(
        functools.partial(edges_body, levels, count), [tile, rim, rim], in_vmem(8), "edges"
    )(sums, ct_surface, b1, b2, m0, w, fx, fn)
    row_before, row_after = exchange(up, down)
    (u2,) = kernel(functools.partial(inner_body, levels), [field], in_vmem(5), "inner")(m0, w, solution, fx, fn)

    finish = pl.pallas_call(
        functools.partial(finish_body, levels),
        out_shape=jax.ShapeDtypeStruct((tall, width), FLOAT),
        in_specs=in_vmem(11),
        out_specs=anywhere,
        scratch_shapes=[pltpu.VMEM((rows, 8, width), FLOAT), pltpu.VMEM((tall, width), FLOAT), pltpu.SemaphoreType.DMA((levels // 8,))],
        name="finish",
        compiler_params=pltpu.CompilerParams(vmem_limit_bytes=LIMIT),
    )
    values = finish(u2, fx, fn, up, down, rim_up, rim_down, row_before, row_after, rim_before, rim_after)
    return (values.reshape(levels, rows, width), solution)


def solution(mesh):
    in_specs = (
        P(None, ("grp", "tile"), None),
        P(("grp", "tile"), None),
        P(None, "tile", None),
        P(None, "tile", None),
        P(None, "tile", None),
        P("tile", None),
        P("tile", None),
        P(),
    )
    out_specs = (P(None, ("grp", "tile"), None), P(("grp", "tile"), None))
    return jax.shard_map(body, mesh=mesh, in_specs=in_specs, out_specs=out_specs, check_vma=False)
```

time: 102 us -> 80.9 us (0.79)
  the two profiles are of different devices: /device:TPU:5 before, /device:TPU:8 now
where the time goes in v2:
time: 80.9 us; the launch traced here: 80.1 us
  Pallas kernels  30.3 us (37%)
  starting transfers between devices  26.4 us (33%)
  local copies, waits for them, and re-layouts  20.8 us (26%)
  waiting for transfers between devices  1.66 us (2%)
  between operations  0.85 us (1%)
    unnamed x53, local copies, waits for them, and re-layouts  20.8 us
    pallas_call x1, Pallas kernels, body(): kernel(functools.partial(inner_body, levels), [field], in_vmem(5), 'inner')  14.8 us
    ppermute x3, starting transfers between devices, exchange(): lax.ppermute(to_previous, 'tile', down)  13.8 us
    all_to_all x1, starting transfers between devices, body(): lax.all_to_all(sums.reshape(count, 8, 128), 'tile', 0, 0, tiled=True)  6.53 us
    ppermute x3, starting transfers between devices, exchange(): lax.ppermute(to_next, 'tile', up)  6.16 us
    pallas_call x1, Pallas kernels, body(): kernel(functools.partial(faces_body, levels), [field, field], in_vmem(2),...  4.4 us
    pallas_call x1, Pallas kernels, body(): finish(u2, fx, fn, up, down, rim_up, rim_down, row_before, row_after, rim...  3.47 us
    pallas_call x1, Pallas kernels, body(): kernel(functools.partial(columns_body, levels), [field, field], [scalars]...  2.61 us
  transfers between devices with their start and end apart: 7, of which 1 were waited for; matrix products, arithmetic and copies ran while one was open for 1% of the time, Pallas kernels for 29%

profile of v2, /device:TPU:8, one launch (start us, length us, event | category | flops | bytes accessed | tf_op | source)
XLA Modules:
  0.0 80.1 jit_solution(13958777091557199525)
XLA Ops:
  0.6 0.0 copy-start.13
  0.6 1.5 %copy-done.13 = s32[48,8,1280]{2,1,0:T(8,128)S(1)} copy-done((s32[48,8,1280]{2,1,0:T(8,128)S(1)}, s32[48,8,1280]{2,1,0:T(8,128)}, u32[]{:S(2)}) %copy-start.13) | copy-done | bytes 1966104
  2.2 0.8 copy-done.16
  3.0 0.8 copy-done.22
  3.7 0.8 copy-done.23
  4.5 0.7 copy-done.24
  5.2 2.5 %setup.1 = (f32[3840,128]{1,0:T(8,128)S(1)}, f32[8,1280]{1,0:T(8,128)S(1)}, f32[8,1280]{1,0:T(8,128)S(1)}, f32[8,1280]{1,0:T(8,128)S(1)}, f32[8,1280]{1,0:T(8,12...) custom-call(f32[48]{0:T(128)S(1)} %copy-done.24, ...), custom_call_target="tpu_custom_call" | custom-call | tf_op jit(solution)/shard_map/setup/pallas_call | solution.py:442
  7.7 1.9 %collective-permute-start = (f32[8,1280]{1,0:T(8,128)S(1)}, f32[8,1280]{1,0:T(8,128)S(1)}, u32[]{:S(2)}, u32[]{:S(2)}) collective-permute-start(f32[8,1280]{1,0:T(8,128)S(1)} %get-tuple-element.32), channel_id=1, source_target_pairs={{0,1},{1,2},{2,3},{3,4},{4,5},{5,6},{6,7},{7,8},{8,9},{9,10},{10,1... | collective-permute-start | bytes 122888 | tf_op jit(solution)/shard_map/ppermute | solution.py:420
  9.7 4.5 %collective-permute-start.1 = (f32[8,1280]{1,0:T(8,128)S(1)}, f32[8,1280]{1,0:T(8,128)S(1)}, u32[]{:S(2)}, u32[]{:S(2)}) collective-permute-start(f32[8,1280]{1,0:T(8,128)S(1)} %get-tuple-element.33), channel_id=1, source_target_pairs={{1,0},{2,1},{3,2},{4,3},{5,4},{6,5},{7,6},{8,7},{9,8},{10,9},{11,1... | collective-permute-start | bytes 122888 | tf_op jit(solution)/shard_map/ppermute | solution.py:420
  14.2 0.0 collective-permute-done.before
  14.2 1.6 %collective-permute-done.1.after = f32[8,1280]{1,0:T(8,128)S(1)} collective-permute-done((f32[8,1280]{1,0:T(8,128)S(1)}, f32[8,1280]{1,0:T(8,128)S(1)}, u32[]{:S(2)}, u32[]{:S(2)}) %collective-permute-start.1) | collective-permute-done | bytes 40992 | tf_op jit(solution)/shard_map/ppermute | solution.py:420
  15.9 0.9 %basis.1 = (f32[8,1280]{1,0:T(8,128)S(1)}, f32[8,1280]{1,0:T(8,128)S(1)}, f32[128,128]{1,0:T(8,128)}) custom-call(f32[8,1280]{1,0:T(8,128)S(1)} %copy-done.16, f32[8,1280]{1,0:T(8,128)S(1)} %get-tuple-element.26.height, f32[8,1280]{1,0:T(8,128)S(1)} %get-tuple-element.27.surface, f32[8,1280]{1,0:T(8,128)S(1)} %get-tuple-element.28.fx_ref, ...), custom_call_target="tpu_custom_call" | custom-call | flops 1000000 | bytes 1000000 | tf_op jit(solution)/shard_map/basis/pallas_call | solution.py:449
  16.7 0.6 copy-done.18
  17.3 0.6 copy-done.20
  17.9 6.5 %all-to-all-start = ((f32[16,8,128]{2,1,0:T(8,128)}), f32[16,8,128]{2,1,0:T(8,128)S(1)}, u32[]{:S(2)}, u32[]{:S(2)}) async-start(f32[16,8,128]{2,1,0:T(8,128)} %bitcast.3), calls=%async_computation | async-start | bytes 131072 | tf_op jit(solution)/shard_map/all_to_all | solution.py:452
  24.5 1.5 %copy-done.6 = f32[48,8,1280]{2,1,0:T(8,128)S(1)} copy-done((f32[48,8,1280]{2,1,0:T(8,128)S(1)}, f32[48,8,1280]{2,1,0:T(8,128)}, u32[]{:S(2)}) %copy-start.6) | copy-done | bytes 1966104
  26.0 0.5 rims.1
  26.5 2.2 %collective-permute-start.4 = (f32[96,1280]{1,0:T(8,128)S(1)}, f32[96,1280]{1,0:T(8,128)S(1)}, u32[]{:S(2)}, u32[]{:S(2)}) collective-permute-start(f32[96,1280]{1,0:T(8,128)S(1)} %get-tuple-element.42.rim_up), channel_id=1, source_target_pairs={{0,1},{1,2},{2,3},{3,4},{4,5},{5,6},{6,7},{7,8},{8,9},{9,10},{10,1... | collective-permute-start | bytes 1474568 | tf_op jit(solution)/shard_map/ppermute | solution.py:420
  28.7 0.0 copy-start.14
  28.7 0.0 copy-start.15
  28.7 0.0 copy-start.25
  28.7 4.7 %collective-permute-start.5 = (f32[96,1280]{1,0:T(8,128)S(1)}, f32[96,1280]{1,0:T(8,128)}, u32[]{:S(2)}, u32[]{:S(2)}) collective-permute-start(f32[96,1280]{1,0:T(8,128)S(1)} %get-tuple-element.43.rim_down), channel_id=1, source_target_pairs={{1,0},{2,1},{3,2},{4,3},{5,4},{6,5},{7,6},{8,7},{9,8},{10,9},{11,1... | collective-permute-start | bytes 1474568 | tf_op jit(solution)/shard_map/ppermute | solution.py:420
  33.4 4.4 %faces.1 = (f32[3840,128]{1,0:T(8,128)S(1)}, f32[3840,128]{1,0:T(8,128)S(1)}) custom-call(f32[384,1280]{1,0:T(8,128)S(1)} %bitcast.8, f32[3840,128]{1,0:T(8,128)S(1)} %get-tuple-element.23.wet), custom_call_target="tpu_custom_call" | custom-call | flops 1000000 | bytes 1000000 | tf_op jit(solution)/shard_map/faces/pallas_call | solution.py:454
  37.8 1.3 %copy-done = f32[3840,128]{1,0:T(8,128)} copy-done((f32[3840,128]{1,0:T(8,128)}, f32[3840,128]{1,0:T(8,128)S(1)}, u32[]{:S(2)}) %copy-start) | copy-done | bytes 1966104
  39.1 1.3 %copy-done.3 = f32[3840,128]{1,0:T(8,128)} copy-done((f32[3840,128]{1,0:T(8,128)}, f32[3840,128]{1,0:T(8,128)S(1)}, u32[]{:S(2)}) %copy-start.3) | copy-done | bytes 1966104
  40.4 0.0 copy-done.14
  40.4 2.6 %columns.1 = (f32[3840,128]{1,0:T(8,128)S(1)}, f32[3840,128]{1,0:T(8,128)S(1)}) custom-call(f32[48]{0:T(128)S(1)} %copy-done.25, f32[384,1280]{1,0:T(8,128)S(1)} %bitcast.10, f32[384,1280]{1,0:T(8,128)S(1)} %bitcast.11, f32[3840,128]{1,0:T(8,128)S(1)} %get-tuple-element.23.wet), custom_call_target="tpu_custom_call" | custom-call | flops 1000000 | bytes 1000000 | tf_op jit(solution)/shard_map/columns/pallas_call | solution.py:455
  43.0 0.0 copy-start.8
  43.0 1.3 %copy-done.8 = f32[3840,128]{1,0:T(8,128)} copy-done((f32[3840,128]{1,0:T(8,128)}, f32[3840,128]{1,0:T(8,128)S(1)}, u32[]{:S(2)}) %copy-start.8) | copy-done | bytes 1966104
  44.3 1.3 %copy-done.11 = f32[3840,128]{1,0:T(8,128)} copy-done((f32[3840,128]{1,0:T(8,128)}, f32[3840,128]{1,0:T(8,128)S(1)}, u32[]{:S(2)}) %copy-start.11) | copy-done | bytes 1966104
  45.6 0.0 all-to-all-done
  45.6 1.5 %copy-done.1 = f32[3840,128]{1,0:T(8,128)S(1)} copy-done((f32[3840,128]{1,0:T(8,128)S(1)}, f32[3840,128]{1,0:T(8,128)}, u32[]{:S(2)}) %copy-start.1) | copy-done | bytes 1966104
  47.2 1.5 %copy-done.4 = f32[3840,128]{1,0:T(8,128)S(1)} copy-done((f32[3840,128]{1,0:T(8,128)S(1)}, f32[3840,128]{1,0:T(8,128)}, u32[]{:S(2)}) %copy-start.4) | copy-done | bytes 1966104
  48.7 1.5 %copy-done.9 = f32[3840,128]{1,0:T(8,128)S(1)} copy-done((f32[3840,128]{1,0:T(8,128)S(1)}, f32[3840,128]{1,0:T(8,128)}, u32[]{:S(2)}) %copy-start.9) | copy-done | bytes 1966104
  50.2 1.5 %copy-done.12 = f32[3840,128]{1,0:T(8,128)S(1)} copy-done((f32[3840,128]{1,0:T(8,128)S(1)}, f32[3840,128]{1,0:T(8,128)}, u32[]{:S(2)}) %copy-start.12) | copy-done | bytes 1966104
  51.8 0.8 copy-done.19
  52.6 0.8 copy-done.21
  53.4 1.1 %edges.1 = (f32[8,1280]{1,0:T(8,128)S(1)}, f32[96,1280]{1,0:T(8,128)S(1)}, f32[96,1280]{1,0:T(8,128)S(1)}) custom-call(f32[128,128]{1,0:T(8,128)S(1)} %bitcast.12, f32[8,1280]{1,0:T(8,128)S(1)} %copy-done.17, f32[8,1280]{1,0:T(8,128)S(1)} %copy-done.19, f32[8,1280]{1,0:T(8,128)S(1)} %copy-done.21, f32[3840,128]{1,0:T(8,128)S(1)} %copy-done.9, ...), custom_call_target="tpu_custom_call" | custom-call | flops 1000000 | bytes 1000000 | tf_op jit(solution)/shard_map/edges/pallas_call | solution.py:459
  54.5 2.1 %collective-permute-start.2 = (f32[96,1280]{1,0:T(8,128)S(1)}, f32[96,1280]{1,0:T(8,128)S(1)}, u32[]{:S(2)}, u32[]{:S(2)}) collective-permute-start(f32[96,1280]{1,0:T(8,128)S(1)} %get-tuple-element.40.own_up), channel_id=1, source_target_pairs={{0,1},{1,2},{2,3},{3,4},{4,5},{5,6},{6,7},{7,8},{8,9},{9,10},{10,1... | collective-permute-start | bytes 1474568 | tf_op jit(solution)/shard_map/ppermute | solution.py:420
  56.5 4.5 %collective-permute-start.3 = (f32[96,1280]{1,0:T(8,128)S(1)}, f32[96,1280]{1,0:T(8,128)S(1)}, u32[]{:S(2)}, u32[]{:S(2)}) collective-permute-start(f32[96,1280]{1,0:T(8,128)S(1)} %get-tuple-element.41.own_down), channel_id=1, source_target_pairs={{1,0},{2,1},{3,2},{4,3},{5,4},{6,5},{7,6},{8,7},{9,8},{10,9},{11,1... | collective-permute-start | bytes 1474568 | tf_op jit(solution)/shard_map/ppermute | solution.py:420
  61.1 0.6 copy.10
  61.7 0.0 copy-done.5
  61.7 14.8 %inner.1.u2 = f32[3840,128]{1,0:T(8,128)S(1)} custom-call(f32[3840,128]{1,0:T(8,128)S(1)} %copy-done.10, f32[3840,128]{1,0:T(8,128)S(1)} %copy-done.12, f32[8,1280]{1,0:T(8,128)S(1)} %get-tuple-element.45.s_ref, f32[3840,128]{1,0:T(8,128)S(1)} %copy-done.2, f32[3840,128]{1,0:T(8,128)S(1)} %copy-done.5), custom_call_target="tpu_custom_call" | custom-call | flops 1000000 | bytes 1000000 | tf_op jit(solution)/shard_map/inner/pallas_call | solution.py:463
  76.6 0.0 collective-permute-done.4.rim_before
  76.6 0.0 collective-permute-done.5.rim_after
  76.6 0.0 collective-permute-done.2.before
  76.6 0.0 collective-permute-done.3.after
  76.6 3.5 %finish.1 = f32[384,1280]{1,0:T(8,128)} custom-call(f32[3840,128]{1,0:T(8,128)S(1)} %inner.1.u2, f32[3840,128]{1,0:T(8,128)S(1)} %copy-done.2, f32[3840,128]{1,0:T(8,128)S(1)} %copy-done.5, f32[96,1280]{1,0:T(8,128)S(1)} %get-tuple-element.40.own_up, f32[96,1280]{1,0:T(8,128)S(1)} %get-tuple-element.41.own_down, f32[96,1280]{1,0:T(8,128)S(1)} %get-tuple-element.42.rim_up, ...), custom_call_target="tpu_custom_call" | custom-call | tf_op jit(solution)/shard_map/finish/pallas_call | solution.py:474
  (27 shorter events, 0.0 us)
Async XLA Ops:
  0.6 1.5 %copy-start.13 = (s32[48,8,1280]{2,1,0:T(8,128)S(1)}, s32[48,8,1280]{2,1,0:T(8,128)}, u32[]{:S(2)}) copy-start(s32[48,8,1280]{2,1,0:T(8,128)} %param.12) | copy-start | bytes 5898244
  2.2 0.8 copy-start.16
  3.0 0.8 copy-start.22
  3.7 0.8 copy-start.23
  4.5 0.7 copy-start.24
  7.7 6.5 %collective-permute-start = (f32[8,1280]{1,0:T(8,128)S(1)}, f32[8,1280]{1,0:T(8,128)S(1)}, u32[]{:S(2)}, u32[]{:S(2)}) collective-permute-start(f32[8,1280]{1,0:T(8,128)S(1)} %get-tuple-element.32), channel_id=1, source_target_pairs={{0,1},{1,2},{2,3},{3,4},{4,5},{5,6},{6,7},{7,8},{8,9},{9,10},{10,1... | collective-permute-start | bytes 122888 | tf_op jit(solution)/shard_map/ppermute | solution.py:420
  9.7 6.2 %collective-permute-start.1 = (f32[8,1280]{1,0:T(8,128)S(1)}, f32[8,1280]{1,0:T(8,128)S(1)}, u32[]{:S(2)}, u32[]{:S(2)}) collective-permute-start(f32[8,1280]{1,0:T(8,128)S(1)} %get-tuple-element.33), channel_id=1, source_target_pairs={{1,0},{2,1},{3,2},{4,3},{5,4},{6,5},{7,6},{8,7},{9,8},{10,9},{11,1... | collective-permute-start | bytes 122888 | tf_op jit(solution)/shard_map/ppermute | solution.py:420
  16.7 0.6 copy-start.18
  17.3 0.6 copy-start.20
  17.9 27.7 %all-to-all-start = ((f32[16,8,128]{2,1,0:T(8,128)}), f32[16,8,128]{2,1,0:T(8,128)S(1)}, u32[]{:S(2)}, u32[]{:S(2)}) async-start(f32[16,8,128]{2,1,0:T(8,128)} %bitcast.3), calls=%async_computation | async-start | bytes 131072 | tf_op jit(solution)/shard_map/all_to_all | solution.py:452
  24.5 1.5 %copy-start.6 = (f32[48,8,1280]{2,1,0:T(8,128)S(1)}, f32[48,8,1280]{2,1,0:T(8,128)}, u32[]{:S(2)}) copy-start(f32[48,8,1280]{2,1,0:T(8,128)} %param.10) | copy-start | bytes 5898244
  26.0 7.4 %copy-start.7 = (f32[48,8,1280]{2,1,0:T(8,128)S(1)}, f32[48,8,1280]{2,1,0:T(8,128)}, u32[]{:S(2)}) copy-start(f32[48,8,1280]{2,1,0:T(8,128)} %param.10) | copy-start | bytes 5898244
  26.5 50.1 %collective-permute-start.4 = (f32[96,1280]{1,0:T(8,128)S(1)}, f32[96,1280]{1,0:T(8,128)S(1)}, u32[]{:S(2)}, u32[]{:S(2)}) collective-permute-start(f32[96,1280]{1,0:T(8,128)S(1)} %get-tuple-element.42.rim_up), channel_id=1, source_target_pairs={{0,1},{1,2},{2,3},{3,4},{4,5},{5,6},{6,7},{7,8},{8,9},{9,10},{10,1... | collective-permute-start | bytes 1474568 | tf_op jit(solution)/shard_map/ppermute | solution.py:420
  28.7 11.7 %copy-start.14 = (f32[48,8,1280]{2,1,0:T(8,128)S(1)}, f32[48,8,1280]{2,1,0:T(8,128)}, u32[]{:S(2)}) copy-start(f32[48,8,1280]{2,1,0:T(8,128)} %param.8) | copy-start | bytes 5898244
  28.7 11.7 %copy-start.15 = (f32[48,8,1280]{2,1,0:T(8,128)S(1)}, f32[48,8,1280]{2,1,0:T(8,128)}, u32[]{:S(2)}) copy-start(f32[48,8,1280]{2,1,0:T(8,128)} %param.11) | copy-start | bytes 5898244
  28.7 11.7 %copy-start.25 = (f32[48]{0:T(128)S(1)}, f32[48]{0:T(128)}, u32[]{:S(2)}) copy-start(f32[48]{0:T(128)} %weight.3) | copy-start | bytes 580
  28.7 47.9 %collective-permute-start.5 = (f32[96,1280]{1,0:T(8,128)S(1)}, f32[96,1280]{1,0:T(8,128)}, u32[]{:S(2)}, u32[]{:S(2)}) collective-permute-start(f32[96,1280]{1,0:T(8,128)S(1)} %get-tuple-element.43.rim_down), channel_id=1, source_target_pairs={{1,0},{2,1},{3,2},{4,3},{5,4},{6,5},{7,6},{8,7},{9,8},{10,9},{11,1... | collective-permute-start | bytes 1474568 | tf_op jit(solution)/shard_map/ppermute | solution.py:420
  37.8 1.3 %copy-start = (f32[3840,128]{1,0:T(8,128)}, f32[3840,128]{1,0:T(8,128)S(1)}, u32[]{:S(2)}) copy-start(f32[3840,128]{1,0:T(8,128)S(1)} %get-tuple-element.37.fx.fx_ref) | copy-start | bytes 5898244
  39.1 1.3 %copy-start.3 = (f32[3840,128]{1,0:T(8,128)}, f32[3840,128]{1,0:T(8,128)S(1)}, u32[]{:S(2)}) copy-start(f32[3840,128]{1,0:T(8,128)S(1)} %get-tuple-element.38.fn.fn_ref) | copy-start | bytes 5898244
  40.4 5.2 %copy-start.17 = (f32[8,1280]{1,0:T(8,128)S(1)}, f32[8,1280]{1,0:T(8,128)}, u32[]{:S(2)}) copy-start(f32[8,1280]{1,0:T(8,128)} %ct.5) | copy-start | bytes 122884
  43.0 1.3 %copy-start.8 = (f32[3840,128]{1,0:T(8,128)}, f32[3840,128]{1,0:T(8,128)S(1)}, u32[]{:S(2)}) copy-start(f32[3840,128]{1,0:T(8,128)S(1)} %get-tuple-element.24.m0) | copy-start | bytes 5898244
  44.3 1.3 %copy-start.11 = (f32[3840,128]{1,0:T(8,128)}, f32[3840,128]{1,0:T(8,128)S(1)}, u32[]{:S(2)}) copy-start(f32[3840,128]{1,0:T(8,128)S(1)} %get-tuple-element.25.w) | copy-start | bytes 5898244
  45.6 1.5 %copy-start.1 = (f32[3840,128]{1,0:T(8,128)S(1)}, f32[3840,128]{1,0:T(8,128)}, u32[]{:S(2)}) copy-start(f32[3840,128]{1,0:T(8,128)} %copy-done) | copy-start | bytes 5898244
  47.2 1.5 %copy-start.4 = (f32[3840,128]{1,0:T(8,128)S(1)}, f32[3840,128]{1,0:T(8,128)}, u32[]{:S(2)}) copy-start(f32[3840,128]{1,0:T(8,128)} %copy-done.3) | copy-start | bytes 5898244
  48.7 1.5 %copy-start.9 = (f32[3840,128]{1,0:T(8,128)S(1)}, f32[3840,128]{1,0:T(8,128)}, u32[]{:S(2)}) copy-start(f32[3840,128]{1,0:T(8,128)} %copy-done.8) | copy-start | bytes 5898244
  50.2 1.5 %copy-start.12 = (f32[3840,128]{1,0:T(8,128)S(1)}, f32[3840,128]{1,0:T(8,128)}, u32[]{:S(2)}) copy-start(f32[3840,128]{1,0:T(8,128)} %copy-done.11) | copy-start | bytes 5898244
  51.8 0.8 copy-start.19
  52.6 0.8 copy-start.21
  53.3 8.4 %copy-start.2 = (f32[3840,128]{1,0:T(8,128)S(1)}, f32[3840,128]{1,0:T(8,128)}, u32[]{:S(2)}) copy-start(f32[3840,128]{1,0:T(8,128)} %copy-done) | copy-start | bytes 5898244
  53.4 8.4 %copy-start.5 = (f32[3840,128]{1,0:T(8,128)S(1)}, f32[3840,128]{1,0:T(8,128)}, u32[]{:S(2)}) copy-start(f32[3840,128]{1,0:T(8,128)} %copy-done.3) | copy-start | bytes 5898244
  53.4 8.4 %copy-start.10 = (f32[3840,128]{1,0:T(8,128)S(1)}, f32[3840,128]{1,0:T(8,128)}, u32[]{:S(2)}) copy-start(f32[3840,128]{1,0:T(8,128)} %copy-done.8) | copy-start | bytes 5898244
  54.5 22.1 %collective-permute-start.2 = (f32[96,1280]{1,0:T(8,128)S(1)}, f32[96,1280]{1,0:T(8,128)S(1)}, u32[]{:S(2)}, u32[]{:S(2)}) collective-permute-start(f32[96,1280]{1,0:T(8,128)S(1)} %get-tuple-element.40.own_up), channel_id=1, source_target_pairs={{0,1},{1,2},{2,3},{3,4},{4,5},{5,6},{6,7},{7,8},{8,9},{9,10},{10,1... | collective-permute-start | bytes 1474568 | tf_op jit(solution)/shard_map/ppermute | solution.py:420
  56.5 20.1 %collective-permute-start.3 = (f32[96,1280]{1,0:T(8,128)S(1)}, f32[96,1280]{1,0:T(8,128)S(1)}, u32[]{:S(2)}, u32[]{:S(2)}) collective-permute-start(f32[96,1280]{1,0:T(8,128)S(1)} %get-tuple-element.41.own_down), channel_id=1, source_target_pairs={{1,0},{2,1},{3,2},{4,3},{5,4},{6,5},{7,6},{8,7},{9,8},{10,9},{11,1... | collective-permute-start | bytes 1474568 | tf_op jit(solution)/shard_map/ppermute | solution.py:420

commit v3 on v2

v3 whole, which is shorter than its diff:
```python
import functools

import jax
import jax.numpy as jnp
from jax import lax
from jax.experimental import pallas as pl
from jax.experimental.pallas import tpu as pltpu
from jax.sharding import PartitionSpec as P

ITERS = 3
ROWS = 8
LOW = 0.05
HIGH = 9.0
MID = 0.5 * (HIGH + LOW)
HALF = 0.5 * (HIGH - LOW)
FLOAT = jnp.float32
RIM = 12
LIMIT = 24 * 1024 * 1024


def east(values):
    return pltpu.roll(values, values.shape[1] - 1, 1)


def west(values):
    return pltpu.roll(values, 1, 1)


def north(values):
    return pltpu.roll(values, values.shape[0] - 1, 0)


def south(values):
    return pltpu.roll(values, 1, 0)


def stacked(values):
    return jnp.concatenate([values[:, i : i + 128] for i in range(0, values.shape[1], 128)], axis=0)


def unstacked(values):
    return jnp.concatenate([values[i : i + ROWS, :] for i in range(0, values.shape[0], ROWS)], axis=1)


def row_of(ref, block, row, width):
    tall = width // 128 * ROWS
    return jnp.concatenate(
        [ref[pl.ds(block * 8 * tall + j * ROWS + row, 8, stride=tall), :] for j in range(width // 128)], axis=1
    )


def level_at(k, width):
    tall = width // 128 * ROWS
    return pl.ds(pl.multiple_of(k * tall, tall), tall)


def rows_at(k):
    return pl.ds(pl.multiple_of(k * ROWS, ROWS), ROWS)


def row_index(values):
    return lax.broadcasted_iota(jnp.int32, values.shape, 0)


def spread(row, like):
    return jnp.broadcast_to(row, like.shape)


def vmem(*shapes):
    return [pltpu.VMEM(shape, FLOAT) for shape in shapes]


def hbm(*shapes):
    return [pltpu.HBM(shape, FLOAT) for shape in shapes]


def in_vmem(count):
    return [pl.BlockSpec(memory_space=pltpu.VMEM)] * count


def in_hbm(count):
    return [pl.BlockSpec(memory_space=pltpu.HBM)] * count


def kernel(body, outs, ins, out_specs, name, scratch=(), cost=1000000):
    return pl.pallas_call(
        body,
        out_shape=outs,
        in_specs=ins,
        out_specs=out_specs,
        scratch_shapes=list(scratch),
        name=name,
        cost_estimate=pl.CostEstimate(flops=cost, bytes_accessed=cost, transcendentals=0),
        compiler_params=pltpu.CompilerParams(vmem_limit_bytes=LIMIT),
    )


def held(array):
    return pltpu.with_memory_space_constraint(array, pltpu.VMEM)


def left(array):
    return pltpu.with_memory_space_constraint(array, pltpu.HBM)


def is_even():
    return lax.rem(lax.axis_index("tile"), 2) == 0


def dealt(even, low, high):
    return jnp.where(even, high, low), jnp.where(even, low, high)


def setup_body(levels, weight, land, kmt_hbm, ct_hbm, screen_hbm, wet_ref, height_ref, surface_ref,
               fx_ref, fn_ref, dg_ref, q1_ref, base_ref, near_ref, far_ref, buffer, kmt, screen, sems):
    chunk = levels // 4
    small = [
        pltpu.make_async_copy(source, target, sems.at[4 + i])
        for i, (source, target) in enumerate(((kmt_hbm, kmt), (ct_hbm, base_ref), (screen_hbm, screen)))
    ]
    copies = []
    for i in range(4):
        whole = pl.ds(i * chunk * ROWS, chunk * ROWS)
        copies.append(pltpu.make_async_copy(land.at[whole], buffer.at[whole], sems.at[i]))
    for copy in small[:1] + copies + small[1:]:
        copy.start()
    total = weight[0]
    for k in range(1, levels):
        total = total + weight[k]
    small[0].wait()
    depth = kmt[...]
    height = jnp.zeros(depth.shape, FLOAT)
    for i, copy in enumerate(copies):
        copy.wait()

        def level(k, height):
            wet = jnp.where(k < depth, buffer[rows_at(k), :], 0).astype(FLOAT)
            wet_ref[level_at(k, depth.shape[1]), :] = stacked(wet)
            return height + weight[k] * wet

        height = lax.fori_loop(i * chunk, (i + 1) * chunk, level, height, unroll=4)
    height = height / total
    surface = jnp.where(0 < depth, buffer[0:ROWS, :], 0).astype(FLOAT)
    height_ref[...] = height
    surface_ref[...] = surface
    small[1].wait()
    small[2].wait()
    base = base_ref[...]
    rows = row_index(base)
    scale = 0.5 / HALF
    fx = scale * (height + east(height)) * surface * east(surface)
    fn = scale * (height + north(height)) * surface * north(surface)
    fn = jnp.where(rows < ROWS - 1, fn, 0.0)
    fs = south(fn)
    fw = west(fx)
    dg = (screen[...] - MID) * (1.0 / HALF) + fx + fw + fn + fs

    def apply(v):
        return dg * v - fx * east(v) - fw * west(v) - fn * north(v) - fs * south(v)

    q1 = apply(base)
    q2 = apply(q1)
    fx_ref[...] = fx
    fn_ref[...] = fn
    dg_ref[...] = dg
    q1_ref[...] = q1
    even = is_even()
    near_ref[7:8, :] = jnp.zeros_like(base[0:1, :])
    far_ref[7:8, :] = jnp.zeros_like(base[0:1, :])
    for place, values in enumerate((base, q1, q2, fx, dg, height, surface)):
        at = slice(place, place + 1)
        near_ref[at, :], far_ref[at, :] = dealt(even, values[0:1, :], values[ROWS - 1 : ROWS, :])


def basis_body(count, ct, height, surface, fx_ref, fn_ref, dg_ref, q1_ref, near, far, basis_ref, sums_ref):
    even = is_even()
    b0 = ct[...]
    rows = row_index(b0)
    first, last = rows == 0, rows == ROWS - 1
    fx, fn, dg = fx_ref[...], fn_ref[...], dg_ref[...]
    fw, fs = west(fx), south(fn)

    def halo(values, row):
        b0_h, q1_h, q2_h, fx_h, dg_h, high_h, wet_h = (values[i : i + 1, :] for i in range(7))
        face = (0.5 / HALF) * (high_h + height[row : row + 1, :]) * wet_h * surface[row : row + 1, :]
        extra = face * (b0_h - ct[row : row + 1, :])
        return b0_h, q1_h + extra, q2_h, fx_h, dg_h, face, extra

    def lift(row):
        return jnp.broadcast_to(row, b0.shape)

    before, after = dealt(even, near[...], far[...])
    sides = (halo(before, 0), halo(after, ROWS - 1))
    face_b, face_a = lift(sides[0][5]), lift(sides[1][5])
    b1 = q1_ref[...] - jnp.where(first, lift(sides[0][6]), 0.0) - jnp.where(last, lift(sides[1][6]), 0.0)
    dg = dg + jnp.where(first, face_b, 0.0) + jnp.where(last, face_a, 0.0)
    fn = jnp.where(last, face_a, fn)
    fs = jnp.where(first, face_b, fs)

    def apply(v, v_before, v_after):
        v_n = jnp.where(last, lift(v_after), north(v))
        v_s = jnp.where(first, lift(v_before), south(v))
        return dg * v - fx * east(v) - fw * west(v) - fn * v_n - fs * v_s

    b2 = 2.0 * apply(b1, sides[0][1], sides[1][1]) - b0

    def outer(side, own):
        b0_h, b1_h, q2_h, fx_h, dg_h, face, extra = side
        b0_h, b1_h, q2_h, fx_h, dg_h, face, extra, own = (lift(v) for v in (b0_h, b1_h, q2_h, fx_h, dg_h, face, extra, own))
        turned = dg_h * extra - fx_h * east(extra) - west(fx_h) * west(extra)
        return (2.0 * (q2_h + turned + face * (b1_h - own)) - b0_h)[0:1, :]

    b2_b = outer(sides[0], b1[0:1, :])
    b2_a = outer(sides[1], b1[ROWS - 1 : ROWS, :])
    next2 = apply(b2, b2_b, b2_a)
    for place, values in enumerate((b0, b1, b2)):
        basis_ref[place * ROWS : (place + 1) * ROWS, :] = values
    tile_rows = lax.broadcasted_iota(jnp.int32, (8, 128), 0)
    packed = jnp.zeros((8, 128), FLOAT)
    for place, (p, q) in enumerate(((b0, b0), (b0, b1), (b1, b1), (b1, b2), (b2, b2), (b2, next2))):
        product = p * q
        folded = product[:, 0:128]
        for j in range(1, product.shape[1] // 128):
            folded = folded + product[:, j * 128 : (j + 1) * 128]
        packed = jnp.where(tile_rows == place, jnp.sum(folded, axis=0, keepdims=True), packed)
    for j in range(count):
        sums_ref[j * 8 : (j + 1) * 8, :] = packed


def quadratic(left, form):
    total = None
    for i in range(3):
        for j in range(3):
            if left[i] is not None and left[j] is not None:
                term = left[i] * left[j] * form[i][j]
                total = term if total is None else total + term
    return total


def plus(p, q):
    return q if p is None else p if q is None else p + q


def times(scale, p):
    return None if p is None else scale * p


def weights(sums):
    s0, s1, s2, s3, s4, s5 = sums
    g02 = 2.0 * s2 - s0
    gram = ((s0, s1, g02), (s1, s2, s3), (g02, s3, s4))
    b11, b12 = 0.5 * (s3 + s1), 0.5 * (s4 + g02)
    shift = ((s1, s2, s3), (s2, b11, b12), (s3, b12, s5))
    form = [[MID * gram[i][j] + HALF * shift[i][j] for j in range(3)] for i in range(3)]
    one = jnp.ones_like(s0)
    x, r, d = [None] * 3, [one, None, None], [one, None, None]
    rr = s0
    for step in range(ITERS):
        alpha = jnp.clip(rr / quadratic(d, form), 1.0 / HIGH, 1.0 / LOW)
        x = [plus(x[i], times(alpha, d[i])) for i in range(3)]
        if step + 1 < ITERS:
            image = [
                plus(times(MID, d[0]), times(0.5 * HALF, d[1])),
                plus(plus(times(MID, d[1]), times(HALF, d[0])), times(0.5 * HALF, d[2])),
                plus(times(MID, d[2]), times(0.5 * HALF, d[1])),
            ]
            r = [plus(r[i], times(-1.0, times(alpha, image[i]))) for i in range(3)]
            new = quadratic(r, gram)
            beta = jnp.clip(new / rr, 0.0, HIGH / LOW)
            d = [plus(r[i], times(beta, d[i])) for i in range(3)]
            rr = new
    return x


def edges_body(levels, count, sums, basis_ref, rim_hbm, out_hbm, s_ref, near_ref, far_ref, rims, sems):
    blocks = levels // 8
    copies = []
    for block in range(blocks):
        whole = pl.ds(block * RIM * 8, RIM * 8)
        copies.append(pltpu.make_async_copy(rim_hbm.at[whole], rims.at[whole], sems.at[block]))
    for copy in copies:
        copy.start()
    total = sums[0:8, :]
    for j in range(1, count):
        total = total + sums[j * 8 : (j + 1) * 8, :]
    total = jnp.sum(total, axis=1, keepdims=True)
    mix = weights([total[i : i + 1, :] for i in range(6)])
    b0, b1, b2 = (basis_ref[i * ROWS : (i + 1) * ROWS, :] for i in range(3))
    s = mix[0] * b0 + mix[1] * b1 + mix[2] * b2
    s_ref[...] = s
    copy_s = pltpu.make_async_copy(s_ref, out_hbm, sems.at[blocks])
    copy_s.start()
    s_rows = {r: spread(s[r : r + 1, :], s) for r in (0, 1, ROWS - 2, ROWS - 1)}
    even = is_even()

    for block, copy in enumerate(copies):
        copy.wait()
        found = []
        for side, row, inner in ((0, 0, 1), (1, ROWS - 1, ROWS - 2)):
            m, gm, w, q, face, link = (
                rims[pl.ds((block * RIM + side * 6 + i) * 8, 8), :] for i in range(6)
            )
            v = s_rows[row] * w
            flux = face * (east(v) - v)
            found.append((m + v, gm + v + (flux - west(flux)) - link * v + s_rows[inner] * q))
        for place in range(2):
            at = pl.ds(place * levels + block * 8, 8)
            near_ref[at, :], far_ref[at, :] = dealt(even, found[0][place], found[1][place])
    copy_s.wait()


def columns_body(levels, weight, source_hbm, kvert_hbm, kappa_hbm, wet, m0_hbm, w_hbm, rim_hbm, near_ref, far_ref,
                 source, kvert, kappa, m0, w, ratio, bricks, rims, in_sems, out_sems):
    width = source.shape[1]
    parts = 4
    chunk = levels // parts
    ins = []
    for i in range(parts):
        whole = pl.ds(i * chunk * ROWS, chunk * ROWS)
        for a, (far, near) in enumerate(((source_hbm, source), (kvert_hbm, kvert), (kappa_hbm, kappa))):
            ins.append(pltpu.make_async_copy(far.at[whole], near.at[whole], in_sems.at[i * 3 + a]))
    for copy in [ins[i * 3 + a] for i in range(parts) for a in (0, 1)] + ins[2::3]:
        copy.start()
    total = weight[0]
    for k in range(1, levels):
        total = total + weight[k]
    shape = (ROWS * width // 128, 128)
    inverse = 1.0 / jnp.full(shape, total, FLOAT)

    def down(k, carry):
        link, m_in, w_in = carry
        at = level_at(k, width)
        here = wet[at, :]
        below = jnp.where(k + 1 < levels, wet[level_at(jnp.minimum(k + 1, levels - 1), width), :], 0.0)
        coupling = stacked(kvert[rows_at(k), :]) * here * below
        over = 1.0 / (1.0 + coupling + link)
        m_here = (stacked(source[rows_at(k), :]) + m_in) * over
        w_here = (here * (weight[k] * inverse) + w_in) * over
        part = coupling * over
        ratio[at, :] = part
        m0[at, :] = m_here
        w[at, :] = w_here
        return coupling - coupling * part, coupling * m_here, coupling * w_here

    zero = jnp.zeros(shape, FLOAT)
    carry = (zero, zero, zero)
    for i in range(parts):
        ins[i * 3].wait()
        ins[i * 3 + 1].wait()
        carry = lax.fori_loop(i * chunk, (i + 1) * chunk, down, carry)

    def up(i, carry):
        at = level_at(levels - 1 - i, width)
        m_below, w_below = carry
        part = ratio[at, :]
        m_here = m0[at, :] + part * m_below
        w_here = w[at, :] + part * w_below
        m0[at, :] = m_here
        w[at, :] = w_here
        return m_here, w_here

    carry = (zero, zero)
    outs = []
    for i in range(parts):
        carry = lax.fori_loop(i * chunk, (i + 1) * chunk, up, carry)
        size = chunk * shape[0]
        whole = pl.ds((parts - 1 - i) * size, size)
        for a, (near, far) in enumerate(((m0, m0_hbm), (w, w_hbm))):
            copy = pltpu.make_async_copy(near.at[whole], far.at[whole], out_sems.at[i * 2 + a])
            copy.start()
            outs.append(copy)
    for i in range(parts):
        ins[i * 3 + 2].wait()

    def brick(k, carry):
        bricks[level_at(k, width), :] = stacked(kappa[rows_at(k), :])
        return carry

    lax.fori_loop(0, levels, brick, 0, unroll=4)
    even = is_even()
    for block in range(levels // 8):
        found = []
        for side, row, inner in ((0, 0, 1), (1, ROWS - 1, ROWS - 2)):
            kap, kap_in = row_of(bricks, block, row, width), row_of(bricks, block, inner, width)
            here, here_in = row_of(wet, block, row, width), row_of(wet, block, inner, width)
            m, w_row = row_of(m0, block, row, width), row_of(w, block, row, width)
            face = 0.5 * (kap + east(kap)) * here * east(here)
            link = 0.5 * (kap + kap_in) * here * here_in
            flux = face * (east(m) - m)
            gm = m + (flux - west(flux)) + link * (row_of(m0, block, inner, width) - m)
            q = link * row_of(w, block, inner, width)
            for i, values in enumerate((m, gm, w_row, q, face, link)):
                rims[pl.ds((block * RIM + side * 6 + i) * 8, 8), :] = values
            found.append((kap, here))
        for place in range(2):
            at = pl.ds(place * levels + block * 8, 8)
            near_ref[at, :], far_ref[at, :] = dealt(even, found[0][place], found[1][place])
        whole = pl.ds(block * RIM * 8, RIM * 8)
        copy = pltpu.make_async_copy(rims.at[whole], rim_hbm.at[whole], out_sems.at[2 * parts + block])
        copy.start()
        outs.append(copy)
    for copy in outs:
        copy.wait()


def inner_body(levels, kmt, s_ref, m0, w, kappa, land, u2_ref):
    s = s_ref[...]
    depth = kmt[...]
    inside = row_index(s) < ROWS - 1

    def face(here, there):
        return jnp.where(jnp.minimum(here, there) > 0.0, here + there, 0.0)

    def level(k):
        at = rows_at(k)
        sea = jnp.where(k < depth, land[at, :], 0) > 0
        half = jnp.where(sea, 0.5 * kappa[at, :], 0.0)
        fx = face(half, east(half))
        fn = jnp.where(inside, face(half, north(half)), 0.0)
        fw, fs = west(fx), south(fn)
        keep = 1.0 - (fx + fw) - (fn + fs)
        brick = level_at(k, s.shape[1])
        u = unstacked(m0[brick, :]) + s * unstacked(w[brick, :])
        for _ in range(2):
            u = keep * u + (fx * east(u) + fw * west(u)) + (fn * north(u) + fs * south(u))
        return u

    def group(i, carry):
        for values, k in [(level(2 * i + j), 2 * i + j) for j in range(2)]:
            u2_ref[rows_at(k), :] = values
        return carry

    lax.fori_loop(0, levels // 2, group, 0)


def finish_body(levels, u2, rims, own_near, own_far, rim_near, rim_far, near, far, rim_other_near, rim_other_far,
                out, change_ref, buffer, sems):
    width = own_near.shape[1]
    tall = width // 128 * ROWS
    rows = lax.broadcasted_iota(jnp.int32, (ROWS, width), 0)
    on_rim = (rows < 2) | (rows >= ROWS - 2)
    even = is_even()
    copies = []
    for block in range(levels // 8):
        at, below = pl.ds(block * 8, 8), pl.ds(levels + block * 8, 8)

        def pairs(a, b):
            return [dealt(even, a[part, :], b[part, :]) for part in (at, below)]

        own, rim = pairs(own_near, own_far), pairs(rim_near, rim_far)
        other, rim_other = pairs(near, far), pairs(rim_other_near, rim_other_far)
        for side, row, inner in ((0, 0, 1), (1, ROWS - 1, ROWS - 2)):
            face = 0.5 * (rim[0][side] + rim_other[0][side]) * rim[1][side] * rim_other[1][side]
            change = face * (other[0][side] - own[0][side])
            along, link = (rims[pl.ds((block * RIM + side * 6 + i) * 8, 8), :] for i in (4, 5))
            flux = along * (east(change) - change)
            passed = link * change
            on_row = (change + (flux - west(flux)) - passed
                      + face * (other[1][side] - own[1][side] - 2.0 * change))
            for j in range(width // 128):
                lanes = slice(j * 128, (j + 1) * 128)
                change_ref[pl.ds(j * ROWS + row, 8, stride=tall), :] = on_row[:, lanes]
                change_ref[pl.ds(j * ROWS + inner, 8, stride=tall), :] = passed[:, lanes]
        for k in range(8):
            level = block * 8 + k
            change = jnp.where(on_rim, unstacked(change_ref[level_at(k, width), :]), 0.0)
            buffer[rows_at(level), :] = u2[rows_at(level), :] + change
        whole = pl.ds(block * 8 * ROWS, 8 * ROWS)
        copy = pltpu.make_async_copy(buffer.at[whole], out.at[whole], sems.at[block])
        copy.start()
        copies.append(copy)
    for copy in copies:
        copy.wait()


def exchange(to_near, to_far):
    count = lax.axis_size("tile")

    def swap(array, start):
        firsts = range(start, count - 1, 2)
        return lax.ppermute(array, "tile", [(i, i + 1) for i in firsts] + [(i + 1, i) for i in firsts])

    from_far = swap(to_far, 1)
    return swap(to_near, 0), from_far


def body(ct_tracer, ct_surface, kappa, kvert, land, kmt, screen, layer_weight):
    levels, rows, width = ct_tracer.shape
    count = lax.axis_size("tile")
    tall = levels * rows
    tile, brick, flat = (rows, width), (tall * width // 128, 128), (tall, width)
    rim, rim_rows = (2 * levels, width), (levels * RIM, width)
    scalars = [pl.BlockSpec(memory_space=pltpu.SMEM)]
    ct_tracer, kappa, kvert, land = (a.reshape(flat) for a in (ct_tracer, kappa, kvert, land))
    semaphores = pltpu.SemaphoreType.DMA

    wet, height, surface, s_fx, s_fn, s_dg, q1, base, to_near, to_far = kernel(
        functools.partial(setup_body, levels), vmem(brick, *[tile] * 9), scalars + in_hbm(4), in_vmem(10), "setup",
        [pltpu.VMEM(flat, jnp.int32), pltpu.VMEM(tile, jnp.int32), pltpu.VMEM(tile, FLOAT), semaphores((7,))],
    )(layer_weight, left(land), left(kmt), left(ct_surface), left(screen))
    near, far = exchange(to_near, to_far)

    fields = [pltpu.VMEM(flat, FLOAT)] * 3 + [pltpu.VMEM(brick, FLOAT)] * 4 + [pltpu.VMEM(rim_rows, FLOAT)]
    m0, w, rims, rim_near, rim_far = kernel(
        functools.partial(columns_body, levels), hbm(brick, brick, rim_rows) + vmem(rim, rim),
        scalars + in_hbm(3) + in_vmem(1), in_hbm(3) + in_vmem(2), "columns",
        fields + [semaphores((12,)), semaphores((8 + levels // 8,))],
    )(layer_weight, left(ct_tracer), left(kvert), left(kappa), wet)

    basis, sums = kernel(
        functools.partial(basis_body, count), vmem((3 * rows, width), (8 * count, 128)), in_vmem(9), in_vmem(2), "basis"
    )(base, height, surface, s_fx, s_fn, s_dg, q1, near, far)
    sums = lax.all_to_all(sums.reshape(count, 8, 128), "tile", 0, 0, tiled=True).reshape(8 * count, 128)
    rim_other_near, rim_other_far = exchange(rim_near, rim_far)

    solution, s, row_near, row_far = kernel(
        functools.partial(edges_body, levels, count), hbm(tile) + vmem(tile, rim, rim),
        in_vmem(2) + in_hbm(1), in_hbm(1) + in_vmem(3), "edges",
        [pltpu.VMEM(rim_rows, FLOAT), semaphores((levels // 8 + 1,))],
    )(sums, basis, left(rims))
    other_near, other_far = exchange(row_near, row_far)
    u2 = kernel(
        functools.partial(inner_body, levels), vmem(flat), in_vmem(6), in_vmem(1), "inner"
    )(held(kmt), s, held(m0), held(w), held(kappa), held(land))[0]

    values = kernel(
        functools.partial(finish_body, levels), hbm(flat), in_vmem(10), in_hbm(1), "finish",
        [pltpu.VMEM((8 * rows * width // 128, 128), FLOAT), pltpu.VMEM(flat, FLOAT), semaphores((levels // 8,))],
    )(u2, held(rims), row_near, row_far, rim_near, rim_far, other_near, other_far, rim_other_near, rim_other_far)[0]
    return (values.reshape(levels, rows, width), solution)


def solution(mesh):
    in_specs = (
        P(None, ("grp", "tile"), None),
        P(("grp", "tile"), None),
        P(None, "tile", None),
        P(None, "tile", None),
        P(None, "tile", None),
        P("tile", None),
        P("tile", None),
        P(),
    )
    out_specs = (P(None, ("grp", "tile"), None), P(("grp", "tile"), None))
    return jax.shard_map(body, mesh=mesh, in_specs=in_specs, out_specs=out_specs, check_vma=False)
```

time: 80.9 us -> 53.9 us (0.67)
  the two profiles are of different devices: /device:TPU:8 before, /device:TPU:1 now
where the time goes in v3:
time: 53.9 us; the launch traced here: 53.1 us
  Pallas kernels  21.7 us (40%)
  starting transfers between devices  18.5 us (34%)
  local copies, waits for them, and re-layouts  6.91 us (13%)
  waiting for transfers between devices  5.15 us (10%)
  between operations  0.81 us (2%)
    ppermute x6, starting transfers between devices, swap(): lax.ppermute(array, 'tile', [(i, i + 1) for i in firsts] + [(i + 1, i) fo...  12 us
    unnamed x20, local copies, waits for them, and re-layouts  6.91 us
    pallas_call x1, Pallas kernels, body(): kernel(functools.partial(inner_body, levels), vmem(flat), in_vmem(6), in_...  6.79 us
    pallas_call x1, Pallas kernels, body(): kernel(functools.partial(columns_body, levels), hbm(brick, brick, rim_row...  6.57 us
    all_to_all x1, starting transfers between devices, body(): lax.all_to_all(sums.reshape(count, 8, 128), 'tile', 0, 0, tiled=True)  6.5 us
    ppermute x6, waiting for transfers between devices, swap(): lax.ppermute(array, 'tile', [(i, i + 1) for i in firsts] + [(i + 1, i) fo...  5.15 us
    pallas_call x1, Pallas kernels, body(): kernel(functools.partial(finish_body, levels), hbm(flat), in_vmem(10), in...  2.89 us
    pallas_call x1, Pallas kernels, body(): kernel(functools.partial(setup_body, levels), vmem(brick, *[tile] * 9), s...  2.49 us
  transfers between devices with their start and end apart: 7, of which 2 were waited for; matrix products, arithmetic and copies ran while one was open for 0% of the time, Pallas kernels for 29%

profile of v3, /device:TPU:1, one launch (start us, length us, event | category | flops | bytes accessed | tf_op | source)
XLA Modules:
  0.0 53.1 jit_solution(16134858660474199865)
XLA Ops:
  0.6 0.0 copy-start.9
  0.6 0.0 copy-start.8
  0.7 0.7 %copy-done.8 = f32[48]{0:T(128)S(1)} copy-done((f32[48]{0:T(128)S(1)}, f32[48]{0:T(128)}, u32[]{:S(2)}) %copy-start.8) | copy-done | bytes 216
  1.4 2.5 %setup.1 = (f32[3840,128]{1,0:T(8,128)S(1)}, f32[8,1280]{1,0:T(8,128)S(1)}, f32[8,1280]{1,0:T(8,128)S(1)}, f32[8,1280]{1,0:T(8,128)S(1)}, f32[8,1280]{1,0:T(8,12...) custom-call(f32[48]{0:T(128)S(1)} %copy-done.8, ...), custom_call_target="tpu_custom_call" | custom-call | flops 1000000 | bytes 1000000 | tf_op jit(solution)/shard_map/setup/pallas_call | solution.py:497
  3.9 0.1 collective-permute-start
  4.0 4.5 %collective-permute-start.1 = (f32[8,1280]{1,0:T(8,128)S(1)}, f32[8,1280]{1,0:T(8,128)S(1)}, u32[]{:S(2)}, u32[]{:S(2)}) collective-permute-start(f32[8,1280]{1,0:T(8,128)S(1)} %get-tuple-element.31), channel_id=1, source_target_pairs={{1,2},{3,4},{5,6},{7,8},{9,10},{11,12},{13,14},{2,1},{4,3},{6,5},{... | collective-permute-start | bytes 122888 | tf_op jit(solution)/shard_map/ppermute | solution.py:481
  8.5 0.0 collective-permute-done.near
  8.5 1.7 %collective-permute-done.1.far = f32[8,1280]{1,0:T(8,128)S(1)} collective-permute-done((f32[8,1280]{1,0:T(8,128)S(1)}, f32[8,1280]{1,0:T(8,128)S(1)}, u32[]{:S(2)}, u32[]{:S(2)}) %collective-permute-start.1) | collective-permute-done | bytes 40992 | tf_op jit(solution)/shard_map/ppermute | solution.py:481
  10.2 0.9 %basis.1 = (f32[24,1280]{1,0:T(8,128)S(1)}, f32[128,128]{1,0:T(8,128)}) custom-call(f32[8,1280]{1,0:T(8,128)S(1)} %get-tuple-element.23.ct, f32[8,1280]{1,0:T(8,128)S(1)} %get-tuple-element.24.height, f32[8,1280]{1,0:T(8,128)S(1)} %get-tuple-element.25.surface, f32[8,1280]{1,0:T(8,128)S(1)} %get-tuple-element.26.fx_ref, ...), custom_call_target="tpu_custom_call" | custom-call | flops 1000000 | bytes 1000000 | tf_op jit(solution)/shard_map/basis/pallas_call | solution.py:510
  11.0 0.0 copy-start.6
  11.0 0.7 %copy-done.6 = f32[24,1280]{1,0:T(8,128)} copy-done((f32[24,1280]{1,0:T(8,128)}, f32[24,1280]{1,0:T(8,128)S(1)}, u32[]{:S(2)}) %copy-start.6) | copy-done | bytes 122904
  11.7 6.5 %all-to-all-start = ((f32[16,8,128]{2,1,0:T(8,128)}), f32[16,8,128]{2,1,0:T(8,128)S(1)}, u32[]{:S(2)}, u32[]{:S(2)}) async-start(f32[16,8,128]{2,1,0:T(8,128)} %bitcast.1), calls=%async_computation | async-start | bytes 131072 | tf_op jit(solution)/shard_map/all_to_all | solution.py:513
  18.2 0.0 copy-done.9
  18.2 6.6 %columns.1 = (f32[3840,128]{1,0:T(8,128)}, f32[3840,128]{1,0:T(8,128)}, f32[576,1280]{1,0:T(8,128)}, f32[96,1280]{1,0:T(8,128)S(1)}, f32[96,1280]{1,0:T(8,128)S(1)}) custom-call(f32[48]{0:T(128)S(1)} %copy-done.9, f32[384,1280]{1,0:T(8,128)} %bitcast.13, f32[384,1280]{1,0:T(8,128)} %bitcast.14, f32[384,1280]{1,0:T(8,128)} %bitcast.9, ...), custom_call_target="tpu_custom_call" | custom-call | flops 1000000 | bytes 1000000 | tf_op jit(solution)/shard_map/columns/pallas_call | solution.py:504
  24.8 0.0 copy-start.1
  24.8 0.0 copy-start.5
  24.8 0.2 collective-permute-start.4
  24.9 3.7 %collective-permute-start.5 = (f32[96,1280]{1,0:T(8,128)S(1)}, f32[96,1280]{1,0:T(8,128)}, u32[]{:S(2)}, u32[]{:S(2)}) collective-permute-start(f32[96,1280]{1,0:T(8,128)S(1)} %get-tuple-element.42.rim_far), channel_id=1, source_target_pairs={{1,2},{3,4},{5,6},{7,8},{9,10},{11,12},{13,14},{2,1},{4,3},{6,5},{... | collective-permute-start | bytes 1474568 | tf_op jit(solution)/shard_map/ppermute | solution.py:481
  28.7 0.0 all-to-all-done
  28.7 0.0 copy-start.7
  28.7 0.9 %copy-done.7 = f32[24,1280]{1,0:T(8,128)S(1)} copy-done((f32[24,1280]{1,0:T(8,128)S(1)}, f32[24,1280]{1,0:T(8,128)}, u32[]{:S(2)}) %copy-start.7) | copy-done | bytes 122904
  29.6 2.1 %edges.1 = (f32[8,1280]{1,0:T(8,128)}, f32[8,1280]{1,0:T(8,128)S(1)}, f32[96,1280]{1,0:T(8,128)S(1)}, f32[96,1280]{1,0:T(8,128)S(1)}) custom-call(f32[128,128]{1,0:T(8,128)S(1)} %bitcast.11, f32[24,1280]{1,0:T(8,128)S(1)} %copy-done.7, f32[576,1280]{1,0:T(8,128)} %get-tuple-element.35.rim_hbm.rims), custom_call_target="tpu_custom_call" | custom-call | flops 1000000 | bytes 1000000 | tf_op jit(solution)/shard_map/edges/pallas_call | solution.py:516
  31.7 0.1 collective-permute-start.2
  31.8 3.5 %collective-permute-start.3 = (f32[96,1280]{1,0:T(8,128)S(1)}, f32[96,1280]{1,0:T(8,128)S(1)}, u32[]{:S(2)}, u32[]{:S(2)}) collective-permute-start(f32[96,1280]{1,0:T(8,128)S(1)} %get-tuple-element.40.own_far), channel_id=1, source_target_pairs={{1,2},{3,4},{5,6},{7,8},{9,10},{11,12},{13,14},{2,1},{4,3},{6,5},{... | collective-permute-start | bytes 1474568 | tf_op jit(solution)/shard_map/ppermute | solution.py:481
  35.2 0.0 copy-done.1
  35.3 0.0 copy-done.5
  35.3 0.0 copy-start.2
  35.3 1.5 %copy-done.2 = f32[48,8,1280]{2,1,0:T(8,128)S(1)} copy-done((f32[48,8,1280]{2,1,0:T(8,128)S(1)}, f32[48,8,1280]{2,1,0:T(8,128)}, u32[]{:S(2)}) %copy-start.2) | copy-done | bytes 1966104
  36.8 0.0 copy-start.3
  36.8 1.5 %copy-done.3 = f32[3840,128]{1,0:T(8,128)S(1)} copy-done((f32[3840,128]{1,0:T(8,128)S(1)}, f32[3840,128]{1,0:T(8,128)}, u32[]{:S(2)}) %copy-start.3) | copy-done | bytes 1966104
  38.4 0.0 copy-start.4
  38.4 1.5 %copy-done.4 = f32[3840,128]{1,0:T(8,128)S(1)} copy-done((f32[3840,128]{1,0:T(8,128)S(1)}, f32[3840,128]{1,0:T(8,128)}, u32[]{:S(2)}) %copy-start.4) | copy-done | bytes 1966104
  39.9 0.0 copy-start
  39.9 6.8 %inner.1.u2 = f32[384,1280]{1,0:T(8,128)S(1)} custom-call(s32[8,1280]{1,0:T(8,128)S(1)} %copy-done.5, f32[8,1280]{1,0:T(8,128)S(1)} %get-tuple-element.36.s_ref, f32[3840,128]{1,0:T(8,128)S(1)} %copy-done.3, f32[3840,128]{1,0:T(8,128)S(1)} %copy-done.4, f32[384,1280]{1,0:T(8,128)S(1)} %bitcast.10, s32[384,1280]{1,0:T(8,128)S(1)} %bitcast.8), custom_call_target="tpu_custom_call" | custom-call | flops 1000000 | bytes 1000000 | tf_op jit(solution)/shard_map/inner/pallas_call | solution.py:522
  46.7 0.0 collective-permute-done.4.rim_other_near
  46.7 0.0 collective-permute-done.5.rim_other_far
  46.7 0.0 collective-permute-done.2.near
  46.7 3.5 %collective-permute-done.3.far = f32[96,1280]{1,0:T(8,128)S(1)} collective-permute-done((f32[96,1280]{1,0:T(8,128)S(1)}, f32[96,1280]{1,0:T(8,128)S(1)}, u32[]{:S(2)}, u32[]{:S(2)}) %collective-permute-start.3) | collective-permute-done | bytes 491552 | tf_op jit(solution)/shard_map/ppermute | solution.py:481
  50.2 0.0 copy-done
  50.2 2.9 %finish.1 = f32[384,1280]{1,0:T(8,128)} custom-call(f32[384,1280]{1,0:T(8,128)S(1)} %inner.1.u2, f32[576,1280]{1,0:T(8,128)S(1)} %copy-done, f32[96,1280]{1,0:T(8,128)S(1)} %get-tuple-element.39.own_near, f32[96,1280]{1,0:T(8,128)S(1)} %get-tuple-element.40.own_far, f32[96,1280]{1,0:T(8,128)S(1)} %get-tuple-element.41.rim_near, ...), custom_call_target="tpu_custom_call" | custom-call | flops 1000000 | bytes 1000000 | tf_op jit(solution)/shard_map/finish/pallas_call | solution.py:526
Async XLA Ops:
  0.6 17.5 %copy-start.9 = (f32[48]{0:T(128)S(1)}, f32[48]{0:T(128)}, u32[]{:S(2)}) copy-start(f32[48]{0:T(128)} %weight.3) | copy-start | bytes 580
  0.6 0.7 %copy-start.8 = (f32[48]{0:T(128)S(1)}, f32[48]{0:T(128)}, u32[]{:S(2)}) copy-start(f32[48]{0:T(128)} %weight.3) | copy-start | bytes 580
  3.9 4.6 %collective-permute-start = (f32[8,1280]{1,0:T(8,128)S(1)}, f32[8,1280]{1,0:T(8,128)S(1)}, u32[]{:S(2)}, u32[]{:S(2)}) collective-permute-start(f32[8,1280]{1,0:T(8,128)S(1)} %get-tuple-element.30), channel_id=1, source_target_pairs={{0,1},{2,3},{4,5},{6,7},{8,9},{10,11},{12,13},{14,15},{1,0},{3,2},... | collective-permute-start | bytes 122888 | tf_op jit(solution)/shard_map/ppermute | solution.py:481
  4.0 6.2 %collective-permute-start.1 = (f32[8,1280]{1,0:T(8,128)S(1)}, f32[8,1280]{1,0:T(8,128)S(1)}, u32[]{:S(2)}, u32[]{:S(2)}) collective-permute-start(f32[8,1280]{1,0:T(8,128)S(1)} %get-tuple-element.31), channel_id=1, source_target_pairs={{1,2},{3,4},{5,6},{7,8},{9,10},{11,12},{13,14},{2,1},{4,3},{6,5},{... | collective-permute-start | bytes 122888 | tf_op jit(solution)/shard_map/ppermute | solution.py:481
  11.0 0.7 %copy-start.6 = (f32[24,1280]{1,0:T(8,128)}, f32[24,1280]{1,0:T(8,128)S(1)}, u32[]{:S(2)}) copy-start(f32[24,1280]{1,0:T(8,128)S(1)} %get-tuple-element.33.basis_ref) | copy-start | bytes 368644
  11.7 17.0 %all-to-all-start = ((f32[16,8,128]{2,1,0:T(8,128)}), f32[16,8,128]{2,1,0:T(8,128)S(1)}, u32[]{:S(2)}, u32[]{:S(2)}) async-start(f32[16,8,128]{2,1,0:T(8,128)} %bitcast.1), calls=%async_computation | async-start | bytes 131072 | tf_op jit(solution)/shard_map/all_to_all | solution.py:513
  24.8 10.5 %copy-start.1 = (s32[48,8,1280]{2,1,0:T(8,128)S(1)}, s32[48,8,1280]{2,1,0:T(8,128)}, u32[]{:S(2)}) copy-start(s32[48,8,1280]{2,1,0:T(8,128)} %param.12) | copy-start | bytes 5898244
  24.8 10.5 %copy-start.5 = (s32[8,1280]{1,0:T(8,128)S(1)}, s32[8,1280]{1,0:T(8,128)}, u32[]{:S(2)}) copy-start(s32[8,1280]{1,0:T(8,128)} %kmt.1) | copy-start | bytes 122884
  24.8 21.9 %collective-permute-start.4 = (f32[96,1280]{1,0:T(8,128)S(1)}, f32[96,1280]{1,0:T(8,128)S(1)}, u32[]{:S(2)}, u32[]{:S(2)}) collective-permute-start(f32[96,1280]{1,0:T(8,128)S(1)} %get-tuple-element.41.rim_near), channel_id=1, source_target_pairs={{0,1},{2,3},{4,5},{6,7},{8,9},{10,11},{12,13},{14,15},{1,0},{3,2},... | collective-permute-start | bytes 1474568 | tf_op jit(solution)/shard_map/ppermute | solution.py:481
  24.9 21.8 %collective-permute-start.5 = (f32[96,1280]{1,0:T(8,128)S(1)}, f32[96,1280]{1,0:T(8,128)}, u32[]{:S(2)}, u32[]{:S(2)}) collective-permute-start(f32[96,1280]{1,0:T(8,128)S(1)} %get-tuple-element.42.rim_far), channel_id=1, source_target_pairs={{1,2},{3,4},{5,6},{7,8},{9,10},{11,12},{13,14},{2,1},{4,3},{6,5},{... | collective-permute-start | bytes 1474568 | tf_op jit(solution)/shard_map/ppermute | solution.py:481
  28.7 0.9 %copy-start.7 = (f32[24,1280]{1,0:T(8,128)S(1)}, f32[24,1280]{1,0:T(8,128)}, u32[]{:S(2)}) copy-start(f32[24,1280]{1,0:T(8,128)} %copy-done.6) | copy-start | bytes 368644
  31.7 15.0 %collective-permute-start.2 = (f32[96,1280]{1,0:T(8,128)S(1)}, f32[96,1280]{1,0:T(8,128)S(1)}, u32[]{:S(2)}, u32[]{:S(2)}) collective-permute-start(f32[96,1280]{1,0:T(8,128)S(1)} %get-tuple-element.39.own_near), channel_id=1, source_target_pairs={{0,1},{2,3},{4,5},{6,7},{8,9},{10,11},{12,13},{14,15},{1,0},{3,2},... | collective-permute-start | bytes 1474568 | tf_op jit(solution)/shard_map/ppermute | solution.py:481
  31.8 18.4 %collective-permute-start.3 = (f32[96,1280]{1,0:T(8,128)S(1)}, f32[96,1280]{1,0:T(8,128)S(1)}, u32[]{:S(2)}, u32[]{:S(2)}) collective-permute-start(f32[96,1280]{1,0:T(8,128)S(1)} %get-tuple-element.40.own_far), channel_id=1, source_target_pairs={{1,2},{3,4},{5,6},{7,8},{9,10},{11,12},{13,14},{2,1},{4,3},{6,5},{... | collective-permute-start | bytes 1474568 | tf_op jit(solution)/shard_map/ppermute | solution.py:481
  35.3 1.5 %copy-start.2 = (f32[48,8,1280]{2,1,0:T(8,128)S(1)}, f32[48,8,1280]{2,1,0:T(8,128)}, u32[]{:S(2)}) copy-start(f32[48,8,1280]{2,1,0:T(8,128)} %param.10) | copy-start | bytes 5898244
  36.8 1.5 %copy-start.3 = (f32[3840,128]{1,0:T(8,128)S(1)}, f32[3840,128]{1,0:T(8,128)}, u32[]{:S(2)}) copy-start(f32[3840,128]{1,0:T(8,128)} %get-tuple-element.37.m0) | copy-start | bytes 5898244
  38.4 1.5 %copy-start.4 = (f32[3840,128]{1,0:T(8,128)S(1)}, f32[3840,128]{1,0:T(8,128)}, u32[]{:S(2)}) copy-start(f32[3840,128]{1,0:T(8,128)} %get-tuple-element.38.w) | copy-start | bytes 5898244
  39.9 10.3 %copy-start = (f32[576,1280]{1,0:T(8,128)S(1)}, f32[576,1280]{1,0:T(8,128)}, u32[]{:S(2)}) copy-start(f32[576,1280]{1,0:T(8,128)} %get-tuple-element.35.rim_hbm.rims) | copy-start | bytes 8847364

commit v4 on v3

--- a/solution.py
+++ b/solution.py
@@ -14,7 +14,8 @@
 MID = 0.5 * (HIGH + LOW)
 HALF = 0.5 * (HIGH - LOW)
 FLOAT = jnp.float32
-RIM = 12
+RIM = 8
+LINKS = 4
 LIMIT = 24 * 1024 * 1024
 
 
@@ -111,40 +112,54 @@
     return jnp.where(even, high, low), jnp.where(even, low, high)
 
 
-def setup_body(levels, weight, land, kmt_hbm, ct_hbm, screen_hbm, wet_ref, height_ref, surface_ref,
-               fx_ref, fn_ref, dg_ref, q1_ref, base_ref, near_ref, far_ref, buffer, kmt, screen, sems):
-    chunk = levels // 4
-    small = [
-        pltpu.make_async_copy(source, target, sems.at[4 + i])
-        for i, (source, target) in enumerate(((kmt_hbm, kmt), (ct_hbm, base_ref), (screen_hbm, screen)))
-    ]
-    copies = []
-    for i in range(4):
-        whole = pl.ds(i * chunk * ROWS, chunk * ROWS)
-        copies.append(pltpu.make_async_copy(land.at[whole], buffer.at[whole], sems.at[i]))
-    for copy in small[:1] + copies + small[1:]:
+def loads(pairs, sems, first=0):
+    copies = [pltpu.make_async_copy(far, near, sems.at[first + i]) for i, (far, near) in enumerate(pairs)]
+    for copy in copies:
         copy.start()
+    return copies
+
+
+def in_parts(far, near, parts):
+    size = far.shape[0] // parts
+    return [(far.at[pl.ds(i * size, size)], near.at[pl.ds(i * size, size)]) for i in range(parts)]
+
+
+def weight_sum(weight, levels):
     total = weight[0]
     for k in range(1, levels):
         total = total + weight[k]
+    return total
+
+
+def setup_body(levels, weight_hbm, land_hbm, kmt_hbm, ct_hbm, screen_hbm, kappa_hbm, height_ref, surface_ref,
+               fx_ref, fn_ref, dg_ref, q1_ref, base_ref, near_ref, far_ref, rim_near_ref, rim_far_ref, links_hbm,
+               weight, land, kmt, screen, kappa, wet_bricks, kappa_bricks, links, sems, out_sems):
+    chunk = levels // 4
+    small = loads(((weight_hbm, weight), (kmt_hbm, kmt)), sems)
+    land_copies = loads(in_parts(land_hbm, land, 4), sems, 2)
+    small += loads(((ct_hbm, base_ref), (screen_hbm, screen)), sems, 6)
+    kappa_copies = loads(in_parts(kappa_hbm, kappa, 4), sems, 8)
     small[0].wait()
+    total = weight_sum(weight, levels)
+    small[1].wait()
     depth = kmt[...]
+    width = depth.shape[1]
     height = jnp.zeros(depth.shape, FLOAT)
-    for i, copy in enumerate(copies):
+    for i, copy in enumerate(land_copies):
         copy.wait()
 
         def level(k, height):
-            wet = jnp.where(k < depth, buffer[rows_at(k), :], 0).astype(FLOAT)
-            wet_ref[level_at(k, depth.shape[1]), :] = stacked(wet)
+            wet = jnp.where(k < depth, land[rows_at(k), :], 0).astype(FLOAT)
+            wet_bricks[level_at(k, width), :] = stacked(wet)
             return height + weight[k] * wet
 
         height = lax.fori_loop(i * chunk, (i + 1) * chunk, level, height, unroll=4)
     height = height / total
-    surface = jnp.where(0 < depth, buffer[0:ROWS, :], 0).astype(FLOAT)
+    surface = jnp.where(0 < depth, land[0:ROWS, :], 0).astype(FLOAT)
     height_ref[...] = height
     surface_ref[...] = surface
-    small[1].wait()
     small[2].wait()
+    small[3].wait()
     base = base_ref[...]
     rows = row_index(base)
     scale = 0.5 / HALF
@@ -171,8 +186,32 @@
         at = slice(place, place + 1)
         near_ref[at, :], far_ref[at, :] = dealt(even, values[0:1, :], values[ROWS - 1 : ROWS, :])
 
-
-def basis_body(count, ct, height, surface, fx_ref, fn_ref, dg_ref, q1_ref, near, far, basis_ref, sums_ref):
+    for i, copy in enumerate(kappa_copies):
+        copy.wait()
+
+        def brick(k, carry):
+            kappa_bricks[level_at(k, width), :] = stacked(kappa[rows_at(k), :])
+            return carry
+
+        lax.fori_loop(i * chunk, (i + 1) * chunk, brick, 0, unroll=4)
+    for block in range(levels // 8):
+        found = []
+        for side, row, inner in ((0, 0, 1), (1, ROWS - 1, ROWS - 2)):
+            kap, kap_in = row_of(kappa_bricks, block, row, width), row_of(kappa_bricks, block, inner, width)
+            here, here_in = row_of(wet_bricks, block, row, width), row_of(wet_bricks, block, inner, width)
+            at = (block * LINKS + side * 2) * 8
+            links[pl.ds(at, 8), :] = 0.5 * (kap + east(kap)) * here * east(here)
+            links[pl.ds(at + 8, 8), :] = 0.5 * (kap + kap_in) * here * here_in
+            found.append((kap, here))
+        for place in range(2):
+            at = pl.ds(place * levels + block * 8, 8)
+            rim_near_ref[at, :], rim_far_ref[at, :] = dealt(even, found[0][place], found[1][place])
+    out = pltpu.make_async_copy(links, links_hbm, out_sems.at[0])
+    out.start()
+    out.wait()
+
+
+def basis_body(count, ct, height, surface, fx_ref, fn_ref, dg_ref, q1_ref, near, far, basis_hbm, sums_ref, basis_ref, sems):
     even = is_even()
     b0 = ct[...]
     rows = row_index(b0)
@@ -210,11 +249,14 @@
         turned = dg_h * extra - fx_h * east(extra) - west(fx_h) * west(extra)
         return (2.0 * (q2_h + turned + face * (b1_h - own)) - b0_h)[0:1, :]
 
+    copies = []
+    for place, values in enumerate((b0, b1, b2)):
+        whole = pl.ds(place * ROWS, ROWS)
+        basis_ref[whole, :] = values
+        copies += loads([(basis_ref.at[whole], basis_hbm.at[whole])], sems, place)
     b2_b = outer(sides[0], b1[0:1, :])
     b2_a = outer(sides[1], b1[ROWS - 1 : ROWS, :])
     next2 = apply(b2, b2_b, b2_a)
-    for place, values in enumerate((b0, b1, b2)):
-        basis_ref[place * ROWS : (place + 1) * ROWS, :] = values
     tile_rows = lax.broadcasted_iota(jnp.int32, (8, 128), 0)
     packed = jnp.zeros((8, 128), FLOAT)
     for place, (p, q) in enumerate(((b0, b0), (b0, b1), (b1, b1), (b1, b2), (b2, b2), (b2, next2))):
@@ -225,6 +267,8 @@
         packed = jnp.where(tile_rows == place, jnp.sum(folded, axis=0, keepdims=True), packed)
     for j in range(count):
         sums_ref[j * 8 : (j + 1) * 8, :] = packed
+    for copy in copies:
+        copy.wait()
 
 
 def quadratic(left, form):
@@ -272,34 +316,32 @@
     return x
 
 
-def edges_body(levels, count, sums, basis_ref, rim_hbm, out_hbm, s_ref, near_ref, far_ref, rims, sems):
+def edges_body(levels, count, sums, basis_hbm, rim_hbm, links_hbm, out_hbm, s_ref, near_ref, far_ref,
+               basis_ref, rims, links, sems):
     blocks = levels // 8
-    copies = []
-    for block in range(blocks):
-        whole = pl.ds(block * RIM * 8, RIM * 8)
-        copies.append(pltpu.make_async_copy(rim_hbm.at[whole], rims.at[whole], sems.at[block]))
-    for copy in copies:
-        copy.start()
+    basis_copy = loads([(basis_hbm, basis_ref)], sems)[0]
+    both = [pair for pairs in zip(in_parts(rim_hbm, rims, blocks), in_parts(links_hbm, links, blocks)) for pair in pairs]
+    copies = loads(both, sems, 1)
     total = sums[0:8, :]
     for j in range(1, count):
         total = total + sums[j * 8 : (j + 1) * 8, :]
     total = jnp.sum(total, axis=1, keepdims=True)
     mix = weights([total[i : i + 1, :] for i in range(6)])
+    basis_copy.wait()
     b0, b1, b2 = (basis_ref[i * ROWS : (i + 1) * ROWS, :] for i in range(3))
     s = mix[0] * b0 + mix[1] * b1 + mix[2] * b2
     s_ref[...] = s
-    copy_s = pltpu.make_async_copy(s_ref, out_hbm, sems.at[blocks])
-    copy_s.start()
+    copy_s = loads([(s_ref, out_hbm)], sems, 2 * blocks + 1)[0]
     s_rows = {r: spread(s[r : r + 1, :], s) for r in (0, 1, ROWS - 2, ROWS - 1)}
     even = is_even()
 
-    for block, copy in enumerate(copies):
-        copy.wait()
+    for block in range(blocks):
+        copies[2 * block].wait()
+        copies[2 * block + 1].wait()
         found = []
         for side, row, inner in ((0, 0, 1), (1, ROWS - 1, ROWS - 2)):
-            m, gm, w, q, face, link = (
-                rims[pl.ds((block * RIM + side * 6 + i) * 8, 8), :] for i in range(6)
-            )
+            m, gm, w, q = (rims[pl.ds((block * RIM + side * 4 + i) * 8, 8), :] for i in range(4))
+            face, link = (links[pl.ds((block * LINKS + side * 2 + i) * 8, 8), :] for i in range(2))
             v = s_rows[row] * w
             flux = face * (east(v) - v)
             found.append((m + v, gm + v + (flux - west(flux)) - link * v + s_rows[inner] * q))
@@ -309,29 +351,29 @@
     copy_s.wait()
 
 
-def columns_body(levels, weight, source_hbm, kvert_hbm, kappa_hbm, wet, m0_hbm, w_hbm, rim_hbm, near_ref, far_ref,
-                 source, kvert, kappa, m0, w, ratio, bricks, rims, in_sems, out_sems):
+def columns_body(levels, weight_hbm, kmt_hbm, source_hbm, kvert_hbm, land_hbm, links_hbm, m0_hbm, w_hbm, rim_hbm,
+                 weight, kmt, source, kvert, land, links, m0, w, ratio, rims, in_sems, out_sems):
     width = source.shape[1]
     parts = 4
     chunk = levels // parts
-    ins = []
-    for i in range(parts):
-        whole = pl.ds(i * chunk * ROWS, chunk * ROWS)
-        for a, (far, near) in enumerate(((source_hbm, source), (kvert_hbm, kvert), (kappa_hbm, kappa))):
-            ins.append(pltpu.make_async_copy(far.at[whole], near.at[whole], in_sems.at[i * 3 + a]))
-    for copy in [ins[i * 3 + a] for i in range(parts) for a in (0, 1)] + ins[2::3]:
-        copy.start()
-    total = weight[0]
-    for k in range(1, levels):
-        total = total + weight[k]
+    small = loads(((weight_hbm, weight), (kmt_hbm, kmt)), in_sems)
+    parted = [in_parts(far, near, parts) for far, near in ((land_hbm, land), (kvert_hbm, kvert), (source_hbm, source))]
+    big = loads([pairs[i] for i in range(parts) for pairs in parted], in_sems, 2)
+    links_copy = loads([(links_hbm, links)], in_sems, 2 + 3 * parts)[0]
+    small[0].wait()
+    total = weight_sum(weight, levels)
     shape = (ROWS * width // 128, 128)
     inverse = 1.0 / jnp.full(shape, total, FLOAT)
+    small[1].wait()
+    depth = stacked(kmt[...])
+
+    def sea(k):
+        return jnp.where(k < depth, stacked(land[rows_at(k), :]), 0).astype(FLOAT)
 
     def down(k, carry):
-        link, m_in, w_in = carry
+        here, link, m_in, w_in = carry
         at = level_at(k, width)
-        here = wet[at, :]
-        below = jnp.where(k + 1 < levels, wet[level_at(jnp.minimum(k + 1, levels - 1), width), :], 0.0)
+        below = jnp.where(k + 1 < levels, sea(jnp.minimum(k + 1, levels - 1)), 0.0)
         coupling = stacked(kvert[rows_at(k), :]) * here * below
         over = 1.0 / (1.0 + coupling + link)
         m_here = (stacked(source[rows_at(k), :]) + m_in) * over
@@ -340,13 +382,16 @@
         ratio[at, :] = part
         m0[at, :] = m_here
         w[at, :] = w_here
-        return coupling - coupling * part, coupling * m_here, coupling * w_here
+        return below, coupling - coupling * part, coupling * m_here, coupling * w_here
 
     zero = jnp.zeros(shape, FLOAT)
-    carry = (zero, zero, zero)
+    big[0].wait()
+    carry = (sea(0), zero, zero, zero)
     for i in range(parts):
-        ins[i * 3].wait()
-        ins[i * 3 + 1].wait()
+        big[3 * i + 1].wait()
+        big[3 * i + 2].wait()
+        if i + 1 < parts:
+            big[3 * i + 3].wait()
         carry = lax.fori_loop(i * chunk, (i + 1) * chunk, down, carry)
 
     def up(i, carry):
@@ -369,42 +414,30 @@
             copy = pltpu.make_async_copy(near.at[whole], far.at[whole], out_sems.at[i * 2 + a])
             copy.start()
             outs.append(copy)
-    for i in range(parts):
-        ins[i * 3 + 2].wait()
-
-    def brick(k, carry):
-        bricks[level_at(k, width), :] = stacked(kappa[rows_at(k), :])
-        return carry
-
-    lax.fori_loop(0, levels, brick, 0, unroll=4)
-    even = is_even()
+    links_copy.wait()
     for block in range(levels // 8):
-        found = []
         for side, row, inner in ((0, 0, 1), (1, ROWS - 1, ROWS - 2)):
-            kap, kap_in = row_of(bricks, block, row, width), row_of(bricks, block, inner, width)
-            here, here_in = row_of(wet, block, row, width), row_of(wet, block, inner, width)
             m, w_row = row_of(m0, block, row, width), row_of(w, block, row, width)
-            face = 0.5 * (kap + east(kap)) * here * east(here)
-            link = 0.5 * (kap + kap_in) * here * here_in
+            face, link = (links[pl.ds((block * LINKS + side * 2 + i) * 8, 8), :] for i in range(2))
             flux = face * (east(m) - m)
             gm = m + (flux - west(flux)) + link * (row_of(m0, block, inner, width) - m)
             q = link * row_of(w, block, inner, width)
-            for i, values in enumerate((m, gm, w_row, q, face, link)):
-                rims[pl.ds((block * RIM + side * 6 + i) * 8, 8), :] = values
-            found.append((kap, here))
-        for place in range(2):
-            at = pl.ds(place * levels + block * 8, 8)
-            near_ref[at, :], far_ref[at, :] = dealt(even, found[0][place], found[1][place])
+            for i, values in enumerate((m, gm, w_row, q)):
+                rims[pl.ds((block * RIM + side * 4 + i) * 8, 8), :] = values
         whole = pl.ds(block * RIM * 8, RIM * 8)
-        copy = pltpu.make_async_copy(rims.at[whole], rim_hbm.at[whole], out_sems.at[2 * parts + block])
-        copy.start()
-        outs.append(copy)
+        outs += loads([(rims.at[whole], rim_hbm.at[whole])], out_sems, 2 * parts + block)
     for copy in outs:
         copy.wait()
 
 
-def inner_body(levels, kmt, s_ref, m0, w, kappa, land, u2_ref):
+def inner_body(levels, s_ref, kmt_hbm, m0_hbm, w_hbm, kappa_hbm, land_hbm, u2_ref, kmt, m0, w, kappa, land, sems):
+    parts = 4
+    kmt_copy = loads([(kmt_hbm, kmt)], sems)[0]
+    pairs = ((kappa_hbm, kappa), (land_hbm, land), (m0_hbm, m0), (w_hbm, w))
+    parted = [in_parts(far, near, parts) for far, near in pairs]
+    copies = loads([pairs[i] for i in range(parts) for pairs in parted], sems, 1)
     s = s_ref[...]
+    kmt_copy.wait()
     depth = kmt[...]
     inside = row_index(s) < ROWS - 1
 
@@ -430,10 +463,14 @@
             u2_ref[rows_at(k), :] = values
         return carry
 
-    lax.fori_loop(0, levels // 2, group, 0)
-
-
-def finish_body(levels, u2, rims, own_near, own_far, rim_near, rim_far, near, far, rim_other_near, rim_other_far,
+    chunk = levels // 2 // parts
+    for i in range(parts):
+        for copy in copies[4 * i : 4 * i + 4]:
+            copy.wait()
+        lax.fori_loop(i * chunk, (i + 1) * chunk, group, 0)
+
+
+def finish_body(levels, u2, links, own_near, own_far, rim_near, rim_far, near, far, rim_other_near, rim_other_far,
                 out, change_ref, buffer, sems):
     width = own_near.shape[1]
     tall = width // 128 * ROWS
@@ -452,7 +489,7 @@
         for side, row, inner in ((0, 0, 1), (1, ROWS - 1, ROWS - 2)):
             face = 0.5 * (rim[0][side] + rim_other[0][side]) * rim[1][side] * rim_other[1][side]
             change = face * (other[0][side] - own[0][side])
-            along, link = (rims[pl.ds((block * RIM + side * 6 + i) * 8, 8), :] for i in (4, 5))
+            along, link = (links[pl.ds((block * LINKS + side * 2 + i) * 8, 8), :] for i in range(2))
             flux = along * (east(change) - change)
             passed = link * change
             on_row = (change + (flux - west(flux)) - passed
@@ -489,44 +526,51 @@
     count = lax.axis_size("tile")
     tall = levels * rows
     tile, brick, flat = (rows, width), (tall * width // 128, 128), (tall, width)
-    rim, rim_rows = (2 * levels, width), (levels * RIM, width)
-    scalars = [pl.BlockSpec(memory_space=pltpu.SMEM)]
-    ct_tracer, kappa, kvert, land = (a.reshape(flat) for a in (ct_tracer, kappa, kvert, land))
+    rim, rim_rows, link_rows = (2 * levels, width), (levels * RIM, width), (levels * LINKS, width)
+    scalars, whole = pltpu.SMEM((levels,), FLOAT), pltpu.VMEM(flat, FLOAT)
+    ints, tile_ints = pltpu.VMEM(flat, jnp.int32), pltpu.VMEM(tile, jnp.int32)
+    bricks, tiles = pltpu.VMEM(brick, FLOAT), pltpu.VMEM(tile, FLOAT)
+    ct_tracer, kappa, kvert, land = (left(a.reshape(flat)) for a in (ct_tracer, kappa, kvert, land))
+    kmt, layer_weight = left(kmt), left(layer_weight)
     semaphores = pltpu.SemaphoreType.DMA
 
-    wet, height, surface, s_fx, s_fn, s_dg, q1, base, to_near, to_far = kernel(
-        functools.partial(setup_body, levels), vmem(brick, *[tile] * 9), scalars + in_hbm(4), in_vmem(10), "setup",
-        [pltpu.VMEM(flat, jnp.int32), pltpu.VMEM(tile, jnp.int32), pltpu.VMEM(tile, FLOAT), semaphores((7,))],
-    )(layer_weight, left(land), left(kmt), left(ct_surface), left(screen))
+    height, surface, s_fx, s_fn, s_dg, q1, base, to_near, to_far, rim_near, rim_far, links = kernel(
+        functools.partial(setup_body, levels), vmem(*[tile] * 9, rim, rim) + hbm(link_rows), in_hbm(6),
+        in_vmem(11) + in_hbm(1), "setup",
+        [scalars, ints, tile_ints, tiles, whole, bricks, bricks, pltpu.VMEM(link_rows, FLOAT), semaphores((12,)),
+         semaphores((1,))],
+    )(layer_weight, land, kmt, left(ct_surface), left(screen), kappa)
     near, far = exchange(to_near, to_far)
-
-    fields = [pltpu.VMEM(flat, FLOAT)] * 3 + [pltpu.VMEM(brick, FLOAT)] * 4 + [pltpu.VMEM(rim_rows, FLOAT)]
-    m0, w, rims, rim_near, rim_far = kernel(
-        functools.partial(columns_body, levels), hbm(brick, brick, rim_rows) + vmem(rim, rim),
-        scalars + in_hbm(3) + in_vmem(1), in_hbm(3) + in_vmem(2), "columns",
-        fields + [semaphores((12,)), semaphores((8 + levels // 8,))],
-    )(layer_weight, left(ct_tracer), left(kvert), left(kappa), wet)
+    rim_other_near, rim_other_far = exchange(rim_near, rim_far)
 
     basis, sums = kernel(
-        functools.partial(basis_body, count), vmem((3 * rows, width), (8 * count, 128)), in_vmem(9), in_vmem(2), "basis"
+        functools.partial(basis_body, count), hbm((3 * rows, width)) + vmem((8 * count, 128)), in_vmem(9),
+        in_hbm(1) + in_vmem(1), "basis", [pltpu.VMEM((3 * rows, width), FLOAT), semaphores((3,))],
     )(base, height, surface, s_fx, s_fn, s_dg, q1, near, far)
     sums = lax.all_to_all(sums.reshape(count, 8, 128), "tile", 0, 0, tiled=True).reshape(8 * count, 128)
-    rim_other_near, rim_other_far = exchange(rim_near, rim_far)
+
+    m0, w, rims = kernel(
+        functools.partial(columns_body, levels), hbm(brick, brick, rim_rows), in_hbm(6), in_hbm(3), "columns",
+        [scalars, tile_ints, whole, whole, ints, pltpu.VMEM(link_rows, FLOAT), bricks, bricks, bricks,
+         pltpu.VMEM(rim_rows, FLOAT), semaphores((15,)), semaphores((8 + levels // 8,))],
+    )(layer_weight, kmt, ct_tracer, kvert, land, left(links))
 
     solution, s, row_near, row_far = kernel(
         functools.partial(edges_body, levels, count), hbm(tile) + vmem(tile, rim, rim),
-        in_vmem(2) + in_hbm(1), in_hbm(1) + in_vmem(3), "edges",
-        [pltpu.VMEM(rim_rows, FLOAT), semaphores((levels // 8 + 1,))],
-    )(sums, basis, left(rims))
+        in_vmem(1) + in_hbm(3), in_hbm(1) + in_vmem(3), "edges",
+        [pltpu.VMEM((3 * rows, width), FLOAT), pltpu.VMEM(rim_rows, FLOAT), pltpu.VMEM(link_rows, FLOAT),
+         semaphores((levels // 4 + 2,))],
+    )(sums, left(basis), left(rims), left(links))
     other_near, other_far = exchange(row_near, row_far)
     u2 = kernel(
-        functools.partial(inner_body, levels), vmem(flat), in_vmem(6), in_vmem(1), "inner"
-    )(held(kmt), s, held(m0), held(w), held(kappa), held(land))[0]
+        functools.partial(inner_body, levels), vmem(flat), in_vmem(1) + in_hbm(5), in_vmem(1), "inner",
+        [tile_ints, bricks, bricks, whole, ints, semaphores((17,))],
+    )(s, kmt, left(m0), left(w), kappa, land)[0]
 
     values = kernel(
         functools.partial(finish_body, levels), hbm(flat), in_vmem(10), in_hbm(1), "finish",
-        [pltpu.VMEM((8 * rows * width // 128, 128), FLOAT), pltpu.VMEM(flat, FLOAT), semaphores((levels // 8,))],
-    )(u2, held(rims), row_near, row_far, rim_near, rim_far, other_near, other_far, rim_other_near, rim_other_far)[0]
+        [pltpu.VMEM((8 * rows * width // 128, 128), FLOAT), whole, semaphores((levels // 8,))],
+    )(u2, held(links), row_near, row_far, rim_near, rim_far, other_near, other_far, rim_other_near, rim_other_far)[0]
     return (values.reshape(levels, rows, width), solution)
 
 

time: 53.9 us -> 48.1 us (0.89)
  local copies, waits for them, and re-layouts: 6.91 us -> 0.01 us
  Pallas kernels: 21.7 us -> 24.2 us
  waiting for transfers between devices: 5.15 us -> 4.2 us
    unnamed x20 -> x2, local copies, waits for them, and re-layouts: 6.91 us -> 0.01 us
    pallas_call x3, Pallas kernels: 10.1 us -> 13.8 us  [the longest x1 8.44 us: body(): kernel(functools.partial(inner_body, levels), vmem(flat), in_vmem(1) + in...]
    pallas_call x1, Pallas kernels: 2.89 us -> 1.89 us  [body(): kernel(functools.partial(finish_body, levels), hbm(flat), in_vmem(10), in...]
    ppermute x6, waiting for transfers between devices: 5.15 us -> 4.2 us  [swap(): lax.ppermute(array, 'tile', [(i, i + 1) for i in firsts] + [(i + 1, i) fo...]
  transfers between devices with their start and end apart: 7 -> 7, of which waited for: 2 -> 2; matrix products, arithmetic and copies ran while one was open for 0% -> 0% of each run, Pallas kernels for 29% -> 36%
where the time goes in v4:
time: 48.1 us; the launch traced here: 47.5 us
  Pallas kernels  24.2 us (50%)
  starting transfers between devices  18.3 us (38%)
  waiting for transfers between devices  4.2 us (9%)
  between operations  0.75 us (2%)
    ppermute x6, starting transfers between devices, swap(): lax.ppermute(array, 'tile', [(i, i + 1) for i in firsts] + [(i + 1, i) fo...  11.8 us
    pallas_call x1, Pallas kernels, body(): kernel(functools.partial(inner_body, levels), vmem(flat), in_vmem(1) + in...  8.44 us
    all_to_all x1, starting transfers between devices, body(): lax.all_to_all(sums.reshape(count, 8, 128), 'tile', 0, 0, tiled=True)  6.51 us
    pallas_call x1, Pallas kernels, body(): kernel(functools.partial(columns_body, levels), hbm(brick, brick, rim_row...  6.28 us
    ppermute x6, waiting for transfers between devices, swap(): lax.ppermute(array, 'tile', [(i, i + 1) for i in firsts] + [(i + 1, i) fo...  4.2 us
    pallas_call x1, Pallas kernels, body(): kernel(functools.partial(setup_body, levels), vmem(*[tile] * 9, rim, rim)...  3.92 us
    pallas_call x1, Pallas kernels, body(): kernel(functools.partial(edges_body, levels, count), hbm(tile) + vmem(til...  2.24 us
    pallas_call x1, Pallas kernels, body(): kernel(functools.partial(finish_body, levels), hbm(flat), in_vmem(10), in...  1.89 us
  transfers between devices with their start and end apart: 7, of which 2 were waited for; matrix products, arithmetic and copies ran while one was open for 0% of the time, Pallas kernels for 36%

profile of v4, /device:TPU:1, one launch (start us, length us, event | category | flops | bytes accessed | tf_op | source)
XLA Modules:
  0.0 47.5 jit_solution(2238203684198499270)
XLA Ops:
  0.6 3.9 %setup.1 = (f32[8,1280]{1,0:T(8,128)S(1)}, f32[8,1280]{1,0:T(8,128)S(1)}, f32[8,1280]{1,0:T(8,128)S(1)}, f32[8,1280]{1,0:T(8,128)S(1)}, f32[8,1280]{1,0:T(8,128)...) custom-call(f32[48]{0:T(128)} %weight_hbm.3, ...), custom_call_target="tpu_custom_call" | custom-call | flops 1000000 | bytes 1000000 | tf_op jit(solution)/shard_map/setup/pallas_call | solution.py:537
  4.6 0.1 collective-permute-start
  4.7 4.5 %collective-permute-start.1 = (f32[8,1280]{1,0:T(8,128)S(1)}, f32[8,1280]{1,0:T(8,128)S(1)}, u32[]{:S(2)}, u32[]{:S(2)}) collective-permute-start(f32[8,1280]{1,0:T(8,128)S(1)} %get-tuple-element.31), channel_id=1, source_target_pairs={{1,2},{3,4},{5,6},{7,8},{9,10},{11,12},{13,14},{2,1},{4,3},{6,5},{... | collective-permute-start | bytes 122888 | tf_op jit(solution)/shard_map/ppermute | solution.py:518
  9.2 0.0 collective-permute-done.near
  9.2 1.7 %collective-permute-done.1.far = f32[8,1280]{1,0:T(8,128)S(1)} collective-permute-done((f32[8,1280]{1,0:T(8,128)S(1)}, f32[8,1280]{1,0:T(8,128)S(1)}, u32[]{:S(2)}, u32[]{:S(2)}) %collective-permute-start.1) | collective-permute-done | bytes 40992 | tf_op jit(solution)/shard_map/ppermute | solution.py:518
  10.9 1.4 %basis.1 = (f32[24,1280]{1,0:T(8,128)}, f32[128,128]{1,0:T(8,128)}) custom-call(f32[8,1280]{1,0:T(8,128)S(1)} %get-tuple-element.23.ct, f32[8,1280]{1,0:T(8,128)S(1)} %get-tuple-element.24.height, f32[8,1280]{1,0:T(8,128)S(1)} %get-tuple-element.25.surface, f32[8,1280]{1,0:T(8,128)S(1)} %get-tuple-element.26.fx_ref, f32[8,1280]{1,0:T(8,128)S(1)} %get-tuple-element.27.fn_ref, ...), custom_call_target="tpu_custom_call" | custom-call | flops 1000000 | bytes 1000000 | tf_op jit(solution)/shard_map/basis/pallas_call | solution.py:546
  12.3 6.5 %all-to-all-start = ((f32[16,8,128]{2,1,0:T(8,128)}), f32[16,8,128]{2,1,0:T(8,128)S(1)}, u32[]{:S(2)}, u32[]{:S(2)}) async-start(f32[16,8,128]{2,1,0:T(8,128)} %bitcast.2), calls=%async_computation | async-start | bytes 131072 | tf_op jit(solution)/shard_map/all_to_all | solution.py:550
  18.8 0.2 collective-permute-start.4
  18.9 3.5 %collective-permute-start.5 = (f32[96,1280]{1,0:T(8,128)S(1)}, f32[96,1280]{1,0:T(8,128)S(1)}, u32[]{:S(2)}, u32[]{:S(2)}) collective-permute-start(f32[96,1280]{1,0:T(8,128)S(1)} %get-tuple-element.42.rim_far), channel_id=1, source_target_pairs={{1,2},{3,4},{5,6},{7,8},{9,10},{11,12},{13,14},{2,1},{4,3},{6,5},{... | collective-permute-start | bytes 1474568 | tf_op jit(solution)/shard_map/ppermute | solution.py:518
  22.5 6.3 %columns.1 = (f32[3840,128]{1,0:T(8,128)}, f32[3840,128]{1,0:T(8,128)}, f32[384,1280]{1,0:T(8,128)}) custom-call(f32[48]{0:T(128)} %weight_hbm.3, s32[8,1280]{1,0:T(8,128)} %kmt_hbm.5, f32[384,1280]{1,0:T(8,128)} %bitcast.14, f32[384,1280]{1,0:T(8,128)} %bitcast.15, s32[384,1280]{1,0:T(8,128)} %bitcast.9, f32[192,1280]{1,0:T(8,128)} %get-tuple-element.34.links_hbm.links), custom_call_target="tpu_custom_call" | custom-call | flops 1000000 | bytes 1000000 | tf_op jit(solution)/shard_map/columns/pallas_call | solution.py:552
  28.8 0.0 all-to-all-done
  28.8 2.2 %edges.1 = (f32[8,1280]{1,0:T(8,128)}, f32[8,1280]{1,0:T(8,128)S(1)}, f32[96,1280]{1,0:T(8,128)S(1)}, f32[96,1280]{1,0:T(8,128)S(1)}) custom-call(f32[128,128]{1,0:T(8,128)S(1)} %bitcast.7, f32[24,1280]{1,0:T(8,128)} %get-tuple-element.33.basis_hbm, f32[384,1280]{1,0:T(8,128)} %get-tuple-element.35.rim_hbm, f32[192,1280]{1,0:T(8,128)} %get-tuple-element.34.links_hbm.links), custom_call_target="tpu_custom_call" | custom-call | flops 1000000 | bytes 1000000 | tf_op jit(solution)/shard_map/edges/pallas_call | solution.py:558
  31.0 0.1 collective-permute-start.2
  31.1 3.5 %collective-permute-start.3 = (f32[96,1280]{1,0:T(8,128)S(1)}, f32[96,1280]{1,0:T(8,128)S(1)}, u32[]{:S(2)}, u32[]{:S(2)}) collective-permute-start(f32[96,1280]{1,0:T(8,128)S(1)} %get-tuple-element.40.own_far), channel_id=1, source_target_pairs={{1,2},{3,4},{5,6},{7,8},{9,10},{11,12},{13,14},{2,1},{4,3},{6,5},{... | collective-permute-start | bytes 1474568 | tf_op jit(solution)/shard_map/ppermute | solution.py:518
  34.6 0.0 copy-start
  34.6 8.4 %inner.1.u2 = f32[384,1280]{1,0:T(8,128)S(1)} custom-call(f32[8,1280]{1,0:T(8,128)S(1)} %get-tuple-element.36.s_ref, s32[8,1280]{1,0:T(8,128)} %kmt_hbm.5, f32[3840,128]{1,0:T(8,128)} %get-tuple-element.37.m0_hbm, f32[3840,128]{1,0:T(8,128)} %get-tuple-element.38.w_hbm, f32[384,1280]{1,0:T(8,128)} %bitcast.12, s32[384,1280]{1,0:T(8,128)} %bitcast.10), custom_call_target="tpu_custom_call" | custom-call | flops 1000000 | bytes 1000000 | tf_op jit(solution)/shard_map/inner/pallas_call | solution.py:565
  43.0 0.0 collective-permute-done.4.rim_other_near
  43.0 0.0 collective-permute-done.5.rim_other_far
  43.0 0.0 collective-permute-done.2.near
  43.1 2.5 %collective-permute-done.3.far = f32[96,1280]{1,0:T(8,128)S(1)} collective-permute-done((f32[96,1280]{1,0:T(8,128)S(1)}, f32[96,1280]{1,0:T(8,128)S(1)}, u32[]{:S(2)}, u32[]{:S(2)}) %collective-permute-start.3) | collective-permute-done | bytes 491552 | tf_op jit(solution)/shard_map/ppermute | solution.py:518
  45.6 0.0 copy-done
  45.6 1.9 %finish.1 = f32[384,1280]{1,0:T(8,128)} custom-call(f32[384,1280]{1,0:T(8,128)S(1)} %inner.1.u2, f32[192,1280]{1,0:T(8,128)S(1)} %copy-done, f32[96,1280]{1,0:T(8,128)S(1)} %get-tuple-element.39.own_near, f32[96,1280]{1,0:T(8,128)S(1)} %get-tuple-element.40.own_far, f32[96,1280]{1,0:T(8,128)S(1)} %get-tuple-element.41.rim_near, ...), custom_call_target="tpu_custom_call" | custom-call | flops 1000000 | bytes 1000000 | tf_op jit(solution)/shard_map/finish/pallas_call | solution.py:570
Async XLA Ops:
  4.6 4.6 %collective-permute-start = (f32[8,1280]{1,0:T(8,128)S(1)}, f32[8,1280]{1,0:T(8,128)S(1)}, u32[]{:S(2)}, u32[]{:S(2)}) collective-permute-start(f32[8,1280]{1,0:T(8,128)S(1)} %get-tuple-element.30), channel_id=1, source_target_pairs={{0,1},{2,3},{4,5},{6,7},{8,9},{10,11},{12,13},{14,15},{1,0},{3,2},... | collective-permute-start | bytes 122888 | tf_op jit(solution)/shard_map/ppermute | solution.py:518
  4.7 6.2 %collective-permute-start.1 = (f32[8,1280]{1,0:T(8,128)S(1)}, f32[8,1280]{1,0:T(8,128)S(1)}, u32[]{:S(2)}, u32[]{:S(2)}) collective-permute-start(f32[8,1280]{1,0:T(8,128)S(1)} %get-tuple-element.31), channel_id=1, source_target_pairs={{1,2},{3,4},{5,6},{7,8},{9,10},{11,12},{13,14},{2,1},{4,3},{6,5},{... | collective-permute-start | bytes 122888 | tf_op jit(solution)/shard_map/ppermute | solution.py:518
  12.3 16.5 %all-to-all-start = ((f32[16,8,128]{2,1,0:T(8,128)}), f32[16,8,128]{2,1,0:T(8,128)S(1)}, u32[]{:S(2)}, u32[]{:S(2)}) async-start(f32[16,8,128]{2,1,0:T(8,128)} %bitcast.2), calls=%async_computation | async-start | bytes 131072 | tf_op jit(solution)/shard_map/all_to_all | solution.py:550
  18.8 24.2 %collective-permute-start.4 = (f32[96,1280]{1,0:T(8,128)S(1)}, f32[96,1280]{1,0:T(8,128)S(1)}, u32[]{:S(2)}, u32[]{:S(2)}) collective-permute-start(f32[96,1280]{1,0:T(8,128)S(1)} %get-tuple-element.41.rim_near), channel_id=1, source_target_pairs={{0,1},{2,3},{4,5},{6,7},{8,9},{10,11},{12,13},{14,15},{1,0},{3,2},... | collective-permute-start | bytes 1474568 | tf_op jit(solution)/shard_map/ppermute | solution.py:518
  18.9 24.1 %collective-permute-start.5 = (f32[96,1280]{1,0:T(8,128)S(1)}, f32[96,1280]{1,0:T(8,128)S(1)}, u32[]{:S(2)}, u32[]{:S(2)}) collective-permute-start(f32[96,1280]{1,0:T(8,128)S(1)} %get-tuple-element.42.rim_far), channel_id=1, source_target_pairs={{1,2},{3,4},{5,6},{7,8},{9,10},{11,12},{13,14},{2,1},{4,3},{6,5},{... | collective-permute-start | bytes 1474568 | tf_op jit(solution)/shard_map/ppermute | solution.py:518
  31.0 12.0 %collective-permute-start.2 = (f32[96,1280]{1,0:T(8,128)S(1)}, f32[96,1280]{1,0:T(8,128)S(1)}, u32[]{:S(2)}, u32[]{:S(2)}) collective-permute-start(f32[96,1280]{1,0:T(8,128)S(1)} %get-tuple-element.39.own_near), channel_id=1, source_target_pairs={{0,1},{2,3},{4,5},{6,7},{8,9},{10,11},{12,13},{14,15},{1,0},{3,2},... | collective-permute-start | bytes 1474568 | tf_op jit(solution)/shard_map/ppermute | solution.py:518
  31.1 14.5 %collective-permute-start.3 = (f32[96,1280]{1,0:T(8,128)S(1)}, f32[96,1280]{1,0:T(8,128)S(1)}, u32[]{:S(2)}, u32[]{:S(2)}) collective-permute-start(f32[96,1280]{1,0:T(8,128)S(1)} %get-tuple-element.40.own_far), channel_id=1, source_target_pairs={{1,2},{3,4},{5,6},{7,8},{9,10},{11,12},{13,14},{2,1},{4,3},{6,5},{... | collective-permute-start | bytes 1474568 | tf_op jit(solution)/shard_map/ppermute | solution.py:518
  34.6 11.0 %copy-start = (f32[192,1280]{1,0:T(8,128)S(1)}, f32[192,1280]{1,0:T(8,128)}, u32[]{:S(2)}) copy-start(f32[192,1280]{1,0:T(8,128)} %get-tuple-element.34.links_hbm.links) | copy-start | bytes 2949124

commit v5 on v4

--- a/solution.py
+++ b/solution.py
@@ -83,7 +83,7 @@
     return [pl.BlockSpec(memory_space=pltpu.HBM)] * count
 
 
-def kernel(body, outs, ins, out_specs, name, scratch=(), cost=1000000):
+def kernel(body, outs, ins, out_specs, name, scratch=(), cost=1):
     return pl.pallas_call(
         body,
         out_shape=outs,
@@ -211,7 +211,7 @@
     out.wait()
 
 
-def basis_body(count, ct, height, surface, fx_ref, fn_ref, dg_ref, q1_ref, near, far, basis_hbm, sums_ref, basis_ref, sems):
+def basis_body(count, ct, height, surface, fx_ref, fn_ref, dg_ref, q1_ref, near, far, basis_ref, sums_ref):
     even = is_even()
     b0 = ct[...]
     rows = row_index(b0)
@@ -249,11 +249,8 @@
         turned = dg_h * extra - fx_h * east(extra) - west(fx_h) * west(extra)
         return (2.0 * (q2_h + turned + face * (b1_h - own)) - b0_h)[0:1, :]
 
-    copies = []
     for place, values in enumerate((b0, b1, b2)):
-        whole = pl.ds(place * ROWS, ROWS)
-        basis_ref[whole, :] = values
-        copies += loads([(basis_ref.at[whole], basis_hbm.at[whole])], sems, place)
+        basis_ref[pl.ds(place * ROWS, ROWS), :] = values
     b2_b = outer(sides[0], b1[0:1, :])
     b2_a = outer(sides[1], b1[ROWS - 1 : ROWS, :])
     next2 = apply(b2, b2_b, b2_a)
@@ -267,8 +264,6 @@
         packed = jnp.where(tile_rows == place, jnp.sum(folded, axis=0, keepdims=True), packed)
     for j in range(count):
         sums_ref[j * 8 : (j + 1) * 8, :] = packed
-    for copy in copies:
-        copy.wait()
 
 
 def quadratic(left, form):
@@ -316,22 +311,20 @@
     return x
 
 
-def edges_body(levels, count, sums, basis_hbm, rim_hbm, links_hbm, out_hbm, s_ref, near_ref, far_ref,
-               basis_ref, rims, links, sems):
+def edges_body(levels, count, sums, basis_ref, rim_hbm, links_hbm, out_hbm, s_ref, near_ref, far_ref,
+               rims, links, sems):
     blocks = levels // 8
-    basis_copy = loads([(basis_hbm, basis_ref)], sems)[0]
     both = [pair for pairs in zip(in_parts(rim_hbm, rims, blocks), in_parts(links_hbm, links, blocks)) for pair in pairs]
-    copies = loads(both, sems, 1)
+    copies = loads(both, sems)
     total = sums[0:8, :]
     for j in range(1, count):
         total = total + sums[j * 8 : (j + 1) * 8, :]
     total = jnp.sum(total, axis=1, keepdims=True)
     mix = weights([total[i : i + 1, :] for i in range(6)])
-    basis_copy.wait()
     b0, b1, b2 = (basis_ref[i * ROWS : (i + 1) * ROWS, :] for i in range(3))
     s = mix[0] * b0 + mix[1] * b1 + mix[2] * b2
     s_ref[...] = s
-    copy_s = loads([(s_ref, out_hbm)], sems, 2 * blocks + 1)[0]
+    copy_s = loads([(s_ref, out_hbm)], sems, 2 * blocks)[0]
     s_rows = {r: spread(s[r : r + 1, :], s) for r in (0, 1, ROWS - 2, ROWS - 1)}
     even = is_even()
 
@@ -544,8 +537,7 @@
     rim_other_near, rim_other_far = exchange(rim_near, rim_far)
 
     basis, sums = kernel(
-        functools.partial(basis_body, count), hbm((3 * rows, width)) + vmem((8 * count, 128)), in_vmem(9),
-        in_hbm(1) + in_vmem(1), "basis", [pltpu.VMEM((3 * rows, width), FLOAT), semaphores((3,))],
+        functools.partial(basis_body, count), vmem((3 * rows, width), (8 * count, 128)), in_vmem(9), in_vmem(2), "basis"
     )(base, height, surface, s_fx, s_fn, s_dg, q1, near, far)
     sums = lax.all_to_all(sums.reshape(count, 8, 128), "tile", 0, 0, tiled=True).reshape(8 * count, 128)
 
@@ -557,10 +549,10 @@
 
     solution, s, row_near, row_far = kernel(
         functools.partial(edges_body, levels, count), hbm(tile) + vmem(tile, rim, rim),
-        in_vmem(1) + in_hbm(3), in_hbm(1) + in_vmem(3), "edges",
-        [pltpu.VMEM((3 * rows, width), FLOAT), pltpu.VMEM(rim_rows, FLOAT), pltpu.VMEM(link_rows, FLOAT),
-         semaphores((levels // 4 + 2,))],
-    )(sums, left(basis), left(rims), left(links))
+        in_vmem(2) + in_hbm(2), in_hbm(1) + in_vmem(3), "edges",
+        [pltpu.VMEM(rim_rows, FLOAT), pltpu.VMEM(link_rows, FLOAT),
+         semaphores((levels // 4 + 1,))],
+    )(sums, basis, left(rims), left(links))
     other_near, other_far = exchange(row_near, row_far)
     u2 = kernel(
         functools.partial(inner_body, levels), vmem(flat), in_vmem(1) + in_hbm(5), in_vmem(1), "inner",

time: 48.1 us -> 47.4 us (0.985)
  Pallas kernels: 24.2 us -> 23.6 us
    pallas_call x1, Pallas kernels: 1.4 us -> 0.88 us  [body(): kernel(functools.partial(basis_body, count), vmem((3 * rows, width), (8 *...]
where the time goes in v5:
time: 47.4 us; the launch traced here: 46.9 us
  Pallas kernels  23.6 us (50%)
  starting transfers between devices  18.3 us (39%)
  waiting for transfers between devices  4.2 us (9%)
  between operations  0.74 us (2%)
    ppermute x6, starting transfers between devices, swap(): lax.ppermute(array, 'tile', [(i, i + 1) for i in firsts] + [(i + 1, i) fo...  11.8 us
    pallas_call x1, Pallas kernels, body(): kernel(functools.partial(inner_body, levels), vmem(flat), in_vmem(1) + in...  8.44 us
    all_to_all x1, starting transfers between devices, body(): lax.all_to_all(sums.reshape(count, 8, 128), 'tile', 0, 0, tiled=True)  6.5 us
    pallas_call x1, Pallas kernels, body(): kernel(functools.partial(columns_body, levels), hbm(brick, brick, rim_row...  6.28 us
    ppermute x6, waiting for transfers between devices, swap(): lax.ppermute(array, 'tile', [(i, i + 1) for i in firsts] + [(i + 1, i) fo...  4.2 us
    pallas_call x1, Pallas kernels, body(): kernel(functools.partial(setup_body, levels), vmem(*[tile] * 9, rim, rim)...  3.92 us
    pallas_call x1, Pallas kernels, body(): kernel(functools.partial(edges_body, levels, count), hbm(tile) + vmem(til...  2.19 us
    pallas_call x1, Pallas kernels, body(): kernel(functools.partial(finish_body, levels), hbm(flat), in_vmem(10), in...  1.87 us
  transfers between devices with their start and end apart: 7, of which 2 were waited for; matrix products, arithmetic and copies ran while one was open for 0% of the time, Pallas kernels for 36%

profile of v5, /device:TPU:1, one launch (start us, length us, event | category | flops | bytes accessed | tf_op | source)
XLA Modules:
  0.0 46.9 jit_solution(238223358607652461)
XLA Ops:
  0.6 3.9 %setup.1 = (f32[8,1280]{1,0:T(8,128)S(1)}, f32[8,1280]{1,0:T(8,128)S(1)}, f32[8,1280]{1,0:T(8,128)S(1)}, f32[8,1280]{1,0:T(8,128)S(1)}, f32[8,1280]{1,0:T(8,128)...) custom-call(f32[48]{0:T(128)} %weight_hbm.3, ...), custom_call_target="tpu_custom_call" | custom-call | flops 1 | bytes 1 | tf_op jit(solution)/shard_map/setup/pallas_call | solution.py:530
  4.6 0.1 collective-permute-start
  4.7 4.5 %collective-permute-start.1 = (f32[8,1280]{1,0:T(8,128)S(1)}, f32[8,1280]{1,0:T(8,128)S(1)}, u32[]{:S(2)}, u32[]{:S(2)}) collective-permute-start(f32[8,1280]{1,0:T(8,128)S(1)} %get-tuple-element.31), channel_id=1, source_target_pairs={{1,2},{3,4},{5,6},{7,8},{9,10},{11,12},{13,14},{2,1},{4,3},{6,5},{... | collective-permute-start | bytes 122888 | tf_op jit(solution)/shard_map/ppermute | solution.py:511
  9.2 0.0 collective-permute-done.near
  9.2 1.7 %collective-permute-done.1.far = f32[8,1280]{1,0:T(8,128)S(1)} collective-permute-done((f32[8,1280]{1,0:T(8,128)S(1)}, f32[8,1280]{1,0:T(8,128)S(1)}, u32[]{:S(2)}, u32[]{:S(2)}) %collective-permute-start.1) | collective-permute-done | bytes 40992 | tf_op jit(solution)/shard_map/ppermute | solution.py:511
  10.9 0.9 %basis.1 = (f32[24,1280]{1,0:T(8,128)S(1)}, f32[128,128]{1,0:T(8,128)}) custom-call(f32[8,1280]{1,0:T(8,128)S(1)} %get-tuple-element.23.ct, f32[8,1280]{1,0:T(8,128)S(1)} %get-tuple-element.24.height, f32[8,1280]{1,0:T(8,128)S(1)} %get-tuple-element.25.surface, f32[8,1280]{1,0:T(8,128)S(1)} %get-tuple-element.26.fx_ref, ...), custom_call_target="tpu_custom_call" | custom-call | flops 1 | bytes 1 | tf_op jit(solution)/shard_map/basis/pallas_call | solution.py:539
  11.7 6.5 %all-to-all-start = ((f32[16,8,128]{2,1,0:T(8,128)}), f32[16,8,128]{2,1,0:T(8,128)S(1)}, u32[]{:S(2)}, u32[]{:S(2)}) async-start(f32[16,8,128]{2,1,0:T(8,128)} %bitcast.2), calls=%async_computation | async-start | bytes 131072 | tf_op jit(solution)/shard_map/all_to_all | solution.py:542
  18.2 0.2 collective-permute-start.4
  18.4 3.5 %collective-permute-start.5 = (f32[96,1280]{1,0:T(8,128)S(1)}, f32[96,1280]{1,0:T(8,128)S(1)}, u32[]{:S(2)}, u32[]{:S(2)}) collective-permute-start(f32[96,1280]{1,0:T(8,128)S(1)} %get-tuple-element.42.rim_far), channel_id=1, source_target_pairs={{1,2},{3,4},{5,6},{7,8},{9,10},{11,12},{13,14},{2,1},{4,3},{6,5},{... | collective-permute-start | bytes 1474568 | tf_op jit(solution)/shard_map/ppermute | solution.py:511
  21.9 6.3 %columns.1 = (f32[3840,128]{1,0:T(8,128)}, f32[3840,128]{1,0:T(8,128)}, f32[384,1280]{1,0:T(8,128)}) custom-call(f32[48]{0:T(128)} %weight_hbm.3, s32[8,1280]{1,0:T(8,128)} %kmt_hbm.5, f32[384,1280]{1,0:T(8,128)} %bitcast.14, f32[384,1280]{1,0:T(8,128)} %bitcast.15, s32[384,1280]{1,0:T(8,128)} %bitcast.9, f32[192,1280]{1,0:T(8,128)} %get-tuple-element.34.links_hbm.links), custom_call_target="tpu_custom_call" | custom-call | flops 1 | bytes 1 | tf_op jit(solution)/shard_map/columns/pallas_call | solution.py:544
  28.2 0.0 all-to-all-done
  28.2 2.2 %edges.1 = (f32[8,1280]{1,0:T(8,128)}, f32[8,1280]{1,0:T(8,128)S(1)}, f32[96,1280]{1,0:T(8,128)S(1)}, f32[96,1280]{1,0:T(8,128)S(1)}) custom-call(f32[128,128]{1,0:T(8,128)S(1)} %bitcast.7, f32[24,1280]{1,0:T(8,128)S(1)} %get-tuple-element.33.basis_ref, f32[384,1280]{1,0:T(8,128)} %get-tuple-element.35.rim_hbm, f32[192,1280]{1,0:T(8,128)} %get-tuple-element.34.links_hbm.links), custom_call_target="tpu_custom_call" | custom-call | flops 1 | bytes 1 | tf_op jit(solution)/shard_map/edges/pallas_call | solution.py:550
  30.4 0.1 collective-permute-start.2
  30.5 3.5 %collective-permute-start.3 = (f32[96,1280]{1,0:T(8,128)S(1)}, f32[96,1280]{1,0:T(8,128)S(1)}, u32[]{:S(2)}, u32[]{:S(2)}) collective-permute-start(f32[96,1280]{1,0:T(8,128)S(1)} %get-tuple-element.40.own_far), channel_id=1, source_target_pairs={{1,2},{3,4},{5,6},{7,8},{9,10},{11,12},{13,14},{2,1},{4,3},{6,5},{... | collective-permute-start | bytes 1474568 | tf_op jit(solution)/shard_map/ppermute | solution.py:511
  34.0 0.0 copy-start
  34.0 8.4 %inner.1.u2 = f32[384,1280]{1,0:T(8,128)S(1)} custom-call(f32[8,1280]{1,0:T(8,128)S(1)} %get-tuple-element.36.s_ref, s32[8,1280]{1,0:T(8,128)} %kmt_hbm.5, f32[3840,128]{1,0:T(8,128)} %get-tuple-element.37.m0_hbm, f32[3840,128]{1,0:T(8,128)} %get-tuple-element.38.w_hbm, f32[384,1280]{1,0:T(8,128)} %bitcast.12, s32[384,1280]{1,0:T(8,128)} %bitcast.10), custom_call_target="tpu_custom_call" | custom-call | flops 1 | bytes 1 | tf_op jit(solution)/shard_map/inner/pallas_call | solution.py:557
  42.4 0.0 collective-permute-done.4.rim_other_near
  42.4 0.0 collective-permute-done.5.rim_other_far
  42.4 0.0 collective-permute-done.2.near
  42.5 2.5 %collective-permute-done.3.far = f32[96,1280]{1,0:T(8,128)S(1)} collective-permute-done((f32[96,1280]{1,0:T(8,128)S(1)}, f32[96,1280]{1,0:T(8,128)S(1)}, u32[]{:S(2)}, u32[]{:S(2)}) %collective-permute-start.3) | collective-permute-done | bytes 491552 | tf_op jit(solution)/shard_map/ppermute | solution.py:511
  45.0 0.0 copy-done
  45.0 1.9 %finish.1 = f32[384,1280]{1,0:T(8,128)} custom-call(f32[384,1280]{1,0:T(8,128)S(1)} %inner.1.u2, f32[192,1280]{1,0:T(8,128)S(1)} %copy-done, f32[96,1280]{1,0:T(8,128)S(1)} %get-tuple-element.39.own_near, f32[96,1280]{1,0:T(8,128)S(1)} %get-tuple-element.40.own_far, f32[96,1280]{1,0:T(8,128)S(1)} %get-tuple-element.41.rim_near, ...), custom_call_target="tpu_custom_call" | custom-call | flops 1 | bytes 1 | tf_op jit(solution)/shard_map/finish/pallas_call | solution.py:562
Async XLA Ops:
  4.6 4.6 %collective-permute-start = (f32[8,1280]{1,0:T(8,128)S(1)}, f32[8,1280]{1,0:T(8,128)S(1)}, u32[]{:S(2)}, u32[]{:S(2)}) collective-permute-start(f32[8,1280]{1,0:T(8,128)S(1)} %get-tuple-element.30), channel_id=1, source_target_pairs={{0,1},{2,3},{4,5},{6,7},{8,9},{10,11},{12,13},{14,15},{1,0},{3,2},... | collective-permute-start | bytes 122888 | tf_op jit(solution)/shard_map/ppermute | solution.py:511
  4.7 6.2 %collective-permute-start.1 = (f32[8,1280]{1,0:T(8,128)S(1)}, f32[8,1280]{1,0:T(8,128)S(1)}, u32[]{:S(2)}, u32[]{:S(2)}) collective-permute-start(f32[8,1280]{1,0:T(8,128)S(1)} %get-tuple-element.31), channel_id=1, source_target_pairs={{1,2},{3,4},{5,6},{7,8},{9,10},{11,12},{13,14},{2,1},{4,3},{6,5},{... | collective-permute-start | bytes 122888 | tf_op jit(solution)/shard_map/ppermute | solution.py:511
  11.7 16.5 %all-to-all-start = ((f32[16,8,128]{2,1,0:T(8,128)}), f32[16,8,128]{2,1,0:T(8,128)S(1)}, u32[]{:S(2)}, u32[]{:S(2)}) async-start(f32[16,8,128]{2,1,0:T(8,128)} %bitcast.2), calls=%async_computation | async-start | bytes 131072 | tf_op jit(solution)/shard_map/all_to_all | solution.py:542
  18.2 24.2 %collective-permute-start.4 = (f32[96,1280]{1,0:T(8,128)S(1)}, f32[96,1280]{1,0:T(8,128)S(1)}, u32[]{:S(2)}, u32[]{:S(2)}) collective-permute-start(f32[96,1280]{1,0:T(8,128)S(1)} %get-tuple-element.41.rim_near), channel_id=1, source_target_pairs={{0,1},{2,3},{4,5},{6,7},{8,9},{10,11},{12,13},{14,15},{1,0},{3,2},... | collective-permute-start | bytes 1474568 | tf_op jit(solution)/shard_map/ppermute | solution.py:511
  18.4 24.0 %collective-permute-start.5 = (f32[96,1280]{1,0:T(8,128)S(1)}, f32[96,1280]{1,0:T(8,128)S(1)}, u32[]{:S(2)}, u32[]{:S(2)}) collective-permute-start(f32[96,1280]{1,0:T(8,128)S(1)} %get-tuple-element.42.rim_far), channel_id=1, source_target_pairs={{1,2},{3,4},{5,6},{7,8},{9,10},{11,12},{13,14},{2,1},{4,3},{6,5},{... | collective-permute-start | bytes 1474568 | tf_op jit(solution)/shard_map/ppermute | solution.py:511
  30.4 12.0 %collective-permute-start.2 = (f32[96,1280]{1,0:T(8,128)S(1)}, f32[96,1280]{1,0:T(8,128)S(1)}, u32[]{:S(2)}, u32[]{:S(2)}) collective-permute-start(f32[96,1280]{1,0:T(8,128)S(1)} %get-tuple-element.39.own_near), channel_id=1, source_target_pairs={{0,1},{2,3},{4,5},{6,7},{8,9},{10,11},{12,13},{14,15},{1,0},{3,2},... | collective-permute-start | bytes 1474568 | tf_op jit(solution)/shard_map/ppermute | solution.py:511
  30.5 14.5 %collective-permute-start.3 = (f32[96,1280]{1,0:T(8,128)S(1)}, f32[96,1280]{1,0:T(8,128)S(1)}, u32[]{:S(2)}, u32[]{:S(2)}) collective-permute-start(f32[96,1280]{1,0:T(8,128)S(1)} %get-tuple-element.40.own_far), channel_id=1, source_target_pairs={{1,2},{3,4},{5,6},{7,8},{9,10},{11,12},{13,14},{2,1},{4,3},{6,5},{... | collective-permute-start | bytes 1474568 | tf_op jit(solution)/shard_map/ppermute | solution.py:511
  34.0 11.0 %copy-start = (f32[192,1280]{1,0:T(8,128)S(1)}, f32[192,1280]{1,0:T(8,128)}, u32[]{:S(2)}) copy-start(f32[192,1280]{1,0:T(8,128)} %get-tuple-element.34.links_hbm.links) | copy-start | bytes 2949124

commit v6 on v5

--- a/solution.py
+++ b/solution.py
@@ -211,7 +211,7 @@
     out.wait()
 
 
-def basis_body(count, ct, height, surface, fx_ref, fn_ref, dg_ref, q1_ref, near, far, basis_ref, sums_ref):
+def basis_body(ct, height, surface, fx_ref, fn_ref, dg_ref, q1_ref, near, far, basis_ref, sums_ref):
     even = is_even()
     b0 = ct[...]
     rows = row_index(b0)
@@ -262,8 +262,7 @@
         for j in range(1, product.shape[1] // 128):
             folded = folded + product[:, j * 128 : (j + 1) * 128]
         packed = jnp.where(tile_rows == place, jnp.sum(folded, axis=0, keepdims=True), packed)
-    for j in range(count):
-        sums_ref[j * 8 : (j + 1) * 8, :] = packed
+    sums_ref[...] = packed
 
 
 def quadratic(left, form):
@@ -311,7 +310,8 @@
     return x
 
 
-def edges_body(levels, count, sums, basis_ref, rim_hbm, links_hbm, out_hbm, s_ref, near_ref, far_ref,
+def edges_body(levels, count, sums, basis_ref, rim_near, rim_far, rim_other_near, rim_other_far, rim_hbm, links_hbm,
+               out_hbm, s_ref, near_ref, far_ref, faces_ref,
                rims, links, sems):
     blocks = levels // 8
     both = [pair for pairs in zip(in_parts(rim_hbm, rims, blocks), in_parts(links_hbm, links, blocks)) for pair in pairs]
@@ -329,6 +329,15 @@
     even = is_even()
 
     for block in range(blocks):
+        at, below = pl.ds(block * 8, 8), pl.ds(levels + block * 8, 8)
+        kap, wet, kap_other, wet_other = (
+            dealt(even, near[part, :], far[part, :])
+            for near, far in ((rim_near, rim_far), (rim_other_near, rim_other_far)) for part in (at, below)
+        )
+        for side in range(2):
+            faces_ref[pl.ds(side * levels + block * 8, 8), :] = (
+                0.5 * (kap[side] + kap_other[side]) * wet[side] * wet_other[side]
+            )
         copies[2 * block].wait()
         copies[2 * block + 1].wait()
         found = []
@@ -342,6 +351,12 @@
             at = pl.ds(place * levels + block * 8, 8)
             near_ref[at, :], far_ref[at, :] = dealt(even, found[0][place], found[1][place])
     copy_s.wait()
+
+
+def inverse_of(values):
+    guess = pl.reciprocal(values, approx=True)
+    guess = guess * (2.0 - values * guess)
+    return guess * (2.0 - values * guess)
 
 
 def columns_body(levels, weight_hbm, kmt_hbm, source_hbm, kvert_hbm, land_hbm, links_hbm, m0_hbm, w_hbm, rim_hbm,
@@ -368,7 +383,7 @@
         at = level_at(k, width)
         below = jnp.where(k + 1 < levels, sea(jnp.minimum(k + 1, levels - 1)), 0.0)
         coupling = stacked(kvert[rows_at(k), :]) * here * below
-        over = 1.0 / (1.0 + coupling + link)
+        over = inverse_of(1.0 + coupling + link)
         m_here = (stacked(source[rows_at(k), :]) + m_in) * over
         w_here = (here * (weight[k] * inverse) + w_in) * over
         part = coupling * over
@@ -385,7 +400,7 @@
         big[3 * i + 2].wait()
         if i + 1 < parts:
             big[3 * i + 3].wait()
-        carry = lax.fori_loop(i * chunk, (i + 1) * chunk, down, carry)
+        carry = lax.fori_loop(i * chunk, (i + 1) * chunk, down, carry, unroll=4)
 
     def up(i, carry):
         at = level_at(levels - 1 - i, width)
@@ -400,7 +415,7 @@
     carry = (zero, zero)
     outs = []
     for i in range(parts):
-        carry = lax.fori_loop(i * chunk, (i + 1) * chunk, up, carry)
+        carry = lax.fori_loop(i * chunk, (i + 1) * chunk, up, carry, unroll=4)
         size = chunk * shape[0]
         whole = pl.ds((parts - 1 - i) * size, size)
         for a, (near, far) in enumerate(((m0, m0_hbm), (w, w_hbm))):
@@ -463,7 +478,7 @@
         lax.fori_loop(i * chunk, (i + 1) * chunk, group, 0)
 
 
-def finish_body(levels, u2, links, own_near, own_far, rim_near, rim_far, near, far, rim_other_near, rim_other_far,
+def finish_body(levels, u2, links, own_near, own_far, near, far, faces,
                 out, change_ref, buffer, sems):
     width = own_near.shape[1]
     tall = width // 128 * ROWS
@@ -477,10 +492,9 @@
         def pairs(a, b):
             return [dealt(even, a[part, :], b[part, :]) for part in (at, below)]
 
-        own, rim = pairs(own_near, own_far), pairs(rim_near, rim_far)
-        other, rim_other = pairs(near, far), pairs(rim_other_near, rim_other_far)
+        own, other = pairs(own_near, own_far), pairs(near, far)
         for side, row, inner in ((0, 0, 1), (1, ROWS - 1, ROWS - 2)):
-            face = 0.5 * (rim[0][side] + rim_other[0][side]) * rim[1][side] * rim_other[1][side]
+            face = faces[pl.ds(side * levels + block * 8, 8), :]
             change = face * (other[0][side] - own[0][side])
             along, link = (links[pl.ds((block * LINKS + side * 2 + i) * 8, 8), :] for i in range(2))
             flux = along * (east(change) - change)
@@ -537,9 +551,9 @@
     rim_other_near, rim_other_far = exchange(rim_near, rim_far)
 
     basis, sums = kernel(
-        functools.partial(basis_body, count), vmem((3 * rows, width), (8 * count, 128)), in_vmem(9), in_vmem(2), "basis"
+        basis_body, vmem((3 * rows, width), (8, 128)), in_vmem(9), in_vmem(2), "basis"
     )(base, height, surface, s_fx, s_fn, s_dg, q1, near, far)
-    sums = lax.all_to_all(sums.reshape(count, 8, 128), "tile", 0, 0, tiled=True).reshape(8 * count, 128)
+    sums = lax.all_gather(sums, "tile", axis=0, tiled=True)
 
     m0, w, rims = kernel(
         functools.partial(columns_body, levels), hbm(brick, brick, rim_rows), in_hbm(6), in_hbm(3), "columns",
@@ -547,12 +561,12 @@
          pltpu.VMEM(rim_rows, FLOAT), semaphores((15,)), semaphores((8 + levels // 8,))],
     )(layer_weight, kmt, ct_tracer, kvert, land, left(links))
 
-    solution, s, row_near, row_far = kernel(
-        functools.partial(edges_body, levels, count), hbm(tile) + vmem(tile, rim, rim),
-        in_vmem(2) + in_hbm(2), in_hbm(1) + in_vmem(3), "edges",
+    solution, s, row_near, row_far, faces = kernel(
+        functools.partial(edges_body, levels, count), hbm(tile) + vmem(tile, rim, rim, rim),
+        in_vmem(6) + in_hbm(2), in_hbm(1) + in_vmem(4), "edges",
         [pltpu.VMEM(rim_rows, FLOAT), pltpu.VMEM(link_rows, FLOAT),
          semaphores((levels // 4 + 1,))],
-    )(sums, basis, left(rims), left(links))
+    )(sums, basis, rim_near, rim_far, rim_other_near, rim_other_far, left(rims), left(links))
     other_near, other_far = exchange(row_near, row_far)
     u2 = kernel(
         functools.partial(inner_body, levels), vmem(flat), in_vmem(1) + in_hbm(5), in_vmem(1), "inner",
@@ -560,9 +574,9 @@
     )(s, kmt, left(m0), left(w), kappa, land)[0]
 
     values = kernel(
-        functools.partial(finish_body, levels), hbm(flat), in_vmem(10), in_hbm(1), "finish",
+        functools.partial(finish_body, levels), hbm(flat), in_vmem(7), in_hbm(1), "finish",
         [pltpu.VMEM((8 * rows * width // 128, 128), FLOAT), whole, semaphores((levels // 8,))],
-    )(u2, held(links), row_near, row_far, rim_near, rim_far, other_near, other_far, rim_other_near, rim_other_far)[0]
+    )(u2, held(links), row_near, row_far, other_near, other_far, faces)[0]
     return (values.reshape(levels, rows, width), solution)
 
 

time: 47.4 us -> 59.4 us (1.25)
  blocking collectives: 0 us -> 21.7 us
  starting transfers between devices: 18.3 us -> 10.3 us
  waiting for transfers between devices: 4.2 us -> 3.29 us
  Pallas kernels: 23.6 us -> 23 us
    all_gather x0 -> x1, blocking collectives: none -> 21.7 us  [body(): sums = lax.all_gather(sums, 'tile', axis=0, tiled=True)]
    all_to_all x1 -> x0, starting transfers between devices: 6.5 us -> none  [body(): lax.all_to_all(sums.reshape(count, 8, 128), 'tile', 0, 0, tiled=True)]
    ppermute x6, starting transfers between devices: 11.8 us -> 10.3 us  [swap(): lax.ppermute(array, 'tile', [(i, i + 1) for i in firsts] + [(i + 1, i) fo...]
    ppermute x6, waiting for transfers between devices: 4.2 us -> 3.29 us  [swap(): lax.ppermute(array, 'tile', [(i, i + 1) for i in firsts] + [(i + 1, i) fo...]
    pallas_call x2, Pallas kernels: 2.75 us -> 2.04 us  [the longest x1 1.8 us: body(): kernel(functools.partial(finish_body, levels), hbm(flat), in_vmem(7), in_...]
  transfers between devices with their start and end apart: 7 -> 6, of which waited for: 2 -> 2; matrix products, arithmetic and copies ran while one was open for 0% -> 0% of each run, Pallas kernels for 36% -> 25%
where the time goes in v6:
time: 59.4 us; the launch traced here: 59.1 us
  Pallas kernels  23 us (39%)
  blocking collectives  21.7 us (37%)
  starting transfers between devices  10.3 us (17%)
  waiting for transfers between devices  3.29 us (6%)
  between operations  0.73 us (1%)
    all_gather x1, blocking collectives, body(): sums = lax.all_gather(sums, 'tile', axis=0, tiled=True)  21.7 us
    ppermute x6, starting transfers between devices, swap(): lax.ppermute(array, 'tile', [(i, i + 1) for i in firsts] + [(i + 1, i) fo...  10.3 us
    pallas_call x1, Pallas kernels, body(): kernel(functools.partial(inner_body, levels), vmem(flat), in_vmem(1) + in...  8.44 us
    pallas_call x1, Pallas kernels, body(): kernel(functools.partial(columns_body, levels), hbm(brick, brick, rim_row...  6.27 us
    pallas_call x1, Pallas kernels, body(): kernel(functools.partial(setup_body, levels), vmem(*[tile] * 9, rim, rim)...  3.92 us
    ppermute x6, waiting for transfers between devices, swap(): lax.ppermute(array, 'tile', [(i, i + 1) for i in firsts] + [(i + 1, i) fo...  3.29 us
    pallas_call x1, Pallas kernels, body(): kernel(functools.partial(edges_body, levels, count), hbm(tile) + vmem(til...  2.34 us
    pallas_call x1, Pallas kernels, body(): kernel(functools.partial(finish_body, levels), hbm(flat), in_vmem(7), in_...  1.8 us
  transfers between devices with their start and end apart: 6, of which 2 were waited for; matrix products, arithmetic and copies ran while one was open for 0% of the time, Pallas kernels for 25%

profile of v6, /device:TPU:1, one launch (start us, length us, event | category | flops | bytes accessed | tf_op | source)
XLA Modules:
  0.0 59.1 jit_solution(16533930811696303942)
XLA Ops:
  0.6 3.9 %setup.1 = (f32[8,1280]{1,0:T(8,128)S(1)}, f32[8,1280]{1,0:T(8,128)S(1)}, f32[8,1280]{1,0:T(8,128)S(1)}, f32[8,1280]{1,0:T(8,128)S(1)}, f32[8,1280]{1,0:T(8,128)...) custom-call(f32[48]{0:T(128)} %weight_hbm.3, ...), custom_call_target="tpu_custom_call" | custom-call | flops 1 | bytes 1 | tf_op jit(solution)/shard_map/setup/pallas_call | solution.py:544
  4.6 0.1 collective-permute-start.2
  4.7 4.5 %collective-permute-start.3 = (f32[96,1280]{1,0:T(8,128)S(1)}, f32[96,1280]{1,0:T(8,128)S(1)}, u32[]{:S(2)}, u32[]{:S(2)}) collective-permute-start(f32[96,1280]{1,0:T(8,128)S(1)} %get-tuple-element.36.rim_far), channel_id=1, source_target_pairs={{1,2},{3,4},{5,6},{7,8},{9,10},{11,12},{13,14},{2,1},{4,3},{6,5},{... | collective-permute-start | bytes 1474568 | tf_op jit(solution)/shard_map/ppermute | solution.py:525
  9.2 0.1 collective-permute-start
  9.3 3.5 %collective-permute-start.1 = (f32[8,1280]{1,0:T(8,128)S(1)}, f32[8,1280]{1,0:T(8,128)S(1)}, u32[]{:S(2)}, u32[]{:S(2)}) collective-permute-start(f32[8,1280]{1,0:T(8,128)S(1)} %get-tuple-element.32), channel_id=1, source_target_pairs={{1,2},{3,4},{5,6},{7,8},{9,10},{11,12},{13,14},{2,1},{4,3},{6,5},{... | collective-permute-start | bytes 122888 | tf_op jit(solution)/shard_map/ppermute | solution.py:525
  12.8 6.3 %columns.1 = (f32[3840,128]{1,0:T(8,128)}, f32[3840,128]{1,0:T(8,128)}, f32[384,1280]{1,0:T(8,128)}) custom-call(f32[48]{0:T(128)} %weight_hbm.3, s32[8,1280]{1,0:T(8,128)} %kmt_hbm.5, f32[384,1280]{1,0:T(8,128)} %bitcast.11, f32[384,1280]{1,0:T(8,128)} %bitcast.12, s32[384,1280]{1,0:T(8,128)} %bitcast.6, f32[192,1280]{1,0:T(8,128)} %get-tuple-element.37.links_hbm.links), custom_call_target="tpu_custom_call" | custom-call | flops 1 | bytes 1 | tf_op jit(solution)/shard_map/columns/pallas_call | solution.py:558
  19.1 0.0 collective-permute-done.near
  19.1 2.0 %collective-permute-done.1.far = f32[8,1280]{1,0:T(8,128)S(1)} collective-permute-done((f32[8,1280]{1,0:T(8,128)S(1)}, f32[8,1280]{1,0:T(8,128)S(1)}, u32[]{:S(2)}, u32[]{:S(2)}) %collective-permute-start.1) | collective-permute-done | bytes 40992 | tf_op jit(solution)/shard_map/ppermute | solution.py:525
  21.1 0.2 basis.1
  21.3 21.7 %all_gather.3.sums = f32[128,128]{1,0:T(8,128)S(1)} all-gather(f32[8,128]{1,0:T(8,128)S(1)} %get-tuple-element.33), channel_id=1, replica_groups=mesh['grp'=2,'tile'=16] {'tile'}, dimensions={0}, use_global_device_ids=true | all-gather | bytes 69632 | tf_op jit(solution)/shard_map/all_gather | solution.py:556
  43.0 0.0 collective-permute-done.2.rim_other_near
  43.0 0.0 collective-permute-done.3.rim_other_far
  43.0 2.3 %edges.1 = (f32[8,1280]{1,0:T(8,128)}, f32[8,1280]{1,0:T(8,128)S(1)}, f32[96,1280]{1,0:T(8,128)S(1)}, f32[96,1280]{1,0:T(8,128)S(1)}, f32[96,1280]{1,0:T(8,128)S(1)}) custom-call(f32[128,128]{1,0:T(8,128)S(1)} %all_gather.3.sums, f32[24,1280]{1,0:T(8,128)S(1)} %get-tuple-element.34.basis_ref, f32[96,1280]{1,0:T(8,128)S(1)} %get-tuple-element.35.rim_near, ...), custom_call_target="tpu_custom_call" | custom-call | flops 1 | bytes 1 | tf_op jit(solution)/shard_map/edges/pallas_call | solution.py:564
  45.4 0.2 collective-permute-start.4
  45.6 1.9 %collective-permute-start.5 = (f32[96,1280]{1,0:T(8,128)S(1)}, f32[96,1280]{1,0:T(8,128)S(1)}, u32[]{:S(2)}, u32[]{:S(2)}) collective-permute-start(f32[96,1280]{1,0:T(8,128)S(1)} %get-tuple-element.43.own_far), channel_id=1, source_target_pairs={{1,2},{3,4},{5,6},{7,8},{9,10},{11,12},{13,14},{2,1},{4,3},{6,5},{... | collective-permute-start | bytes 1474568 | tf_op jit(solution)/shard_map/ppermute | solution.py:525
  47.5 0.0 copy-start
  47.5 8.4 %inner.1.u2 = f32[384,1280]{1,0:T(8,128)S(1)} custom-call(f32[8,1280]{1,0:T(8,128)S(1)} %get-tuple-element.39.s_ref, s32[8,1280]{1,0:T(8,128)} %kmt_hbm.5, f32[3840,128]{1,0:T(8,128)} %get-tuple-element.40.m0_hbm, f32[3840,128]{1,0:T(8,128)} %get-tuple-element.41.w_hbm, f32[384,1280]{1,0:T(8,128)} %bitcast.9, s32[384,1280]{1,0:T(8,128)} %bitcast.7), custom_call_target="tpu_custom_call" | custom-call | flops 1 | bytes 1 | tf_op jit(solution)/shard_map/inner/pallas_call | solution.py:571
  56.0 0.0 collective-permute-done.4.near
  56.0 1.3 %collective-permute-done.5.far = f32[96,1280]{1,0:T(8,128)S(1)} collective-permute-done((f32[96,1280]{1,0:T(8,128)S(1)}, f32[96,1280]{1,0:T(8,128)S(1)}, u32[]{:S(2)}, u32[]{:S(2)}) %collective-permute-start.5) | collective-permute-done | bytes 491552 | tf_op jit(solution)/shard_map/ppermute | solution.py:525
  57.3 0.0 copy-done
  57.3 1.8 %finish.1 = f32[384,1280]{1,0:T(8,128)} custom-call(f32[384,1280]{1,0:T(8,128)S(1)} %inner.1.u2, f32[192,1280]{1,0:T(8,128)S(1)} %copy-done, f32[96,1280]{1,0:T(8,128)S(1)} %get-tuple-element.42.own_near, f32[96,1280]{1,0:T(8,128)S(1)} %get-tuple-element.43.own_far, f32[96,1280]{1,0:T(8,128)S(1)} %collective-permute-done.4.near, ...), custom_call_target="tpu_custom_call" | custom-call | flops 1 | bytes 1 | tf_op jit(solution)/shard_map/finish/pallas_call | solution.py:576
Async XLA Ops:
  4.6 38.5 %collective-permute-start.2 = (f32[96,1280]{1,0:T(8,128)S(1)}, f32[96,1280]{1,0:T(8,128)S(1)}, u32[]{:S(2)}, u32[]{:S(2)}) collective-permute-start(f32[96,1280]{1,0:T(8,128)S(1)} %get-tuple-element.35.rim_near), channel_id=1, source_target_pairs={{0,1},{2,3},{4,5},{6,7},{8,9},{10,11},{12,13},{14,15},{1,0},{3,2},... | collective-permute-start | bytes 1474568 | tf_op jit(solution)/shard_map/ppermute | solution.py:525
  4.7 38.3 %collective-permute-start.3 = (f32[96,1280]{1,0:T(8,128)S(1)}, f32[96,1280]{1,0:T(8,128)S(1)}, u32[]{:S(2)}, u32[]{:S(2)}) collective-permute-start(f32[96,1280]{1,0:T(8,128)S(1)} %get-tuple-element.36.rim_far), channel_id=1, source_target_pairs={{1,2},{3,4},{5,6},{7,8},{9,10},{11,12},{13,14},{2,1},{4,3},{6,5},{... | collective-permute-start | bytes 1474568 | tf_op jit(solution)/shard_map/ppermute | solution.py:525
  9.2 9.9 %collective-permute-start = (f32[8,1280]{1,0:T(8,128)S(1)}, f32[8,1280]{1,0:T(8,128)S(1)}, u32[]{:S(2)}, u32[]{:S(2)}) collective-permute-start(f32[8,1280]{1,0:T(8,128)S(1)} %get-tuple-element.31), channel_id=1, source_target_pairs={{0,1},{2,3},{4,5},{6,7},{8,9},{10,11},{12,13},{14,15},{1,0},{3,2},... | collective-permute-start | bytes 122888 | tf_op jit(solution)/shard_map/ppermute | solution.py:525
  9.3 11.8 %collective-permute-start.1 = (f32[8,1280]{1,0:T(8,128)S(1)}, f32[8,1280]{1,0:T(8,128)S(1)}, u32[]{:S(2)}, u32[]{:S(2)}) collective-permute-start(f32[8,1280]{1,0:T(8,128)S(1)} %get-tuple-element.32), channel_id=1, source_target_pairs={{1,2},{3,4},{5,6},{7,8},{9,10},{11,12},{13,14},{2,1},{4,3},{6,5},{... | collective-permute-start | bytes 122888 | tf_op jit(solution)/shard_map/ppermute | solution.py:525
  45.4 10.6 %collective-permute-start.4 = (f32[96,1280]{1,0:T(8,128)S(1)}, f32[96,1280]{1,0:T(8,128)S(1)}, u32[]{:S(2)}, u32[]{:S(2)}) collective-permute-start(f32[96,1280]{1,0:T(8,128)S(1)} %get-tuple-element.42.own_near), channel_id=1, source_target_pairs={{0,1},{2,3},{4,5},{6,7},{8,9},{10,11},{12,13},{14,15},{1,0},{3,2},... | collective-permute-start | bytes 1474568 | tf_op jit(solution)/shard_map/ppermute | solution.py:525
  45.6 11.7 %collective-permute-start.5 = (f32[96,1280]{1,0:T(8,128)S(1)}, f32[96,1280]{1,0:T(8,128)S(1)}, u32[]{:S(2)}, u32[]{:S(2)}) collective-permute-start(f32[96,1280]{1,0:T(8,128)S(1)} %get-tuple-element.43.own_far), channel_id=1, source_target_pairs={{1,2},{3,4},{5,6},{7,8},{9,10},{11,12},{13,14},{2,1},{4,3},{6,5},{... | collective-permute-start | bytes 1474568 | tf_op jit(solution)/shard_map/ppermute | solution.py:525
  47.5 9.7 %copy-start = (f32[192,1280]{1,0:T(8,128)S(1)}, f32[192,1280]{1,0:T(8,128)}, u32[]{:S(2)}) copy-start(f32[192,1280]{1,0:T(8,128)} %get-tuple-element.37.links_hbm.links) | copy-start | bytes 2949124

commit v7 on v5

--- a/solution.py
+++ b/solution.py
@@ -14,7 +14,6 @@
 MID = 0.5 * (HIGH + LOW)
 HALF = 0.5 * (HIGH - LOW)
 FLOAT = jnp.float32
-RIM = 8
 LINKS = 4
 LIMIT = 24 * 1024 * 1024
 
@@ -131,14 +130,13 @@
     return total
 
 
-def setup_body(levels, weight_hbm, land_hbm, kmt_hbm, ct_hbm, screen_hbm, kappa_hbm, height_ref, surface_ref,
-               fx_ref, fn_ref, dg_ref, q1_ref, base_ref, near_ref, far_ref, rim_near_ref, rim_far_ref, links_hbm,
-               weight, land, kmt, screen, kappa, wet_bricks, kappa_bricks, links, sems, out_sems):
+def setup_body(levels, weight_hbm, land_hbm, kmt_hbm, ct_hbm, screen_hbm, height_ref, surface_ref,
+               fx_ref, fn_ref, dg_ref, q1_ref, base_ref, near_ref, far_ref, wet_bricks,
+               weight, land, kmt, screen, sems):
     chunk = levels // 4
     small = loads(((weight_hbm, weight), (kmt_hbm, kmt)), sems)
     land_copies = loads(in_parts(land_hbm, land, 4), sems, 2)
     small += loads(((ct_hbm, base_ref), (screen_hbm, screen)), sems, 6)
-    kappa_copies = loads(in_parts(kappa_hbm, kappa, 4), sems, 8)
     small[0].wait()
     total = weight_sum(weight, levels)
     small[1].wait()
@@ -186,7 +184,11 @@
         at = slice(place, place + 1)
         near_ref[at, :], far_ref[at, :] = dealt(even, values[0:1, :], values[ROWS - 1 : ROWS, :])
 
-    for i, copy in enumerate(kappa_copies):
+
+def rims_body(levels, kappa_hbm, wet_bricks, near_ref, far_ref, links_hbm, kappa, kappa_bricks, links, sems):
+    chunk = levels // 4
+    width = kappa.shape[1]
+    for i, copy in enumerate(loads(in_parts(kappa_hbm, kappa, 4), sems)):
         copy.wait()
 
         def brick(k, carry):
@@ -194,6 +196,8 @@
             return carry
 
         lax.fori_loop(i * chunk, (i + 1) * chunk, brick, 0, unroll=4)
+    even = is_even()
+    outs = []
     for block in range(levels // 8):
         found = []
         for side, row, inner in ((0, 0, 1), (1, ROWS - 1, ROWS - 2)):
@@ -205,13 +209,14 @@
             found.append((kap, here))
         for place in range(2):
             at = pl.ds(place * levels + block * 8, 8)
-            rim_near_ref[at, :], rim_far_ref[at, :] = dealt(even, found[0][place], found[1][place])
-    out = pltpu.make_async_copy(links, links_hbm, out_sems.at[0])
-    out.start()
-    out.wait()
-
-
-def basis_body(count, ct, height, surface, fx_ref, fn_ref, dg_ref, q1_ref, near, far, basis_ref, sums_ref):
+            near_ref[at, :], far_ref[at, :] = dealt(even, found[0][place], found[1][place])
+        whole = pl.ds(block * LINKS * 8, LINKS * 8)
+        outs += loads([(links.at[whole], links_hbm.at[whole])], sems, 4 + block)
+    for copy in outs:
+        copy.wait()
+
+
+def basis_body(count, ct, height, surface, fx_ref, fn_ref, dg_ref, q1_ref, near, far, links_hbm, basis_ref, sums_ref):
     even = is_even()
     b0 = ct[...]
     rows = row_index(b0)
@@ -311,52 +316,34 @@
     return x
 
 
-def edges_body(levels, count, sums, basis_ref, rim_hbm, links_hbm, out_hbm, s_ref, near_ref, far_ref,
-               rims, links, sems):
-    blocks = levels // 8
-    both = [pair for pairs in zip(in_parts(rim_hbm, rims, blocks), in_parts(links_hbm, links, blocks)) for pair in pairs]
-    copies = loads(both, sems)
-    total = sums[0:8, :]
+def inverse_of(values):
+    guess = pl.reciprocal(values, approx=True)
+    guess = guess * (2.0 - values * guess)
+    return guess * (2.0 - values * guess)
+
+
+def columns_body(levels, count, sums, basis_ref, weight_hbm, kmt_hbm, source_hbm, kvert_hbm, land_hbm, links_hbm,
+                 out_hbm, u, near_ref, far_ref, weight, kmt, source, kvert, land, links, s_ref, ratio, sems, out_sems):
+    width = source.shape[1]
+    parts = 4
+    chunk = levels // parts
+    small = loads(((weight_hbm, weight), (kmt_hbm, kmt)), sems)
+    parted = [in_parts(far, near, parts) for far, near in ((land_hbm, land), (kvert_hbm, kvert), (source_hbm, source))]
+    big = loads([pairs[i] for i in range(parts) for pairs in parted], sems, 2)
+    links_copy = loads([(links_hbm, links)], sems, 2 + 3 * parts)[0]
+
+    tile_sums = sums[0:8, :]
     for j in range(1, count):
-        total = total + sums[j * 8 : (j + 1) * 8, :]
-    total = jnp.sum(total, axis=1, keepdims=True)
-    mix = weights([total[i : i + 1, :] for i in range(6)])
+        tile_sums = tile_sums + sums[j * 8 : (j + 1) * 8, :]
+    tile_sums = jnp.sum(tile_sums, axis=1, keepdims=True)
+    mix = weights([tile_sums[i : i + 1, :] for i in range(6)])
     b0, b1, b2 = (basis_ref[i * ROWS : (i + 1) * ROWS, :] for i in range(3))
     s = mix[0] * b0 + mix[1] * b1 + mix[2] * b2
     s_ref[...] = s
-    copy_s = loads([(s_ref, out_hbm)], sems, 2 * blocks)[0]
-    s_rows = {r: spread(s[r : r + 1, :], s) for r in (0, 1, ROWS - 2, ROWS - 1)}
-    even = is_even()
-
-    for block in range(blocks):
-        copies[2 * block].wait()
-        copies[2 * block + 1].wait()
-        found = []
-        for side, row, inner in ((0, 0, 1), (1, ROWS - 1, ROWS - 2)):
-            m, gm, w, q = (rims[pl.ds((block * RIM + side * 4 + i) * 8, 8), :] for i in range(4))
-            face, link = (links[pl.ds((block * LINKS + side * 2 + i) * 8, 8), :] for i in range(2))
-            v = s_rows[row] * w
-            flux = face * (east(v) - v)
-            found.append((m + v, gm + v + (flux - west(flux)) - link * v + s_rows[inner] * q))
-        for place in range(2):
-            at = pl.ds(place * levels + block * 8, 8)
-            near_ref[at, :], far_ref[at, :] = dealt(even, found[0][place], found[1][place])
-    copy_s.wait()
-
-
-def columns_body(levels, weight_hbm, kmt_hbm, source_hbm, kvert_hbm, land_hbm, links_hbm, m0_hbm, w_hbm, rim_hbm,
-                 weight, kmt, source, kvert, land, links, m0, w, ratio, rims, in_sems, out_sems):
-    width = source.shape[1]
-    parts = 4
-    chunk = levels // parts
-    small = loads(((weight_hbm, weight), (kmt_hbm, kmt)), in_sems)
-    parted = [in_parts(far, near, parts) for far, near in ((land_hbm, land), (kvert_hbm, kvert), (source_hbm, source))]
-    big = loads([pairs[i] for i in range(parts) for pairs in parted], in_sems, 2)
-    links_copy = loads([(links_hbm, links)], in_sems, 2 + 3 * parts)[0]
+    outs = loads([(s_ref, out_hbm)], out_sems)
+
     small[0].wait()
-    total = weight_sum(weight, levels)
-    shape = (ROWS * width // 128, 128)
-    inverse = 1.0 / jnp.full(shape, total, FLOAT)
+    scaled = stacked(s) / jnp.full((ROWS * width // 128, 128), weight_sum(weight, levels), FLOAT)
     small[1].wait()
     depth = stacked(kmt[...])
 
@@ -364,75 +351,60 @@
         return jnp.where(k < depth, stacked(land[rows_at(k), :]), 0).astype(FLOAT)
 
     def down(k, carry):
-        here, link, m_in, w_in = carry
+        here, link, passed = carry
         at = level_at(k, width)
         below = jnp.where(k + 1 < levels, sea(jnp.minimum(k + 1, levels - 1)), 0.0)
         coupling = stacked(kvert[rows_at(k), :]) * here * below
-        over = 1.0 / (1.0 + coupling + link)
-        m_here = (stacked(source[rows_at(k), :]) + m_in) * over
-        w_here = (here * (weight[k] * inverse) + w_in) * over
+        over = inverse_of(1.0 + coupling + link)
+        value = (stacked(source[rows_at(k), :]) + here * (weight[k] * scaled) + passed) * over
         part = coupling * over
         ratio[at, :] = part
-        m0[at, :] = m_here
-        w[at, :] = w_here
-        return below, coupling - coupling * part, coupling * m_here, coupling * w_here
-
-    zero = jnp.zeros(shape, FLOAT)
+        u[at, :] = value
+        return below, coupling - coupling * part, coupling * value
+
+    zero = jnp.zeros(scaled.shape, FLOAT)
     big[0].wait()
-    carry = (sea(0), zero, zero, zero)
+    carry = (sea(0), zero, zero)
     for i in range(parts):
         big[3 * i + 1].wait()
         big[3 * i + 2].wait()
         if i + 1 < parts:
             big[3 * i + 3].wait()
-        carry = lax.fori_loop(i * chunk, (i + 1) * chunk, down, carry)
-
-    def up(i, carry):
+        carry = lax.fori_loop(i * chunk, (i + 1) * chunk, down, carry, unroll=4)
+
+    def up(i, below):
         at = level_at(levels - 1 - i, width)
-        m_below, w_below = carry
-        part = ratio[at, :]
-        m_here = m0[at, :] + part * m_below
-        w_here = w[at, :] + part * w_below
-        m0[at, :] = m_here
-        w[at, :] = w_here
-        return m_here, w_here
-
-    carry = (zero, zero)
-    outs = []
-    for i in range(parts):
-        carry = lax.fori_loop(i * chunk, (i + 1) * chunk, up, carry)
-        size = chunk * shape[0]
-        whole = pl.ds((parts - 1 - i) * size, size)
-        for a, (near, far) in enumerate(((m0, m0_hbm), (w, w_hbm))):
-            copy = pltpu.make_async_copy(near.at[whole], far.at[whole], out_sems.at[i * 2 + a])
-            copy.start()
-            outs.append(copy)
+        value = u[at, :] + ratio[at, :] * below
+        u[at, :] = value
+        return value
+
+    lax.fori_loop(0, levels, up, zero, unroll=4)
     links_copy.wait()
+    even = is_even()
     for block in range(levels // 8):
+        found = []
         for side, row, inner in ((0, 0, 1), (1, ROWS - 1, ROWS - 2)):
-            m, w_row = row_of(m0, block, row, width), row_of(w, block, row, width)
+            value, value_in = row_of(u, block, row, width), row_of(u, block, inner, width)
             face, link = (links[pl.ds((block * LINKS + side * 2 + i) * 8, 8), :] for i in range(2))
-            flux = face * (east(m) - m)
-            gm = m + (flux - west(flux)) + link * (row_of(m0, block, inner, width) - m)
-            q = link * row_of(w, block, inner, width)
-            for i, values in enumerate((m, gm, w_row, q)):
-                rims[pl.ds((block * RIM + side * 4 + i) * 8, 8), :] = values
-        whole = pl.ds(block * RIM * 8, RIM * 8)
-        outs += loads([(rims.at[whole], rim_hbm.at[whole])], out_sems, 2 * parts + block)
+            flux = face * (east(value) - value)
+            found.append((value, value + (flux - west(flux)) + link * (value_in - value)))
+        for place in range(2):
+            at = pl.ds(place * levels + block * 8, 8)
+            near_ref[at, :], far_ref[at, :] = dealt(even, found[0][place], found[1][place])
     for copy in outs:
         copy.wait()
 
 
-def inner_body(levels, s_ref, kmt_hbm, m0_hbm, w_hbm, kappa_hbm, land_hbm, u2_ref, kmt, m0, w, kappa, land, sems):
+def inner_body(levels, u0, kmt_hbm, kappa_hbm, land_hbm, u2_ref, kmt, kappa, land, sems):
     parts = 4
     kmt_copy = loads([(kmt_hbm, kmt)], sems)[0]
-    pairs = ((kappa_hbm, kappa), (land_hbm, land), (m0_hbm, m0), (w_hbm, w))
+    pairs = ((kappa_hbm, kappa), (land_hbm, land))
     parted = [in_parts(far, near, parts) for far, near in pairs]
     copies = loads([pairs[i] for i in range(parts) for pairs in parted], sems, 1)
-    s = s_ref[...]
     kmt_copy.wait()
     depth = kmt[...]
-    inside = row_index(s) < ROWS - 1
+    width = depth.shape[1]
+    inside = row_index(depth) < ROWS - 1
 
     def face(here, there):
         return jnp.where(jnp.minimum(here, there) > 0.0, here + there, 0.0)
@@ -445,8 +417,7 @@
         fn = jnp.where(inside, face(half, north(half)), 0.0)
         fw, fs = west(fx), south(fn)
         keep = 1.0 - (fx + fw) - (fn + fs)
-        brick = level_at(k, s.shape[1])
-        u = unstacked(m0[brick, :]) + s * unstacked(w[brick, :])
+        u = unstacked(u0[level_at(k, width), :])
         for _ in range(2):
             u = keep * u + (fx * east(u) + fw * west(u)) + (fn * north(u) + fs * south(u))
         return u
@@ -458,7 +429,7 @@
 
     chunk = levels // 2 // parts
     for i in range(parts):
-        for copy in copies[4 * i : 4 * i + 4]:
+        for copy in copies[2 * i : 2 * i + 2]:
             copy.wait()
         lax.fori_loop(i * chunk, (i + 1) * chunk, group, 0)
 
@@ -519,7 +490,7 @@
     count = lax.axis_size("tile")
     tall = levels * rows
     tile, brick, flat = (rows, width), (tall * width // 128, 128), (tall, width)
-    rim, rim_rows, link_rows = (2 * levels, width), (levels * RIM, width), (levels * LINKS, width)
+    rim, link_rows = (2 * levels, width), (levels * LINKS, width)
     scalars, whole = pltpu.SMEM((levels,), FLOAT), pltpu.VMEM(flat, FLOAT)
     ints, tile_ints = pltpu.VMEM(flat, jnp.int32), pltpu.VMEM(tile, jnp.int32)
     bricks, tiles = pltpu.VMEM(brick, FLOAT), pltpu.VMEM(tile, FLOAT)
@@ -527,37 +498,36 @@
     kmt, layer_weight = left(kmt), left(layer_weight)
     semaphores = pltpu.SemaphoreType.DMA
 
-    height, surface, s_fx, s_fn, s_dg, q1, base, to_near, to_far, rim_near, rim_far, links = kernel(
-        functools.partial(setup_body, levels), vmem(*[tile] * 9, rim, rim) + hbm(link_rows), in_hbm(6),
-        in_vmem(11) + in_hbm(1), "setup",
-        [scalars, ints, tile_ints, tiles, whole, bricks, bricks, pltpu.VMEM(link_rows, FLOAT), semaphores((12,)),
+    height, surface, s_fx, s_fn, s_dg, q1, base, to_near, to_far, wet = kernel(
+        functools.partial(setup_body, levels), vmem(*[tile] * 9, brick), in_hbm(5), in_vmem(10), "setup",
+        [scalars, ints, tile_ints, tiles, semaphores((8,))],
+    )(layer_weight, land, kmt, left(ct_surface), left(screen))
+    near, far = exchange(to_near, to_far)
+
+    rim_near, rim_far, links = kernel(
+        functools.partial(rims_body, levels), vmem(rim, rim) + hbm(link_rows), in_hbm(1) + in_vmem(1),
+        in_vmem(2) + in_hbm(1), "rims", [whole, bricks, pltpu.VMEM(link_rows, FLOAT), semaphores((4 + levels // 8,))],
+    )(kappa, wet)
+    links = left(links)
+    rim_other_near, rim_other_far = exchange(rim_near, rim_far)
+
+    basis, sums = kernel(
+        functools.partial(basis_body, count), vmem((3 * rows, width), (8 * count, 128)), in_vmem(9) + in_hbm(1),
+        in_vmem(2), "basis"
+    )(base, height, surface, s_fx, s_fn, s_dg, q1, near, far, links)
+    sums = lax.all_to_all(sums.reshape(count, 8, 128), "tile", 0, 0, tiled=True).reshape(8 * count, 128)
+
+    solution, u0, row_near, row_far = kernel(
+        functools.partial(columns_body, levels, count), hbm(tile) + vmem(brick, rim, rim), in_vmem(2) + in_hbm(6),
+        in_hbm(1) + in_vmem(3), "columns",
+        [scalars, tile_ints, whole, whole, ints, pltpu.VMEM(link_rows, FLOAT), tiles, bricks, semaphores((15,)),
          semaphores((1,))],
-    )(layer_weight, land, kmt, left(ct_surface), left(screen), kappa)
-    near, far = exchange(to_near, to_far)
-    rim_other_near, rim_other_far = exchange(rim_near, rim_far)
-
-    basis, sums = kernel(
-        functools.partial(basis_body, count), vmem((3 * rows, width), (8 * count, 128)), in_vmem(9), in_vmem(2), "basis"
-    )(base, height, surface, s_fx, s_fn, s_dg, q1, near, far)
-    sums = lax.all_to_all(sums.reshape(count, 8, 128), "tile", 0, 0, tiled=True).reshape(8 * count, 128)
-
-    m0, w, rims = kernel(
-        functools.partial(columns_body, levels), hbm(brick, brick, rim_rows), in_hbm(6), in_hbm(3), "columns",
-        [scalars, tile_ints, whole, whole, ints, pltpu.VMEM(link_rows, FLOAT), bricks, bricks, bricks,
-         pltpu.VMEM(rim_rows, FLOAT), semaphores((15,)), semaphores((8 + levels // 8,))],
-    )(layer_weight, kmt, ct_tracer, kvert, land, left(links))
-
-    solution, s, row_near, row_far = kernel(
-        functools.partial(edges_body, levels, count), hbm(tile) + vmem(tile, rim, rim),
-        in_vmem(2) + in_hbm(2), in_hbm(1) + in_vmem(3), "edges",
-        [pltpu.VMEM(rim_rows, FLOAT), pltpu.VMEM(link_rows, FLOAT),
-         semaphores((levels // 4 + 1,))],
-    )(sums, basis, left(rims), left(links))
+    )(sums, basis, layer_weight, kmt, ct_tracer, kvert, land, links)
     other_near, other_far = exchange(row_near, row_far)
     u2 = kernel(
-        functools.partial(inner_body, levels), vmem(flat), in_vmem(1) + in_hbm(5), in_vmem(1), "inner",
-        [tile_ints, bricks, bricks, whole, ints, semaphores((17,))],
-    )(s, kmt, left(m0), left(w), kappa, land)[0]
+        functools.partial(inner_body, levels), vmem(flat), in_vmem(1) + in_hbm(3), in_vmem(1), "inner",
+        [tile_ints, whole, ints, semaphores((9,))],
+    )(u0, kmt, kappa, land)[0]
 
     values = kernel(
         functools.partial(finish_body, levels), hbm(flat), in_vmem(10), in_hbm(1), "finish",

time: 47.4 us -> 44.2 us (0.932)
  Pallas kernels: 23.6 us -> 20.1 us
  waiting for transfers between devices: 4.2 us -> 6.24 us
  starting transfers between devices: 18.3 us -> 16.5 us
    pallas_call x3, Pallas kernels: 12.4 us -> 9.29 us  [the longest x1 4.35 us: body(): kernel(functools.partial(columns_body, levels, count), hbm(tile) + vmem(b...]
    all_to_all x1, waiting for transfers between devices: 0.01 us -> 2.36 us  [body(): lax.all_to_all(sums.reshape(count, 8, 128), 'tile', 0, 0, tiled=True)]
    all_to_all x1, starting transfers between devices: 6.5 us -> 5.32 us  [body(): lax.all_to_all(sums.reshape(count, 8, 128), 'tile', 0, 0, tiled=True)]
    ppermute x6, starting transfers between devices: 11.8 us -> 11.2 us  [swap(): lax.ppermute(array, 'tile', [(i, i + 1) for i in firsts] + [(i + 1, i) fo...]
  transfers between devices with their start and end apart: 7 -> 7, of which waited for: 2 -> 2; matrix products, arithmetic and copies ran while one was open for 0% -> 0% of each run, Pallas kernels for 36% -> 35%
where the time goes in v7:
time: 44.2 us; the launch traced here: 43.7 us
  Pallas kernels  20.1 us (45%)
  starting transfers between devices  16.5 us (37%)
  waiting for transfers between devices  6.24 us (14%)
  between operations  0.74 us (2%)
    ppermute x6, starting transfers between devices, swap(): lax.ppermute(array, 'tile', [(i, i + 1) for i in firsts] + [(i + 1, i) fo...  11.2 us
    pallas_call x1, Pallas kernels, body(): kernel(functools.partial(inner_body, levels), vmem(flat), in_vmem(1) + in...  8.07 us
    all_to_all x1, starting transfers between devices, body(): lax.all_to_all(sums.reshape(count, 8, 128), 'tile', 0, 0, tiled=True)  5.32 us
    pallas_call x1, Pallas kernels, body(): kernel(functools.partial(columns_body, levels, count), hbm(tile) + vmem(b...  4.35 us
    ppermute x6, waiting for transfers between devices, swap(): lax.ppermute(array, 'tile', [(i, i + 1) for i in firsts] + [(i + 1, i) fo...  3.88 us
    pallas_call x1, Pallas kernels, body(): kernel(functools.partial(rims_body, levels), vmem(rim, rim) + hbm(link_ro...  2.98 us
    all_to_all x1, waiting for transfers between devices, body(): lax.all_to_all(sums.reshape(count, 8, 128), 'tile', 0, 0, tiled=True)  2.36 us
    pallas_call x1, Pallas kernels, body(): kernel(functools.partial(setup_body, levels), vmem(*[tile] * 9, brick), i...  1.97 us
  transfers between devices with their start and end apart: 7, of which 2 were waited for; matrix products, arithmetic and copies ran while one was open for 0% of the time, Pallas kernels for 35%

profile of v7, /device:TPU:1, one launch (start us, length us, event | category | flops | bytes accessed | tf_op | source)
XLA Modules:
  0.0 43.7 jit_solution(5432085994619252946)
XLA Ops:
  0.6 2.0 %setup.1 = (f32[8,1280]{1,0:T(8,128)S(1)}, f32[8,1280]{1,0:T(8,128)S(1)}, f32[8,1280]{1,0:T(8,128)S(1)}, f32[8,1280]{1,0:T(8,128)S(1)}, f32[8,1280]{1,0:T(8,128)...) custom-call(f32[48]{0:T(128)} %weight_hbm.3, ...), custom_call_target="tpu_custom_call" | custom-call | flops 1 | bytes 1 | tf_op jit(solution)/shard_map/setup/pallas_call | solution.py:501
  2.6 0.1 collective-permute-start
  2.7 4.5 %collective-permute-start.1 = (f32[8,1280]{1,0:T(8,128)S(1)}, f32[8,1280]{1,0:T(8,128)S(1)}, u32[]{:S(2)}, u32[]{:S(2)}) collective-permute-start(f32[8,1280]{1,0:T(8,128)S(1)} %get-tuple-element.29), channel_id=1, source_target_pairs={{1,2},{3,4},{5,6},{7,8},{9,10},{11,12},{13,14},{2,1},{4,3},{6,5},{... | collective-permute-start | bytes 122888 | tf_op jit(solution)/shard_map/ppermute | solution.py:482
  7.2 3.0 %rims.1 = (f32[96,1280]{1,0:T(8,128)S(1)}, f32[96,1280]{1,0:T(8,128)S(1)}, f32[192,1280]{1,0:T(8,128)}) custom-call(f32[384,1280]{1,0:T(8,128)} %bitcast.11, f32[3840,128]{1,0:T(8,128)S(1)} %get-tuple-element.30.wet_bricks), custom_call_target="tpu_custom_call" | custom-call | flops 1 | bytes 1 | tf_op jit(solution)/shard_map/rims/pallas_call | solution.py:507
  10.2 0.0 collective-permute-done.near
  10.2 0.0 collective-permute-done.1.far
  10.2 0.9 %basis.1 = (f32[24,1280]{1,0:T(8,128)S(1)}, f32[128,128]{1,0:T(8,128)}) custom-call(f32[8,1280]{1,0:T(8,128)S(1)} %get-tuple-element.21.ct, f32[8,1280]{1,0:T(8,128)S(1)} %get-tuple-element.22.height, f32[8,1280]{1,0:T(8,128)S(1)} %get-tuple-element.23.surface, f32[8,1280]{1,0:T(8,128)S(1)} %get-tuple-element.24.fx_ref, ...), custom_call_target="tpu_custom_call" | custom-call | flops 1 | bytes 1 | tf_op jit(solution)/shard_map/basis/pallas_call | solution.py:514
  11.1 5.3 %all-to-all-start = ((f32[16,8,128]{2,1,0:T(8,128)}), f32[16,8,128]{2,1,0:T(8,128)S(1)}, u32[]{:S(2)}, u32[]{:S(2)}) async-start(f32[16,8,128]{2,1,0:T(8,128)} %bitcast.2), calls=%async_computation | async-start | bytes 131072 | tf_op jit(solution)/shard_map/all_to_all | solution.py:518
  16.4 0.2 collective-permute-start.4
  16.6 3.5 %collective-permute-start.5 = (f32[96,1280]{1,0:T(8,128)S(1)}, f32[96,1280]{1,0:T(8,128)S(1)}, u32[]{:S(2)}, u32[]{:S(2)}) collective-permute-start(f32[96,1280]{1,0:T(8,128)S(1)} %get-tuple-element.38.rim_far), channel_id=1, source_target_pairs={{1,2},{3,4},{5,6},{7,8},{9,10},{11,12},{13,14},{2,1},{4,3},{6,5},{... | collective-permute-start | bytes 1474568 | tf_op jit(solution)/shard_map/ppermute | solution.py:482
  20.1 2.4 %all-to-all-done = f32[16,8,128]{2,1,0:T(8,128)S(1)} async-done(((f32[16,8,128]{2,1,0:T(8,128)}), f32[16,8,128]{2,1,0:T(8,128)S(1)}, u32[]{:S(2)}, u32[]{:S(2)}) %all-to-all-start) | async-done | bytes 65568 | tf_op jit(solution)/shard_map/all_to_all | solution.py:518
  22.5 4.3 %columns.1 = (f32[8,1280]{1,0:T(8,128)}, f32[3840,128]{1,0:T(8,128)S(1)}, f32[96,1280]{1,0:T(8,128)S(1)}, f32[96,1280]{1,0:T(8,128)S(1)}) custom-call(f32[128,128]{1,0:T(8,128)S(1)} %bitcast.7, f32[24,1280]{1,0:T(8,128)S(1)} %get-tuple-element.33.basis_ref, f32[48]{0:T(128)} %weight_hbm.3, s32[8,1280]{1,0:T(8,128)} %kmt_hbm.5, f32[384,1280]{1,0:T(8,128)} %bitcast.13, ...), custom_call_target="tpu_custom_call" | custom-call | flops 1 | bytes 1 | tf_op jit(solution)/shard_map/columns/pallas_call | solution.py:520
  26.8 1.0 %collective-permute-start.2 = (f32[96,1280]{1,0:T(8,128)S(1)}, f32[96,1280]{1,0:T(8,128)S(1)}, u32[]{:S(2)}, u32[]{:S(2)}) collective-permute-start(f32[96,1280]{1,0:T(8,128)S(1)} %get-tuple-element.35.own_near), channel_id=1, source_target_pairs={{0,1},{2,3},{4,5},{6,7},{8,9},{10,11},{12,13},{14,15},{1,0},{3,2},... | collective-permute-start | bytes 1474568 | tf_op jit(solution)/shard_map/ppermute | solution.py:482
  27.9 1.9 %collective-permute-start.3 = (f32[96,1280]{1,0:T(8,128)S(1)}, f32[96,1280]{1,0:T(8,128)S(1)}, u32[]{:S(2)}, u32[]{:S(2)}) collective-permute-start(f32[96,1280]{1,0:T(8,128)S(1)} %get-tuple-element.36.own_far), channel_id=1, source_target_pairs={{1,2},{3,4},{5,6},{7,8},{9,10},{11,12},{13,14},{2,1},{4,3},{6,5},{... | collective-permute-start | bytes 1474568 | tf_op jit(solution)/shard_map/ppermute | solution.py:482
  29.8 0.0 copy-start
  29.8 8.1 %inner.1.u2 = f32[384,1280]{1,0:T(8,128)S(1)} custom-call(f32[3840,128]{1,0:T(8,128)S(1)} %get-tuple-element.34.u0, s32[8,1280]{1,0:T(8,128)} %kmt_hbm.5, f32[384,1280]{1,0:T(8,128)} %bitcast.12, s32[384,1280]{1,0:T(8,128)} %bitcast.10), custom_call_target="tpu_custom_call" | custom-call | flops 1 | bytes 1 | tf_op jit(solution)/shard_map/inner/pallas_call | solution.py:527
  37.9 0.0 collective-permute-done.4.rim_other_near
  37.9 0.0 collective-permute-done.5.rim_other_far
  37.9 0.0 collective-permute-done.2.near
  37.9 3.9 %collective-permute-done.3.far = f32[96,1280]{1,0:T(8,128)S(1)} collective-permute-done((f32[96,1280]{1,0:T(8,128)S(1)}, f32[96,1280]{1,0:T(8,128)S(1)}, u32[]{:S(2)}, u32[]{:S(2)}) %collective-permute-start.3) | collective-permute-done | bytes 491552 | tf_op jit(solution)/shard_map/ppermute | solution.py:482
  41.8 0.0 copy-done
  41.8 1.9 %finish.1 = f32[384,1280]{1,0:T(8,128)} custom-call(f32[384,1280]{1,0:T(8,128)S(1)} %inner.1.u2, f32[192,1280]{1,0:T(8,128)S(1)} %copy-done, f32[96,1280]{1,0:T(8,128)S(1)} %get-tuple-element.35.own_near, f32[96,1280]{1,0:T(8,128)S(1)} %get-tuple-element.36.own_far, f32[96,1280]{1,0:T(8,128)S(1)} %get-tuple-element.37.rim_near, ...), custom_call_target="tpu_custom_call" | custom-call | flops 1 | bytes 1 | tf_op jit(solution)/shard_map/finish/pallas_call | solution.py:532
Async XLA Ops:
  2.6 7.6 %collective-permute-start = (f32[8,1280]{1,0:T(8,128)S(1)}, f32[8,1280]{1,0:T(8,128)S(1)}, u32[]{:S(2)}, u32[]{:S(2)}) collective-permute-start(f32[8,1280]{1,0:T(8,128)S(1)} %get-tuple-element.28), channel_id=1, source_target_pairs={{0,1},{2,3},{4,5},{6,7},{8,9},{10,11},{12,13},{14,15},{1,0},{3,2},... | collective-permute-start | bytes 122888 | tf_op jit(solution)/shard_map/ppermute | solution.py:482
  2.7 7.5 %collective-permute-start.1 = (f32[8,1280]{1,0:T(8,128)S(1)}, f32[8,1280]{1,0:T(8,128)S(1)}, u32[]{:S(2)}, u32[]{:S(2)}) collective-permute-start(f32[8,1280]{1,0:T(8,128)S(1)} %get-tuple-element.29), channel_id=1, source_target_pairs={{1,2},{3,4},{5,6},{7,8},{9,10},{11,12},{13,14},{2,1},{4,3},{6,5},{... | collective-permute-start | bytes 122888 | tf_op jit(solution)/shard_map/ppermute | solution.py:482
  11.1 11.4 %all-to-all-start = ((f32[16,8,128]{2,1,0:T(8,128)}), f32[16,8,128]{2,1,0:T(8,128)S(1)}, u32[]{:S(2)}, u32[]{:S(2)}) async-start(f32[16,8,128]{2,1,0:T(8,128)} %bitcast.2), calls=%async_computation | async-start | bytes 131072 | tf_op jit(solution)/shard_map/all_to_all | solution.py:518
  16.4 21.4 %collective-permute-start.4 = (f32[96,1280]{1,0:T(8,128)S(1)}, f32[96,1280]{1,0:T(8,128)S(1)}, u32[]{:S(2)}, u32[]{:S(2)}) collective-permute-start(f32[96,1280]{1,0:T(8,128)S(1)} %get-tuple-element.37.rim_near), channel_id=1, source_target_pairs={{0,1},{2,3},{4,5},{6,7},{8,9},{10,11},{12,13},{14,15},{1,0},{3,2},... | collective-permute-start | bytes 1474568 | tf_op jit(solution)/shard_map/ppermute | solution.py:482
  16.6 21.3 %collective-permute-start.5 = (f32[96,1280]{1,0:T(8,128)S(1)}, f32[96,1280]{1,0:T(8,128)S(1)}, u32[]{:S(2)}, u32[]{:S(2)}) collective-permute-start(f32[96,1280]{1,0:T(8,128)S(1)} %get-tuple-element.38.rim_far), channel_id=1, source_target_pairs={{1,2},{3,4},{5,6},{7,8},{9,10},{11,12},{13,14},{2,1},{4,3},{6,5},{... | collective-permute-start | bytes 1474568 | tf_op jit(solution)/shard_map/ppermute | solution.py:482
  26.8 11.0 %collective-permute-start.2 = (f32[96,1280]{1,0:T(8,128)S(1)}, f32[96,1280]{1,0:T(8,128)S(1)}, u32[]{:S(2)}, u32[]{:S(2)}) collective-permute-start(f32[96,1280]{1,0:T(8,128)S(1)} %get-tuple-element.35.own_near), channel_id=1, source_target_pairs={{0,1},{2,3},{4,5},{6,7},{8,9},{10,11},{12,13},{14,15},{1,0},{3,2},... | collective-permute-start | bytes 1474568 | tf_op jit(solution)/shard_map/ppermute | solution.py:482
  27.9 13.9 %collective-permute-start.3 = (f32[96,1280]{1,0:T(8,128)S(1)}, f32[96,1280]{1,0:T(8,128)S(1)}, u32[]{:S(2)}, u32[]{:S(2)}) collective-permute-start(f32[96,1280]{1,0:T(8,128)S(1)} %get-tuple-element.36.own_far), channel_id=1, source_target_pairs={{1,2},{3,4},{5,6},{7,8},{9,10},{11,12},{13,14},{2,1},{4,3},{6,5},{... | collective-permute-start | bytes 1474568 | tf_op jit(solution)/shard_map/ppermute | solution.py:482
  29.8 12.0 %copy-start = (f32[192,1280]{1,0:T(8,128)S(1)}, f32[192,1280]{1,0:T(8,128)}, u32[]{:S(2)}) copy-start(f32[192,1280]{1,0:T(8,128)} %get-tuple-element.31.links_hbm.links) | copy-start | bytes 2949124

commit v8 on v7

--- a/solution.py
+++ b/solution.py
@@ -82,7 +82,7 @@
     return [pl.BlockSpec(memory_space=pltpu.HBM)] * count
 
 
-def kernel(body, outs, ins, out_specs, name, scratch=(), cost=1):
+def kernel(body, outs, ins, out_specs, name, scratch=(), cost=1, aliases={}):
     return pl.pallas_call(
         body,
         out_shape=outs,
@@ -90,6 +90,7 @@
         out_specs=out_specs,
         scratch_shapes=list(scratch),
         name=name,
+        input_output_aliases=aliases,
         cost_estimate=pl.CostEstimate(flops=cost, bytes_accessed=cost, transcendentals=0),
         compiler_params=pltpu.CompilerParams(vmem_limit_bytes=LIMIT),
     )
@@ -216,7 +217,7 @@
         copy.wait()
 
 
-def basis_body(count, ct, height, surface, fx_ref, fn_ref, dg_ref, q1_ref, near, far, links_hbm, basis_ref, sums_ref):
+def basis_body(ct, height, surface, fx_ref, fn_ref, dg_ref, q1_ref, near, far, links_hbm, basis_ref, sums_ref):
     even = is_even()
     b0 = ct[...]
     rows = row_index(b0)
@@ -259,16 +260,16 @@
     b2_b = outer(sides[0], b1[0:1, :])
     b2_a = outer(sides[1], b1[ROWS - 1 : ROWS, :])
     next2 = apply(b2, b2_b, b2_a)
-    tile_rows = lax.broadcasted_iota(jnp.int32, (8, 128), 0)
-    packed = jnp.zeros((8, 128), FLOAT)
+    lanes = lax.broadcasted_iota(jnp.int32, (1, 128), 1)
+    packed = jnp.zeros((1, 128), FLOAT)
     for place, (p, q) in enumerate(((b0, b0), (b0, b1), (b1, b1), (b1, b2), (b2, b2), (b2, next2))):
         product = p * q
         folded = product[:, 0:128]
         for j in range(1, product.shape[1] // 128):
             folded = folded + product[:, j * 128 : (j + 1) * 128]
-        packed = jnp.where(tile_rows == place, jnp.sum(folded, axis=0, keepdims=True), packed)
-    for j in range(count):
-        sums_ref[j * 8 : (j + 1) * 8, :] = packed
+        total = jnp.sum(jnp.sum(folded, axis=0, keepdims=True), axis=1, keepdims=True)
+        packed = jnp.where(lanes == place, total, packed)
+    sums_ref[...] = jnp.broadcast_to(packed, sums_ref.shape)
 
 
 def quadratic(left, form):
@@ -322,65 +323,9 @@
     return guess * (2.0 - values * guess)
 
 
-def columns_body(levels, count, sums, basis_ref, weight_hbm, kmt_hbm, source_hbm, kvert_hbm, land_hbm, links_hbm,
-                 out_hbm, u, near_ref, far_ref, weight, kmt, source, kvert, land, links, s_ref, ratio, sems, out_sems):
-    width = source.shape[1]
-    parts = 4
-    chunk = levels // parts
-    small = loads(((weight_hbm, weight), (kmt_hbm, kmt)), sems)
-    parted = [in_parts(far, near, parts) for far, near in ((land_hbm, land), (kvert_hbm, kvert), (source_hbm, source))]
-    big = loads([pairs[i] for i in range(parts) for pairs in parted], sems, 2)
-    links_copy = loads([(links_hbm, links)], sems, 2 + 3 * parts)[0]
-
-    tile_sums = sums[0:8, :]
-    for j in range(1, count):
-        tile_sums = tile_sums + sums[j * 8 : (j + 1) * 8, :]
-    tile_sums = jnp.sum(tile_sums, axis=1, keepdims=True)
-    mix = weights([tile_sums[i : i + 1, :] for i in range(6)])
-    b0, b1, b2 = (basis_ref[i * ROWS : (i + 1) * ROWS, :] for i in range(3))
-    s = mix[0] * b0 + mix[1] * b1 + mix[2] * b2
-    s_ref[...] = s
-    outs = loads([(s_ref, out_hbm)], out_sems)
-
-    small[0].wait()
-    scaled = stacked(s) / jnp.full((ROWS * width // 128, 128), weight_sum(weight, levels), FLOAT)
-    small[1].wait()
-    depth = stacked(kmt[...])
-
-    def sea(k):
-        return jnp.where(k < depth, stacked(land[rows_at(k), :]), 0).astype(FLOAT)
-
-    def down(k, carry):
-        here, link, passed = carry
-        at = level_at(k, width)
-        below = jnp.where(k + 1 < levels, sea(jnp.minimum(k + 1, levels - 1)), 0.0)
-        coupling = stacked(kvert[rows_at(k), :]) * here * below
-        over = inverse_of(1.0 + coupling + link)
-        value = (stacked(source[rows_at(k), :]) + here * (weight[k] * scaled) + passed) * over
-        part = coupling * over
-        ratio[at, :] = part
-        u[at, :] = value
-        return below, coupling - coupling * part, coupling * value
-
-    zero = jnp.zeros(scaled.shape, FLOAT)
-    big[0].wait()
-    carry = (sea(0), zero, zero)
-    for i in range(parts):
-        big[3 * i + 1].wait()
-        big[3 * i + 2].wait()
-        if i + 1 < parts:
-            big[3 * i + 3].wait()
-        carry = lax.fori_loop(i * chunk, (i + 1) * chunk, down, carry, unroll=4)
-
-    def up(i, below):
-        at = level_at(levels - 1 - i, width)
-        value = u[at, :] + ratio[at, :] * below
-        u[at, :] = value
-        return value
-
-    lax.fori_loop(0, levels, up, zero, unroll=4)
-    links_copy.wait()
+def send_rows(u, links, near_ref, far_ref, width):
     even = is_even()
+    levels = near_ref.shape[0] // 2
     for block in range(levels // 8):
         found = []
         for side, row, inner in ((0, 0, 1), (1, ROWS - 1, ROWS - 2)):
@@ -391,12 +336,88 @@
         for place in range(2):
             at = pl.ds(place * levels + block * 8, 8)
             near_ref[at, :], far_ref[at, :] = dealt(even, found[0][place], found[1][place])
+
+
+def columns_body(levels, sums, basis_ref, weight_hbm, kmt_hbm, source_hbm, kvert_hbm, land_hbm, links_hbm,
+                 out_hbm, high, ratio, low, links_high, near_ref, far_ref,
+                 weight, kmt, source, kvert, land, links_low, s_ref, ratio_low, sems, out_sems):
+    width = source.shape[1]
+    parts = 4
+    chunk = levels // parts
+    half = levels // 2
+    small = loads(((weight_hbm, weight), (kmt_hbm, kmt)), sems)
+    parted = [in_parts(far, near, parts) for far, near in ((land_hbm, land), (kvert_hbm, kvert), (source_hbm, source))]
+    big = loads([pairs[i] for i in range(parts) for pairs in parted], sems, 2)
+    top, bottom = (pl.ds(i * half * LINKS, half * LINKS) for i in range(2))
+    links_copies = loads([(links_hbm.at[bottom], links_low), (links_hbm.at[top], links_high)], sems, 2 + 3 * parts)
+
+    total = jnp.sum(sums[...], axis=0, keepdims=True)
+    mix = weights([total[:, i : i + 1] for i in range(6)])
+    b0, b1, b2 = (basis_ref[i * ROWS : (i + 1) * ROWS, :] for i in range(3))
+    s = mix[0] * b0 + mix[1] * b1 + mix[2] * b2
+    s_ref[...] = s
+    outs = loads([(s_ref, out_hbm)], out_sems)
+
+    small[0].wait()
+    scaled = stacked(s) / jnp.full((ROWS * width // 128, 128), weight_sum(weight, levels), FLOAT)
+    small[1].wait()
+    depth = stacked(kmt[...])
+
+    def sea(k):
+        return jnp.where(k < depth, stacked(land[rows_at(k), :]), 0).astype(FLOAT)
+
+    def down(values, parts_of, first, k, carry):
+        here, link, passed = carry
+        at = level_at(k - first, width)
+        below = jnp.where(k + 1 < levels, sea(jnp.minimum(k + 1, levels - 1)), 0.0)
+        coupling = stacked(kvert[rows_at(k), :]) * here * below
+        over = inverse_of(1.0 + coupling + link)
+        value = (stacked(source[rows_at(k), :]) + here * (weight[k] * scaled) + passed) * over
+        part = coupling * over
+        parts_of[at, :] = part
+        values[at, :] = value
+        return below, coupling - coupling * part, coupling * value
+
+    zero = jnp.zeros(scaled.shape, FLOAT)
+    big[0].wait()
+    carry = (sea(0), zero, zero)
+    for i in range(parts):
+        big[3 * i + 1].wait()
+        big[3 * i + 2].wait()
+        if i + 1 < parts:
+            big[3 * i + 3].wait()
+        step = functools.partial(down, high, ratio, 0) if 2 * i < parts else functools.partial(down, low, ratio_low, half)
+        carry = lax.fori_loop(i * chunk, (i + 1) * chunk, step, carry, unroll=4)
+    ascend(low, low, ratio_low, zero, width)
+    for copy in links_copies:
+        copy.wait()
+    send_rows(low, links_low, near_ref, far_ref, width)
     for copy in outs:
         copy.wait()
 
 
-def inner_body(levels, u0, kmt_hbm, kappa_hbm, land_hbm, u2_ref, kmt, kappa, land, sems):
+def ascend(target, source, ratio, below, width):
+    levels = target.shape[0] * 128 // (ROWS * width)
+
+    def up(i, below):
+        at = level_at(levels - 1 - i, width)
+        value = source[at, :] + ratio[at, :] * below
+        target[at, :] = value
+        return value
+
+    lax.fori_loop(0, levels, up, below, unroll=4)
+
+
+def upper_body(high, ratio, low, links, u, near_ref, far_ref):
+    width = near_ref.shape[1]
+    ascend(u, high, ratio, low[level_at(0, width), :], width)
+    send_rows(u, links, near_ref, far_ref, width)
+
+
+def inner_body(levels, high, low, kmt_hbm, kappa_hbm, land_hbm, u2_ref,
+               kmt, kappa, land, fx_ref, fw_ref, fn_ref, fs_ref, keep_ref, u1_ref, sems):
     parts = 4
+    half = levels // 2
     kmt_copy = loads([(kmt_hbm, kmt)], sems)[0]
     pairs = ((kappa_hbm, kappa), (land_hbm, land))
     parted = [in_parts(far, near, parts) for far, near in pairs]
@@ -409,51 +430,72 @@
     def face(here, there):
         return jnp.where(jnp.minimum(here, there) > 0.0, here + there, 0.0)
 
-    def level(k):
+    def coefficients(k, carry):
         at = rows_at(k)
         sea = jnp.where(k < depth, land[at, :], 0) > 0
-        half = jnp.where(sea, 0.5 * kappa[at, :], 0.0)
-        fx = face(half, east(half))
-        fn = jnp.where(inside, face(half, north(half)), 0.0)
+        halved = jnp.where(sea, 0.5 * kappa[at, :], 0.0)
+        fx = face(halved, east(halved))
+        fn = jnp.where(inside, face(halved, north(halved)), 0.0)
         fw, fs = west(fx), south(fn)
-        keep = 1.0 - (fx + fw) - (fn + fs)
-        u = unstacked(u0[level_at(k, width), :])
-        for _ in range(2):
-            u = keep * u + (fx * east(u) + fw * west(u)) + (fn * north(u) + fs * south(u))
-        return u
-
-    def group(i, carry):
-        for values, k in [(level(2 * i + j), 2 * i + j) for j in range(2)]:
-            u2_ref[rows_at(k), :] = values
+        for ref, values in ((fx_ref, fx), (fw_ref, fw), (fn_ref, fn), (fs_ref, fs)):
+            ref[at, :] = values
+        keep_ref[at, :] = 1.0 - (fx + fw) - (fn + fs)
         return carry
 
-    chunk = levels // 2 // parts
+    chunk = levels // parts
     for i in range(parts):
         for copy in copies[2 * i : 2 * i + 2]:
             copy.wait()
-        lax.fori_loop(i * chunk, (i + 1) * chunk, group, 0)
-
-
-def finish_body(levels, u2, links, own_near, own_far, rim_near, rim_far, near, far, rim_other_near, rim_other_far,
-                out, change_ref, buffer, sems):
+        lax.fori_loop(i * chunk, (i + 1) * chunk, coefficients, 0, unroll=2)
+
+    def spread_out(u, at):
+        return (keep_ref[at, :] * u + (fx_ref[at, :] * east(u) + fw_ref[at, :] * west(u))
+                + (fn_ref[at, :] * north(u) + fs_ref[at, :] * south(u)))
+
+    for first, part in ((0, high), (half, low)):
+
+        def once(k, carry):
+            at = rows_at(k + first)
+            u1_ref[at, :] = spread_out(unstacked(part[level_at(k, width), :]), at)
+            return carry
+
+        lax.fori_loop(0, half, once, 0, unroll=2)
+
+    def twice(k, carry):
+        at = rows_at(k)
+        u2_ref[at, :] = spread_out(u1_ref[at, :], at)
+        return carry
+
+    lax.fori_loop(0, levels, twice, 0, unroll=2)
+
+
+def finish_body(levels, first, last, skipped, u2, links, own_near, own_far, near, far, rim_near, rim_far, rim_other_near, rim_other_far,
+                *refs):
+    out, change_ref, buffer, sems = refs[-4:]
     width = own_near.shape[1]
     tall = width // 128 * ROWS
+    count = last - first
     rows = lax.broadcasted_iota(jnp.int32, (ROWS, width), 0)
     on_rim = (rows < 2) | (rows >= ROWS - 2)
     even = is_even()
     copies = []
-    for block in range(levels // 8):
-        at, below = pl.ds(block * 8, 8), pl.ds(levels + block * 8, 8)
+    for block in range(count // 8):
+        at, below = pl.ds(block * 8, 8), pl.ds(count + block * 8, 8)
 
         def pairs(a, b):
             return [dealt(even, a[part, :], b[part, :]) for part in (at, below)]
 
-        own, rim = pairs(own_near, own_far), pairs(rim_near, rim_far)
-        other, rim_other = pairs(near, far), pairs(rim_other_near, rim_other_far)
+        own, other = pairs(own_near, own_far), pairs(near, far)
+        kap, wet, kap_other, wet_other = (
+            dealt(even, a[pl.ds(part * levels + first + block * 8, 8), :], b[pl.ds(part * levels + first + block * 8, 8), :])
+            for a, b in ((rim_near, rim_far), (rim_other_near, rim_other_far)) for part in range(2)
+        )
         for side, row, inner in ((0, 0, 1), (1, ROWS - 1, ROWS - 2)):
-            face = 0.5 * (rim[0][side] + rim_other[0][side]) * rim[1][side] * rim_other[1][side]
+            face = 0.5 * (kap[side] + kap_other[side]) * wet[side] * wet_other[side]
             change = face * (other[0][side] - own[0][side])
-            along, link = (links[pl.ds((block * LINKS + side * 2 + i) * 8, 8), :] for i in range(2))
+            along, link = (
+                links[pl.ds(((skipped + block) * LINKS + side * 2 + i) * 8, 8), :] for i in range(2)
+            )
             flux = along * (east(change) - change)
             passed = link * change
             on_row = (change + (flux - west(flux)) - passed
@@ -463,13 +505,12 @@
                 change_ref[pl.ds(j * ROWS + row, 8, stride=tall), :] = on_row[:, lanes]
                 change_ref[pl.ds(j * ROWS + inner, 8, stride=tall), :] = passed[:, lanes]
         for k in range(8):
-            level = block * 8 + k
+            here = block * 8 + k
             change = jnp.where(on_rim, unstacked(change_ref[level_at(k, width), :]), 0.0)
-            buffer[rows_at(level), :] = u2[rows_at(level), :] + change
+            buffer[rows_at(here), :] = u2[rows_at(first + here), :] + change
         whole = pl.ds(block * 8 * ROWS, 8 * ROWS)
-        copy = pltpu.make_async_copy(buffer.at[whole], out.at[whole], sems.at[block])
-        copy.start()
-        copies.append(copy)
+        target = pl.ds((first + block * 8) * ROWS, 8 * ROWS)
+        copies += loads([(buffer.at[whole], out.at[target])], sems, block)
     for copy in copies:
         copy.wait()
 
@@ -508,31 +549,46 @@
         functools.partial(rims_body, levels), vmem(rim, rim) + hbm(link_rows), in_hbm(1) + in_vmem(1),
         in_vmem(2) + in_hbm(1), "rims", [whole, bricks, pltpu.VMEM(link_rows, FLOAT), semaphores((4 + levels // 8,))],
     )(kappa, wet)
-    links = left(links)
+    links_left = left(links)
     rim_other_near, rim_other_far = exchange(rim_near, rim_far)
 
     basis, sums = kernel(
-        functools.partial(basis_body, count), vmem((3 * rows, width), (8 * count, 128)), in_vmem(9) + in_hbm(1),
+        basis_body, vmem((3 * rows, width), (count, 128)), in_vmem(9) + in_hbm(1),
         in_vmem(2), "basis"
-    )(base, height, surface, s_fx, s_fn, s_dg, q1, near, far, links)
-    sums = lax.all_to_all(sums.reshape(count, 8, 128), "tile", 0, 0, tiled=True).reshape(8 * count, 128)
-
-    solution, u0, row_near, row_far = kernel(
-        functools.partial(columns_body, levels, count), hbm(tile) + vmem(brick, rim, rim), in_vmem(2) + in_hbm(6),
-        in_hbm(1) + in_vmem(3), "columns",
-        [scalars, tile_ints, whole, whole, ints, pltpu.VMEM(link_rows, FLOAT), tiles, bricks, semaphores((15,)),
-         semaphores((1,))],
-    )(sums, basis, layer_weight, kmt, ct_tracer, kvert, land, links)
-    other_near, other_far = exchange(row_near, row_far)
+    )(base, height, surface, s_fx, s_fn, s_dg, q1, near, far, links_left)
+    sums = lax.all_to_all(sums.reshape(count, 1, 128), "tile", 0, 0, tiled=True).reshape(count, 128)
+
+    rims = (rim_near, rim_far, rim_other_near, rim_other_far)
+    half = levels // 2
+    halved = lambda shape: (shape[0] // 2, shape[1])
+    half_bricks, half_links = halved(brick), halved(link_rows)
+    solution, carried, ratio, low, links_high, low_near, low_far = kernel(
+        functools.partial(columns_body, levels),
+        hbm(tile) + vmem(half_bricks, half_bricks, half_bricks, half_links, halved(rim), halved(rim)),
+        in_vmem(2) + in_hbm(6), in_hbm(1) + in_vmem(6), "columns",
+        [scalars, tile_ints, whole, whole, ints, pltpu.VMEM(half_links, FLOAT), tiles, pltpu.VMEM(half_bricks, FLOAT),
+         semaphores((16,)), semaphores((1,))],
+    )(sums, basis, layer_weight, kmt, ct_tracer, kvert, land, links_left)
+    low_other_near, low_other_far = exchange(low_near, low_far)
+    high, high_near, high_far = kernel(
+        upper_body, vmem(half_bricks, halved(rim), halved(rim)), in_vmem(4), in_vmem(3), "upper_columns"
+    )(carried, ratio, low, links_high)
+    high_other_near, high_other_far = exchange(high_near, high_far)
     u2 = kernel(
-        functools.partial(inner_body, levels), vmem(flat), in_vmem(1) + in_hbm(3), in_vmem(1), "inner",
-        [tile_ints, whole, ints, semaphores((9,))],
-    )(u0, kmt, kappa, land)[0]
-
+        functools.partial(inner_body, levels), vmem(flat), in_vmem(2) + in_hbm(3), in_vmem(1), "inner",
+        [tile_ints, whole, ints] + [whole] * 6 + [semaphores((9,))],
+    )(high, low, kmt, kappa, land)[0]
+
+    scratch = [
+        pltpu.VMEM((8 * rows * width // 128, 128), FLOAT), pltpu.VMEM(halved(flat), FLOAT), semaphores((half // 8,))
+    ]
+    deep = kernel(
+        functools.partial(finish_body, levels, half, levels, half // 8), hbm(flat), in_vmem(10), in_hbm(1), "finish_low", scratch,
+    )(u2, held(links), low_near, low_far, low_other_near, low_other_far, *rims)[0]
     values = kernel(
-        functools.partial(finish_body, levels), hbm(flat), in_vmem(10), in_hbm(1), "finish",
-        [pltpu.VMEM((8 * rows * width // 128, 128), FLOAT), whole, semaphores((levels // 8,))],
-    )(u2, held(links), row_near, row_far, rim_near, rim_far, other_near, other_far, rim_other_near, rim_other_far)[0]
+        functools.partial(finish_body, levels, 0, half, 0), hbm(flat), in_vmem(10) + in_hbm(1), in_hbm(1), "finish_high",
+        scratch, aliases={10: 0},
+    )(u2, links_high, high_near, high_far, high_other_near, high_other_far, *rims, left(deep))[0]
     return (values.reshape(levels, rows, width), solution)
 
 

time: 44.2 us -> 47.1 us (1.066)
  waiting for transfers between devices: 6.24 us -> 2.05 us
  Pallas kernels: 20.1 us -> 23.9 us
  starting transfers between devices: 16.5 us -> 20 us
    ppermute x6 -> x8, waiting for transfers between devices: 3.88 us -> 0.02 us  [swap(): lax.ppermute(array, 'tile', [(i, i + 1) for i in firsts] + [(i + 1, i) fo...]
    pallas_call x4 -> x6, Pallas kernels: 15.2 us -> 19 us  [the longest x1 11 us: body(): kernel(functools.partial(inner_body, levels), vmem(flat), in_vmem(2) + in...]
    ppermute x6 -> x8, starting transfers between devices: 11.2 us -> 14.7 us  [swap(): lax.ppermute(array, 'tile', [(i, i + 1) for i in firsts] + [(i + 1, i) fo...]
  transfers between devices with their start and end apart: 7 -> 9, of which waited for: 2 -> 1; matrix products, arithmetic and copies ran while one was open for 0% -> 0% of each run, Pallas kernels for 35% -> 42%
where the time goes in v8:
time: 47.1 us; the launch traced here: 46.8 us
  Pallas kernels  23.9 us (51%)
  starting transfers between devices  20 us (42%)
  waiting for transfers between devices  2.05 us (4%)
  between operations  0.79 us (2%)
    ppermute x8, starting transfers between devices, swap(): lax.ppermute(array, 'tile', [(i, i + 1) for i in firsts] + [(i + 1, i) fo...  14.7 us
    pallas_call x1, Pallas kernels, body(): kernel(functools.partial(inner_body, levels), vmem(flat), in_vmem(2) + in...  11 us
    all_to_all x1, starting transfers between devices, body(): lax.all_to_all(sums.reshape(count, 1, 128), 'tile', 0, 0, tiled=True)  5.32 us
    pallas_call x1, Pallas kernels, body(): kernel(functools.partial(columns_body, levels), hbm(tile) + vmem(half_bri...  4 us
    pallas_call x1, Pallas kernels, body(): kernel(functools.partial(rims_body, levels), vmem(rim, rim) + hbm(link_ro...  2.98 us
    all_to_all x1, waiting for transfers between devices, body(): lax.all_to_all(sums.reshape(count, 1, 128), 'tile', 0, 0, tiled=True)  2.02 us
    pallas_call x1, Pallas kernels, body(): kernel(functools.partial(setup_body, levels), vmem(*[tile] * 9, brick), i...  1.97 us
    pallas_call x1, Pallas kernels, body(): kernel(functools.partial(finish_body, levels, 0, half, 0), hbm(flat), in_...  1.32 us
  transfers between devices with their start and end apart: 9, of which 1 were waited for; matrix products, arithmetic and copies ran while one was open for 0% of the time, Pallas kernels for 42%

profile of v8, /device:TPU:1, one launch (start us, length us, event | category | flops | bytes accessed | tf_op | source)
XLA Modules:
  0.0 46.8 jit_solution(1767910422033860541)
XLA Ops:
  0.6 2.0 %setup.1 = (f32[8,1280]{1,0:T(8,128)S(1)}, f32[8,1280]{1,0:T(8,128)S(1)}, f32[8,1280]{1,0:T(8,128)S(1)}, f32[8,1280]{1,0:T(8,128)S(1)}, f32[8,1280]{1,0:T(8,128)...) custom-call(f32[48]{0:T(128)} %weight_hbm.3, ...), custom_call_target="tpu_custom_call" | custom-call | flops 1 | bytes 1 | tf_op jit(solution)/shard_map/setup/pallas_call | solution.py:542
  2.6 0.1 collective-permute-start
  2.7 4.5 %collective-permute-start.1 = (f32[8,1280]{1,0:T(8,128)S(1)}, f32[8,1280]{1,0:T(8,128)S(1)}, u32[]{:S(2)}, u32[]{:S(2)}) collective-permute-start(f32[8,1280]{1,0:T(8,128)S(1)} %get-tuple-element.35), channel_id=1, source_target_pairs={{1,2},{3,4},{5,6},{7,8},{9,10},{11,12},{13,14},{2,1},{4,3},{6,5},{... | collective-permute-start | bytes 122888 | tf_op jit(solution)/shard_map/ppermute | solution.py:523
  7.2 3.0 %rims.1 = (f32[96,1280]{1,0:T(8,128)S(1)}, f32[96,1280]{1,0:T(8,128)S(1)}, f32[192,1280]{1,0:T(8,128)}) custom-call(f32[384,1280]{1,0:T(8,128)} %bitcast.13, f32[3840,128]{1,0:T(8,128)S(1)} %get-tuple-element.36.wet_bricks), custom_call_target="tpu_custom_call" | custom-call | flops 1 | bytes 1 | tf_op jit(solution)/shard_map/rims/pallas_call | solution.py:548
  10.2 0.0 collective-permute-done.near
  10.2 0.0 collective-permute-done.1.far
  10.2 0.9 %basis.1 = (f32[24,1280]{1,0:T(8,128)S(1)}, f32[16,128]{1,0:T(8,128)}) custom-call(f32[8,1280]{1,0:T(8,128)S(1)} %get-tuple-element.27.ct, f32[8,1280]{1,0:T(8,128)S(1)} %get-tuple-element.28.height, f32[8,1280]{1,0:T(8,128)S(1)} %get-tuple-element.29.surface, f32[8,1280]{1,0:T(8,128)S(1)} %get-tuple-element.30.fx_ref, ...), custom_call_target="tpu_custom_call" | custom-call | flops 1 | bytes 1 | tf_op jit(solution)/shard_map/basis/pallas_call | solution.py:555
  11.2 5.3 %all-to-all-start = ((f32[16,1,128]{2,1,0:T(1,128)}), f32[16,1,128]{2,1,0:T(1,128)S(1)}, u32[]{:S(2)}, u32[]{:S(2)}) async-start(f32[16,1,128]{2,1,0:T(1,128)} %bitcast.3), calls=%async_computation | async-start | bytes 16384 | tf_op jit(solution)/shard_map/all_to_all | solution.py:559
  16.5 0.2 collective-permute-start.4
  16.6 3.5 %collective-permute-start.5 = (f32[96,1280]{1,0:T(8,128)S(1)}, f32[96,1280]{1,0:T(8,128)S(1)}, u32[]{:S(2)}, u32[]{:S(2)}) collective-permute-start(f32[96,1280]{1,0:T(8,128)S(1)} %get-tuple-element.48.rim_far), channel_id=1, source_target_pairs={{1,2},{3,4},{5,6},{7,8},{9,10},{11,12},{13,14},{2,1},{4,3},{6,5},{... | collective-permute-start | bytes 1474568 | tf_op jit(solution)/shard_map/ppermute | solution.py:523
  20.2 2.0 %all-to-all-done = f32[16,1,128]{2,1,0:T(1,128)S(1)} async-done(((f32[16,1,128]{2,1,0:T(1,128)}), f32[16,1,128]{2,1,0:T(1,128)S(1)}, u32[]{:S(2)}, u32[]{:S(2)}) %all-to-all-start) | async-done | bytes 8224 | tf_op jit(solution)/shard_map/all_to_all | solution.py:559
  22.2 4.0 %columns.1 = (f32[8,1280]{1,0:T(8,128)}, f32[1920,128]{1,0:T(8,128)S(1)}, f32[1920,128]{1,0:T(8,128)S(1)}, f32[1920,128]{1,0:T(8,128)S(1)}, f32[96,1280]{1,0:T(8...) custom-call(f32[16,128]{1,0:T(8,128)S(1)} %bitcast.9, f32[24,1280]{1,0:T(8,128)S(1)} %get-tuple-element.39.basis_ref, ...), custom_call_target="tpu_custom_call" | custom-call | flops 1 | bytes 1 | tf_op jit(solution)/shard_map/columns/pallas_call | solution.py:565
  26.2 0.8 %collective-permute-start.6 = (f32[48,1280]{1,0:T(8,128)S(1)}, f32[48,1280]{1,0:T(8,128)S(1)}, u32[]{:S(2)}, u32[]{:S(2)}) collective-permute-start(f32[48,1280]{1,0:T(8,128)S(1)} %get-tuple-element.49.own_near), channel_id=1, source_target_pairs={{0,1},{2,3},{4,5},{6,7},{8,9},{10,11},{12,13},{14,15},{1,0},{3,2},... | collective-permute-start | bytes 737288 | tf_op jit(solution)/shard_map/ppermute | solution.py:523
  27.0 2.0 %collective-permute-start.7 = (f32[48,1280]{1,0:T(8,128)S(1)}, f32[48,1280]{1,0:T(8,128)S(1)}, u32[]{:S(2)}, u32[]{:S(2)}) collective-permute-start(f32[48,1280]{1,0:T(8,128)S(1)} %get-tuple-element.50.own_far), channel_id=1, source_target_pairs={{1,2},{3,4},{5,6},{7,8},{9,10},{11,12},{13,14},{2,1},{4,3},{6,5},{... | collective-permute-start | bytes 737288 | tf_op jit(solution)/shard_map/ppermute | solution.py:523
  29.0 0.4 upper_columns.1
  29.4 0.1 collective-permute-start.2
  29.5 0.0 collective-permute-done.6.near
  29.5 3.5 %collective-permute-start.3 = (f32[48,1280]{1,0:T(8,128)S(1)}, f32[48,1280]{1,0:T(8,128)S(1)}, u32[]{:S(2)}, u32[]{:S(2)}) collective-permute-start(f32[48,1280]{1,0:T(8,128)S(1)} %get-tuple-element.46.own_far), channel_id=1, source_target_pairs={{1,2},{3,4},{5,6},{7,8},{9,10},{11,12},{13,14},{2,1},{4,3},{6,5},{... | collective-permute-start | bytes 737288 | tf_op jit(solution)/shard_map/ppermute | solution.py:523
  33.1 0.0 copy-start
  33.1 11.0 %inner.1.u2 = f32[384,1280]{1,0:T(8,128)S(1)} custom-call(f32[1920,128]{1,0:T(8,128)S(1)} %get-tuple-element.44.high, f32[1920,128]{1,0:T(8,128)S(1)} %get-tuple-element.42.low, s32[8,1280]{1,0:T(8,128)} %kmt_hbm.5, f32[384,1280]{1,0:T(8,128)} %bitcast.14, s32[384,1280]{1,0:T(8,128)} %bitcast.12), custom_call_target="tpu_custom_call" | custom-call | flops 1 | bytes 1 | tf_op jit(solution)/shard_map/inner/pallas_call | solution.py:577
  44.1 0.0 collective-permute-done.7.far
  44.1 0.0 collective-permute-done.4.rim_other_near
  44.1 0.0 collective-permute-done.5.rim_other_far
  44.1 0.0 copy-done
  44.1 1.3 %finish_low.1.refs_0_ = f32[384,1280]{1,0:T(8,128)} custom-call(f32[384,1280]{1,0:T(8,128)S(1)} %inner.1.u2, f32[192,1280]{1,0:T(8,128)S(1)} %copy-done, f32[48,1280]{1,0:T(8,128)S(1)} %get-tuple-element.49.own_near, f32[48,1280]{1,0:T(8,128)S(1)} %get-tuple-element.50.own_far, f32[48,1280]{1,0:T(8,128)S(1)} %collective-permute-done.6.near, ...), custom_call_target="tpu_custom_call" | custom-call | flops 1 | bytes 1 | tf_op jit(solution)/shard_map/finish_low/pallas_call | solution.py:585
  45.4 0.0 collective-permute-done.2.near
  45.4 0.0 collective-permute-done.3.far
  45.5 1.3 %finish_high.1 = f32[384,1280]{1,0:T(8,128)} custom-call(f32[384,1280]{1,0:T(8,128)S(1)} %inner.1.u2, f32[96,1280]{1,0:T(8,128)S(1)} %get-tuple-element.43.links, f32[48,1280]{1,0:T(8,128)S(1)} %get-tuple-element.45.own_near, f32[48,1280]{1,0:T(8,128)S(1)} %get-tuple-element.46.own_far, ...), custom_call_target="tpu_custom_call", output_to_operand_aliasing={{}: (10, {})} | custom-call | flops 1 | bytes 1 | tf_op jit(solution)/shard_map/finish_high/pallas_call | solution.py:588
Async XLA Ops:
  2.6 7.6 %collective-permute-start = (f32[8,1280]{1,0:T(8,128)S(1)}, f32[8,1280]{1,0:T(8,128)S(1)}, u32[]{:S(2)}, u32[]{:S(2)}) collective-permute-start(f32[8,1280]{1,0:T(8,128)S(1)} %get-tuple-element.34), channel_id=1, source_target_pairs={{0,1},{2,3},{4,5},{6,7},{8,9},{10,11},{12,13},{14,15},{1,0},{3,2},... | collective-permute-start | bytes 122888 | tf_op jit(solution)/shard_map/ppermute | solution.py:523
  2.7 7.5 %collective-permute-start.1 = (f32[8,1280]{1,0:T(8,128)S(1)}, f32[8,1280]{1,0:T(8,128)S(1)}, u32[]{:S(2)}, u32[]{:S(2)}) collective-permute-start(f32[8,1280]{1,0:T(8,128)S(1)} %get-tuple-element.35), channel_id=1, source_target_pairs={{1,2},{3,4},{5,6},{7,8},{9,10},{11,12},{13,14},{2,1},{4,3},{6,5},{... | collective-permute-start | bytes 122888 | tf_op jit(solution)/shard_map/ppermute | solution.py:523
  11.2 11.0 %all-to-all-start = ((f32[16,1,128]{2,1,0:T(1,128)}), f32[16,1,128]{2,1,0:T(1,128)S(1)}, u32[]{:S(2)}, u32[]{:S(2)}) async-start(f32[16,1,128]{2,1,0:T(1,128)} %bitcast.3), calls=%async_computation | async-start | bytes 16384 | tf_op jit(solution)/shard_map/all_to_all | solution.py:559
  16.5 27.6 %collective-permute-start.4 = (f32[96,1280]{1,0:T(8,128)S(1)}, f32[96,1280]{1,0:T(8,128)S(1)}, u32[]{:S(2)}, u32[]{:S(2)}) collective-permute-start(f32[96,1280]{1,0:T(8,128)S(1)} %get-tuple-element.47.rim_near), channel_id=1, source_target_pairs={{0,1},{2,3},{4,5},{6,7},{8,9},{10,11},{12,13},{14,15},{1,0},{3,2},... | collective-permute-start | bytes 1474568 | tf_op jit(solution)/shard_map/ppermute | solution.py:523
  16.6 27.5 %collective-permute-start.5 = (f32[96,1280]{1,0:T(8,128)S(1)}, f32[96,1280]{1,0:T(8,128)S(1)}, u32[]{:S(2)}, u32[]{:S(2)}) collective-permute-start(f32[96,1280]{1,0:T(8,128)S(1)} %get-tuple-element.48.rim_far), channel_id=1, source_target_pairs={{1,2},{3,4},{5,6},{7,8},{9,10},{11,12},{13,14},{2,1},{4,3},{6,5},{... | collective-permute-start | bytes 1474568 | tf_op jit(solution)/shard_map/ppermute | solution.py:523
  26.2 3.3 %collective-permute-start.6 = (f32[48,1280]{1,0:T(8,128)S(1)}, f32[48,1280]{1,0:T(8,128)S(1)}, u32[]{:S(2)}, u32[]{:S(2)}) collective-permute-start(f32[48,1280]{1,0:T(8,128)S(1)} %get-tuple-element.49.own_near), channel_id=1, source_target_pairs={{0,1},{2,3},{4,5},{6,7},{8,9},{10,11},{12,13},{14,15},{1,0},{3,2},... | collective-permute-start | bytes 737288 | tf_op jit(solution)/shard_map/ppermute | solution.py:523
  27.0 17.1 %collective-permute-start.7 = (f32[48,1280]{1,0:T(8,128)S(1)}, f32[48,1280]{1,0:T(8,128)S(1)}, u32[]{:S(2)}, u32[]{:S(2)}) collective-permute-start(f32[48,1280]{1,0:T(8,128)S(1)} %get-tuple-element.50.own_far), channel_id=1, source_target_pairs={{1,2},{3,4},{5,6},{7,8},{9,10},{11,12},{13,14},{2,1},{4,3},{6,5},{... | collective-permute-start | bytes 737288 | tf_op jit(solution)/shard_map/ppermute | solution.py:523
  29.4 16.0 %collective-permute-start.2 = (f32[48,1280]{1,0:T(8,128)S(1)}, f32[48,1280]{1,0:T(8,128)S(1)}, u32[]{:S(2)}, u32[]{:S(2)}) collective-permute-start(f32[48,1280]{1,0:T(8,128)S(1)} %get-tuple-element.45.own_near), channel_id=1, source_target_pairs={{0,1},{2,3},{4,5},{6,7},{8,9},{10,11},{12,13},{14,15},{1,0},{3,2},... | collective-permute-start | bytes 737288 | tf_op jit(solution)/shard_map/ppermute | solution.py:523
  29.5 15.9 %collective-permute-start.3 = (f32[48,1280]{1,0:T(8,128)S(1)}, f32[48,1280]{1,0:T(8,128)S(1)}, u32[]{:S(2)}, u32[]{:S(2)}) collective-permute-start(f32[48,1280]{1,0:T(8,128)S(1)} %get-tuple-element.46.own_far), channel_id=1, source_target_pairs={{1,2},{3,4},{5,6},{7,8},{9,10},{11,12},{13,14},{2,1},{4,3},{6,5},{... | collective-permute-start | bytes 737288 | tf_op jit(solution)/shard_map/ppermute | solution.py:523
  33.1 11.0 %copy-start = (f32[192,1280]{1,0:T(8,128)S(1)}, f32[192,1280]{1,0:T(8,128)}, u32[]{:S(2)}) copy-start(f32[192,1280]{1,0:T(8,128)} %get-tuple-element.37.links_hbm.links) | copy-start | bytes 2949124

commit v9 on v8

--- a/solution.py
+++ b/solution.py
@@ -40,6 +40,36 @@
 
 def unstacked(values):
     return jnp.concatenate([values[i : i + ROWS, :] for i in range(0, values.shape[0], ROWS)], axis=1)
+
+
+def padded(shape):
+    return (shape[0] + 2 * ROWS, shape[1])
+
+
+def clear_pads(ref):
+    zero = jnp.zeros((ROWS, ref.shape[1]), FLOAT)
+    ref[0:ROWS, :] = zero
+    ref[ref.shape[0] - ROWS :, :] = zero
+
+
+def within(ref):
+    return ref.at[pl.ds(ROWS, ref.shape[0] - 2 * ROWS)]
+
+
+def lane_index(values):
+    return lax.broadcasted_iota(jnp.int32, values.shape, 1)
+
+
+def east_of(values):
+    turned = pltpu.roll(values, 127, 1)
+    further = jnp.concatenate([turned[ROWS:, :], turned[:ROWS, :]], axis=0)
+    return jnp.where(lane_index(values) == 127, further, turned)
+
+
+def west_of(values):
+    turned = pltpu.roll(values, 1, 1)
+    further = jnp.concatenate([turned[-ROWS:, :], turned[:-ROWS, :]], axis=0)
+    return jnp.where(lane_index(values) == 0, further, turned)
 
 
 def row_of(ref, block, row, width):
@@ -339,12 +369,14 @@
 
 
 def columns_body(levels, sums, basis_ref, weight_hbm, kmt_hbm, source_hbm, kvert_hbm, land_hbm, links_hbm,
-                 out_hbm, high, ratio, low, links_high, near_ref, far_ref,
+                 out_hbm, high, ratio, low_ref, links_high, near_ref, far_ref,
                  weight, kmt, source, kvert, land, links_low, s_ref, ratio_low, sems, out_sems):
     width = source.shape[1]
     parts = 4
     chunk = levels // parts
     half = levels // 2
+    low = within(low_ref)
+    clear_pads(low_ref)
     small = loads(((weight_hbm, weight), (kmt_hbm, kmt)), sems)
     parted = [in_parts(far, near, parts) for far, near in ((land_hbm, land), (kvert_hbm, kvert), (source_hbm, source))]
     big = loads([pairs[i] for i in range(parts) for pairs in parted], sems, 2)
@@ -408,65 +440,65 @@
     lax.fori_loop(0, levels, up, below, unroll=4)
 
 
-def upper_body(high, ratio, low, links, u, near_ref, far_ref):
+def upper_body(high, ratio, low, links, u_ref, near_ref, far_ref):
     width = near_ref.shape[1]
+    low, u = within(low), within(u_ref)
+    clear_pads(u_ref)
     ascend(u, high, ratio, low[level_at(0, width), :], width)
     send_rows(u, links, near_ref, far_ref, width)
 
 
 def inner_body(levels, high, low, kmt_hbm, kappa_hbm, land_hbm, u2_ref,
-               kmt, kappa, land, fx_ref, fw_ref, fn_ref, fs_ref, keep_ref, u1_ref, sems):
+               kmt, kappa, land, halves_ref, fn_ref, u1_ref, sems):
     parts = 4
     half = levels // 2
     kmt_copy = loads([(kmt_hbm, kmt)], sems)[0]
     pairs = ((kappa_hbm, kappa), (land_hbm, land))
     parted = [in_parts(far, near, parts) for far, near in pairs]
     copies = loads([pairs[i] for i in range(parts) for pairs in parted], sems, 1)
+    width = u2_ref.shape[1]
+    tall = width // 128 * ROWS
+    zero = jnp.zeros((ROWS, 128), FLOAT)
+    for ref in (halves_ref, fn_ref, u1_ref):
+        ref[0:ROWS, :] = zero
+        for k in range(levels + 1):
+            ref[pl.ds(ROWS + k * tall, ROWS), :] = zero
     kmt_copy.wait()
-    depth = kmt[...]
-    width = depth.shape[1]
-    inside = row_index(depth) < ROWS - 1
+    depth = stacked(kmt[...])
+    inside = lax.rem(row_index(depth), ROWS) < ROWS - 1
 
     def face(here, there):
         return jnp.where(jnp.minimum(here, there) > 0.0, here + there, 0.0)
 
-    def coefficients(k, carry):
-        at = rows_at(k)
-        sea = jnp.where(k < depth, land[at, :], 0) > 0
-        halved = jnp.where(sea, 0.5 * kappa[at, :], 0.0)
-        fx = face(halved, east(halved))
-        fn = jnp.where(inside, face(halved, north(halved)), 0.0)
-        fw, fs = west(fx), south(fn)
-        for ref, values in ((fx_ref, fx), (fw_ref, fw), (fn_ref, fn), (fs_ref, fs)):
-            ref[at, :] = values
-        keep_ref[at, :] = 1.0 - (fx + fw) - (fn + fs)
+    def shifted(ref, k):
+        start = ROWS + k * tall
+        return ref[pl.ds(start + 1, tall), :], ref[pl.ds(start - 1, tall), :]
+
+    def level(source, first, k, carry):
+        at = pl.ds(pl.multiple_of(ROWS + k * tall, ROWS), tall)
+        sea = jnp.where(k < depth, stacked(land[rows_at(k), :]), 0) > 0
+        halved = jnp.where(sea, 0.5 * stacked(kappa[rows_at(k), :]), 0.0)
+        halves_ref[at, :] = halved
+        fx = face(halved, east_of(halved))
+        fn = jnp.where(inside, face(halved, shifted(halves_ref, k)[0]), 0.0)
+        fn_ref[at, :] = fn
+        fw, fs = west_of(fx), shifted(fn_ref, k)[1]
+        keep = 1.0 - (fx + fw) - (fn + fs)
+        u = source[pl.ds(pl.multiple_of(ROWS + (k - first) * tall, ROWS), tall), :]
+        north, south = shifted(source, k - first)
+        u = keep * u + (fx * east_of(u) + fw * west_of(u)) + (fn * north + fs * south)
+        u1_ref[at, :] = u
+        north, south = shifted(u1_ref, k)
+        u = keep * u + (fx * east_of(u) + fw * west_of(u)) + (fn * north + fs * south)
+        u2_ref[rows_at(k), :] = unstacked(u)
         return carry
 
     chunk = levels // parts
     for i in range(parts):
         for copy in copies[2 * i : 2 * i + 2]:
             copy.wait()
-        lax.fori_loop(i * chunk, (i + 1) * chunk, coefficients, 0, unroll=2)
-
-    def spread_out(u, at):
-        return (keep_ref[at, :] * u + (fx_ref[at, :] * east(u) + fw_ref[at, :] * west(u))
-                + (fn_ref[at, :] * north(u) + fs_ref[at, :] * south(u)))
-
-    for first, part in ((0, high), (half, low)):
-
-        def once(k, carry):
-            at = rows_at(k + first)
-            u1_ref[at, :] = spread_out(unstacked(part[level_at(k, width), :]), at)
-            return carry
-
-        lax.fori_loop(0, half, once, 0, unroll=2)
-
-    def twice(k, carry):
-        at = rows_at(k)
-        u2_ref[at, :] = spread_out(u1_ref[at, :], at)
-        return carry
-
-    lax.fori_loop(0, levels, twice, 0, unroll=2)
+        source, first = (high, 0) if 2 * i < parts else (low, half)
+        lax.fori_loop(i * chunk, (i + 1) * chunk, functools.partial(level, source, first), 0, unroll=2)
 
 
 def finish_body(levels, first, last, skipped, u2, links, own_near, own_far, near, far, rim_near, rim_far, rim_other_near, rim_other_far,
@@ -564,19 +596,19 @@
     half_bricks, half_links = halved(brick), halved(link_rows)
     solution, carried, ratio, low, links_high, low_near, low_far = kernel(
         functools.partial(columns_body, levels),
-        hbm(tile) + vmem(half_bricks, half_bricks, half_bricks, half_links, halved(rim), halved(rim)),
+        hbm(tile) + vmem(half_bricks, half_bricks, padded(half_bricks), half_links, halved(rim), halved(rim)),
         in_vmem(2) + in_hbm(6), in_hbm(1) + in_vmem(6), "columns",
         [scalars, tile_ints, whole, whole, ints, pltpu.VMEM(half_links, FLOAT), tiles, pltpu.VMEM(half_bricks, FLOAT),
          semaphores((16,)), semaphores((1,))],
     )(sums, basis, layer_weight, kmt, ct_tracer, kvert, land, links_left)
     low_other_near, low_other_far = exchange(low_near, low_far)
     high, high_near, high_far = kernel(
-        upper_body, vmem(half_bricks, halved(rim), halved(rim)), in_vmem(4), in_vmem(3), "upper_columns"
+        upper_body, vmem(padded(half_bricks), halved(rim), halved(rim)), in_vmem(4), in_vmem(3), "upper_columns"
     )(carried, ratio, low, links_high)
     high_other_near, high_other_far = exchange(high_near, high_far)
     u2 = kernel(
         functools.partial(inner_body, levels), vmem(flat), in_vmem(2) + in_hbm(3), in_vmem(1), "inner",
-        [tile_ints, whole, ints] + [whole] * 6 + [semaphores((9,))],
+        [tile_ints, whole, ints] + [pltpu.VMEM(padded(brick), FLOAT)] * 3 + [semaphores((9,))],
     )(high, low, kmt, kappa, land)[0]
 
     scratch = [

time: 47.1 us -> 44.4 us (0.943)
  Pallas kernels: 23.9 us -> 21.2 us
    pallas_call x1, Pallas kernels: 11 us -> 8.25 us  [body(): kernel(functools.partial(inner_body, levels), vmem(flat), in_vmem(2) + in...]
  transfers between devices with their start and end apart: 9 -> 9, of which waited for: 1 -> 1; matrix products, arithmetic and copies ran while one was open for 0% -> 0% of each run, Pallas kernels for 42% -> 38%
where the time goes in v9:
time: 44.4 us; the launch traced here: 44.1 us
  Pallas kernels  21.2 us (48%)
  starting transfers between devices  20 us (45%)
  waiting for transfers between devices  2.05 us (5%)
  between operations  0.79 us (2%)
    ppermute x8, starting transfers between devices, swap(): lax.ppermute(array, 'tile', [(i, i + 1) for i in firsts] + [(i + 1, i) fo...  14.7 us
    pallas_call x1, Pallas kernels, body(): kernel(functools.partial(inner_body, levels), vmem(flat), in_vmem(2) + in...  8.25 us
    all_to_all x1, starting transfers between devices, body(): lax.all_to_all(sums.reshape(count, 1, 128), 'tile', 0, 0, tiled=True)  5.32 us
    pallas_call x1, Pallas kernels, body(): kernel(functools.partial(columns_body, levels), hbm(tile) + vmem(half_bri...  3.99 us
    pallas_call x1, Pallas kernels, body(): kernel(functools.partial(rims_body, levels), vmem(rim, rim) + hbm(link_ro...  2.98 us
    all_to_all x1, waiting for transfers between devices, body(): lax.all_to_all(sums.reshape(count, 1, 128), 'tile', 0, 0, tiled=True)  2.02 us
    pallas_call x1, Pallas kernels, body(): kernel(functools.partial(setup_body, levels), vmem(*[tile] * 9, brick), i...  1.97 us
    pallas_call x1, Pallas kernels, body(): kernel(functools.partial(finish_body, levels, 0, half, 0), hbm(flat), in_...  1.34 us
  transfers between devices with their start and end apart: 9, of which 1 were waited for; matrix products, arithmetic and copies ran while one was open for 0% of the time, Pallas kernels for 38%

profile of v9, /device:TPU:1, one launch (start us, length us, event | category | flops | bytes accessed | tf_op | source)
XLA Modules:
  0.0 44.1 jit_solution(7029583784238720533)
XLA Ops:
  0.6 2.0 %setup.1 = (f32[8,1280]{1,0:T(8,128)S(1)}, f32[8,1280]{1,0:T(8,128)S(1)}, f32[8,1280]{1,0:T(8,128)S(1)}, f32[8,1280]{1,0:T(8,128)S(1)}, f32[8,1280]{1,0:T(8,128)...) custom-call(f32[48]{0:T(128)} %weight_hbm.3, ...), custom_call_target="tpu_custom_call" | custom-call | flops 1 | bytes 1 | tf_op jit(solution)/shard_map/setup/pallas_call | solution.py:574
  2.6 0.1 collective-permute-start
  2.7 4.5 %collective-permute-start.1 = (f32[8,1280]{1,0:T(8,128)S(1)}, f32[8,1280]{1,0:T(8,128)S(1)}, u32[]{:S(2)}, u32[]{:S(2)}) collective-permute-start(f32[8,1280]{1,0:T(8,128)S(1)} %get-tuple-element.35), channel_id=1, source_target_pairs={{1,2},{3,4},{5,6},{7,8},{9,10},{11,12},{13,14},{2,1},{4,3},{6,5},{... | collective-permute-start | bytes 122888 | tf_op jit(solution)/shard_map/ppermute | solution.py:555
  7.2 3.0 %rims.1 = (f32[96,1280]{1,0:T(8,128)S(1)}, f32[96,1280]{1,0:T(8,128)S(1)}, f32[192,1280]{1,0:T(8,128)}) custom-call(f32[384,1280]{1,0:T(8,128)} %bitcast.13, f32[3840,128]{1,0:T(8,128)S(1)} %get-tuple-element.36.wet_bricks), custom_call_target="tpu_custom_call" | custom-call | flops 1 | bytes 1 | tf_op jit(solution)/shard_map/rims/pallas_call | solution.py:580
  10.2 0.0 collective-permute-done.near
  10.2 0.0 collective-permute-done.1.far
  10.2 0.9 %basis.1 = (f32[24,1280]{1,0:T(8,128)S(1)}, f32[16,128]{1,0:T(8,128)}) custom-call(f32[8,1280]{1,0:T(8,128)S(1)} %get-tuple-element.27.ct, f32[8,1280]{1,0:T(8,128)S(1)} %get-tuple-element.28.height, f32[8,1280]{1,0:T(8,128)S(1)} %get-tuple-element.29.surface, f32[8,1280]{1,0:T(8,128)S(1)} %get-tuple-element.30.fx_ref, ...), custom_call_target="tpu_custom_call" | custom-call | flops 1 | bytes 1 | tf_op jit(solution)/shard_map/basis/pallas_call | solution.py:587
  11.2 5.3 %all-to-all-start = ((f32[16,1,128]{2,1,0:T(1,128)}), f32[16,1,128]{2,1,0:T(1,128)S(1)}, u32[]{:S(2)}, u32[]{:S(2)}) async-start(f32[16,1,128]{2,1,0:T(1,128)} %bitcast.3), calls=%async_computation | async-start | bytes 16384 | tf_op jit(solution)/shard_map/all_to_all | solution.py:591
  16.5 0.2 collective-permute-start.4
  16.6 3.5 %collective-permute-start.5 = (f32[96,1280]{1,0:T(8,128)S(1)}, f32[96,1280]{1,0:T(8,128)S(1)}, u32[]{:S(2)}, u32[]{:S(2)}) collective-permute-start(f32[96,1280]{1,0:T(8,128)S(1)} %get-tuple-element.48.rim_far), channel_id=1, source_target_pairs={{1,2},{3,4},{5,6},{7,8},{9,10},{11,12},{13,14},{2,1},{4,3},{6,5},{... | collective-permute-start | bytes 1474568 | tf_op jit(solution)/shard_map/ppermute | solution.py:555
  20.2 2.0 %all-to-all-done = f32[16,1,128]{2,1,0:T(1,128)S(1)} async-done(((f32[16,1,128]{2,1,0:T(1,128)}), f32[16,1,128]{2,1,0:T(1,128)S(1)}, u32[]{:S(2)}, u32[]{:S(2)}) %all-to-all-start) | async-done | bytes 8224 | tf_op jit(solution)/shard_map/all_to_all | solution.py:591
  22.2 4.0 %columns.1 = (f32[8,1280]{1,0:T(8,128)}, f32[1920,128]{1,0:T(8,128)S(1)}, f32[1920,128]{1,0:T(8,128)S(1)}, f32[1936,128]{1,0:T(8,128)S(1)}, f32[96,1280]{1,0:T(8...) custom-call(f32[16,128]{1,0:T(8,128)S(1)} %bitcast.9, f32[24,1280]{1,0:T(8,128)S(1)} %get-tuple-element.39.basis_ref, ...), custom_call_target="tpu_custom_call" | custom-call | flops 1 | bytes 1 | tf_op jit(solution)/shard_map/columns/pallas_call | solution.py:597
  26.2 0.8 %collective-permute-start.6 = (f32[48,1280]{1,0:T(8,128)S(1)}, f32[48,1280]{1,0:T(8,128)S(1)}, u32[]{:S(2)}, u32[]{:S(2)}) collective-permute-start(f32[48,1280]{1,0:T(8,128)S(1)} %get-tuple-element.49.own_near), channel_id=1, source_target_pairs={{0,1},{2,3},{4,5},{6,7},{8,9},{10,11},{12,13},{14,15},{1,0},{3,2},... | collective-permute-start | bytes 737288 | tf_op jit(solution)/shard_map/ppermute | solution.py:555
  27.0 2.0 %collective-permute-start.7 = (f32[48,1280]{1,0:T(8,128)S(1)}, f32[48,1280]{1,0:T(8,128)S(1)}, u32[]{:S(2)}, u32[]{:S(2)}) collective-permute-start(f32[48,1280]{1,0:T(8,128)S(1)} %get-tuple-element.50.own_far), channel_id=1, source_target_pairs={{1,2},{3,4},{5,6},{7,8},{9,10},{11,12},{13,14},{2,1},{4,3},{6,5},{... | collective-permute-start | bytes 737288 | tf_op jit(solution)/shard_map/ppermute | solution.py:555
  29.0 0.4 upper_columns.1
  29.4 0.1 collective-permute-start.2
  29.5 0.0 collective-permute-done.6.near
  29.5 3.5 %collective-permute-start.3 = (f32[48,1280]{1,0:T(8,128)S(1)}, f32[48,1280]{1,0:T(8,128)S(1)}, u32[]{:S(2)}, u32[]{:S(2)}) collective-permute-start(f32[48,1280]{1,0:T(8,128)S(1)} %get-tuple-element.46.own_far), channel_id=1, source_target_pairs={{1,2},{3,4},{5,6},{7,8},{9,10},{11,12},{13,14},{2,1},{4,3},{6,5},{... | collective-permute-start | bytes 737288 | tf_op jit(solution)/shard_map/ppermute | solution.py:555
  33.1 0.0 copy-start
  33.1 8.3 %inner.1.u2 = f32[384,1280]{1,0:T(8,128)S(1)} custom-call(f32[1936,128]{1,0:T(8,128)S(1)} %get-tuple-element.44.high, f32[1936,128]{1,0:T(8,128)S(1)} %get-tuple-element.42.low, s32[8,1280]{1,0:T(8,128)} %kmt_hbm.5, f32[384,1280]{1,0:T(8,128)} %bitcast.14, s32[384,1280]{1,0:T(8,128)} %bitcast.12), custom_call_target="tpu_custom_call" | custom-call | flops 1 | bytes 1 | tf_op jit(solution)/shard_map/inner/pallas_call | solution.py:609
  41.3 0.0 collective-permute-done.7.far
  41.3 0.0 collective-permute-done.4.rim_other_near
  41.4 0.0 collective-permute-done.5.rim_other_far
  41.4 0.0 copy-done
  41.4 1.3 %finish_low.1.refs_0_ = f32[384,1280]{1,0:T(8,128)} custom-call(f32[384,1280]{1,0:T(8,128)S(1)} %inner.1.u2, f32[192,1280]{1,0:T(8,128)S(1)} %copy-done, f32[48,1280]{1,0:T(8,128)S(1)} %get-tuple-element.49.own_near, f32[48,1280]{1,0:T(8,128)S(1)} %get-tuple-element.50.own_far, f32[48,1280]{1,0:T(8,128)S(1)} %collective-permute-done.6.near, ...), custom_call_target="tpu_custom_call" | custom-call | flops 1 | bytes 1 | tf_op jit(solution)/shard_map/finish_low/pallas_call | solution.py:617
  42.7 0.0 collective-permute-done.2.near
  42.7 0.0 collective-permute-done.3.far
  42.7 1.3 %finish_high.1 = f32[384,1280]{1,0:T(8,128)} custom-call(f32[384,1280]{1,0:T(8,128)S(1)} %inner.1.u2, f32[96,1280]{1,0:T(8,128)S(1)} %get-tuple-element.43.links, f32[48,1280]{1,0:T(8,128)S(1)} %get-tuple-element.45.own_near, f32[48,1280]{1,0:T(8,128)S(1)} %get-tuple-element.46.own_far, ...), custom_call_target="tpu_custom_call", output_to_operand_aliasing={{}: (10, {})} | custom-call | flops 1 | bytes 1 | tf_op jit(solution)/shard_map/finish_high/pallas_call | solution.py:620
Async XLA Ops:
  2.6 7.6 %collective-permute-start = (f32[8,1280]{1,0:T(8,128)S(1)}, f32[8,1280]{1,0:T(8,128)S(1)}, u32[]{:S(2)}, u32[]{:S(2)}) collective-permute-start(f32[8,1280]{1,0:T(8,128)S(1)} %get-tuple-element.34), channel_id=1, source_target_pairs={{0,1},{2,3},{4,5},{6,7},{8,9},{10,11},{12,13},{14,15},{1,0},{3,2},... | collective-permute-start | bytes 122888 | tf_op jit(solution)/shard_map/ppermute | solution.py:555
  2.7 7.5 %collective-permute-start.1 = (f32[8,1280]{1,0:T(8,128)S(1)}, f32[8,1280]{1,0:T(8,128)S(1)}, u32[]{:S(2)}, u32[]{:S(2)}) collective-permute-start(f32[8,1280]{1,0:T(8,128)S(1)} %get-tuple-element.35), channel_id=1, source_target_pairs={{1,2},{3,4},{5,6},{7,8},{9,10},{11,12},{13,14},{2,1},{4,3},{6,5},{... | collective-permute-start | bytes 122888 | tf_op jit(solution)/shard_map/ppermute | solution.py:555
  11.2 11.0 %all-to-all-start = ((f32[16,1,128]{2,1,0:T(1,128)}), f32[16,1,128]{2,1,0:T(1,128)S(1)}, u32[]{:S(2)}, u32[]{:S(2)}) async-start(f32[16,1,128]{2,1,0:T(1,128)} %bitcast.3), calls=%async_computation | async-start | bytes 16384 | tf_op jit(solution)/shard_map/all_to_all | solution.py:591
  16.5 24.9 %collective-permute-start.4 = (f32[96,1280]{1,0:T(8,128)S(1)}, f32[96,1280]{1,0:T(8,128)S(1)}, u32[]{:S(2)}, u32[]{:S(2)}) collective-permute-start(f32[96,1280]{1,0:T(8,128)S(1)} %get-tuple-element.47.rim_near), channel_id=1, source_target_pairs={{0,1},{2,3},{4,5},{6,7},{8,9},{10,11},{12,13},{14,15},{1,0},{3,2},... | collective-permute-start | bytes 1474568 | tf_op jit(solution)/shard_map/ppermute | solution.py:555
  16.6 24.7 %collective-permute-start.5 = (f32[96,1280]{1,0:T(8,128)S(1)}, f32[96,1280]{1,0:T(8,128)S(1)}, u32[]{:S(2)}, u32[]{:S(2)}) collective-permute-start(f32[96,1280]{1,0:T(8,128)S(1)} %get-tuple-element.48.rim_far), channel_id=1, source_target_pairs={{1,2},{3,4},{5,6},{7,8},{9,10},{11,12},{13,14},{2,1},{4,3},{6,5},{... | collective-permute-start | bytes 1474568 | tf_op jit(solution)/shard_map/ppermute | solution.py:555
  26.2 3.3 %collective-permute-start.6 = (f32[48,1280]{1,0:T(8,128)S(1)}, f32[48,1280]{1,0:T(8,128)S(1)}, u32[]{:S(2)}, u32[]{:S(2)}) collective-permute-start(f32[48,1280]{1,0:T(8,128)S(1)} %get-tuple-element.49.own_near), channel_id=1, source_target_pairs={{0,1},{2,3},{4,5},{6,7},{8,9},{10,11},{12,13},{14,15},{1,0},{3,2},... | collective-permute-start | bytes 737288 | tf_op jit(solution)/shard_map/ppermute | solution.py:555
  27.0 14.4 %collective-permute-start.7 = (f32[48,1280]{1,0:T(8,128)S(1)}, f32[48,1280]{1,0:T(8,128)S(1)}, u32[]{:S(2)}, u32[]{:S(2)}) collective-permute-start(f32[48,1280]{1,0:T(8,128)S(1)} %get-tuple-element.50.own_far), channel_id=1, source_target_pairs={{1,2},{3,4},{5,6},{7,8},{9,10},{11,12},{13,14},{2,1},{4,3},{6,5},{... | collective-permute-start | bytes 737288 | tf_op jit(solution)/shard_map/ppermute | solution.py:555
  29.4 13.3 %collective-permute-start.2 = (f32[48,1280]{1,0:T(8,128)S(1)}, f32[48,1280]{1,0:T(8,128)S(1)}, u32[]{:S(2)}, u32[]{:S(2)}) collective-permute-start(f32[48,1280]{1,0:T(8,128)S(1)} %get-tuple-element.45.own_near), channel_id=1, source_target_pairs={{0,1},{2,3},{4,5},{6,7},{8,9},{10,11},{12,13},{14,15},{1,0},{3,2},... | collective-permute-start | bytes 737288 | tf_op jit(solution)/shard_map/ppermute | solution.py:555
  29.5 13.2 %collective-permute-start.3 = (f32[48,1280]{1,0:T(8,128)S(1)}, f32[48,1280]{1,0:T(8,128)S(1)}, u32[]{:S(2)}, u32[]{:S(2)}) collective-permute-start(f32[48,1280]{1,0:T(8,128)S(1)} %get-tuple-element.46.own_far), channel_id=1, source_target_pairs={{1,2},{3,4},{5,6},{7,8},{9,10},{11,12},{13,14},{2,1},{4,3},{6,5},{... | collective-permute-start | bytes 737288 | tf_op jit(solution)/shard_map/ppermute | solution.py:555
  33.1 8.3 %copy-start = (f32[192,1280]{1,0:T(8,128)S(1)}, f32[192,1280]{1,0:T(8,128)}, u32[]{:S(2)}) copy-start(f32[192,1280]{1,0:T(8,128)} %get-tuple-element.37.links_hbm.links) | copy-start | bytes 2949124

commit v10 on v8

--- a/solution.py
+++ b/solution.py
@@ -15,6 +15,8 @@
 HALF = 0.5 * (HIGH - LOW)
 FLOAT = jnp.float32
 LINKS = 4
+GROUP = 4
+UPPER = 8
 LIMIT = 24 * 1024 * 1024
 
 
@@ -338,20 +340,24 @@
             near_ref[at, :], far_ref[at, :] = dealt(even, found[0][place], found[1][place])
 
 
-def columns_body(levels, sums, basis_ref, weight_hbm, kmt_hbm, source_hbm, kvert_hbm, land_hbm, links_hbm,
+def segments(start, stop):
+    cuts = [start] + ([UPPER] if start < UPPER < stop else []) + [stop]
+    return [(a, b, b <= UPPER) for a, b in zip(cuts[:-1], cuts[1:])]
+
+
+def columns_body(levels, sums, sums_near, basis_ref, weight_hbm, kmt_hbm, source_hbm, kvert_hbm, land_hbm, links_hbm,
                  out_hbm, high, ratio, low, links_high, near_ref, far_ref,
                  weight, kmt, source, kvert, land, links_low, s_ref, ratio_low, sems, out_sems):
     width = source.shape[1]
     parts = 4
     chunk = levels // parts
-    half = levels // 2
     small = loads(((weight_hbm, weight), (kmt_hbm, kmt)), sems)
     parted = [in_parts(far, near, parts) for far, near in ((land_hbm, land), (kvert_hbm, kvert), (source_hbm, source))]
     big = loads([pairs[i] for i in range(parts) for pairs in parted], sems, 2)
-    top, bottom = (pl.ds(i * half * LINKS, half * LINKS) for i in range(2))
+    top, bottom = pl.ds(0, UPPER * LINKS), pl.ds(UPPER * LINKS, (levels - UPPER) * LINKS)
     links_copies = loads([(links_hbm.at[bottom], links_low), (links_hbm.at[top], links_high)], sems, 2 + 3 * parts)
 
-    total = jnp.sum(sums[...], axis=0, keepdims=True)
+    total = jnp.sum(sums[...], axis=0, keepdims=True) + jnp.sum(sums_near[...], axis=0, keepdims=True)
     mix = weights([total[:, i : i + 1] for i in range(6)])
     b0, b1, b2 = (basis_ref[i * ROWS : (i + 1) * ROWS, :] for i in range(3))
     s = mix[0] * b0 + mix[1] * b1 + mix[2] * b2
@@ -386,8 +392,9 @@
         big[3 * i + 2].wait()
         if i + 1 < parts:
             big[3 * i + 3].wait()
-        step = functools.partial(down, high, ratio, 0) if 2 * i < parts else functools.partial(down, low, ratio_low, half)
-        carry = lax.fori_loop(i * chunk, (i + 1) * chunk, step, carry, unroll=4)
+        for start, stop, is_high in segments(i * chunk, (i + 1) * chunk):
+            target = (high, ratio, 0) if is_high else (low, ratio_low, UPPER)
+            carry = lax.fori_loop(start, stop, functools.partial(down, *target), carry, unroll=4)
     ascend(low, low, ratio_low, zero, width)
     for copy in links_copies:
         copy.wait()
@@ -414,10 +421,8 @@
     send_rows(u, links, near_ref, far_ref, width)
 
 
-def inner_body(levels, high, low, kmt_hbm, kappa_hbm, land_hbm, u2_ref,
-               kmt, kappa, land, fx_ref, fw_ref, fn_ref, fs_ref, keep_ref, u1_ref, sems):
+def inner_body(levels, high, low, kmt_hbm, kappa_hbm, land_hbm, u2_ref, kmt, kappa, land, sems):
     parts = 4
-    half = levels // 2
     kmt_copy = loads([(kmt_hbm, kmt)], sems)[0]
     pairs = ((kappa_hbm, kappa), (land_hbm, land))
     parted = [in_parts(far, near, parts) for far, near in pairs]
@@ -430,43 +435,28 @@
     def face(here, there):
         return jnp.where(jnp.minimum(here, there) > 0.0, here + there, 0.0)
 
-    def coefficients(k, carry):
-        at = rows_at(k)
-        sea = jnp.where(k < depth, land[at, :], 0) > 0
-        halved = jnp.where(sea, 0.5 * kappa[at, :], 0.0)
-        fx = face(halved, east(halved))
-        fn = jnp.where(inside, face(halved, north(halved)), 0.0)
-        fw, fs = west(fx), south(fn)
-        for ref, values in ((fx_ref, fx), (fw_ref, fw), (fn_ref, fn), (fs_ref, fs)):
-            ref[at, :] = values
-        keep_ref[at, :] = 1.0 - (fx + fw) - (fn + fs)
+    def group(source, first, i, carry):
+        ks = [GROUP * i + j for j in range(GROUP)]
+        sea = [jnp.where(k < depth, land[rows_at(k), :], 0) > 0 for k in ks]
+        halved = [jnp.where(wet, 0.5 * kappa[rows_at(k), :], 0.0) for wet, k in zip(sea, ks)]
+        u = [unstacked(source[level_at(k - first, width), :]) for k in ks]
+        fx = [face(v, east(v)) for v in halved]
+        fn = [jnp.where(inside, face(v, north(v)), 0.0) for v in halved]
+        for _ in range(2):
+            flux_x = [f * (east(v) - v) for f, v in zip(fx, u)]
+            flux_y = [f * (north(v) - v) for f, v in zip(fn, u)]
+            u = [v + (x - west(x)) + (y - south(y)) for v, x, y in zip(u, flux_x, flux_y)]
+        for k, v in zip(ks, u):
+            u2_ref[rows_at(k), :] = v
         return carry
 
     chunk = levels // parts
     for i in range(parts):
         for copy in copies[2 * i : 2 * i + 2]:
             copy.wait()
-        lax.fori_loop(i * chunk, (i + 1) * chunk, coefficients, 0, unroll=2)
-
-    def spread_out(u, at):
-        return (keep_ref[at, :] * u + (fx_ref[at, :] * east(u) + fw_ref[at, :] * west(u))
-                + (fn_ref[at, :] * north(u) + fs_ref[at, :] * south(u)))
-
-    for first, part in ((0, high), (half, low)):
-
-        def once(k, carry):
-            at = rows_at(k + first)
-            u1_ref[at, :] = spread_out(unstacked(part[level_at(k, width), :]), at)
-            return carry
-
-        lax.fori_loop(0, half, once, 0, unroll=2)
-
-    def twice(k, carry):
-        at = rows_at(k)
-        u2_ref[at, :] = spread_out(u1_ref[at, :], at)
-        return carry
-
-    lax.fori_loop(0, levels, twice, 0, unroll=2)
+        for start, stop, is_high in segments(i * chunk, (i + 1) * chunk):
+            step = functools.partial(group, *((high, 0) if is_high else (low, UPPER)))
+            lax.fori_loop(start // GROUP, stop // GROUP, step, 0)
 
 
 def finish_body(levels, first, last, skipped, u2, links, own_near, own_far, near, far, rim_near, rim_far, rim_other_near, rim_other_far,
@@ -515,13 +505,12 @@
         copy.wait()
 
 
+def swap(array, start):
+    firsts = range(start, lax.axis_size("tile") - 1, 2)
+    return lax.ppermute(array, "tile", [(i, i + 1) for i in firsts] + [(i + 1, i) for i in firsts])
+
+
 def exchange(to_near, to_far):
-    count = lax.axis_size("tile")
-
-    def swap(array, start):
-        firsts = range(start, count - 1, 2)
-        return lax.ppermute(array, "tile", [(i, i + 1) for i in firsts] + [(i + 1, i) for i in firsts])
-
     from_far = swap(to_far, 1)
     return swap(to_near, 0), from_far
 
@@ -553,42 +542,53 @@
     rim_other_near, rim_other_far = exchange(rim_near, rim_far)
 
     basis, sums = kernel(
-        basis_body, vmem((3 * rows, width), (count, 128)), in_vmem(9) + in_hbm(1),
+        basis_body, vmem((3 * rows, width), (count // 2, 128)), in_vmem(9) + in_hbm(1),
         in_vmem(2), "basis"
     )(base, height, surface, s_fx, s_fn, s_dg, q1, near, far, links_left)
-    sums = lax.all_to_all(sums.reshape(count, 1, 128), "tile", 0, 0, tiled=True).reshape(count, 128)
+    share = count // 2
+    every_other = [[2 * i + core for i in range(share)] for core in range(2)]
+    sums = lax.all_to_all(sums.reshape(share, 1, 128), "tile", 0, 0, axis_index_groups=every_other, tiled=True)
+    sums = sums.reshape(share, 128)
+    sums_near = swap(sums, 0)
 
     rims = (rim_near, rim_far, rim_other_near, rim_other_far)
-    half = levels // 2
-    halved = lambda shape: (shape[0] // 2, shape[1])
-    half_bricks, half_links = halved(brick), halved(link_rows)
+    lower = levels - UPPER
+    per_level = brick[0] // levels
+    high_bricks, low_bricks = (UPPER * per_level, 128), (lower * per_level, 128)
+    high_links, low_links = (UPPER * LINKS, width), (lower * LINKS, width)
+    high_rim, low_rim = (2 * UPPER, width), (2 * lower, width)
     solution, carried, ratio, low, links_high, low_near, low_far = kernel(
         functools.partial(columns_body, levels),
-        hbm(tile) + vmem(half_bricks, half_bricks, half_bricks, half_links, halved(rim), halved(rim)),
-        in_vmem(2) + in_hbm(6), in_hbm(1) + in_vmem(6), "columns",
-        [scalars, tile_ints, whole, whole, ints, pltpu.VMEM(half_links, FLOAT), tiles, pltpu.VMEM(half_bricks, FLOAT),
+        hbm(tile) + vmem(high_bricks, high_bricks, low_bricks, high_links, low_rim, low_rim),
+        in_vmem(3) + in_hbm(6), in_hbm(1) + in_vmem(6), "columns",
+        [scalars, tile_ints, whole, whole, ints, pltpu.VMEM(low_links, FLOAT), tiles, pltpu.VMEM(low_bricks, FLOAT),
          semaphores((16,)), semaphores((1,))],
-    )(sums, basis, layer_weight, kmt, ct_tracer, kvert, land, links_left)
+    )(sums, sums_near, basis, layer_weight, kmt, ct_tracer, kvert, land, links_left)
     low_other_near, low_other_far = exchange(low_near, low_far)
     high, high_near, high_far = kernel(
-        upper_body, vmem(half_bricks, halved(rim), halved(rim)), in_vmem(4), in_vmem(3), "upper_columns"
+        upper_body, vmem(high_bricks, high_rim, high_rim), in_vmem(4), in_vmem(3), "upper_columns"
     )(carried, ratio, low, links_high)
     high_other_near, high_other_far = exchange(high_near, high_far)
     u2 = kernel(
         functools.partial(inner_body, levels), vmem(flat), in_vmem(2) + in_hbm(3), in_vmem(1), "inner",
-        [tile_ints, whole, ints] + [whole] * 6 + [semaphores((9,))],
+        [tile_ints, whole, ints, semaphores((9,))],
     )(high, low, kmt, kappa, land)[0]
 
-    scratch = [
-        pltpu.VMEM((8 * rows * width // 128, 128), FLOAT), pltpu.VMEM(halved(flat), FLOAT), semaphores((half // 8,))
-    ]
-    deep = kernel(
-        functools.partial(finish_body, levels, half, levels, half // 8), hbm(flat), in_vmem(10), in_hbm(1), "finish_low", scratch,
-    )(u2, held(links), low_near, low_far, low_other_near, low_other_far, *rims)[0]
-    values = kernel(
-        functools.partial(finish_body, levels, 0, half, 0), hbm(flat), in_vmem(10) + in_hbm(1), in_hbm(1), "finish_high",
-        scratch, aliases={10: 0},
-    )(u2, links_high, high_near, high_far, high_other_near, high_other_far, *rims, left(deep))[0]
+    def finish(first, last, skipped, name, more=(), aliases={}):
+        count = last - first
+        return kernel(
+            functools.partial(finish_body, levels, first, last, skipped), hbm(flat), in_vmem(10) + in_hbm(len(more)),
+            in_hbm(1), name,
+            [pltpu.VMEM((8 * per_level, 128), FLOAT), pltpu.VMEM((count * rows, width), FLOAT), semaphores((count // 8,))],
+            aliases=aliases,
+        )
+
+    deep = finish(UPPER, levels, UPPER // 8, "finish_low")(
+        u2, held(links), low_near, low_far, low_other_near, low_other_far, *rims
+    )[0]
+    values = finish(0, UPPER, 0, "finish_high", (deep,), {10: 0})(
+        u2, links_high, high_near, high_far, high_other_near, high_other_far, *rims, left(deep)
+    )[0]
     return (values.reshape(levels, rows, width), solution)
 
 

time: 47.1 us -> 48.3 us (1.025)
  blocking collectives: 0 us -> 9.78 us
  Pallas kernels: 23.9 us -> 18.5 us
  starting transfers between devices: 20 us -> 15.5 us
  waiting for transfers between devices: 2.05 us -> 3.41 us
    all_to_all x0 -> x1, blocking collectives: none -> 9.78 us  [body(): lax.all_to_all(sums.reshape(share, 1, 128), 'tile', 0, 0, axis_index_grou...]
    all_to_all x1 -> x0, starting transfers between devices: 5.32 us -> none  [body(): lax.all_to_all(sums.reshape(count, 1, 128), 'tile', 0, 0, tiled=True)]
    pallas_call x1, Pallas kernels: 11 us -> 5.98 us  [body(): kernel(functools.partial(inner_body, levels), vmem(flat), in_vmem(2) + in...]
    ppermute x8 -> x9, waiting for transfers between devices: 0.02 us -> 3.41 us  [swap(): lax.ppermute(array, 'tile', [(i, i + 1) for i in firsts] + [(i + 1, i) fo...]
    all_to_all x1 -> x0, waiting for transfers between devices: 2.02 us -> none  [body(): lax.all_to_all(sums.reshape(count, 1, 128), 'tile', 0, 0, tiled=True)]
    ppermute x8 -> x9, starting transfers between devices: 14.7 us -> 15.5 us  [swap(): lax.ppermute(array, 'tile', [(i, i + 1) for i in firsts] + [(i + 1, i) fo...]
  transfers between devices with their start and end apart: 9 -> 9, of which waited for: 1 -> 1; matrix products, arithmetic and copies ran while one was open for 0% -> 0% of each run, Pallas kernels for 42% -> 32%
where the time goes in v10:
time: 48.3 us; the launch traced here: 48 us
  Pallas kernels  18.5 us (38%)
  starting transfers between devices  15.5 us (32%)
  blocking collectives  9.78 us (20%)
  waiting for transfers between devices  3.41 us (7%)
  between operations  0.79 us (2%)
    ppermute x9, starting transfers between devices, swap(): lax.ppermute(array, 'tile', [(i, i + 1) for i in firsts] + [(i + 1, i) fo...  15.5 us
    all_to_all x1, blocking collectives, body(): lax.all_to_all(sums.reshape(share, 1, 128), 'tile', 0, 0, axis_index_grou...  9.78 us
    pallas_call x1, Pallas kernels, body(): kernel(functools.partial(inner_body, levels), vmem(flat), in_vmem(2) + in...  5.98 us
    pallas_call x1, Pallas kernels, body(): kernel(functools.partial(columns_body, levels), hbm(tile) + vmem(high_bri...  4.41 us
    ppermute x9, waiting for transfers between devices, swap(): lax.ppermute(array, 'tile', [(i, i + 1) for i in firsts] + [(i + 1, i) fo...  3.41 us
    pallas_call x1, Pallas kernels, body(): kernel(functools.partial(rims_body, levels), vmem(rim, rim) + hbm(link_ro...  2.98 us
    pallas_call x1, Pallas kernels, body(): kernel(functools.partial(setup_body, levels), vmem(*[tile] * 9, brick), i...  1.97 us
    pallas_call x1, Pallas kernels, body(): finish(UPPER, levels, UPPER // 8, 'finish_low')  1.65 us
  transfers between devices with their start and end apart: 9, of which 1 were waited for; matrix products, arithmetic and copies ran while one was open for 0% of the time, Pallas kernels for 32%

profile of v10, /device:TPU:1, one launch (start us, length us, event | category | flops | bytes accessed | tf_op | source)
XLA Modules:
  0.0 48.0 jit_solution(3846512951277856340)
XLA Ops:
  0.6 2.0 %setup.1 = (f32[8,1280]{1,0:T(8,128)S(1)}, f32[8,1280]{1,0:T(8,128)S(1)}, f32[8,1280]{1,0:T(8,128)S(1)}, f32[8,1280]{1,0:T(8,128)S(1)}, f32[8,1280]{1,0:T(8,128)...) custom-call(f32[48]{0:T(128)} %weight_hbm.3, ...), custom_call_target="tpu_custom_call" | custom-call | flops 1 | bytes 1 | tf_op jit(solution)/shard_map/setup/pallas_call | solution.py:531
  2.6 0.1 collective-permute-start
  2.7 4.5 %collective-permute-start.1 = (f32[8,1280]{1,0:T(8,128)S(1)}, f32[8,1280]{1,0:T(8,128)S(1)}, u32[]{:S(2)}, u32[]{:S(2)}) collective-permute-start(f32[8,1280]{1,0:T(8,128)S(1)} %get-tuple-element.35), channel_id=1, source_target_pairs={{1,2},{3,4},{5,6},{7,8},{9,10},{11,12},{13,14},{2,1},{4,3},{6,5},{... | collective-permute-start | bytes 122888 | tf_op jit(solution)/shard_map/ppermute | solution.py:510
  7.2 3.0 %rims.1 = (f32[96,1280]{1,0:T(8,128)S(1)}, f32[96,1280]{1,0:T(8,128)S(1)}, f32[192,1280]{1,0:T(8,128)}) custom-call(f32[384,1280]{1,0:T(8,128)} %bitcast.15, f32[3840,128]{1,0:T(8,128)S(1)} %get-tuple-element.36.wet_bricks), custom_call_target="tpu_custom_call" | custom-call | flops 1 | bytes 1 | tf_op jit(solution)/shard_map/rims/pallas_call | solution.py:537
  10.2 0.0 collective-permute-done.near
  10.2 0.0 collective-permute-done.1.far
  10.2 0.3 basis.1
  10.6 9.8 %all_to_all.5 = f32[8,1,128]{2,1,0:T(1,128)S(1)} all-to-all(f32[8,1,128]{2,1,0:T(1,128)S(1)} %bitcast.11), channel_id=1, replica_groups={{0,2,4,6,8,10,12,14},{1,3,5,7,9,11,13,15},{16,18,20,22,24,26,28,30},{17..., dimensions={0} | all-to-all | bytes 8192 | tf_op jit(solution)/shard_map/all_to_all | solution.py:550
  20.3 1.8 %collective-permute-start.2 = (f32[8,128]{1,0:T(8,128)S(1)}, f32[8,128]{1,0:T(8,128)S(1)}, u32[]{:S(2)}, u32[]{:S(2)}) collective-permute-start(f32[8,128]{1,0:T(8,128)S(1)} %bitcast.9), channel_id=1, source_target_pairs={{0,1},{2,3},{4,5},{6,7},{8,9},{10,11},{12,13},{14,15},{1,0},{3,2},... | collective-permute-start | bytes 12296 | tf_op jit(solution)/shard_map/ppermute | solution.py:510
  22.1 0.0 collective-permute-start.5
  22.1 2.6 %collective-permute-start.6 = (f32[96,1280]{1,0:T(8,128)S(1)}, f32[96,1280]{1,0:T(8,128)S(1)}, u32[]{:S(2)}, u32[]{:S(2)}) collective-permute-start(f32[96,1280]{1,0:T(8,128)S(1)} %get-tuple-element.48.rim_far), channel_id=1, source_target_pairs={{1,2},{3,4},{5,6},{7,8},{9,10},{11,12},{13,14},{2,1},{4,3},{6,5},{... | collective-permute-start | bytes 1474568 | tf_op jit(solution)/shard_map/ppermute | solution.py:510
  24.7 0.0 collective-permute-done.2.sums_near
  24.7 4.4 %columns.1 = (f32[8,1280]{1,0:T(8,128)}, f32[640,128]{1,0:T(8,128)S(1)}, f32[640,128]{1,0:T(8,128)S(1)}, f32[3200,128]{1,0:T(8,128)S(1)}, f32[32,1280]{1,0:T(8,1...) custom-call(f32[8,128]{1,0:T(8,128)S(1)} %bitcast.10, f32[8,128]{1,0:T(8,128)S(1)} %collective-permute-done.2.sums_near, ...), custom_call_target="tpu_custom_call" | custom-call | flops 1 | bytes 1 | tf_op jit(solution)/shard_map/columns/pallas_call | solution.py:560
  29.1 0.1 collective-permute-start.7
  29.2 3.5 %collective-permute-start.8 = (f32[80,1280]{1,0:T(8,128)S(1)}, f32[80,1280]{1,0:T(8,128)S(1)}, u32[]{:S(2)}, u32[]{:S(2)}) collective-permute-start(f32[80,1280]{1,0:T(8,128)S(1)} %get-tuple-element.50.own_far), channel_id=1, source_target_pairs={{1,2},{3,4},{5,6},{7,8},{9,10},{11,12},{13,14},{2,1},{4,3},{6,5},{... | collective-permute-start | bytes 1228808 | tf_op jit(solution)/shard_map/ppermute | solution.py:510
  32.6 0.2 upper_columns.1
  32.9 0.1 collective-permute-start.3
  33.0 0.0 collective-permute-done.7.near
  33.0 3.0 %collective-permute-start.4 = (f32[16,1280]{1,0:T(8,128)S(1)}, f32[16,1280]{1,0:T(8,128)S(1)}, u32[]{:S(2)}, u32[]{:S(2)}) collective-permute-start(f32[16,1280]{1,0:T(8,128)S(1)} %get-tuple-element.46.own_far), channel_id=1, source_target_pairs={{1,2},{3,4},{5,6},{7,8},{9,10},{11,12},{13,14},{2,1},{4,3},{6,5},{... | collective-permute-start | bytes 245768 | tf_op jit(solution)/shard_map/ppermute | solution.py:510
  36.0 0.0 copy-start
  36.0 6.0 %inner.1.u2 = f32[384,1280]{1,0:T(8,128)S(1)} custom-call(f32[640,128]{1,0:T(8,128)S(1)} %get-tuple-element.44.high, f32[3200,128]{1,0:T(8,128)S(1)} %get-tuple-element.42.low, s32[8,1280]{1,0:T(8,128)} %kmt_hbm.5, f32[384,1280]{1,0:T(8,128)} %bitcast.16, s32[384,1280]{1,0:T(8,128)} %bitcast.14), custom_call_target="tpu_custom_call" | custom-call | flops 1 | bytes 1 | tf_op jit(solution)/shard_map/inner/pallas_call | solution.py:572
  42.0 3.4 %collective-permute-done.8.far = f32[80,1280]{1,0:T(8,128)S(1)} collective-permute-done((f32[80,1280]{1,0:T(8,128)S(1)}, f32[80,1280]{1,0:T(8,128)S(1)}, u32[]{:S(2)}, u32[]{:S(2)}) %collective-permute-start.8) | collective-permute-done | bytes 409632 | tf_op jit(solution)/shard_map/ppermute | solution.py:510
  45.4 0.0 collective-permute-done.5.rim_other_near
  45.4 0.0 collective-permute-done.6.rim_other_far
  45.4 0.0 copy-done
  45.4 1.7 %finish_low.1.refs_0_ = f32[384,1280]{1,0:T(8,128)} custom-call(f32[384,1280]{1,0:T(8,128)S(1)} %inner.1.u2, f32[192,1280]{1,0:T(8,128)S(1)} %copy-done, f32[80,1280]{1,0:T(8,128)S(1)} %get-tuple-element.49.own_near, f32[80,1280]{1,0:T(8,128)S(1)} %get-tuple-element.50.own_far, f32[80,1280]{1,0:T(8,128)S(1)} %collective-permute-done.7.near, ...), custom_call_target="tpu_custom_call" | custom-call | flops 1 | bytes 1 | tf_op jit(solution)/shard_map/finish_low/pallas_call | solution.py:586
  47.0 0.0 collective-permute-done.3.near
  47.0 0.0 collective-permute-done.4.far
  47.1 1.0 %finish_high.1 = f32[384,1280]{1,0:T(8,128)} custom-call(f32[384,1280]{1,0:T(8,128)S(1)} %inner.1.u2, f32[32,1280]{1,0:T(8,128)S(1)} %get-tuple-element.43.links, f32[16,1280]{1,0:T(8,128)S(1)} %get-tuple-element.45.own_near, f32[16,1280]{1,0:T(8,128)S(1)} %get-tuple-element.46.own_far, ...), custom_call_target="tpu_custom_call", output_to_operand_aliasing={{}: (10, {})} | custom-call | flops 1 | bytes 1 | tf_op jit(solution)/shard_map/finish_high/pallas_call | solution.py:589
Async XLA Ops:
  2.6 7.6 %collective-permute-start = (f32[8,1280]{1,0:T(8,128)S(1)}, f32[8,1280]{1,0:T(8,128)S(1)}, u32[]{:S(2)}, u32[]{:S(2)}) collective-permute-start(f32[8,1280]{1,0:T(8,128)S(1)} %get-tuple-element.34), channel_id=1, source_target_pairs={{0,1},{2,3},{4,5},{6,7},{8,9},{10,11},{12,13},{14,15},{1,0},{3,2},... | collective-permute-start | bytes 122888 | tf_op jit(solution)/shard_map/ppermute | solution.py:510
  2.7 7.5 %collective-permute-start.1 = (f32[8,1280]{1,0:T(8,128)S(1)}, f32[8,1280]{1,0:T(8,128)S(1)}, u32[]{:S(2)}, u32[]{:S(2)}) collective-permute-start(f32[8,1280]{1,0:T(8,128)S(1)} %get-tuple-element.35), channel_id=1, source_target_pairs={{1,2},{3,4},{5,6},{7,8},{9,10},{11,12},{13,14},{2,1},{4,3},{6,5},{... | collective-permute-start | bytes 122888 | tf_op jit(solution)/shard_map/ppermute | solution.py:510
  20.3 4.4 %collective-permute-start.2 = (f32[8,128]{1,0:T(8,128)S(1)}, f32[8,128]{1,0:T(8,128)S(1)}, u32[]{:S(2)}, u32[]{:S(2)}) collective-permute-start(f32[8,128]{1,0:T(8,128)S(1)} %bitcast.9), channel_id=1, source_target_pairs={{0,1},{2,3},{4,5},{6,7},{8,9},{10,11},{12,13},{14,15},{1,0},{3,2},... | collective-permute-start | bytes 12296 | tf_op jit(solution)/shard_map/ppermute | solution.py:510
  22.1 23.3 %collective-permute-start.5 = (f32[96,1280]{1,0:T(8,128)S(1)}, f32[96,1280]{1,0:T(8,128)S(1)}, u32[]{:S(2)}, u32[]{:S(2)}) collective-permute-start(f32[96,1280]{1,0:T(8,128)S(1)} %get-tuple-element.47.rim_near), channel_id=1, source_target_pairs={{0,1},{2,3},{4,5},{6,7},{8,9},{10,11},{12,13},{14,15},{1,0},{3,2},... | collective-permute-start | bytes 1474568 | tf_op jit(solution)/shard_map/ppermute | solution.py:510
  22.1 23.2 %collective-permute-start.6 = (f32[96,1280]{1,0:T(8,128)S(1)}, f32[96,1280]{1,0:T(8,128)S(1)}, u32[]{:S(2)}, u32[]{:S(2)}) collective-permute-start(f32[96,1280]{1,0:T(8,128)S(1)} %get-tuple-element.48.rim_far), channel_id=1, source_target_pairs={{1,2},{3,4},{5,6},{7,8},{9,10},{11,12},{13,14},{2,1},{4,3},{6,5},{... | collective-permute-start | bytes 1474568 | tf_op jit(solution)/shard_map/ppermute | solution.py:510
  29.1 3.9 %collective-permute-start.7 = (f32[80,1280]{1,0:T(8,128)S(1)}, f32[80,1280]{1,0:T(8,128)S(1)}, u32[]{:S(2)}, u32[]{:S(2)}) collective-permute-start(f32[80,1280]{1,0:T(8,128)S(1)} %get-tuple-element.49.own_near), channel_id=1, source_target_pairs={{0,1},{2,3},{4,5},{6,7},{8,9},{10,11},{12,13},{14,15},{1,0},{3,2},... | collective-permute-start | bytes 1228808 | tf_op jit(solution)/shard_map/ppermute | solution.py:510
  29.2 16.2 %collective-permute-start.8 = (f32[80,1280]{1,0:T(8,128)S(1)}, f32[80,1280]{1,0:T(8,128)S(1)}, u32[]{:S(2)}, u32[]{:S(2)}) collective-permute-start(f32[80,1280]{1,0:T(8,128)S(1)} %get-tuple-element.50.own_far), channel_id=1, source_target_pairs={{1,2},{3,4},{5,6},{7,8},{9,10},{11,12},{13,14},{2,1},{4,3},{6,5},{... | collective-permute-start | bytes 1228808 | tf_op jit(solution)/shard_map/ppermute | solution.py:510
  32.9 14.2 %collective-permute-start.3 = (f32[16,1280]{1,0:T(8,128)S(1)}, f32[16,1280]{1,0:T(8,128)S(1)}, u32[]{:S(2)}, u32[]{:S(2)}) collective-permute-start(f32[16,1280]{1,0:T(8,128)S(1)} %get-tuple-element.45.own_near), channel_id=1, source_target_pairs={{0,1},{2,3},{4,5},{6,7},{8,9},{10,11},{12,13},{14,15},{1,0},{3,2},... | collective-permute-start | bytes 245768 | tf_op jit(solution)/shard_map/ppermute | solution.py:510
  33.0 14.1 %collective-permute-start.4 = (f32[16,1280]{1,0:T(8,128)S(1)}, f32[16,1280]{1,0:T(8,128)S(1)}, u32[]{:S(2)}, u32[]{:S(2)}) collective-permute-start(f32[16,1280]{1,0:T(8,128)S(1)} %get-tuple-element.46.own_far), channel_id=1, source_target_pairs={{1,2},{3,4},{5,6},{7,8},{9,10},{11,12},{13,14},{2,1},{4,3},{6,5},{... | collective-permute-start | bytes 245768 | tf_op jit(solution)/shard_map/ppermute | solution.py:510
  36.0 9.4 %copy-start = (f32[192,1280]{1,0:T(8,128)S(1)}, f32[192,1280]{1,0:T(8,128)}, u32[]{:S(2)}) copy-start(f32[192,1280]{1,0:T(8,128)} %get-tuple-element.37.links_hbm.links) | copy-start | bytes 2949124

commit v11 on v7

--- a/solution.py
+++ b/solution.py
@@ -15,6 +15,9 @@
 HALF = 0.5 * (HIGH - LOW)
 FLOAT = jnp.float32
 LINKS = 4
+GROUP = 4
+PART = 8
+BEFORE_SWAP = 16
 LIMIT = 24 * 1024 * 1024
 
 
@@ -105,6 +108,10 @@
 
 def is_even():
     return lax.rem(lax.axis_index("tile"), 2) == 0
+
+
+def is_first():
+    return lax.rem(lax.axis_index("grp"), 2) == 0
 
 
 def dealt(even, low, high):
@@ -185,7 +192,7 @@
         near_ref[at, :], far_ref[at, :] = dealt(even, values[0:1, :], values[ROWS - 1 : ROWS, :])
 
 
-def rims_body(levels, kappa_hbm, wet_bricks, near_ref, far_ref, links_hbm, kappa, kappa_bricks, links, sems):
+def rims_body(levels, kappa_hbm, wet_bricks, near_ref, far_ref, sent_ref, links_hbm, kappa, kappa_bricks, links, sems):
     chunk = levels // 4
     width = kappa.shape[1]
     for i, copy in enumerate(loads(in_parts(kappa_hbm, kappa, 4), sems)):
@@ -197,6 +204,7 @@
 
         lax.fori_loop(i * chunk, (i + 1) * chunk, brick, 0, unroll=4)
     even = is_even()
+    first_group = is_first()
     outs = []
     for block in range(levels // 8):
         found = []
@@ -210,13 +218,15 @@
         for place in range(2):
             at = pl.ds(place * levels + block * 8, 8)
             near_ref[at, :], far_ref[at, :] = dealt(even, found[0][place], found[1][place])
+        at, below = pl.ds(block * 8, 8), pl.ds(levels + block * 8, 8)
+        sent_ref[at, :] = jnp.where(first_group, far_ref[at, :], far_ref[below, :])
         whole = pl.ds(block * LINKS * 8, LINKS * 8)
         outs += loads([(links.at[whole], links_hbm.at[whole])], sems, 4 + block)
     for copy in outs:
         copy.wait()
 
 
-def basis_body(count, ct, height, surface, fx_ref, fn_ref, dg_ref, q1_ref, near, far, links_hbm, basis_ref, sums_ref):
+def basis_body(ct, height, surface, fx_ref, fn_ref, dg_ref, q1_ref, near, far, links_hbm, basis_ref, sums_ref):
     even = is_even()
     b0 = ct[...]
     rows = row_index(b0)
@@ -259,16 +269,16 @@
     b2_b = outer(sides[0], b1[0:1, :])
     b2_a = outer(sides[1], b1[ROWS - 1 : ROWS, :])
     next2 = apply(b2, b2_b, b2_a)
-    tile_rows = lax.broadcasted_iota(jnp.int32, (8, 128), 0)
-    packed = jnp.zeros((8, 128), FLOAT)
+    lanes = lax.broadcasted_iota(jnp.int32, (1, 128), 1)
+    packed = jnp.zeros((1, 128), FLOAT)
     for place, (p, q) in enumerate(((b0, b0), (b0, b1), (b1, b1), (b1, b2), (b2, b2), (b2, next2))):
         product = p * q
         folded = product[:, 0:128]
         for j in range(1, product.shape[1] // 128):
             folded = folded + product[:, j * 128 : (j + 1) * 128]
-        packed = jnp.where(tile_rows == place, jnp.sum(folded, axis=0, keepdims=True), packed)
-    for j in range(count):
-        sums_ref[j * 8 : (j + 1) * 8, :] = packed
+        total = jnp.sum(jnp.sum(folded, axis=0, keepdims=True), axis=1, keepdims=True)
+        packed = jnp.where(lanes == place, total, packed)
+    sums_ref[...] = jnp.broadcast_to(packed, sums_ref.shape)
 
 
 def quadratic(left, form):
@@ -322,7 +332,7 @@
     return guess * (2.0 - values * guess)
 
 
-def columns_body(levels, count, sums, basis_ref, weight_hbm, kmt_hbm, source_hbm, kvert_hbm, land_hbm, links_hbm,
+def columns_body(levels, sums, basis_ref, weight_hbm, kmt_hbm, source_hbm, kvert_hbm, land_hbm, links_hbm,
                  out_hbm, u, near_ref, far_ref, weight, kmt, source, kvert, land, links, s_ref, ratio, sems, out_sems):
     width = source.shape[1]
     parts = 4
@@ -332,11 +342,8 @@
     big = loads([pairs[i] for i in range(parts) for pairs in parted], sems, 2)
     links_copy = loads([(links_hbm, links)], sems, 2 + 3 * parts)[0]
 
-    tile_sums = sums[0:8, :]
-    for j in range(1, count):
-        tile_sums = tile_sums + sums[j * 8 : (j + 1) * 8, :]
-    tile_sums = jnp.sum(tile_sums, axis=1, keepdims=True)
-    mix = weights([tile_sums[i : i + 1, :] for i in range(6)])
+    total = jnp.sum(sums[...], axis=0, keepdims=True)
+    mix = weights([total[:, i : i + 1] for i in range(6)])
     b0, b1, b2 = (basis_ref[i * ROWS : (i + 1) * ROWS, :] for i in range(3))
     s = mix[0] * b0 + mix[1] * b1 + mix[2] * b2
     s_ref[...] = s
@@ -395,12 +402,22 @@
         copy.wait()
 
 
-def inner_body(levels, u0, kmt_hbm, kappa_hbm, land_hbm, u2_ref, kmt, kappa, land, sems):
-    parts = 4
+def inner_body(first, last, with_relay, u0, kmt_hbm, kappa_hbm, land_hbm, *refs):
+    if with_relay:
+        passed, u2_ref, relay_ref = refs[:3]
+        relay_ref[...] = passed[...]
+        refs = refs[3:]
+    else:
+        u2_ref, refs = refs[0], refs[1:]
+    kmt, kappa, land, sems = refs
+    size = PART * ROWS
+    parts = (last - first) // PART
     kmt_copy = loads([(kmt_hbm, kmt)], sems)[0]
-    pairs = ((kappa_hbm, kappa), (land_hbm, land))
-    parted = [in_parts(far, near, parts) for far, near in pairs]
-    copies = loads([pairs[i] for i in range(parts) for pairs in parted], sems, 1)
+    pairs = []
+    for i in range(parts):
+        source, target = pl.ds((first + i * PART) * ROWS, size), pl.ds(i * size, size)
+        pairs += [(kappa_hbm.at[source], kappa.at[target]), (land_hbm.at[source], land.at[target])]
+    copies = loads(pairs, sems, 1)
     kmt_copy.wait()
     depth = kmt[...]
     width = depth.shape[1]
@@ -409,38 +426,35 @@
     def face(here, there):
         return jnp.where(jnp.minimum(here, there) > 0.0, here + there, 0.0)
 
-    def level(k):
-        at = rows_at(k)
-        sea = jnp.where(k < depth, land[at, :], 0) > 0
-        half = jnp.where(sea, 0.5 * kappa[at, :], 0.0)
-        fx = face(half, east(half))
-        fn = jnp.where(inside, face(half, north(half)), 0.0)
-        fw, fs = west(fx), south(fn)
-        keep = 1.0 - (fx + fw) - (fn + fs)
-        u = unstacked(u0[level_at(k, width), :])
+    def group(i, carry):
+        ks = [GROUP * i + j for j in range(GROUP)]
+        sea = [jnp.where(k + first < depth, land[rows_at(k), :], 0) > 0 for k in ks]
+        halved = [jnp.where(wet, 0.5 * kappa[rows_at(k), :], 0.0) for wet, k in zip(sea, ks)]
+        u = [unstacked(u0[level_at(k + first, width), :]) for k in ks]
+        fx = [face(v, east(v)) for v in halved]
+        fn = [jnp.where(inside, face(v, north(v)), 0.0) for v in halved]
         for _ in range(2):
-            u = keep * u + (fx * east(u) + fw * west(u)) + (fn * north(u) + fs * south(u))
-        return u
-
-    def group(i, carry):
-        for values, k in [(level(2 * i + j), 2 * i + j) for j in range(2)]:
-            u2_ref[rows_at(k), :] = values
+            flux_x = [f * (east(v) - v) for f, v in zip(fx, u)]
+            flux_y = [f * (north(v) - v) for f, v in zip(fn, u)]
+            u = [v + (x - west(x)) + (y - south(y)) for v, x, y in zip(u, flux_x, flux_y)]
+        for k, v in zip(ks, u):
+            u2_ref[rows_at(k), :] = v
         return carry
 
-    chunk = levels // 2 // parts
     for i in range(parts):
-        for copy in copies[2 * i : 2 * i + 2]:
-            copy.wait()
-        lax.fori_loop(i * chunk, (i + 1) * chunk, group, 0)
-
-
-def finish_body(levels, u2, links, own_near, own_far, rim_near, rim_far, near, far, rim_other_near, rim_other_far,
+        copies[2 * i].wait()
+        copies[2 * i + 1].wait()
+        lax.fori_loop(i * PART // GROUP, (i + 1) * PART // GROUP, group, 0)
+
+
+def finish_body(levels, u2_high, u2_low, links, own_near, own_far, rim_near, rim_far, near, far, rim_other_near, kept, swapped,
                 out, change_ref, buffer, sems):
     width = own_near.shape[1]
     tall = width // 128 * ROWS
     rows = lax.broadcasted_iota(jnp.int32, (ROWS, width), 0)
     on_rim = (rows < 2) | (rows >= ROWS - 2)
     even = is_even()
+    first_group = is_first()
     copies = []
     for block in range(levels // 8):
         at, below = pl.ds(block * 8, 8), pl.ds(levels + block * 8, 8)
@@ -449,7 +463,10 @@
             return [dealt(even, a[part, :], b[part, :]) for part in (at, below)]
 
         own, rim = pairs(own_near, own_far), pairs(rim_near, rim_far)
-        other, rim_other = pairs(near, far), pairs(rim_other_near, rim_other_far)
+        other = pairs(near, far)
+        far_kap = jnp.where(first_group, kept[at, :], swapped[at, :])
+        far_wet = jnp.where(first_group, swapped[at, :], kept[at, :])
+        rim_other = [dealt(even, rim_other_near[at, :], far_kap), dealt(even, rim_other_near[below, :], far_wet)]
         for side, row, inner in ((0, 0, 1), (1, ROWS - 1, ROWS - 2)):
             face = 0.5 * (rim[0][side] + rim_other[0][side]) * rim[1][side] * rim_other[1][side]
             change = face * (other[0][side] - own[0][side])
@@ -465,7 +482,8 @@
         for k in range(8):
             level = block * 8 + k
             change = jnp.where(on_rim, unstacked(change_ref[level_at(k, width), :]), 0.0)
-            buffer[rows_at(level), :] = u2[rows_at(level), :] + change
+            u2, first = (u2_high, 0) if level < BEFORE_SWAP else (u2_low, BEFORE_SWAP)
+            buffer[rows_at(level), :] = u2[rows_at(level - first), :] + change
         whole = pl.ds(block * 8 * ROWS, 8 * ROWS)
         copy = pltpu.make_async_copy(buffer.at[whole], out.at[whole], sems.at[block])
         copy.start()
@@ -474,13 +492,12 @@
         copy.wait()
 
 
+def swap(array, start, axis="tile"):
+    firsts = range(start, lax.axis_size(axis) - 1, 2)
+    return lax.ppermute(array, axis, [(i, i + 1) for i in firsts] + [(i + 1, i) for i in firsts])
+
+
 def exchange(to_near, to_far):
-    count = lax.axis_size("tile")
-
-    def swap(array, start):
-        firsts = range(start, count - 1, 2)
-        return lax.ppermute(array, "tile", [(i, i + 1) for i in firsts] + [(i + 1, i) for i in firsts])
-
     from_far = swap(to_far, 1)
     return swap(to_near, 0), from_far
 
@@ -504,35 +521,44 @@
     )(layer_weight, land, kmt, left(ct_surface), left(screen))
     near, far = exchange(to_near, to_far)
 
-    rim_near, rim_far, links = kernel(
-        functools.partial(rims_body, levels), vmem(rim, rim) + hbm(link_rows), in_hbm(1) + in_vmem(1),
-        in_vmem(2) + in_hbm(1), "rims", [whole, bricks, pltpu.VMEM(link_rows, FLOAT), semaphores((4 + levels // 8,))],
+    rim_near, rim_far, rim_sent, links = kernel(
+        functools.partial(rims_body, levels), vmem(rim, rim, (levels, width)) + hbm(link_rows), in_hbm(1) + in_vmem(1),
+        in_vmem(3) + in_hbm(1), "rims", [whole, bricks, pltpu.VMEM(link_rows, FLOAT), semaphores((4 + levels // 8,))],
     )(kappa, wet)
-    links = left(links)
-    rim_other_near, rim_other_far = exchange(rim_near, rim_far)
+    links_free, links = links, left(links)
+    rim_other_near, kept = exchange(rim_near, rim_sent)
 
     basis, sums = kernel(
-        functools.partial(basis_body, count), vmem((3 * rows, width), (8 * count, 128)), in_vmem(9) + in_hbm(1),
+        basis_body, vmem((3 * rows, width), (count, 128)), in_vmem(9) + in_hbm(1),
         in_vmem(2), "basis"
     )(base, height, surface, s_fx, s_fn, s_dg, q1, near, far, links)
-    sums = lax.all_to_all(sums.reshape(count, 8, 128), "tile", 0, 0, tiled=True).reshape(8 * count, 128)
+    sums = lax.all_to_all(sums.reshape(count, 1, 128), "tile", 0, 0, tiled=True).reshape(count, 128)
 
     solution, u0, row_near, row_far = kernel(
-        functools.partial(columns_body, levels, count), hbm(tile) + vmem(brick, rim, rim), in_vmem(2) + in_hbm(6),
+        functools.partial(columns_body, levels), hbm(tile) + vmem(brick, rim, rim), in_vmem(2) + in_hbm(6),
         in_hbm(1) + in_vmem(3), "columns",
         [scalars, tile_ints, whole, whole, ints, pltpu.VMEM(link_rows, FLOAT), tiles, bricks, semaphores((15,)),
          semaphores((1,))],
     )(sums, basis, layer_weight, kmt, ct_tracer, kvert, land, links)
     other_near, other_far = exchange(row_near, row_far)
-    u2 = kernel(
-        functools.partial(inner_body, levels), vmem(flat), in_vmem(1) + in_hbm(3), in_vmem(1), "inner",
-        [tile_ints, whole, ints, semaphores((9,))],
-    )(u0, kmt, kappa, land)[0]
+
+    def inner(first, last, name, *relayed):
+        size = ((last - first) * rows, width)
+        return kernel(
+            functools.partial(inner_body, first, last, bool(relayed)), vmem(size, *[(levels, width) for _ in relayed]),
+            in_vmem(1) + in_hbm(3) + in_vmem(len(relayed)), in_vmem(1 + len(relayed)), name,
+            [tile_ints, pltpu.VMEM(size, FLOAT), pltpu.VMEM(size, jnp.int32), semaphores((1 + 2 * (last - first) // PART,))],
+        )(u0, kmt, kappa, land, *relayed)
+
+    u2_high, relayed = inner(0, BEFORE_SWAP, "inner_high", kept)
+    swapped = swap(relayed, 0, "grp")
+    (u2_low,) = inner(BEFORE_SWAP, levels, "inner_low")
 
     values = kernel(
-        functools.partial(finish_body, levels), hbm(flat), in_vmem(10), in_hbm(1), "finish",
+        functools.partial(finish_body, levels), hbm(flat), in_vmem(12), in_hbm(1), "finish",
         [pltpu.VMEM((8 * rows * width // 128, 128), FLOAT), whole, semaphores((levels // 8,))],
-    )(u2, held(links), row_near, row_far, rim_near, rim_far, other_near, other_far, rim_other_near, rim_other_far)[0]
+    )(u2_high, u2_low, held(links_free), row_near, row_far, rim_near, rim_far, other_near, other_far, rim_other_near,
+      kept, swapped)[0]
     return (values.reshape(levels, rows, width), solution)
 
 

time: 44.2 us -> 43 us (0.973)
  waiting for transfers between devices: 6.24 us -> 4.85 us
  Pallas kernels: 20.1 us -> 19 us
  starting transfers between devices: 16.5 us -> 17.6 us
    ppermute x6 -> x7, waiting for transfers between devices: 3.88 us -> 2.76 us  [swap(): lax.ppermute(array, axis, [(i, i + 1) for i in firsts] + [(i + 1, i) for...]
    ppermute x6 -> x7, starting transfers between devices: 11.2 us -> 12.3 us  [swap(): lax.ppermute(array, axis, [(i, i + 1) for i in firsts] + [(i + 1, i) for...]
    pallas_call x5 -> x6, Pallas kernels: 18.2 us -> 17.1 us  [the longest x2 6.95 us: inner(): kernel(functools.partial(inner_body, first, last, bool(relayed)), vmem(si...]
  transfers between devices with their start and end apart: 7 -> 8, of which waited for: 2 -> 3; matrix products, arithmetic and copies ran while one was open for 0% -> 0% of each run, Pallas kernels for 35% -> 34%
where the time goes in v11:
time: 43 us; the launch traced here: 42.3 us
  Pallas kernels  19 us (44%)
  starting transfers between devices  17.6 us (41%)
  waiting for transfers between devices  4.85 us (11%)
  between operations  0.75 us (2%)
    ppermute x7, starting transfers between devices, swap(): lax.ppermute(array, axis, [(i, i + 1) for i in firsts] + [(i + 1, i) for...  12.3 us
    pallas_call x2, Pallas kernels, inner(): kernel(functools.partial(inner_body, first, last, bool(relayed)), vmem(si...  6.95 us
    all_to_all x1, starting transfers between devices, body(): lax.all_to_all(sums.reshape(count, 1, 128), 'tile', 0, 0, tiled=True)  5.32 us
    pallas_call x1, Pallas kernels, body(): kernel(functools.partial(columns_body, levels), hbm(tile) + vmem(brick, r...  4.39 us
    pallas_call x1, Pallas kernels, body(): kernel(functools.partial(rims_body, levels), vmem(rim, rim, (levels, widt...  3 us
    ppermute x7, waiting for transfers between devices, swap(): lax.ppermute(array, axis, [(i, i + 1) for i in firsts] + [(i + 1, i) for...  2.76 us
    all_to_all x1, waiting for transfers between devices, body(): lax.all_to_all(sums.reshape(count, 1, 128), 'tile', 0, 0, tiled=True)  2.09 us
    pallas_call x1, Pallas kernels, body(): kernel(functools.partial(setup_body, levels), vmem(*[tile] * 9, brick), i...  1.97 us
  transfers between devices with their start and end apart: 8, of which 3 were waited for; matrix products, arithmetic and copies ran while one was open for 0% of the time, Pallas kernels for 34%

profile of v11, /device:TPU:1, one launch (start us, length us, event | category | flops | bytes accessed | tf_op | source)
XLA Modules:
  0.0 42.3 jit_solution(8125382634981332252)
XLA Ops:
  0.6 2.0 %setup.1 = (f32[8,1280]{1,0:T(8,128)S(1)}, f32[8,1280]{1,0:T(8,128)S(1)}, f32[8,1280]{1,0:T(8,128)S(1)}, f32[8,1280]{1,0:T(8,128)S(1)}, f32[8,1280]{1,0:T(8,128)...) custom-call(f32[48]{0:T(128)} %weight_hbm.3, ...), custom_call_target="tpu_custom_call" | custom-call | flops 1 | bytes 1 | tf_op jit(solution)/shard_map/setup/pallas_call | solution.py:518
  2.6 0.1 collective-permute-start
  2.7 4.5 %collective-permute-start.1 = (f32[8,1280]{1,0:T(8,128)S(1)}, f32[8,1280]{1,0:T(8,128)S(1)}, u32[]{:S(2)}, u32[]{:S(2)}) collective-permute-start(f32[8,1280]{1,0:T(8,128)S(1)} %get-tuple-element.32), channel_id=1, source_target_pairs={{1,2},{3,4},{5,6},{7,8},{9,10},{11,12},{13,14},{2,1},{4,3},{6,5},{... | collective-permute-start | bytes 122888 | tf_op jit(solution)/shard_map/ppermute | solution.py:497
  7.2 3.0 %rims.1 = (f32[96,1280]{1,0:T(8,128)S(1)}, f32[96,1280]{1,0:T(8,128)S(1)}, f32[48,1280]{1,0:T(8,128)S(1)}, f32[192,1280]{1,0:T(8,128)}) custom-call(f32[384,1280]{1,0:T(8,128)} %bitcast.14, f32[3840,128]{1,0:T(8,128)S(1)} %get-tuple-element.33.wet_bricks), custom_call_target="tpu_custom_call" | custom-call | flops 1 | bytes 1 | tf_op jit(solution)/shard_map/rims/pallas_call | solution.py:524
  10.2 0.0 collective-permute-done.near
  10.2 0.0 collective-permute-done.1.far
  10.3 0.9 %basis.1 = (f32[24,1280]{1,0:T(8,128)S(1)}, f32[16,128]{1,0:T(8,128)}) custom-call(f32[8,1280]{1,0:T(8,128)S(1)} %get-tuple-element.24.ct, f32[8,1280]{1,0:T(8,128)S(1)} %get-tuple-element.25.height, f32[8,1280]{1,0:T(8,128)S(1)} %get-tuple-element.26.surface, f32[8,1280]{1,0:T(8,128)S(1)} %get-tuple-element.27.fx_ref, ...), custom_call_target="tpu_custom_call" | custom-call | flops 1 | bytes 1 | tf_op jit(solution)/shard_map/basis/pallas_call | solution.py:531
  11.2 5.3 %all-to-all-start = ((f32[16,1,128]{2,1,0:T(1,128)}), f32[16,1,128]{2,1,0:T(1,128)S(1)}, u32[]{:S(2)}, u32[]{:S(2)}) async-start(f32[16,1,128]{2,1,0:T(1,128)} %bitcast.3), calls=%async_computation | async-start | bytes 16384 | tf_op jit(solution)/shard_map/all_to_all | solution.py:535
  16.5 3.5 %collective-permute-start.2 = (f32[48,1280]{1,0:T(8,128)S(1)}, f32[48,1280]{1,0:T(8,128)S(1)}, u32[]{:S(2)}, u32[]{:S(2)}) collective-permute-start(f32[48,1280]{1,0:T(8,128)S(1)} %get-tuple-element.38), channel_id=1, source_target_pairs={{1,2},{3,4},{5,6},{7,8},{9,10},{11,12},{13,14},{2,1},{4,3},{6,5},{... | collective-permute-start | bytes 737288 | tf_op jit(solution)/shard_map/ppermute | solution.py:497
  20.0 0.1 collective-permute-start.5
  20.1 2.1 %all-to-all-done = f32[16,1,128]{2,1,0:T(1,128)S(1)} async-done(((f32[16,1,128]{2,1,0:T(1,128)}), f32[16,1,128]{2,1,0:T(1,128)S(1)}, u32[]{:S(2)}, u32[]{:S(2)}) %all-to-all-start) | async-done | bytes 8224 | tf_op jit(solution)/shard_map/all_to_all | solution.py:535
  22.2 4.4 %columns.1 = (f32[8,1280]{1,0:T(8,128)}, f32[3840,128]{1,0:T(8,128)S(1)}, f32[96,1280]{1,0:T(8,128)S(1)}, f32[96,1280]{1,0:T(8,128)S(1)}) custom-call(f32[16,128]{1,0:T(8,128)S(1)} %bitcast.9, f32[24,1280]{1,0:T(8,128)S(1)} %get-tuple-element.36.basis_ref, f32[48]{0:T(128)} %weight_hbm.3, s32[8,1280]{1,0:T(8,128)} %kmt_hbm.7, f32[384,1280]{1,0:T(8,128)} %bitcast.17, ...), custom_call_target="tpu_custom_call" | custom-call | flops 1 | bytes 1 | tf_op jit(solution)/shard_map/columns/pallas_call | solution.py:537
  26.6 0.8 %collective-permute-start.3 = (f32[96,1280]{1,0:T(8,128)S(1)}, f32[96,1280]{1,0:T(8,128)S(1)}, u32[]{:S(2)}, u32[]{:S(2)}) collective-permute-start(f32[96,1280]{1,0:T(8,128)S(1)} %get-tuple-element.40.own_near), channel_id=1, source_target_pairs={{0,1},{2,3},{4,5},{6,7},{8,9},{10,11},{12,13},{14,15},{1,0},{3,2},... | collective-permute-start | bytes 1474568 | tf_op jit(solution)/shard_map/ppermute | solution.py:497
  27.4 2.0 %collective-permute-start.4 = (f32[96,1280]{1,0:T(8,128)S(1)}, f32[96,1280]{1,0:T(8,128)S(1)}, u32[]{:S(2)}, u32[]{:S(2)}) collective-permute-start(f32[96,1280]{1,0:T(8,128)S(1)} %get-tuple-element.41.own_far), channel_id=1, source_target_pairs={{1,2},{3,4},{5,6},{7,8},{9,10},{11,12},{13,14},{2,1},{4,3},{6,5},{... | collective-permute-start | bytes 1474568 | tf_op jit(solution)/shard_map/ppermute | solution.py:497
  29.4 0.0 collective-permute-done.2.refs_0_.kept
  29.4 2.7 %inner_high.1 = (f32[128,1280]{1,0:T(8,128)S(1)}, f32[48,1280]{1,0:T(8,128)S(1)}) custom-call(f32[3840,128]{1,0:T(8,128)S(1)} %get-tuple-element.37.u0, s32[8,1280]{1,0:T(8,128)} %kmt_hbm.7, f32[384,1280]{1,0:T(8,128)} %bitcast.15, s32[384,1280]{1,0:T(8,128)} %bitcast.12, f32[48,1280]{1,0:T(8,128)S(1)} %collective-permute-done.2.refs_0_.kept), custom_call_target="tpu_custom_call" | custom-call | flops 1 | bytes 1 | tf_op jit(solution)/shard_map/inner_high/pallas_call | solution.py:547
  32.1 0.0 copy-start
  32.1 1.3 %collective-permute-start.6 = (f32[48,1280]{1,0:T(8,128)S(1)}, f32[48,1280]{1,0:T(8,128)S(1)}, u32[]{:S(2)}, u32[]{:S(2)}) collective-permute-start(f32[48,1280]{1,0:T(8,128)S(1)} %get-tuple-element.44), channel_id=1, source_target_pairs={{0,16},{16,0},{1,17},{17,1},{2,18},{18,2},{3,19},{19,3},{4,20},{20... | collective-permute-start | bytes 737288 | tf_op jit(solution)/shard_map/ppermute | solution.py:497
  33.4 4.3 %inner_low.1.u2_low = f32[256,1280]{1,0:T(8,128)S(1)} custom-call(f32[3840,128]{1,0:T(8,128)S(1)} %get-tuple-element.37.u0, s32[8,1280]{1,0:T(8,128)} %kmt_hbm.7, f32[384,1280]{1,0:T(8,128)} %bitcast.16, s32[384,1280]{1,0:T(8,128)} %bitcast.13), custom_call_target="tpu_custom_call" | custom-call | flops 1 | bytes 1 | tf_op jit(solution)/shard_map/inner_low/pallas_call | solution.py:547
  37.7 0.0 collective-permute-done.5.rim_other_near
  37.7 1.3 %collective-permute-done.6.swapped = f32[48,1280]{1,0:T(8,128)S(1)} collective-permute-done((f32[48,1280]{1,0:T(8,128)S(1)}, f32[48,1280]{1,0:T(8,128)S(1)}, u32[]{:S(2)}, u32[]{:S(2)}) %collective-permute-start.6) | collective-permute-done | bytes 245792 | tf_op jit(solution)/shard_map/ppermute | solution.py:497
  39.0 0.0 collective-permute-done.3.near
  39.0 1.4 %collective-permute-done.4.far = f32[96,1280]{1,0:T(8,128)S(1)} collective-permute-done((f32[96,1280]{1,0:T(8,128)S(1)}, f32[96,1280]{1,0:T(8,128)S(1)}, u32[]{:S(2)}, u32[]{:S(2)}) %collective-permute-start.4) | collective-permute-done | bytes 491552 | tf_op jit(solution)/shard_map/ppermute | solution.py:497
  40.4 0.0 copy-done
  40.5 1.8 %finish.1 = f32[384,1280]{1,0:T(8,128)} custom-call(f32[128,1280]{1,0:T(8,128)S(1)} %get-tuple-element.39.u2_high, f32[256,1280]{1,0:T(8,128)S(1)} %inner_low.1.u2_low, f32[192,1280]{1,0:T(8,128)S(1)} %copy-done, f32[96,1280]{1,0:T(8,128)S(1)} %get-tuple-element.40.own_near, f32[96,1280]{1,0:T(8,128)S(1)} %get-tuple-element.41.own_far, ...), custom_call_target="tpu_custom_call" | custom-call | flops 1 | bytes 1 | tf_op jit(solution)/shard_map/finish/pallas_call | solution.py:557
Async XLA Ops:
  2.6 7.6 %collective-permute-start = (f32[8,1280]{1,0:T(8,128)S(1)}, f32[8,1280]{1,0:T(8,128)S(1)}, u32[]{:S(2)}, u32[]{:S(2)}) collective-permute-start(f32[8,1280]{1,0:T(8,128)S(1)} %get-tuple-element.31), channel_id=1, source_target_pairs={{0,1},{2,3},{4,5},{6,7},{8,9},{10,11},{12,13},{14,15},{1,0},{3,2},... | collective-permute-start | bytes 122888 | tf_op jit(solution)/shard_map/ppermute | solution.py:497
  2.7 7.5 %collective-permute-start.1 = (f32[8,1280]{1,0:T(8,128)S(1)}, f32[8,1280]{1,0:T(8,128)S(1)}, u32[]{:S(2)}, u32[]{:S(2)}) collective-permute-start(f32[8,1280]{1,0:T(8,128)S(1)} %get-tuple-element.32), channel_id=1, source_target_pairs={{1,2},{3,4},{5,6},{7,8},{9,10},{11,12},{13,14},{2,1},{4,3},{6,5},{... | collective-permute-start | bytes 122888 | tf_op jit(solution)/shard_map/ppermute | solution.py:497
  11.2 11.0 %all-to-all-start = ((f32[16,1,128]{2,1,0:T(1,128)}), f32[16,1,128]{2,1,0:T(1,128)S(1)}, u32[]{:S(2)}, u32[]{:S(2)}) async-start(f32[16,1,128]{2,1,0:T(1,128)} %bitcast.3), calls=%async_computation | async-start | bytes 16384 | tf_op jit(solution)/shard_map/all_to_all | solution.py:535
  16.5 12.9 %collective-permute-start.2 = (f32[48,1280]{1,0:T(8,128)S(1)}, f32[48,1280]{1,0:T(8,128)S(1)}, u32[]{:S(2)}, u32[]{:S(2)}) collective-permute-start(f32[48,1280]{1,0:T(8,128)S(1)} %get-tuple-element.38), channel_id=1, source_target_pairs={{1,2},{3,4},{5,6},{7,8},{9,10},{11,12},{13,14},{2,1},{4,3},{6,5},{... | collective-permute-start | bytes 737288 | tf_op jit(solution)/shard_map/ppermute | solution.py:497
  20.0 17.7 %collective-permute-start.5 = (f32[96,1280]{1,0:T(8,128)S(1)}, f32[96,1280]{1,0:T(8,128)S(1)}, u32[]{:S(2)}, u32[]{:S(2)}) collective-permute-start(f32[96,1280]{1,0:T(8,128)S(1)} %get-tuple-element.42.rim_near), channel_id=1, source_target_pairs={{0,1},{2,3},{4,5},{6,7},{8,9},{10,11},{12,13},{14,15},{1,0},{3,2},... | collective-permute-start | bytes 1474568 | tf_op jit(solution)/shard_map/ppermute | solution.py:497
  26.6 12.4 %collective-permute-start.3 = (f32[96,1280]{1,0:T(8,128)S(1)}, f32[96,1280]{1,0:T(8,128)S(1)}, u32[]{:S(2)}, u32[]{:S(2)}) collective-permute-start(f32[96,1280]{1,0:T(8,128)S(1)} %get-tuple-element.40.own_near), channel_id=1, source_target_pairs={{0,1},{2,3},{4,5},{6,7},{8,9},{10,11},{12,13},{14,15},{1,0},{3,2},... | collective-permute-start | bytes 1474568 | tf_op jit(solution)/shard_map/ppermute | solution.py:497
  27.4 13.1 %collective-permute-start.4 = (f32[96,1280]{1,0:T(8,128)S(1)}, f32[96,1280]{1,0:T(8,128)S(1)}, u32[]{:S(2)}, u32[]{:S(2)}) collective-permute-start(f32[96,1280]{1,0:T(8,128)S(1)} %get-tuple-element.41.own_far), channel_id=1, source_target_pairs={{1,2},{3,4},{5,6},{7,8},{9,10},{11,12},{13,14},{2,1},{4,3},{6,5},{... | collective-permute-start | bytes 1474568 | tf_op jit(solution)/shard_map/ppermute | solution.py:497
  32.1 8.3 %copy-start = (f32[192,1280]{1,0:T(8,128)S(1)}, f32[192,1280]{1,0:T(8,128)}, u32[]{:S(2)}) copy-start(f32[192,1280]{1,0:T(8,128)} %get-tuple-element.34.links_hbm.links) | copy-start | bytes 2949124
  32.1 6.9 %collective-permute-start.6 = (f32[48,1280]{1,0:T(8,128)S(1)}, f32[48,1280]{1,0:T(8,128)S(1)}, u32[]{:S(2)}, u32[]{:S(2)}) collective-permute-start(f32[48,1280]{1,0:T(8,128)S(1)} %get-tuple-element.44), channel_id=1, source_target_pairs={{0,16},{16,0},{1,17},{17,1},{2,18},{18,2},{3,19},{19,3},{4,20},{20... | collective-permute-start | bytes 737288 | tf_op jit(solution)/shard_map/ppermute | solution.py:497

commit v12 on v10

--- a/solution.py
+++ b/solution.py
@@ -16,7 +16,8 @@
 FLOAT = jnp.float32
 LINKS = 4
 GROUP = 4
-UPPER = 8
+UPPER = 24
+BEFORE_SWAP = 16
 LIMIT = 24 * 1024 * 1024
 
 
@@ -108,6 +109,10 @@
 
 def is_even():
     return lax.rem(lax.axis_index("tile"), 2) == 0
+
+
+def is_first():
+    return lax.rem(lax.axis_index("grp"), 2) == 0
 
 
 def dealt(even, low, high):
@@ -188,7 +193,7 @@
         near_ref[at, :], far_ref[at, :] = dealt(even, values[0:1, :], values[ROWS - 1 : ROWS, :])
 
 
-def rims_body(levels, kappa_hbm, wet_bricks, near_ref, far_ref, links_hbm, kappa, kappa_bricks, links, sems):
+def rims_body(levels, kappa_hbm, wet_bricks, near_ref, far_ref, sent_ref, links_hbm, kappa, kappa_bricks, links, sems):
     chunk = levels // 4
     width = kappa.shape[1]
     for i, copy in enumerate(loads(in_parts(kappa_hbm, kappa, 4), sems)):
@@ -200,6 +205,7 @@
 
         lax.fori_loop(i * chunk, (i + 1) * chunk, brick, 0, unroll=4)
     even = is_even()
+    first_group = is_first()
     outs = []
     for block in range(levels // 8):
         found = []
@@ -213,6 +219,8 @@
         for place in range(2):
             at = pl.ds(place * levels + block * 8, 8)
             near_ref[at, :], far_ref[at, :] = dealt(even, found[0][place], found[1][place])
+        at, below = pl.ds(block * 8, 8), pl.ds(levels + block * 8, 8)
+        sent_ref[at, :] = jnp.where(first_group, far_ref[at, :], far_ref[below, :])
         whole = pl.ds(block * LINKS * 8, LINKS * 8)
         outs += loads([(links.at[whole], links_hbm.at[whole])], sems, 4 + block)
     for copy in outs:
@@ -345,9 +353,9 @@
     return [(a, b, b <= UPPER) for a, b in zip(cuts[:-1], cuts[1:])]
 
 
-def columns_body(levels, sums, sums_near, basis_ref, weight_hbm, kmt_hbm, source_hbm, kvert_hbm, land_hbm, links_hbm,
-                 out_hbm, high, ratio, low, links_high, near_ref, far_ref,
-                 weight, kmt, source, kvert, land, links_low, s_ref, ratio_low, sems, out_sems):
+def columns_body(levels, sums, basis_ref, weight_hbm, kmt_hbm, source_hbm, kvert_hbm, land_hbm, links_hbm,
+                 kappa_hbm, out_hbm, high, ratio, low, links_high, near_ref, far_ref, kmt, kappa, land,
+                 weight, source, kvert, links_low, s_ref, ratio_low, sems, out_sems):
     width = source.shape[1]
     parts = 4
     chunk = levels // parts
@@ -356,8 +364,9 @@
     big = loads([pairs[i] for i in range(parts) for pairs in parted], sems, 2)
     top, bottom = pl.ds(0, UPPER * LINKS), pl.ds(UPPER * LINKS, (levels - UPPER) * LINKS)
     links_copies = loads([(links_hbm.at[bottom], links_low), (links_hbm.at[top], links_high)], sems, 2 + 3 * parts)
-
-    total = jnp.sum(sums[...], axis=0, keepdims=True) + jnp.sum(sums_near[...], axis=0, keepdims=True)
+    kappa_copies = loads(in_parts(kappa_hbm, kappa, parts), sems, 4 + 3 * parts)
+
+    total = jnp.sum(sums[...], axis=0, keepdims=True)
     mix = weights([total[:, i : i + 1] for i in range(6)])
     b0, b1, b2 = (basis_ref[i * ROWS : (i + 1) * ROWS, :] for i in range(3))
     s = mix[0] * b0 + mix[1] * b1 + mix[2] * b2
@@ -399,7 +408,7 @@
     for copy in links_copies:
         copy.wait()
     send_rows(low, links_low, near_ref, far_ref, width)
-    for copy in outs:
+    for copy in kappa_copies + outs:
         copy.wait()
 
 
@@ -421,13 +430,11 @@
     send_rows(u, links, near_ref, far_ref, width)
 
 
-def inner_body(levels, high, low, kmt_hbm, kappa_hbm, land_hbm, u2_ref, kmt, kappa, land, sems):
-    parts = 4
-    kmt_copy = loads([(kmt_hbm, kmt)], sems)[0]
-    pairs = ((kappa_hbm, kappa), (land_hbm, land))
-    parted = [in_parts(far, near, parts) for far, near in pairs]
-    copies = loads([pairs[i] for i in range(parts) for pairs in parted], sems, 1)
-    kmt_copy.wait()
+def inner_body(first, last, with_relay, high, low, kmt, kappa, land, *refs):
+    u2_ref = refs[-1]
+    if with_relay:
+        passed, u2_ref, relay_ref = refs
+        relay_ref[...] = passed[...]
     depth = kmt[...]
     width = depth.shape[1]
     inside = row_index(depth) < ROWS - 1
@@ -435,11 +442,11 @@
     def face(here, there):
         return jnp.where(jnp.minimum(here, there) > 0.0, here + there, 0.0)
 
-    def group(source, first, i, carry):
+    def group(source, source_first, i, carry):
         ks = [GROUP * i + j for j in range(GROUP)]
         sea = [jnp.where(k < depth, land[rows_at(k), :], 0) > 0 for k in ks]
         halved = [jnp.where(wet, 0.5 * kappa[rows_at(k), :], 0.0) for wet, k in zip(sea, ks)]
-        u = [unstacked(source[level_at(k - first, width), :]) for k in ks]
+        u = [unstacked(source[level_at(k - source_first, width), :]) for k in ks]
         fx = [face(v, east(v)) for v in halved]
         fn = [jnp.where(inside, face(v, north(v)), 0.0) for v in halved]
         for _ in range(2):
@@ -447,20 +454,16 @@
             flux_y = [f * (north(v) - v) for f, v in zip(fn, u)]
             u = [v + (x - west(x)) + (y - south(y)) for v, x, y in zip(u, flux_x, flux_y)]
         for k, v in zip(ks, u):
-            u2_ref[rows_at(k), :] = v
+            u2_ref[rows_at(k - first), :] = v
         return carry
 
-    chunk = levels // parts
-    for i in range(parts):
-        for copy in copies[2 * i : 2 * i + 2]:
-            copy.wait()
-        for start, stop, is_high in segments(i * chunk, (i + 1) * chunk):
-            step = functools.partial(group, *((high, 0) if is_high else (low, UPPER)))
-            lax.fori_loop(start // GROUP, stop // GROUP, step, 0)
-
-
-def finish_body(levels, first, last, skipped, u2, links, own_near, own_far, near, far, rim_near, rim_far, rim_other_near, rim_other_far,
-                *refs):
+    for start, stop, is_high in segments(first, last):
+        step = functools.partial(group, *((high, 0) if is_high else (low, UPPER)))
+        lax.fori_loop(start // GROUP, stop // GROUP, step, 0)
+
+
+def finish_body(levels, first, last, skipped, u2_high, u2_low, links, own_near, own_far, near, far, rim_near, rim_far, rim_other_near,
+                kept, swapped, *refs):
     out, change_ref, buffer, sems = refs[-4:]
     width = own_near.shape[1]
     tall = width // 128 * ROWS
@@ -468,6 +471,7 @@
     rows = lax.broadcasted_iota(jnp.int32, (ROWS, width), 0)
     on_rim = (rows < 2) | (rows >= ROWS - 2)
     even = is_even()
+    first_group = is_first()
     copies = []
     for block in range(count // 8):
         at, below = pl.ds(block * 8, 8), pl.ds(count + block * 8, 8)
@@ -476,10 +480,13 @@
             return [dealt(even, a[part, :], b[part, :]) for part in (at, below)]
 
         own, other = pairs(own_near, own_far), pairs(near, far)
-        kap, wet, kap_other, wet_other = (
-            dealt(even, a[pl.ds(part * levels + first + block * 8, 8), :], b[pl.ds(part * levels + first + block * 8, 8), :])
-            for a, b in ((rim_near, rim_far), (rim_other_near, rim_other_far)) for part in range(2)
-        )
+        here = pl.ds(first + block * 8, 8)
+        under = pl.ds(levels + first + block * 8, 8)
+        kap, wet = (dealt(even, rim_near[part, :], rim_far[part, :]) for part in (here, under))
+        far_kap = jnp.where(first_group, kept[here, :], swapped[here, :])
+        far_wet = jnp.where(first_group, swapped[here, :], kept[here, :])
+        kap_other = dealt(even, rim_other_near[here, :], far_kap)
+        wet_other = dealt(even, rim_other_near[under, :], far_wet)
         for side, row, inner in ((0, 0, 1), (1, ROWS - 1, ROWS - 2)):
             face = 0.5 * (kap[side] + kap_other[side]) * wet[side] * wet_other[side]
             change = face * (other[0][side] - own[0][side])
@@ -495,9 +502,10 @@
                 change_ref[pl.ds(j * ROWS + row, 8, stride=tall), :] = on_row[:, lanes]
                 change_ref[pl.ds(j * ROWS + inner, 8, stride=tall), :] = passed[:, lanes]
         for k in range(8):
-            here = block * 8 + k
+            level = first + block * 8 + k
             change = jnp.where(on_rim, unstacked(change_ref[level_at(k, width), :]), 0.0)
-            buffer[rows_at(here), :] = u2[rows_at(first + here), :] + change
+            u2, u2_first = (u2_high, 0) if level < BEFORE_SWAP else (u2_low, BEFORE_SWAP)
+            buffer[rows_at(block * 8 + k), :] = u2[rows_at(level - u2_first), :] + change
         whole = pl.ds(block * 8 * ROWS, 8 * ROWS)
         target = pl.ds((first + block * 8) * ROWS, 8 * ROWS)
         copies += loads([(buffer.at[whole], out.at[target])], sems, block)
@@ -505,9 +513,9 @@
         copy.wait()
 
 
-def swap(array, start):
-    firsts = range(start, lax.axis_size("tile") - 1, 2)
-    return lax.ppermute(array, "tile", [(i, i + 1) for i in firsts] + [(i + 1, i) for i in firsts])
+def swap(array, start, axis="tile"):
+    firsts = range(start, lax.axis_size(axis) - 1, 2)
+    return lax.ppermute(array, axis, [(i, i + 1) for i in firsts] + [(i + 1, i) for i in firsts])
 
 
 def exchange(to_near, to_far):
@@ -534,60 +542,63 @@
     )(layer_weight, land, kmt, left(ct_surface), left(screen))
     near, far = exchange(to_near, to_far)
 
-    rim_near, rim_far, links = kernel(
-        functools.partial(rims_body, levels), vmem(rim, rim) + hbm(link_rows), in_hbm(1) + in_vmem(1),
-        in_vmem(2) + in_hbm(1), "rims", [whole, bricks, pltpu.VMEM(link_rows, FLOAT), semaphores((4 + levels // 8,))],
+    rim_near, rim_far, rim_sent, links = kernel(
+        functools.partial(rims_body, levels), vmem(rim, rim, (levels, width)) + hbm(link_rows), in_hbm(1) + in_vmem(1),
+        in_vmem(3) + in_hbm(1), "rims", [whole, bricks, pltpu.VMEM(link_rows, FLOAT), semaphores((4 + levels // 8,))],
     )(kappa, wet)
     links_left = left(links)
-    rim_other_near, rim_other_far = exchange(rim_near, rim_far)
+    rim_other_near, kept = exchange(rim_near, rim_sent)
 
     basis, sums = kernel(
-        basis_body, vmem((3 * rows, width), (count // 2, 128)), in_vmem(9) + in_hbm(1),
+        basis_body, vmem((3 * rows, width), (count, 128)), in_vmem(9) + in_hbm(1),
         in_vmem(2), "basis"
     )(base, height, surface, s_fx, s_fn, s_dg, q1, near, far, links_left)
-    share = count // 2
-    every_other = [[2 * i + core for i in range(share)] for core in range(2)]
-    sums = lax.all_to_all(sums.reshape(share, 1, 128), "tile", 0, 0, axis_index_groups=every_other, tiled=True)
-    sums = sums.reshape(share, 128)
-    sums_near = swap(sums, 0)
-
-    rims = (rim_near, rim_far, rim_other_near, rim_other_far)
+    sums = lax.all_to_all(sums.reshape(count, 1, 128), "tile", 0, 0, tiled=True).reshape(count, 128)
+
     lower = levels - UPPER
     per_level = brick[0] // levels
     high_bricks, low_bricks = (UPPER * per_level, 128), (lower * per_level, 128)
     high_links, low_links = (UPPER * LINKS, width), (lower * LINKS, width)
     high_rim, low_rim = (2 * UPPER, width), (2 * lower, width)
-    solution, carried, ratio, low, links_high, low_near, low_far = kernel(
+    solution, carried, ratio, low, links_high, low_near, low_far, kmt_held, kappa_held, land_held = kernel(
         functools.partial(columns_body, levels),
-        hbm(tile) + vmem(high_bricks, high_bricks, low_bricks, high_links, low_rim, low_rim),
-        in_vmem(3) + in_hbm(6), in_hbm(1) + in_vmem(6), "columns",
-        [scalars, tile_ints, whole, whole, ints, pltpu.VMEM(low_links, FLOAT), tiles, pltpu.VMEM(low_bricks, FLOAT),
-         semaphores((16,)), semaphores((1,))],
-    )(sums, sums_near, basis, layer_weight, kmt, ct_tracer, kvert, land, links_left)
+        hbm(tile) + vmem(high_bricks, high_bricks, low_bricks, high_links, low_rim, low_rim) + [tile_ints, whole, ints],
+        in_vmem(2) + in_hbm(7), in_hbm(1) + in_vmem(9), "columns",
+        [scalars, whole, whole, pltpu.VMEM(low_links, FLOAT), tiles, pltpu.VMEM(low_bricks, FLOAT), semaphores((20,)),
+         semaphores((1,))],
+    )(sums, basis, layer_weight, kmt, ct_tracer, kvert, land, links_left, kappa)
     low_other_near, low_other_far = exchange(low_near, low_far)
     high, high_near, high_far = kernel(
         upper_body, vmem(high_bricks, high_rim, high_rim), in_vmem(4), in_vmem(3), "upper_columns"
     )(carried, ratio, low, links_high)
     high_other_near, high_other_far = exchange(high_near, high_far)
-    u2 = kernel(
-        functools.partial(inner_body, levels), vmem(flat), in_vmem(2) + in_hbm(3), in_vmem(1), "inner",
-        [tile_ints, whole, ints, semaphores((9,))],
-    )(high, low, kmt, kappa, land)[0]
+
+    def inner(first, last, name, *relayed):
+        return kernel(
+            functools.partial(inner_body, first, last, bool(relayed)),
+            vmem(((last - first) * rows, width), *[(levels, width) for _ in relayed]),
+            in_vmem(5 + len(relayed)), in_vmem(1 + len(relayed)), name,
+        )(high, low, kmt_held, kappa_held, land_held, *relayed)
+
+    u2_high, relayed = inner(0, BEFORE_SWAP, "inner_high", kept)
+    swapped = swap(relayed, 0, "grp")
+    (u2_low,) = inner(BEFORE_SWAP, levels, "inner_low")
+    rims = (rim_near, rim_far, rim_other_near, kept, swapped)
 
     def finish(first, last, skipped, name, more=(), aliases={}):
         count = last - first
         return kernel(
-            functools.partial(finish_body, levels, first, last, skipped), hbm(flat), in_vmem(10) + in_hbm(len(more)),
+            functools.partial(finish_body, levels, first, last, skipped), hbm(flat), in_vmem(12) + in_hbm(len(more)),
             in_hbm(1), name,
             [pltpu.VMEM((8 * per_level, 128), FLOAT), pltpu.VMEM((count * rows, width), FLOAT), semaphores((count // 8,))],
             aliases=aliases,
         )
 
     deep = finish(UPPER, levels, UPPER // 8, "finish_low")(
-        u2, held(links), low_near, low_far, low_other_near, low_other_far, *rims
+        u2_high, u2_low, held(links), low_near, low_far, low_other_near, low_other_far, *rims
     )[0]
-    values = finish(0, UPPER, 0, "finish_high", (deep,), {10: 0})(
-        u2, links_high, high_near, high_far, high_other_near, high_other_far, *rims, left(deep)
+    values = finish(0, UPPER, 0, "finish_high", (deep,), {12: 0})(
+        u2_high, u2_low, links_high, high_near, high_far, high_other_near, high_other_far, *rims, left(deep)
     )[0]
     return (values.reshape(levels, rows, width), solution)
 

time: 48.3 us -> 44.1 us (0.913)
  blocking collectives: 9.78 us -> 0 us
  starting transfers between devices: 15.5 us -> 21.6 us
  Pallas kernels: 18.5 us -> 17.7 us
    all_to_all x1 -> x0, blocking collectives: 9.78 us -> none  [body(): lax.all_to_all(sums.reshape(share, 1, 128), 'tile', 0, 0, axis_index_grou...]
    all_to_all x0 -> x1, starting transfers between devices: none -> 5.32 us  [body(): lax.all_to_all(sums.reshape(count, 1, 128), 'tile', 0, 0, tiled=True)]
    ppermute x9, waiting for transfers between devices: 3.41 us -> 1.24 us  [swap(): lax.ppermute(array, axis, [(i, i + 1) for i in firsts] + [(i + 1, i) for...]
    all_to_all x0 -> x1, waiting for transfers between devices: none -> 2.09 us  [body(): lax.all_to_all(sums.reshape(count, 1, 128), 'tile', 0, 0, tiled=True)]
    ppermute x9, starting transfers between devices: 15.5 us -> 16.2 us  [swap(): lax.ppermute(array, axis, [(i, i + 1) for i in firsts] + [(i + 1, i) for...]
    pallas_call x4 -> x5, Pallas kernels: 10.3 us -> 9.93 us  [the longest x2 4.68 us: inner(): kernel(functools.partial(inner_body, first, last, bool(relayed)), vmem(((...]
  transfers between devices with their start and end apart: 9 -> 10, of which waited for: 1 -> 2; matrix products, arithmetic and copies ran while one was open for 0% -> 0% of each run, Pallas kernels for 32% -> 31%
where the time goes in v12:
time: 44.1 us; the launch traced here: 43.4 us
  starting transfers between devices  21.6 us (49%)
  Pallas kernels  17.7 us (40%)
  waiting for transfers between devices  3.34 us (8%)
  between operations  0.79 us (2%)
    ppermute x9, starting transfers between devices, swap(): lax.ppermute(array, axis, [(i, i + 1) for i in firsts] + [(i + 1, i) for...  16.2 us
    all_to_all x1, starting transfers between devices, body(): lax.all_to_all(sums.reshape(count, 1, 128), 'tile', 0, 0, tiled=True)  5.32 us
    pallas_call x2, Pallas kernels, inner(): kernel(functools.partial(inner_body, first, last, bool(relayed)), vmem(((...  4.68 us
    pallas_call x1, Pallas kernels, body(): kernel(functools.partial(columns_body, levels), hbm(tile) + vmem(high_bri...  4.04 us
    pallas_call x1, Pallas kernels, body(): kernel(functools.partial(rims_body, levels), vmem(rim, rim, (levels, widt...  3 us
    all_to_all x1, waiting for transfers between devices, body(): lax.all_to_all(sums.reshape(count, 1, 128), 'tile', 0, 0, tiled=True)  2.09 us
    pallas_call x1, Pallas kernels, body(): kernel(functools.partial(setup_body, levels), vmem(*[tile] * 9, brick), i...  1.97 us
    pallas_call x1, Pallas kernels, body(): finish(UPPER, levels, UPPER // 8, 'finish_low')  1.35 us
  transfers between devices with their start and end apart: 10, of which 2 were waited for; matrix products, arithmetic and copies ran while one was open for 0% of the time, Pallas kernels for 31%

profile of v12, /device:TPU:1, one launch (start us, length us, event | category | flops | bytes accessed | tf_op | source)
XLA Modules:
  0.0 43.4 jit_solution(450563077532396820)
XLA Ops:
  0.6 2.0 %setup.1 = (f32[8,1280]{1,0:T(8,128)S(1)}, f32[8,1280]{1,0:T(8,128)S(1)}, f32[8,1280]{1,0:T(8,128)S(1)}, f32[8,1280]{1,0:T(8,128)S(1)}, f32[8,1280]{1,0:T(8,128)...) custom-call(f32[48]{0:T(128)} %weight_hbm.3, ...), custom_call_target="tpu_custom_call" | custom-call | flops 1 | bytes 1 | tf_op jit(solution)/shard_map/setup/pallas_call | solution.py:539
  2.6 0.1 collective-permute-start
  2.7 4.5 %collective-permute-start.1 = (f32[8,1280]{1,0:T(8,128)S(1)}, f32[8,1280]{1,0:T(8,128)S(1)}, u32[]{:S(2)}, u32[]{:S(2)}) collective-permute-start(f32[8,1280]{1,0:T(8,128)S(1)} %get-tuple-element.41), channel_id=1, source_target_pairs={{1,2},{3,4},{5,6},{7,8},{9,10},{11,12},{13,14},{2,1},{4,3},{6,5},{... | collective-permute-start | bytes 122888 | tf_op jit(solution)/shard_map/ppermute | solution.py:518
  7.2 3.0 %rims.1 = (f32[96,1280]{1,0:T(8,128)S(1)}, f32[96,1280]{1,0:T(8,128)S(1)}, f32[48,1280]{1,0:T(8,128)S(1)}, f32[192,1280]{1,0:T(8,128)}) custom-call(f32[384,1280]{1,0:T(8,128)} %bitcast.12, f32[3840,128]{1,0:T(8,128)S(1)} %get-tuple-element.42.wet_bricks), custom_call_target="tpu_custom_call" | custom-call | flops 1 | bytes 1 | tf_op jit(solution)/shard_map/rims/pallas_call | solution.py:545
  10.2 0.0 collective-permute-done.near
  10.2 0.0 collective-permute-done.1.far
  10.3 0.9 %basis.1 = (f32[24,1280]{1,0:T(8,128)S(1)}, f32[16,128]{1,0:T(8,128)}) custom-call(f32[8,1280]{1,0:T(8,128)S(1)} %get-tuple-element.33.ct, f32[8,1280]{1,0:T(8,128)S(1)} %get-tuple-element.34.height, f32[8,1280]{1,0:T(8,128)S(1)} %get-tuple-element.35.surface, f32[8,1280]{1,0:T(8,128)S(1)} %get-tuple-element.36.fx_ref, ...), custom_call_target="tpu_custom_call" | custom-call | flops 1 | bytes 1 | tf_op jit(solution)/shard_map/basis/pallas_call | solution.py:552
  11.2 5.3 %all-to-all-start = ((f32[16,1,128]{2,1,0:T(1,128)}), f32[16,1,128]{2,1,0:T(1,128)S(1)}, u32[]{:S(2)}, u32[]{:S(2)}) async-start(f32[16,1,128]{2,1,0:T(1,128)} %bitcast.3), calls=%async_computation | async-start | bytes 16384 | tf_op jit(solution)/shard_map/all_to_all | solution.py:556
  16.5 3.5 %collective-permute-start.2 = (f32[48,1280]{1,0:T(8,128)S(1)}, f32[48,1280]{1,0:T(8,128)S(1)}, u32[]{:S(2)}, u32[]{:S(2)}) collective-permute-start(f32[48,1280]{1,0:T(8,128)S(1)} %get-tuple-element.54), channel_id=1, source_target_pairs={{1,2},{3,4},{5,6},{7,8},{9,10},{11,12},{13,14},{2,1},{4,3},{6,5},{... | collective-permute-start | bytes 737288 | tf_op jit(solution)/shard_map/ppermute | solution.py:518
  20.0 0.1 collective-permute-start.5
  20.1 2.1 %all-to-all-done = f32[16,1,128]{2,1,0:T(1,128)S(1)} async-done(((f32[16,1,128]{2,1,0:T(1,128)}), f32[16,1,128]{2,1,0:T(1,128)S(1)}, u32[]{:S(2)}, u32[]{:S(2)}) %all-to-all-start) | async-done | bytes 8224 | tf_op jit(solution)/shard_map/all_to_all | solution.py:556
  22.2 4.0 %columns.1 = (f32[8,1280]{1,0:T(8,128)}, f32[1920,128]{1,0:T(8,128)S(1)}, f32[1920,128]{1,0:T(8,128)S(1)}, f32[1920,128]{1,0:T(8,128)S(1)}, f32[96,1280]{1,0:T(8...) custom-call(f32[16,128]{1,0:T(8,128)S(1)} %bitcast.9, ...), custom_call_target="tpu_custom_call" | custom-call | flops 1 | bytes 1 | tf_op jit(solution)/shard_map/columns/pallas_call | solution.py:563
  26.2 0.8 %collective-permute-start.7 = (f32[48,1280]{1,0:T(8,128)S(1)}, f32[48,1280]{1,0:T(8,128)S(1)}, u32[]{:S(2)}, u32[]{:S(2)}) collective-permute-start(f32[48,1280]{1,0:T(8,128)S(1)} %get-tuple-element.61.own_near), channel_id=1, source_target_pairs={{0,1},{2,3},{4,5},{6,7},{8,9},{10,11},{12,13},{14,15},{1,0},{3,2},... | collective-permute-start | bytes 737288 | tf_op jit(solution)/shard_map/ppermute | solution.py:518
  27.0 2.0 %collective-permute-start.8 = (f32[48,1280]{1,0:T(8,128)S(1)}, f32[48,1280]{1,0:T(8,128)S(1)}, u32[]{:S(2)}, u32[]{:S(2)}) collective-permute-start(f32[48,1280]{1,0:T(8,128)S(1)} %get-tuple-element.62.own_far), channel_id=1, source_target_pairs={{1,2},{3,4},{5,6},{7,8},{9,10},{11,12},{13,14},{2,1},{4,3},{6,5},{... | collective-permute-start | bytes 737288 | tf_op jit(solution)/shard_map/ppermute | solution.py:518
  29.1 0.4 %upper_columns.1 = (f32[1920,128]{1,0:T(8,128)S(1)}, f32[48,1280]{1,0:T(8,128)S(1)}, f32[48,1280]{1,0:T(8,128)S(1)}) custom-call(f32[1920,128]{1,0:T(8,128)S(1)} %get-tuple-element.46.high, f32[1920,128]{1,0:T(8,128)S(1)} %get-tuple-element.47.ratio, f32[1920,128]{1,0:T(8,128)S(1)} %get-tuple-element.48.low, f32[96,1280]{1,0:T(8,128)S(1)} %get-tuple-element.49.links), custom_call_target="tpu_custom_call" | custom-call | flops 1 | bytes 1 | tf_op jit(solution)/shard_map/upper_columns/pallas_call | solution.py:571
  29.5 0.0 collective-permute-done.2.refs_0_.kept
  29.5 1.6 %inner_high.1 = (f32[128,1280]{1,0:T(8,128)S(1)}, f32[48,1280]{1,0:T(8,128)S(1)}) custom-call(f32[1920,128]{1,0:T(8,128)S(1)} %get-tuple-element.50.high, f32[1920,128]{1,0:T(8,128)S(1)} %get-tuple-element.48.low, s32[8,1280]{1,0:T(8,128)S(1)} %get-tuple-element.51.kmt, f32[384,1280]{1,0:T(8,128)S(1)} %get-tuple-element.52.kappa, ...), custom_call_target="tpu_custom_call" | custom-call | flops 1 | bytes 1 | tf_op jit(solution)/shard_map/inner_high/pallas_call | solution.py:577
  31.1 1.3 %collective-permute-start.6 = (f32[48,1280]{1,0:T(8,128)S(1)}, f32[48,1280]{1,0:T(8,128)S(1)}, u32[]{:S(2)}, u32[]{:S(2)}) collective-permute-start(f32[48,1280]{1,0:T(8,128)S(1)} %get-tuple-element.60), channel_id=1, source_target_pairs={{0,16},{16,0},{1,17},{17,1},{2,18},{18,2},{3,19},{19,3},{4,20},{20... | collective-permute-start | bytes 737288 | tf_op jit(solution)/shard_map/ppermute | solution.py:518
  32.4 0.0 collective-permute-start.3
  32.4 0.0 collective-permute-done.7.near
  32.4 0.0 copy-start
  32.4 3.9 %collective-permute-start.4 = (f32[48,1280]{1,0:T(8,128)S(1)}, f32[48,1280]{1,0:T(8,128)S(1)}, u32[]{:S(2)}, u32[]{:S(2)}) collective-permute-start(f32[48,1280]{1,0:T(8,128)S(1)} %get-tuple-element.57.own_far), channel_id=1, source_target_pairs={{1,2},{3,4},{5,6},{7,8},{9,10},{11,12},{13,14},{2,1},{4,3},{6,5},{... | collective-permute-start | bytes 737288 | tf_op jit(solution)/shard_map/ppermute | solution.py:518
  36.3 3.1 %inner_low.1.u2_low = f32[256,1280]{1,0:T(8,128)S(1)} custom-call(f32[1920,128]{1,0:T(8,128)S(1)} %get-tuple-element.50.high, f32[1920,128]{1,0:T(8,128)S(1)} %get-tuple-element.48.low, s32[8,1280]{1,0:T(8,128)S(1)} %get-tuple-element.51.kmt, f32[384,1280]{1,0:T(8,128)S(1)} %get-tuple-element.52.kappa, s32[384,1280]{1,0:T(8,128)S(1)} %get-tuple-element.53.land), custom_call_target="tpu_custom_call" | custom-call | flops 1 | bytes 1 | tf_op jit(solution)/shard_map/inner_low/pallas_call | solution.py:577
  39.4 0.0 collective-permute-done.8.far
  39.5 0.0 collective-permute-done.6.swapped
  39.5 0.0 collective-permute-done.5.rim_other_near
  39.5 0.0 copy-done
  39.5 1.4 %finish_low.1.refs_0_ = f32[384,1280]{1,0:T(8,128)} custom-call(f32[128,1280]{1,0:T(8,128)S(1)} %get-tuple-element.55.u2_high, f32[256,1280]{1,0:T(8,128)S(1)} %inner_low.1.u2_low, f32[192,1280]{1,0:T(8,128)S(1)} %copy-done, f32[48,1280]{1,0:T(8,128)S(1)} %get-tuple-element.61.own_near, f32[48,1280]{1,0:T(8,128)S(1)} %get-tuple-element.62.own_far, ...), custom_call_target="tpu_custom_call" | custom-call | flops 1 | bytes 1 | tf_op jit(solution)/shard_map/finish_low/pallas_call | solution.py:597
  40.8 0.0 collective-permute-done.3.near
  40.9 1.2 %collective-permute-done.4.far = f32[48,1280]{1,0:T(8,128)S(1)} collective-permute-done((f32[48,1280]{1,0:T(8,128)S(1)}, f32[48,1280]{1,0:T(8,128)S(1)}, u32[]{:S(2)}, u32[]{:S(2)}) %collective-permute-start.4) | collective-permute-done | bytes 245792 | tf_op jit(solution)/shard_map/ppermute | solution.py:518
  42.1 1.3 %finish_high.1 = f32[384,1280]{1,0:T(8,128)} custom-call(f32[128,1280]{1,0:T(8,128)S(1)} %get-tuple-element.55.u2_high, f32[256,1280]{1,0:T(8,128)S(1)} %inner_low.1.u2_low, f32[96,1280]{1,0:T(8,128)S(1)} %get-tuple-element.49.links, f32[48,1280]{1,0:T(8,128)S(1)} %get-tuple-element.56.own_near, ...), custom_call_target="tpu_custom_call", output_to_operand_aliasing={{}: (12, {})} | custom-call | flops 1 | bytes 1 | tf_op jit(solution)/shard_map/finish_high/pallas_call | solution.py:600
Async XLA Ops:
  2.6 7.6 %collective-permute-start = (f32[8,1280]{1,0:T(8,128)S(1)}, f32[8,1280]{1,0:T(8,128)S(1)}, u32[]{:S(2)}, u32[]{:S(2)}) collective-permute-start(f32[8,1280]{1,0:T(8,128)S(1)} %get-tuple-element.40), channel_id=1, source_target_pairs={{0,1},{2,3},{4,5},{6,7},{8,9},{10,11},{12,13},{14,15},{1,0},{3,2},... | collective-permute-start | bytes 122888 | tf_op jit(solution)/shard_map/ppermute | solution.py:518
  2.7 7.5 %collective-permute-start.1 = (f32[8,1280]{1,0:T(8,128)S(1)}, f32[8,1280]{1,0:T(8,128)S(1)}, u32[]{:S(2)}, u32[]{:S(2)}) collective-permute-start(f32[8,1280]{1,0:T(8,128)S(1)} %get-tuple-element.41), channel_id=1, source_target_pairs={{1,2},{3,4},{5,6},{7,8},{9,10},{11,12},{13,14},{2,1},{4,3},{6,5},{... | collective-permute-start | bytes 122888 | tf_op jit(solution)/shard_map/ppermute | solution.py:518
  11.2 11.0 %all-to-all-start = ((f32[16,1,128]{2,1,0:T(1,128)}), f32[16,1,128]{2,1,0:T(1,128)S(1)}, u32[]{:S(2)}, u32[]{:S(2)}) async-start(f32[16,1,128]{2,1,0:T(1,128)} %bitcast.3), calls=%async_computation | async-start | bytes 16384 | tf_op jit(solution)/shard_map/all_to_all | solution.py:556
  16.5 13.0 %collective-permute-start.2 = (f32[48,1280]{1,0:T(8,128)S(1)}, f32[48,1280]{1,0:T(8,128)S(1)}, u32[]{:S(2)}, u32[]{:S(2)}) collective-permute-start(f32[48,1280]{1,0:T(8,128)S(1)} %get-tuple-element.54), channel_id=1, source_target_pairs={{1,2},{3,4},{5,6},{7,8},{9,10},{11,12},{13,14},{2,1},{4,3},{6,5},{... | collective-permute-start | bytes 737288 | tf_op jit(solution)/shard_map/ppermute | solution.py:518
  20.0 19.4 %collective-permute-start.5 = (f32[96,1280]{1,0:T(8,128)S(1)}, f32[96,1280]{1,0:T(8,128)S(1)}, u32[]{:S(2)}, u32[]{:S(2)}) collective-permute-start(f32[96,1280]{1,0:T(8,128)S(1)} %get-tuple-element.58.rim_near), channel_id=1, source_target_pairs={{0,1},{2,3},{4,5},{6,7},{8,9},{10,11},{12,13},{14,15},{1,0},{3,2},... | collective-permute-start | bytes 1474568 | tf_op jit(solution)/shard_map/ppermute | solution.py:518
  26.2 6.1 %collective-permute-start.7 = (f32[48,1280]{1,0:T(8,128)S(1)}, f32[48,1280]{1,0:T(8,128)S(1)}, u32[]{:S(2)}, u32[]{:S(2)}) collective-permute-start(f32[48,1280]{1,0:T(8,128)S(1)} %get-tuple-element.61.own_near), channel_id=1, source_target_pairs={{0,1},{2,3},{4,5},{6,7},{8,9},{10,11},{12,13},{14,15},{1,0},{3,2},... | collective-permute-start | bytes 737288 | tf_op jit(solution)/shard_map/ppermute | solution.py:518
  27.0 12.4 %collective-permute-start.8 = (f32[48,1280]{1,0:T(8,128)S(1)}, f32[48,1280]{1,0:T(8,128)S(1)}, u32[]{:S(2)}, u32[]{:S(2)}) collective-permute-start(f32[48,1280]{1,0:T(8,128)S(1)} %get-tuple-element.62.own_far), channel_id=1, source_target_pairs={{1,2},{3,4},{5,6},{7,8},{9,10},{11,12},{13,14},{2,1},{4,3},{6,5},{... | collective-permute-start | bytes 737288 | tf_op jit(solution)/shard_map/ppermute | solution.py:518
  31.1 8.4 %collective-permute-start.6 = (f32[48,1280]{1,0:T(8,128)S(1)}, f32[48,1280]{1,0:T(8,128)S(1)}, u32[]{:S(2)}, u32[]{:S(2)}) collective-permute-start(f32[48,1280]{1,0:T(8,128)S(1)} %get-tuple-element.60), channel_id=1, source_target_pairs={{0,16},{16,0},{1,17},{17,1},{2,18},{18,2},{3,19},{19,3},{4,20},{20... | collective-permute-start | bytes 737288 | tf_op jit(solution)/shard_map/ppermute | solution.py:518
  32.4 8.5 %collective-permute-start.3 = (f32[48,1280]{1,0:T(8,128)S(1)}, f32[48,1280]{1,0:T(8,128)S(1)}, u32[]{:S(2)}, u32[]{:S(2)}) collective-permute-start(f32[48,1280]{1,0:T(8,128)S(1)} %get-tuple-element.56.own_near), channel_id=1, source_target_pairs={{0,1},{2,3},{4,5},{6,7},{8,9},{10,11},{12,13},{14,15},{1,0},{3,2},... | collective-permute-start | bytes 737288 | tf_op jit(solution)/shard_map/ppermute | solution.py:518
  32.4 7.1 %copy-start = (f32[192,1280]{1,0:T(8,128)S(1)}, f32[192,1280]{1,0:T(8,128)}, u32[]{:S(2)}) copy-start(f32[192,1280]{1,0:T(8,128)} %get-tuple-element.43.links_hbm.links) | copy-start | bytes 2949124
  32.4 9.7 %collective-permute-start.4 = (f32[48,1280]{1,0:T(8,128)S(1)}, f32[48,1280]{1,0:T(8,128)S(1)}, u32[]{:S(2)}, u32[]{:S(2)}) collective-permute-start(f32[48,1280]{1,0:T(8,128)S(1)} %get-tuple-element.57.own_far), channel_id=1, source_target_pairs={{1,2},{3,4},{5,6},{7,8},{9,10},{11,12},{13,14},{2,1},{4,3},{6,5},{... | collective-permute-start | bytes 737288 | tf_op jit(solution)/shard_map/ppermute | solution.py:518

commit v13 on v11

--- a/solution.py
+++ b/solution.py
@@ -402,14 +402,10 @@
         copy.wait()
 
 
-def inner_body(first, last, with_relay, u0, kmt_hbm, kappa_hbm, land_hbm, *refs):
-    if with_relay:
-        passed, u2_ref, relay_ref = refs[:3]
-        relay_ref[...] = passed[...]
-        refs = refs[3:]
-    else:
-        u2_ref, refs = refs[0], refs[1:]
-    kmt, kappa, land, sems = refs
+def inner_body(first, last, relays, u0, kmt_hbm, kappa_hbm, land_hbm, *refs):
+    passed, (u2_ref, *relayed), (kmt, kappa, land, sems) = refs[:relays], refs[relays : 2 * relays + 1], refs[-4:]
+    for source, target in zip(passed, relayed):
+        target[...] = source[...]
     size = PART * ROWS
     parts = (last - first) // PART
     kmt_copy = loads([(kmt_hbm, kmt)], sems)[0]
@@ -540,18 +536,19 @@
         [scalars, tile_ints, whole, whole, ints, pltpu.VMEM(link_rows, FLOAT), tiles, bricks, semaphores((15,)),
          semaphores((1,))],
     )(sums, basis, layer_weight, kmt, ct_tracer, kvert, land, links)
-    other_near, other_far = exchange(row_near, row_far)
+    other_far = swap(row_far, 1)
 
     def inner(first, last, name, *relayed):
         size = ((last - first) * rows, width)
         return kernel(
-            functools.partial(inner_body, first, last, bool(relayed)), vmem(size, *[(levels, width) for _ in relayed]),
+            functools.partial(inner_body, first, last, len(relayed)), vmem(size, *[array.shape for array in relayed]),
             in_vmem(1) + in_hbm(3) + in_vmem(len(relayed)), in_vmem(1 + len(relayed)), name,
             [tile_ints, pltpu.VMEM(size, FLOAT), pltpu.VMEM(size, jnp.int32), semaphores((1 + 2 * (last - first) // PART,))],
         )(u0, kmt, kappa, land, *relayed)
 
-    u2_high, relayed = inner(0, BEFORE_SWAP, "inner_high", kept)
-    swapped = swap(relayed, 0, "grp")
+    u2_high, kept_on, near_on = inner(0, BEFORE_SWAP, "inner_high", kept, row_near)
+    swapped = swap(kept_on, 0, "grp")
+    other_near = swap(near_on, 0)
     (u2_low,) = inner(BEFORE_SWAP, levels, "inner_low")
 
     values = kernel(

time: 43 us -> 50.1 us (1.17)
  waiting for transfers between devices: 4.85 us -> 11.2 us
  starting transfers between devices: 17.6 us -> 18.6 us
    all_to_all x1, waiting for transfers between devices: 2.09 us -> 5.54 us  [body(): lax.all_to_all(sums.reshape(count, 1, 128), 'tile', 0, 0, tiled=True)]
    ppermute x7, waiting for transfers between devices: 2.76 us -> 5.69 us  [swap(): lax.ppermute(array, axis, [(i, i + 1) for i in firsts] + [(i + 1, i) for...]
    all_to_all x1, starting transfers between devices: 5.32 us -> 6.19 us  [body(): lax.all_to_all(sums.reshape(count, 1, 128), 'tile', 0, 0, tiled=True)]
  transfers between devices with their start and end apart: 8 -> 8, of which waited for: 3 -> 4; matrix products, arithmetic and copies ran while one was open for 0% -> 0% of each run, Pallas kernels for 34% -> 25%
where the time goes in v13:
time: 50.1 us; the launch traced here: 49.6 us
  Pallas kernels  19 us (38%)
  starting transfers between devices  18.6 us (37%)
  waiting for transfers between devices  11.2 us (22%)
  between operations  0.75 us (1%)
    ppermute x7, starting transfers between devices, swap(): lax.ppermute(array, axis, [(i, i + 1) for i in firsts] + [(i + 1, i) for...  12.4 us
    pallas_call x2, Pallas kernels, inner(): kernel(functools.partial(inner_body, first, last, len(relayed)), vmem(siz...  6.95 us
    all_to_all x1, starting transfers between devices, body(): lax.all_to_all(sums.reshape(count, 1, 128), 'tile', 0, 0, tiled=True)  6.19 us
    ppermute x7, waiting for transfers between devices, swap(): lax.ppermute(array, axis, [(i, i + 1) for i in firsts] + [(i + 1, i) for...  5.69 us
    all_to_all x1, waiting for transfers between devices, body(): lax.all_to_all(sums.reshape(count, 1, 128), 'tile', 0, 0, tiled=True)  5.54 us
    pallas_call x1, Pallas kernels, body(): kernel(functools.partial(columns_body, levels), hbm(tile) + vmem(brick, r...  4.39 us
    pallas_call x1, Pallas kernels, body(): kernel(functools.partial(rims_body, levels), vmem(rim, rim, (levels, widt...  3 us
    pallas_call x1, Pallas kernels, body(): kernel(functools.partial(setup_body, levels), vmem(*[tile] * 9, brick), i...  1.97 us
  transfers between devices with their start and end apart: 8, of which 4 were waited for; matrix products, arithmetic and copies ran while one was open for 0% of the time, Pallas kernels for 25%

profile of v13, /device:TPU:1, one launch (start us, length us, event | category | flops | bytes accessed | tf_op | source)
XLA Modules:
  0.0 49.6 jit_solution(2570077364778590485)
XLA Ops:
  0.6 2.0 %setup.1 = (f32[8,1280]{1,0:T(8,128)S(1)}, f32[8,1280]{1,0:T(8,128)S(1)}, f32[8,1280]{1,0:T(8,128)S(1)}, f32[8,1280]{1,0:T(8,128)S(1)}, f32[8,1280]{1,0:T(8,128)...) custom-call(f32[48]{0:T(128)} %weight_hbm.3, ...), custom_call_target="tpu_custom_call" | custom-call | flops 1 | bytes 1 | tf_op jit(solution)/shard_map/setup/pallas_call | solution.py:514
  2.6 3.0 %rims.1 = (f32[96,1280]{1,0:T(8,128)S(1)}, f32[96,1280]{1,0:T(8,128)S(1)}, f32[48,1280]{1,0:T(8,128)S(1)}, f32[192,1280]{1,0:T(8,128)}) custom-call(f32[384,1280]{1,0:T(8,128)} %bitcast.14, f32[3840,128]{1,0:T(8,128)S(1)} %get-tuple-element.34.wet_bricks), custom_call_target="tpu_custom_call" | custom-call | flops 1 | bytes 1 | tf_op jit(solution)/shard_map/rims/pallas_call | solution.py:520
  5.6 4.5 %collective-permute-start.2 = (f32[48,1280]{1,0:T(8,128)S(1)}, f32[48,1280]{1,0:T(8,128)S(1)}, u32[]{:S(2)}, u32[]{:S(2)}) collective-permute-start(f32[48,1280]{1,0:T(8,128)S(1)} %get-tuple-element.39), channel_id=1, source_target_pairs={{1,2},{3,4},{5,6},{7,8},{9,10},{11,12},{13,14},{2,1},{4,3},{6,5},{... | collective-permute-start | bytes 737288 | tf_op jit(solution)/shard_map/ppermute | solution.py:493
  10.2 0.1 collective-permute-start
  10.2 3.5 %collective-permute-start.1 = (f32[8,1280]{1,0:T(8,128)S(1)}, f32[8,1280]{1,0:T(8,128)S(1)}, u32[]{:S(2)}, u32[]{:S(2)}) collective-permute-start(f32[8,1280]{1,0:T(8,128)S(1)} %get-tuple-element.33), channel_id=1, source_target_pairs={{1,2},{3,4},{5,6},{7,8},{9,10},{11,12},{13,14},{2,1},{4,3},{6,5},{... | collective-permute-start | bytes 122888 | tf_op jit(solution)/shard_map/ppermute | solution.py:493
  13.8 0.0 collective-permute-done.near
  13.8 3.0 %collective-permute-done.1.far = f32[8,1280]{1,0:T(8,128)S(1)} collective-permute-done((f32[8,1280]{1,0:T(8,128)S(1)}, f32[8,1280]{1,0:T(8,128)S(1)}, u32[]{:S(2)}, u32[]{:S(2)}) %collective-permute-start.1) | collective-permute-done | bytes 40992 | tf_op jit(solution)/shard_map/ppermute | solution.py:493
  16.8 0.9 %basis.1 = (f32[24,1280]{1,0:T(8,128)S(1)}, f32[16,128]{1,0:T(8,128)}) custom-call(f32[8,1280]{1,0:T(8,128)S(1)} %get-tuple-element.25.ct, f32[8,1280]{1,0:T(8,128)S(1)} %get-tuple-element.26.height, f32[8,1280]{1,0:T(8,128)S(1)} %get-tuple-element.27.surface, f32[8,1280]{1,0:T(8,128)S(1)} %get-tuple-element.28.fx_ref, ...), custom_call_target="tpu_custom_call" | custom-call | flops 1 | bytes 1 | tf_op jit(solution)/shard_map/basis/pallas_call | solution.py:527
  17.7 6.2 %all-to-all-start = ((f32[16,1,128]{2,1,0:T(1,128)}), f32[16,1,128]{2,1,0:T(1,128)S(1)}, u32[]{:S(2)}, u32[]{:S(2)}) async-start(f32[16,1,128]{2,1,0:T(1,128)} %bitcast.3), calls=%async_computation | async-start | bytes 16384 | tf_op jit(solution)/shard_map/all_to_all | solution.py:531
  23.9 0.2 collective-permute-start.5
  24.1 5.5 %all-to-all-done = f32[16,1,128]{2,1,0:T(1,128)S(1)} async-done(((f32[16,1,128]{2,1,0:T(1,128)}), f32[16,1,128]{2,1,0:T(1,128)S(1)}, u32[]{:S(2)}, u32[]{:S(2)}) %all-to-all-start) | async-done | bytes 8224 | tf_op jit(solution)/shard_map/all_to_all | solution.py:531
  29.6 4.4 %columns.1 = (f32[8,1280]{1,0:T(8,128)}, f32[3840,128]{1,0:T(8,128)S(1)}, f32[96,1280]{1,0:T(8,128)S(1)}, f32[96,1280]{1,0:T(8,128)S(1)}) custom-call(f32[16,128]{1,0:T(8,128)S(1)} %bitcast.9, f32[24,1280]{1,0:T(8,128)S(1)} %get-tuple-element.37.basis_ref, f32[48]{0:T(128)} %weight_hbm.3, s32[8,1280]{1,0:T(8,128)} %kmt_hbm.7, f32[384,1280]{1,0:T(8,128)} %bitcast.17, ...), custom_call_target="tpu_custom_call" | custom-call | flops 1 | bytes 1 | tf_op jit(solution)/shard_map/columns/pallas_call | solution.py:533
  34.0 2.7 %collective-permute-start.4 = (f32[96,1280]{1,0:T(8,128)S(1)}, f32[96,1280]{1,0:T(8,128)S(1)}, u32[]{:S(2)}, u32[]{:S(2)}) collective-permute-start(f32[96,1280]{1,0:T(8,128)S(1)} %get-tuple-element.42.own_far), channel_id=1, source_target_pairs={{1,2},{3,4},{5,6},{7,8},{9,10},{11,12},{13,14},{2,1},{4,3},{6,5},{... | collective-permute-start | bytes 1474568 | tf_op jit(solution)/shard_map/ppermute | solution.py:493
  36.7 0.0 collective-permute-done.2.refs_0_.kept
  36.8 2.7 %inner_high.1 = (f32[128,1280]{1,0:T(8,128)S(1)}, f32[48,1280]{1,0:T(8,128)S(1)}, f32[96,1280]{1,0:T(8,128)S(1)}) custom-call(f32[3840,128]{1,0:T(8,128)S(1)} %get-tuple-element.38.u0, s32[8,1280]{1,0:T(8,128)} %kmt_hbm.7, f32[384,1280]{1,0:T(8,128)} %bitcast.15, s32[384,1280]{1,0:T(8,128)} %bitcast.12, f32[48,1280]{1,0:T(8,128)S(1)} %collective-permute-done.2.refs_0_.kept, ...), custom_call_target="tpu_custom_call" | custom-call | flops 1 | bytes 1 | tf_op jit(solution)/shard_map/inner_high/pallas_call | solution.py:543
  39.4 0.1 collective-permute-start.3
  39.5 0.0 copy-start
  39.5 1.3 %collective-permute-start.6 = (f32[48,1280]{1,0:T(8,128)S(1)}, f32[48,1280]{1,0:T(8,128)S(1)}, u32[]{:S(2)}, u32[]{:S(2)}) collective-permute-start(f32[48,1280]{1,0:T(8,128)S(1)} %get-tuple-element.46), channel_id=1, source_target_pairs={{0,16},{16,0},{1,17},{17,1},{2,18},{18,2},{3,19},{19,3},{4,20},{20... | collective-permute-start | bytes 737288 | tf_op jit(solution)/shard_map/ppermute | solution.py:493
  40.8 4.3 %inner_low.1.u2_low = f32[256,1280]{1,0:T(8,128)S(1)} custom-call(f32[3840,128]{1,0:T(8,128)S(1)} %get-tuple-element.38.u0, s32[8,1280]{1,0:T(8,128)} %kmt_hbm.7, f32[384,1280]{1,0:T(8,128)} %bitcast.16, s32[384,1280]{1,0:T(8,128)} %bitcast.13), custom_call_target="tpu_custom_call" | custom-call | flops 1 | bytes 1 | tf_op jit(solution)/shard_map/inner_low/pallas_call | solution.py:543
  45.1 0.0 collective-permute-done.5.rim_other_near
  45.1 1.6 %collective-permute-done.6.swapped = f32[48,1280]{1,0:T(8,128)S(1)} collective-permute-done((f32[48,1280]{1,0:T(8,128)S(1)}, f32[48,1280]{1,0:T(8,128)S(1)}, u32[]{:S(2)}, u32[]{:S(2)}) %collective-permute-start.6) | collective-permute-done | bytes 245792 | tf_op jit(solution)/shard_map/ppermute | solution.py:493
  46.7 1.1 %collective-permute-done.4.far = f32[96,1280]{1,0:T(8,128)S(1)} collective-permute-done((f32[96,1280]{1,0:T(8,128)S(1)}, f32[96,1280]{1,0:T(8,128)S(1)}, u32[]{:S(2)}, u32[]{:S(2)}) %collective-permute-start.4) | collective-permute-done | bytes 491552 | tf_op jit(solution)/shard_map/ppermute | solution.py:493
  47.8 0.0 collective-permute-done.3.near
  47.8 0.0 copy-done
  47.8 1.8 %finish.1 = f32[384,1280]{1,0:T(8,128)} custom-call(f32[128,1280]{1,0:T(8,128)S(1)} %get-tuple-element.41.u2_high, f32[256,1280]{1,0:T(8,128)S(1)} %inner_low.1.u2_low, f32[192,1280]{1,0:T(8,128)S(1)} %copy-done, f32[96,1280]{1,0:T(8,128)S(1)} %get-tuple-element.40.refs_1_.own_near, f32[96,1280]{1,0:T(8,128)S(1)} %get-tuple-element.42.own_far, ...), custom_call_target="tpu_custom_call" | custom-call | flops 1 | bytes 1 | tf_op jit(solution)/shard_map/finish/pallas_call | solution.py:554
Async XLA Ops:
  5.6 31.1 %collective-permute-start.2 = (f32[48,1280]{1,0:T(8,128)S(1)}, f32[48,1280]{1,0:T(8,128)S(1)}, u32[]{:S(2)}, u32[]{:S(2)}) collective-permute-start(f32[48,1280]{1,0:T(8,128)S(1)} %get-tuple-element.39), channel_id=1, source_target_pairs={{1,2},{3,4},{5,6},{7,8},{9,10},{11,12},{13,14},{2,1},{4,3},{6,5},{... | collective-permute-start | bytes 737288 | tf_op jit(solution)/shard_map/ppermute | solution.py:493
  10.2 3.6 %collective-permute-start = (f32[8,1280]{1,0:T(8,128)S(1)}, f32[8,1280]{1,0:T(8,128)S(1)}, u32[]{:S(2)}, u32[]{:S(2)}) collective-permute-start(f32[8,1280]{1,0:T(8,128)S(1)} %get-tuple-element.32), channel_id=1, source_target_pairs={{0,1},{2,3},{4,5},{6,7},{8,9},{10,11},{12,13},{14,15},{1,0},{3,2},... | collective-permute-start | bytes 122888 | tf_op jit(solution)/shard_map/ppermute | solution.py:493
  10.2 6.6 %collective-permute-start.1 = (f32[8,1280]{1,0:T(8,128)S(1)}, f32[8,1280]{1,0:T(8,128)S(1)}, u32[]{:S(2)}, u32[]{:S(2)}) collective-permute-start(f32[8,1280]{1,0:T(8,128)S(1)} %get-tuple-element.33), channel_id=1, source_target_pairs={{1,2},{3,4},{5,6},{7,8},{9,10},{11,12},{13,14},{2,1},{4,3},{6,5},{... | collective-permute-start | bytes 122888 | tf_op jit(solution)/shard_map/ppermute | solution.py:493
  17.7 11.9 %all-to-all-start = ((f32[16,1,128]{2,1,0:T(1,128)}), f32[16,1,128]{2,1,0:T(1,128)S(1)}, u32[]{:S(2)}, u32[]{:S(2)}) async-start(f32[16,1,128]{2,1,0:T(1,128)} %bitcast.3), calls=%async_computation | async-start | bytes 16384 | tf_op jit(solution)/shard_map/all_to_all | solution.py:531
  23.9 21.2 %collective-permute-start.5 = (f32[96,1280]{1,0:T(8,128)S(1)}, f32[96,1280]{1,0:T(8,128)S(1)}, u32[]{:S(2)}, u32[]{:S(2)}) collective-permute-start(f32[96,1280]{1,0:T(8,128)S(1)} %get-tuple-element.43.rim_near), channel_id=1, source_target_pairs={{0,1},{2,3},{4,5},{6,7},{8,9},{10,11},{12,13},{14,15},{1,0},{3,2},... | collective-permute-start | bytes 1474568 | tf_op jit(solution)/shard_map/ppermute | solution.py:493
  34.0 13.8 %collective-permute-start.4 = (f32[96,1280]{1,0:T(8,128)S(1)}, f32[96,1280]{1,0:T(8,128)S(1)}, u32[]{:S(2)}, u32[]{:S(2)}) collective-permute-start(f32[96,1280]{1,0:T(8,128)S(1)} %get-tuple-element.42.own_far), channel_id=1, source_target_pairs={{1,2},{3,4},{5,6},{7,8},{9,10},{11,12},{13,14},{2,1},{4,3},{6,5},{... | collective-permute-start | bytes 1474568 | tf_op jit(solution)/shard_map/ppermute | solution.py:493
  39.4 8.3 %collective-permute-start.3 = (f32[96,1280]{1,0:T(8,128)S(1)}, f32[96,1280]{1,0:T(8,128)S(1)}, u32[]{:S(2)}, u32[]{:S(2)}) collective-permute-start(f32[96,1280]{1,0:T(8,128)S(1)} %get-tuple-element.45), channel_id=1, source_target_pairs={{0,1},{2,3},{4,5},{6,7},{8,9},{10,11},{12,13},{14,15},{1,0},{3,2},... | collective-permute-start | bytes 1474568 | tf_op jit(solution)/shard_map/ppermute | solution.py:493
  39.5 8.2 %copy-start = (f32[192,1280]{1,0:T(8,128)S(1)}, f32[192,1280]{1,0:T(8,128)}, u32[]{:S(2)}) copy-start(f32[192,1280]{1,0:T(8,128)} %get-tuple-element.35.links_hbm.links) | copy-start | bytes 2949124
  39.5 7.2 %collective-permute-start.6 = (f32[48,1280]{1,0:T(8,128)S(1)}, f32[48,1280]{1,0:T(8,128)S(1)}, u32[]{:S(2)}, u32[]{:S(2)}) collective-permute-start(f32[48,1280]{1,0:T(8,128)S(1)} %get-tuple-element.46), channel_id=1, source_target_pairs={{0,16},{16,0},{1,17},{17,1},{2,18},{18,2},{3,19},{19,3},{4,20},{20... | collective-permute-start | bytes 737288 | tf_op jit(solution)/shard_map/ppermute | solution.py:493

commit v14 on v11

--- a/solution.py
+++ b/solution.py
@@ -335,7 +335,7 @@
 def columns_body(levels, sums, basis_ref, weight_hbm, kmt_hbm, source_hbm, kvert_hbm, land_hbm, links_hbm,
                  out_hbm, u, near_ref, far_ref, weight, kmt, source, kvert, land, links, s_ref, ratio, sems, out_sems):
     width = source.shape[1]
-    parts = 4
+    parts = 8
     chunk = levels // parts
     small = loads(((weight_hbm, weight), (kmt_hbm, kmt)), sems)
     parted = [in_parts(far, near, parts) for far, near in ((land_hbm, land), (kvert_hbm, kvert), (source_hbm, source))]
@@ -377,7 +377,7 @@
         big[3 * i + 2].wait()
         if i + 1 < parts:
             big[3 * i + 3].wait()
-        carry = lax.fori_loop(i * chunk, (i + 1) * chunk, down, carry, unroll=4)
+        carry = lax.fori_loop(i * chunk, (i + 1) * chunk, down, carry, unroll=3)
 
     def up(i, below):
         at = level_at(levels - 1 - i, width)
@@ -537,7 +537,7 @@
     solution, u0, row_near, row_far = kernel(
         functools.partial(columns_body, levels), hbm(tile) + vmem(brick, rim, rim), in_vmem(2) + in_hbm(6),
         in_hbm(1) + in_vmem(3), "columns",
-        [scalars, tile_ints, whole, whole, ints, pltpu.VMEM(link_rows, FLOAT), tiles, bricks, semaphores((15,)),
+        [scalars, tile_ints, whole, whole, ints, pltpu.VMEM(link_rows, FLOAT), tiles, bricks, semaphores((27,)),
          semaphores((1,))],
     )(sums, basis, layer_weight, kmt, ct_tracer, kvert, land, links)
     other_near, other_far = exchange(row_near, row_far)

time: 43 us -> 43 us (level)
  no operation moved by 1% of the time
where the time goes in v14:
time: 43 us; the launch traced here: 42.3 us
  Pallas kernels  19 us (44%)
  starting transfers between devices  17.6 us (41%)
  waiting for transfers between devices  4.85 us (11%)
  between operations  0.75 us (2%)
    ppermute x7, starting transfers between devices, swap(): lax.ppermute(array, axis, [(i, i + 1) for i in firsts] + [(i + 1, i) for...  12.3 us
    pallas_call x2, Pallas kernels, inner(): kernel(functools.partial(inner_body, first, last, bool(relayed)), vmem(si...  6.95 us
    all_to_all x1, starting transfers between devices, body(): lax.all_to_all(sums.reshape(count, 1, 128), 'tile', 0, 0, tiled=True)  5.32 us
    pallas_call x1, Pallas kernels, body(): kernel(functools.partial(columns_body, levels), hbm(tile) + vmem(brick, r...  4.39 us
    pallas_call x1, Pallas kernels, body(): kernel(functools.partial(rims_body, levels), vmem(rim, rim, (levels, widt...  3 us
    ppermute x7, waiting for transfers between devices, swap(): lax.ppermute(array, axis, [(i, i + 1) for i in firsts] + [(i + 1, i) for...  2.76 us
    all_to_all x1, waiting for transfers between devices, body(): lax.all_to_all(sums.reshape(count, 1, 128), 'tile', 0, 0, tiled=True)  2.09 us
    pallas_call x1, Pallas kernels, body(): kernel(functools.partial(setup_body, levels), vmem(*[tile] * 9, brick), i...  1.97 us
  transfers between devices with their start and end apart: 8, of which 3 were waited for; matrix products, arithmetic and copies ran while one was open for 0% of the time, Pallas kernels for 34%

profile of v14, /device:TPU:1, one launch (start us, length us, event | category | flops | bytes accessed | tf_op | source)
XLA Modules:
  0.0 42.3 jit_solution(1093664705851987476)
XLA Ops:
  0.6 2.0 %setup.1 = (f32[8,1280]{1,0:T(8,128)S(1)}, f32[8,1280]{1,0:T(8,128)S(1)}, f32[8,1280]{1,0:T(8,128)S(1)}, f32[8,1280]{1,0:T(8,128)S(1)}, f32[8,1280]{1,0:T(8,128)...) custom-call(f32[48]{0:T(128)} %weight_hbm.3, ...), custom_call_target="tpu_custom_call" | custom-call | flops 1 | bytes 1 | tf_op jit(solution)/shard_map/setup/pallas_call | solution.py:518
  2.6 0.1 collective-permute-start
  2.7 4.5 %collective-permute-start.1 = (f32[8,1280]{1,0:T(8,128)S(1)}, f32[8,1280]{1,0:T(8,128)S(1)}, u32[]{:S(2)}, u32[]{:S(2)}) collective-permute-start(f32[8,1280]{1,0:T(8,128)S(1)} %get-tuple-element.32), channel_id=1, source_target_pairs={{1,2},{3,4},{5,6},{7,8},{9,10},{11,12},{13,14},{2,1},{4,3},{6,5},{... | collective-permute-start | bytes 122888 | tf_op jit(solution)/shard_map/ppermute | solution.py:497
  7.2 3.0 %rims.1 = (f32[96,1280]{1,0:T(8,128)S(1)}, f32[96,1280]{1,0:T(8,128)S(1)}, f32[48,1280]{1,0:T(8,128)S(1)}, f32[192,1280]{1,0:T(8,128)}) custom-call(f32[384,1280]{1,0:T(8,128)} %bitcast.14, f32[3840,128]{1,0:T(8,128)S(1)} %get-tuple-element.33.wet_bricks), custom_call_target="tpu_custom_call" | custom-call | flops 1 | bytes 1 | tf_op jit(solution)/shard_map/rims/pallas_call | solution.py:524
  10.2 0.0 collective-permute-done.near
  10.2 0.0 collective-permute-done.1.far
  10.3 0.9 %basis.1 = (f32[24,1280]{1,0:T(8,128)S(1)}, f32[16,128]{1,0:T(8,128)}) custom-call(f32[8,1280]{1,0:T(8,128)S(1)} %get-tuple-element.24.ct, f32[8,1280]{1,0:T(8,128)S(1)} %get-tuple-element.25.height, f32[8,1280]{1,0:T(8,128)S(1)} %get-tuple-element.26.surface, f32[8,1280]{1,0:T(8,128)S(1)} %get-tuple-element.27.fx_ref, ...), custom_call_target="tpu_custom_call" | custom-call | flops 1 | bytes 1 | tf_op jit(solution)/shard_map/basis/pallas_call | solution.py:531
  11.2 5.3 %all-to-all-start = ((f32[16,1,128]{2,1,0:T(1,128)}), f32[16,1,128]{2,1,0:T(1,128)S(1)}, u32[]{:S(2)}, u32[]{:S(2)}) async-start(f32[16,1,128]{2,1,0:T(1,128)} %bitcast.3), calls=%async_computation | async-start | bytes 16384 | tf_op jit(solution)/shard_map/all_to_all | solution.py:535
  16.5 3.5 %collective-permute-start.2 = (f32[48,1280]{1,0:T(8,128)S(1)}, f32[48,1280]{1,0:T(8,128)S(1)}, u32[]{:S(2)}, u32[]{:S(2)}) collective-permute-start(f32[48,1280]{1,0:T(8,128)S(1)} %get-tuple-element.38), channel_id=1, source_target_pairs={{1,2},{3,4},{5,6},{7,8},{9,10},{11,12},{13,14},{2,1},{4,3},{6,5},{... | collective-permute-start | bytes 737288 | tf_op jit(solution)/shard_map/ppermute | solution.py:497
  20.0 0.1 collective-permute-start.5
  20.1 2.1 %all-to-all-done = f32[16,1,128]{2,1,0:T(1,128)S(1)} async-done(((f32[16,1,128]{2,1,0:T(1,128)}), f32[16,1,128]{2,1,0:T(1,128)S(1)}, u32[]{:S(2)}, u32[]{:S(2)}) %all-to-all-start) | async-done | bytes 8224 | tf_op jit(solution)/shard_map/all_to_all | solution.py:535
  22.2 4.4 %columns.1 = (f32[8,1280]{1,0:T(8,128)}, f32[3840,128]{1,0:T(8,128)S(1)}, f32[96,1280]{1,0:T(8,128)S(1)}, f32[96,1280]{1,0:T(8,128)S(1)}) custom-call(f32[16,128]{1,0:T(8,128)S(1)} %bitcast.9, f32[24,1280]{1,0:T(8,128)S(1)} %get-tuple-element.36.basis_ref, f32[48]{0:T(128)} %weight_hbm.3, s32[8,1280]{1,0:T(8,128)} %kmt_hbm.7, f32[384,1280]{1,0:T(8,128)} %bitcast.17, ...), custom_call_target="tpu_custom_call" | custom-call | flops 1 | bytes 1 | tf_op jit(solution)/shard_map/columns/pallas_call | solution.py:537
  26.6 0.8 %collective-permute-start.3 = (f32[96,1280]{1,0:T(8,128)S(1)}, f32[96,1280]{1,0:T(8,128)S(1)}, u32[]{:S(2)}, u32[]{:S(2)}) collective-permute-start(f32[96,1280]{1,0:T(8,128)S(1)} %get-tuple-element.40.own_near), channel_id=1, source_target_pairs={{0,1},{2,3},{4,5},{6,7},{8,9},{10,11},{12,13},{14,15},{1,0},{3,2},... | collective-permute-start | bytes 1474568 | tf_op jit(solution)/shard_map/ppermute | solution.py:497
  27.4 2.0 %collective-permute-start.4 = (f32[96,1280]{1,0:T(8,128)S(1)}, f32[96,1280]{1,0:T(8,128)S(1)}, u32[]{:S(2)}, u32[]{:S(2)}) collective-permute-start(f32[96,1280]{1,0:T(8,128)S(1)} %get-tuple-element.41.own_far), channel_id=1, source_target_pairs={{1,2},{3,4},{5,6},{7,8},{9,10},{11,12},{13,14},{2,1},{4,3},{6,5},{... | collective-permute-start | bytes 1474568 | tf_op jit(solution)/shard_map/ppermute | solution.py:497
  29.4 0.0 collective-permute-done.2.refs_0_.kept
  29.4 2.7 %inner_high.1 = (f32[128,1280]{1,0:T(8,128)S(1)}, f32[48,1280]{1,0:T(8,128)S(1)}) custom-call(f32[3840,128]{1,0:T(8,128)S(1)} %get-tuple-element.37.u0, s32[8,1280]{1,0:T(8,128)} %kmt_hbm.7, f32[384,1280]{1,0:T(8,128)} %bitcast.15, s32[384,1280]{1,0:T(8,128)} %bitcast.12, f32[48,1280]{1,0:T(8,128)S(1)} %collective-permute-done.2.refs_0_.kept), custom_call_target="tpu_custom_call" | custom-call | flops 1 | bytes 1 | tf_op jit(solution)/shard_map/inner_high/pallas_call | solution.py:547
  32.1 0.0 copy-start
  32.1 1.3 %collective-permute-start.6 = (f32[48,1280]{1,0:T(8,128)S(1)}, f32[48,1280]{1,0:T(8,128)S(1)}, u32[]{:S(2)}, u32[]{:S(2)}) collective-permute-start(f32[48,1280]{1,0:T(8,128)S(1)} %get-tuple-element.44), channel_id=1, source_target_pairs={{0,16},{16,0},{1,17},{17,1},{2,18},{18,2},{3,19},{19,3},{4,20},{20... | collective-permute-start | bytes 737288 | tf_op jit(solution)/shard_map/ppermute | solution.py:497
  33.4 4.3 %inner_low.1.u2_low = f32[256,1280]{1,0:T(8,128)S(1)} custom-call(f32[3840,128]{1,0:T(8,128)S(1)} %get-tuple-element.37.u0, s32[8,1280]{1,0:T(8,128)} %kmt_hbm.7, f32[384,1280]{1,0:T(8,128)} %bitcast.16, s32[384,1280]{1,0:T(8,128)} %bitcast.13), custom_call_target="tpu_custom_call" | custom-call | flops 1 | bytes 1 | tf_op jit(solution)/shard_map/inner_low/pallas_call | solution.py:547
  37.7 0.0 collective-permute-done.5.rim_other_near
  37.7 1.3 %collective-permute-done.6.swapped = f32[48,1280]{1,0:T(8,128)S(1)} collective-permute-done((f32[48,1280]{1,0:T(8,128)S(1)}, f32[48,1280]{1,0:T(8,128)S(1)}, u32[]{:S(2)}, u32[]{:S(2)}) %collective-permute-start.6) | collective-permute-done | bytes 245792 | tf_op jit(solution)/shard_map/ppermute | solution.py:497
  39.0 0.0 collective-permute-done.3.near
  39.0 1.4 %collective-permute-done.4.far = f32[96,1280]{1,0:T(8,128)S(1)} collective-permute-done((f32[96,1280]{1,0:T(8,128)S(1)}, f32[96,1280]{1,0:T(8,128)S(1)}, u32[]{:S(2)}, u32[]{:S(2)}) %collective-permute-start.4) | collective-permute-done | bytes 491552 | tf_op jit(solution)/shard_map/ppermute | solution.py:497
  40.4 0.0 copy-done
  40.4 1.8 %finish.1 = f32[384,1280]{1,0:T(8,128)} custom-call(f32[128,1280]{1,0:T(8,128)S(1)} %get-tuple-element.39.u2_high, f32[256,1280]{1,0:T(8,128)S(1)} %inner_low.1.u2_low, f32[192,1280]{1,0:T(8,128)S(1)} %copy-done, f32[96,1280]{1,0:T(8,128)S(1)} %get-tuple-element.40.own_near, f32[96,1280]{1,0:T(8,128)S(1)} %get-tuple-element.41.own_far, ...), custom_call_target="tpu_custom_call" | custom-call | flops 1 | bytes 1 | tf_op jit(solution)/shard_map/finish/pallas_call | solution.py:557
Async XLA Ops:
  2.6 7.6 %collective-permute-start = (f32[8,1280]{1,0:T(8,128)S(1)}, f32[8,1280]{1,0:T(8,128)S(1)}, u32[]{:S(2)}, u32[]{:S(2)}) collective-permute-start(f32[8,1280]{1,0:T(8,128)S(1)} %get-tuple-element.31), channel_id=1, source_target_pairs={{0,1},{2,3},{4,5},{6,7},{8,9},{10,11},{12,13},{14,15},{1,0},{3,2},... | collective-permute-start | bytes 122888 | tf_op jit(solution)/shard_map/ppermute | solution.py:497
  2.7 7.5 %collective-permute-start.1 = (f32[8,1280]{1,0:T(8,128)S(1)}, f32[8,1280]{1,0:T(8,128)S(1)}, u32[]{:S(2)}, u32[]{:S(2)}) collective-permute-start(f32[8,1280]{1,0:T(8,128)S(1)} %get-tuple-element.32), channel_id=1, source_target_pairs={{1,2},{3,4},{5,6},{7,8},{9,10},{11,12},{13,14},{2,1},{4,3},{6,5},{... | collective-permute-start | bytes 122888 | tf_op jit(solution)/shard_map/ppermute | solution.py:497
  11.2 11.0 %all-to-all-start = ((f32[16,1,128]{2,1,0:T(1,128)}), f32[16,1,128]{2,1,0:T(1,128)S(1)}, u32[]{:S(2)}, u32[]{:S(2)}) async-start(f32[16,1,128]{2,1,0:T(1,128)} %bitcast.3), calls=%async_computation | async-start | bytes 16384 | tf_op jit(solution)/shard_map/all_to_all | solution.py:535
  16.5 12.9 %collective-permute-start.2 = (f32[48,1280]{1,0:T(8,128)S(1)}, f32[48,1280]{1,0:T(8,128)S(1)}, u32[]{:S(2)}, u32[]{:S(2)}) collective-permute-start(f32[48,1280]{1,0:T(8,128)S(1)} %get-tuple-element.38), channel_id=1, source_target_pairs={{1,2},{3,4},{5,6},{7,8},{9,10},{11,12},{13,14},{2,1},{4,3},{6,5},{... | collective-permute-start | bytes 737288 | tf_op jit(solution)/shard_map/ppermute | solution.py:497
  20.0 17.7 %collective-permute-start.5 = (f32[96,1280]{1,0:T(8,128)S(1)}, f32[96,1280]{1,0:T(8,128)S(1)}, u32[]{:S(2)}, u32[]{:S(2)}) collective-permute-start(f32[96,1280]{1,0:T(8,128)S(1)} %get-tuple-element.42.rim_near), channel_id=1, source_target_pairs={{0,1},{2,3},{4,5},{6,7},{8,9},{10,11},{12,13},{14,15},{1,0},{3,2},... | collective-permute-start | bytes 1474568 | tf_op jit(solution)/shard_map/ppermute | solution.py:497
  26.6 12.4 %collective-permute-start.3 = (f32[96,1280]{1,0:T(8,128)S(1)}, f32[96,1280]{1,0:T(8,128)S(1)}, u32[]{:S(2)}, u32[]{:S(2)}) collective-permute-start(f32[96,1280]{1,0:T(8,128)S(1)} %get-tuple-element.40.own_near), channel_id=1, source_target_pairs={{0,1},{2,3},{4,5},{6,7},{8,9},{10,11},{12,13},{14,15},{1,0},{3,2},... | collective-permute-start | bytes 1474568 | tf_op jit(solution)/shard_map/ppermute | solution.py:497
  27.4 13.1 %collective-permute-start.4 = (f32[96,1280]{1,0:T(8,128)S(1)}, f32[96,1280]{1,0:T(8,128)S(1)}, u32[]{:S(2)}, u32[]{:S(2)}) collective-permute-start(f32[96,1280]{1,0:T(8,128)S(1)} %get-tuple-element.41.own_far), channel_id=1, source_target_pairs={{1,2},{3,4},{5,6},{7,8},{9,10},{11,12},{13,14},{2,1},{4,3},{6,5},{... | collective-permute-start | bytes 1474568 | tf_op jit(solution)/shard_map/ppermute | solution.py:497
  32.1 8.3 %copy-start = (f32[192,1280]{1,0:T(8,128)S(1)}, f32[192,1280]{1,0:T(8,128)}, u32[]{:S(2)}) copy-start(f32[192,1280]{1,0:T(8,128)} %get-tuple-element.34.links_hbm.links) | copy-start | bytes 2949124
  32.1 6.9 %collective-permute-start.6 = (f32[48,1280]{1,0:T(8,128)S(1)}, f32[48,1280]{1,0:T(8,128)S(1)}, u32[]{:S(2)}, u32[]{:S(2)}) collective-permute-start(f32[48,1280]{1,0:T(8,128)S(1)} %get-tuple-element.44), channel_id=1, source_target_pairs={{0,16},{16,0},{1,17},{17,1},{2,18},{18,2},{3,19},{19,3},{4,20},{20... | collective-permute-start | bytes 737288 | tf_op jit(solution)/shard_map/ppermute | solution.py:497
